TPU v7x, 32 devices: a whole 2x2x4 slice. The times are simulated.
32 devices in a mesh: sect: 2 (over y), seq: 16 (over z, x, core).
Axes of the slice: x: 2, y: 2, z: 4, core: 2. Of those that a mesh axis runs over, the one named last changes fastest.
Arguments:
- queries: bfloat16 [1024, 2048], P('seq'), may hold values from -160 to 160
- key_tokens: bfloat16 [1024, 2048], P('seq'), may hold values from -6 to 6
- value_tokens: bfloat16 [1024, 2048], P('seq'), may hold values from -17 to 17
- latent: bfloat16 [64, 2560], P('seq'), may hold values from -6 to 6
- tile_rows: int32 [16], replicated, may hold values from 1 to 4, 32 in all
- conv_in_weight: bfloat16 [3, 3, 3, 16, 384], replicated, may hold values from -0.3125 to 0.3125
- conv_in_bias: float32 [384], replicated, may hold values from -3 to 3
- norm_gain: float32 [384], replicated, may hold values from 0.5 to 2
- conv_mid_weight: bfloat16 [3, 3, 3, 384, 384], replicated, may hold values from -0.0625 to 0.0625
- conv_mid_bias: float32 [384], replicated, may hold values from -3 to 3
Outputs:
- attended: bfloat16 [1024, 2048], P('seq', 'sect')
- frames: bfloat16 [2, 128, 80, 384], P(None, 'seq', 'sect')
Inputs may be any that keep to these rules, and one draw needn't show every extreme that they name: `tile_rows`: the tiles cover the 32 token rows in order; some tile has exactly 4 rows.
All inputs are finite; a program needn't handle non-finite values.
Results may differ from a plain program's by a relative error of at most 0.012.
Values may be sent and summed in bfloat16 or wider, within the bound.
No kernel may reach another device: no remote copies, remote signals or barrier semaphores. Data moves between devices by JAX's collectives and lax.ppermute only.
A program may use at most 128 MiB of HBM per device.

v0:
```python
import math

import jax
import jax.numpy as jnp
from jax import lax
from jax.sharding import PartitionSpec as P

DH = 128
LF = 2
MAXT = 4


def padded_2(block, sides, width):
    for axis, dim in sides:
        count = lax.axis_size(axis)
        forward = [(i, i + 1) for i in range(count - 1)]
        backward = [(target, source) for source, target in forward]
        low = lax.ppermute(
            lax.slice_in_dim(block, block.shape[dim] - width, None, axis=dim), axis, forward
        )
        high = lax.ppermute(lax.slice_in_dim(block, 0, width, axis=dim), axis, backward)
        block = jnp.concatenate([low, block, high], axis=dim)
    return block


def partner(array, axis, distance):
    return lax.ppermute(array, axis, [(i, i ^ 1 << distance) for i in range(lax.axis_size(axis))])


def head_attention(query_head, key_head, value_head):
    token_count = query_head.shape[0]
    block_rows = min(512, token_count)
    scale_factor = 1.0 / math.sqrt(query_head.shape[1])

    def one_block(query_block):
        scores = (
            lax.dot_general(
                query_block, key_head, (((1,), (1,)), ((), ())), preferred_element_type=jnp.float32
            )
            * scale_factor
        )
        exponents = jnp.exp(scores - jnp.max(scores, axis=1, keepdims=True))
        totals = jnp.sum(exponents, axis=1, keepdims=True)
        probabilities = exponents.astype(jnp.bfloat16)
        mixed = jnp.dot(probabilities, value_head, preferred_element_type=jnp.float32) / totals
        return mixed.astype(jnp.bfloat16)

    blocks = query_head.reshape(token_count // block_rows, block_rows, query_head.shape[1])
    return lax.map(one_block, blocks).reshape(token_count, query_head.shape[1])


def attend_heads(triple):
    query_heads, key_heads, value_heads = triple
    results = [head_attention(query_heads[:, 0, 0], key_heads[:, 0, 0], value_heads[:, 0, 0])]
    return jnp.stack(results, axis=1)[:, None]


def attend_tokens(queries, key_tokens, value_tokens):
    token_rows = queries.shape[0]
    devices = lax.axis_size("seq")
    heads_total = queries.shape[1] // DH
    heads_local = heads_total // devices
    query_heads = queries.reshape(token_rows, devices, heads_local, DH)
    key_heads = key_tokens.reshape(token_rows, devices, heads_local, DH)
    value_heads = value_tokens.reshape(token_rows, devices, heads_local, DH)
    per_head = attend_heads(
        (
            lax.all_to_all(query_heads, "seq", split_axis=1, concat_axis=0, tiled=True),
            lax.all_to_all(key_heads, "seq", split_axis=1, concat_axis=0, tiled=True),
            lax.all_to_all(value_heads, "seq", split_axis=1, concat_axis=0, tiled=True),
        )
    )
    returned = lax.all_to_all(per_head, "seq", split_axis=0, concat_axis=1, tiled=True)
    return returned.reshape(token_rows, heads_total * DH)


def causal_conv(extended, kernel, out_rows):
    frame_count, _, col_count, channels = extended.shape
    padded = jnp.pad(extended, ((2, 0), (0, 0), (1, 1), (0, 0)))
    summed = jnp.zeros((frame_count * out_rows * col_count, kernel.shape[4]), jnp.float32)
    for time_tap in range(3):
        for row_tap in range(3):
            strip = padded[time_tap : time_tap + frame_count, row_tap : row_tap + out_rows]
            stacked = jnp.concatenate(
                [strip[:, :, col_tap : col_tap + col_count] for col_tap in range(3)], axis=3
            )
            summed = summed + jnp.dot(
                stacked.reshape(-1, 3 * channels),
                kernel[time_tap, row_tap].reshape(3 * channels, -1),
                preferred_element_type=jnp.float32,
            )
    return summed.reshape(frame_count, out_rows, col_count, -1)


def activate(hidden, norm_gain):
    values_wide = hidden.astype(jnp.float32)
    scaled = (
        values_wide
        * lax.rsqrt(jnp.mean(values_wide * values_wide, axis=-1, keepdims=True) + 1e-06)
        * norm_gain
    )
    return jax.nn.silu(scaled).astype(jnp.bfloat16)


def rim_rows(field, depth, filled):
    leading = field[:, :depth]
    trailing = lax.dynamic_slice_in_dim(field, 2 * filled - depth, depth, 1)
    return jnp.concatenate([leading, trailing], axis=1)


def extend_rows(field, neighbours, depth, filled):
    lower_rows = neighbours[:, :depth]
    upper_rows = neighbours[:, 3 * depth :]
    padding = jnp.zeros((field.shape[0], depth) + field.shape[2:], field.dtype)
    joined = jnp.concatenate([lower_rows, field, padding], axis=1)
    return lax.dynamic_update_slice_in_dim(joined, upper_rows, depth + 2 * filled, 1)


def decode_tile(
    latent, tile_rows, conv_in_weight, conv_in_bias, norm_gain, conv_mid_weight, conv_mid_bias
):
    devices = lax.axis_size("seq")
    position = lax.axis_index("seq")
    channels = conv_in_weight.shape[3]
    row_width = latent.shape[1]
    columns = row_width // (4 * channels)
    grid_rows = latent.shape[0] * devices // LF
    tile_starts = jnp.cumsum(tile_rows) - tile_rows
    first_row = tile_starts[position]
    filled = tile_rows[position]
    slot_ids = jnp.arange(LF * MAXT, dtype=jnp.int32)
    piece = lax.all_gather(latent, "seq", axis=0, tiled=True)
    global_row = jnp.arange(piece.shape[0], dtype=jnp.int32)
    local_row = global_row % grid_rows - first_row
    target = jnp.where(
        (local_row >= 0) & (local_row < filled), global_row // grid_rows * MAXT + local_row, -1
    )
    selector = (slot_ids[:, None] == target[None, :]).astype(jnp.bfloat16)
    collected = jnp.dot(selector, piece, preferred_element_type=jnp.float32)
    tile_grid = collected.astype(jnp.bfloat16).reshape(LF, MAXT, columns, 2, 2, channels)
    tile_grid = tile_grid.transpose(0, 1, 3, 2, 4, 5).reshape(LF, 2 * MAXT, 2 * columns, channels)
    rows_total = 2 * MAXT
    neighbours = padded_2(rim_rows(tile_grid, 1, filled), (("seq", 1),), 1)
    hidden_first = (
        causal_conv(extend_rows(tile_grid, neighbours, 1, filled), conv_in_weight, rows_total)
        + conv_in_bias
    ).astype(jnp.bfloat16)
    activated = activate(hidden_first, norm_gain)
    hidden_edges = padded_2(rim_rows(activated, 1, filled), (("seq", 1),), 1)
    mixed = causal_conv(
        extend_rows(activated, hidden_edges, 1, filled), conv_mid_weight, rows_total
    )
    summed = mixed + conv_mid_bias + hidden_first.astype(jnp.float32)
    in_tile = jnp.arange(rows_total, dtype=jnp.int32) < 2 * filled
    return jnp.where(in_tile[None, :, None, None], summed, 0.0).astype(jnp.bfloat16)


def on_device(
    queries,
    key_tokens,
    value_tokens,
    latent,
    tile_rows,
    conv_in_weight,
    conv_in_bias,
    norm_gain,
    conv_mid_weight,
    conv_mid_bias,
):
    section = lax.axis_index("sect")
    other_section = 1 - section
    is_transformer = section == 0
    attended_own = attend_tokens(queries, key_tokens, value_tokens)
    frames_own = decode_tile(
        latent, tile_rows, conv_in_weight, conv_in_bias, norm_gain, conv_mid_weight, conv_mid_bias
    )
    half_width = attended_own.shape[1] // 2
    half_columns = frames_own.shape[2] // 2
    attended_keep = lax.dynamic_slice_in_dim(attended_own, section * half_width, half_width, 1)
    attended_send = lax.dynamic_slice_in_dim(
        attended_own, other_section * half_width, half_width, 1
    )
    frames_keep = lax.dynamic_slice_in_dim(frames_own, section * half_columns, half_columns, 2)
    frames_send = lax.dynamic_slice_in_dim(
        frames_own, other_section * half_columns, half_columns, 2
    )
    produced = (
        jnp.where(is_transformer, attended_send, jnp.zeros_like(attended_send)),
        jnp.where(is_transformer, jnp.zeros_like(frames_send), frames_send),
    )
    received = partner((produced[0], produced[1]), "sect", 0)
    attended_in = received[0]
    frames_in = received[1]
    attended = jnp.where(is_transformer, attended_keep, attended_in)
    frames = jnp.where(is_transformer, frames_in, frames_keep)
    return (attended, frames)


def solution(mesh):
    in_specs = (
        P("seq", None),
        P("seq", None),
        P("seq", None),
        P("seq", None),
        P(),
        P(),
        P(),
        P(),
        P(),
        P(),
    )
    out_specs = (P("seq", "sect"), P(None, "seq", "sect", None))
    return jax.shard_map(
        on_device, mesh=mesh, in_specs=in_specs, out_specs=out_specs, check_vma=False
    )
```

profile of v0, /device:TPU:0, one launch (start us, length us, event | category | flops | bytes accessed | tf_op | source)
XLA Modules:
  0.0 162.4 jit_solution(13743230720353231201)
XLA Ops:
  2.4 7.5 %all-to-all-start = ((bf16[64,16,1,128]{3,0,2,1:T(8,128)(2,1)}), bf16[64,16,1,128]{3,0,2,1:T(8,128)(2,1)S(1)}, u32[]{:S(2)}, u32[]{:S(2)}) async-start(bf16[64,16,1,128]{3,0,2,1:T(8,128)(2,1)} %copy.33), calls=%async_computation | async-start | bytes 524288 | tf_op jit(solution)/shard_map/all_to_all | solution.py:68
  13.9 1.3 and_select_fusion.1
  15.2 22.8 %all-gather = bf16[16,4,2560]{2,1,0:T(4,128)(2,1)S(1)} all-gather(bf16[1,4,2560]{2,1,0:T(4,128)(2,1)} %bitcast.202), channel_id=1, replica_groups=mesh['sect'=2,'seq'=16] {'seq'}, dimensions={0}, use_global_device_ids=true | all-gather | bytes 348160 | tf_op jit(solution)/shard_map/all_gather | solution.py:132
  40.2 3.0 %collective-permute-start.1 = (bf16[2,1,80,16]{3,2,1,0:T(8,128)(2,1)S(1)}, bf16[2,1,80,16]{3,2,1,0:T(8,128)(2,1)S(1)}, u32[]{:S(2)}, u32[]{:S(2)}) collective-permute-start(bf16[2,1,80,16]{3,2,1,0:T(8,128)(2,1)S(1)} %get-tuple-element.81), channel_id=1, source_target_pairs={{0,1},{1,2},{2,3},{3,4},{4,5},{5,6},{6,7},{7,8},{8,9},{9,10},{10,1... | collective-permute-start | bytes 15368 | tf_op jit(solution)/shard_map/ppermute | solution.py:18
  44.6 6.5 %fusion.26 = (bf16[1,1,3,384,384]{4,3,2,1,0:T(8,128)(2,1)}, bf16[1,1,3,384,384]{4,3,2,1,0:T(8,128)(2,1)}, bf16[1,1,3,384,384]{4,3,2,1,0:T(8,128)(2,1)}, bf16[1,1...) fusion(bf16[3,3,3,384,384]{4,3,2,1,0:T(8,128)(2,1)} %param.20), kind=kLoop, calls=%fused_computation.113 | loop fusion | bytes 15925248 | tf_op jit(solution)/shard_map/slice | solution.py:89
  51.9 1.8 %fusion.30 = f32[1280,384]{1,0:T(8,128)S(1)} fusion(bf16[1280,1152]{1,0:T(8,128)(2,1)S(1)} %bitcast.160, bf16[1152,384]{1,0:T(8,128)(2,1)S(1)} %bitcast.188), kind=kOutput, calls=%fused_computation.117 | convolution fusion | flops 1132462080 | bytes 5799936 | tf_op jit(solution)/shard_map/dot_general | solution.py:87
  53.7 3.1 %convolution_add_fusion.15 = f32[1280,384]{1,0:T(8,128)} fusion(f32[1280,384]{1,0:T(8,128)S(1)} %fusion.30, bf16[1280,1152]{1,0:T(8,128)(2,1)S(1)} %bitcast.161, bf16[1152,384]{1,0:T(8,128)(2,1)S(1)} %bitcast.187), kind=kOutput, calls=%fused_computation.46 | convolution fusion | flops 1132953600 | bytes 7766016 | tf_op jit(solution)/shard_map/dot_general | solution.py:87
  67.2 4.1 %collective-permute-start.3 = (bf16[2,1,80,384]{3,2,1,0:T(8,128)(2,1)}, bf16[2,1,80,384]{3,2,1,0:T(8,128)(2,1)}, u32[]{:S(2)}, u32[]{:S(2)}) collective-permute-start(bf16[2,1,80,384]{3,2,1,0:T(8,128)(2,1)} %get-tuple-element.70), channel_id=1, source_target_pairs={{0,1},{1,2},{2,3},{3,4},{4,5},{5,6},{6,7},{7,8},{8,9},{9,10},{10,1... | collective-permute-start | bytes 368648 | tf_op jit(solution)/shard_map/ppermute | solution.py:18
  71.3 5.0 %convolution_add_fusion.14 = f32[1280,384]{1,0:T(8,128)} fusion(f32[1280,384]{1,0:T(8,128)} %convolution_add_fusion.15, bf16[1280,1152]{1,0:T(8,128)(2,1)S(1)} %bitcast.162, bf16[1152,384]{1,0:T(8,128)(2,1)} %bitcast.186), kind=kOutput, calls=%fused_computation.45 | convolution fusion | flops 1132953600 | bytes 7766016 | tf_op jit(solution)/shard_map/dot_general | solution.py:87
  82.4 5.8 %pad_slice_fusion.1 = (bf16[2,8,80,384]{3,2,1,0:T(8,128)(2,1)S(1)}, bf16[2,8,80,384]{3,2,1,0:T(8,128)(2,1)S(1)}, bf16[2,8,80,384]{3,2,1,0:T(8,128)(2,1)S(1)}, bf...) fusion(bf16[2,10,80,384]{3,2,1,0:T(8,128)(2,1)S(1)} %constant_d, ...), kind=kLoop, calls=%fused_computation.16 | loop fusion | bytes 21872640 | tf_op jit(solution)/shard_map/slice | solution.py:85
  88.2 1.8 %pad_maximum_fusion.6 = bf16[2,8,80,1152]{3,2,1,0:T(8,128)(2,1)} fusion(bf16[2,8,80,384]{3,2,1,0:T(8,128)(2,1)S(1)} %get-tuple-element.64, bf16[2,8,80,384]{3,2,1,0:T(8,128)(2,1)S(1)} %get-tuple-element.65, bf16[2,8,80,384]{3,2,1,0:T(8,128)(2,1)S(1)} %get-tuple-element.51), kind=kLoop, calls=%fused_computation.53 | loop fusion | flops 8847360 | bytes 5898240 | tf_op jit(solution)/shard_map/concatenate | solution.py:84
  91.9 1.8 %convolution_add_fusion.13 = f32[1280,384]{1,0:T(8,128)S(1)} fusion(f32[1280,384]{1,0:T(8,128)S(1)} %copy-done.19, bf16[1280,1152]{1,0:T(8,128)(2,1)S(1)} %bitcast.164, bf16[1152,384]{1,0:T(8,128)(2,1)S(1)} %bitcast.185), kind=kOutput, calls=%fused_computation.44 | convolution fusion | flops 1132953600 | bytes 7766016 | tf_op jit(solution)/shard_map/dot_general | solution.py:87
  94.8 1.8 %convolution_add_fusion.12 = f32[1280,384]{1,0:T(8,128)S(1)} fusion(f32[1280,384]{1,0:T(8,128)S(1)} %convolution_add_fusion.13, bf16[1280,1152]{1,0:T(8,128)(2,1)S(1)} %bitcast.165, bf16[1152,384]{1,0:T(8,128)(2,1)S(1)} %bitcast.184), kind=kOutput, calls=%fused_computation.43 | convolution fusion | flops 1132953600 | bytes 7766016 | tf_op jit(solution)/shard_map/dot_general | solution.py:87
  97.8 1.8 %convolution_add_fusion.11 = f32[1280,384]{1,0:T(8,128)S(1)} fusion(f32[1280,384]{1,0:T(8,128)S(1)} %convolution_add_fusion.12, bf16[1280,1152]{1,0:T(8,128)(2,1)S(1)} %bitcast.166, bf16[1152,384]{1,0:T(8,128)(2,1)S(1)} %bitcast.183), kind=kOutput, calls=%fused_computation.42 | convolution fusion | flops 1132953600 | bytes 7766016 | tf_op jit(solution)/shard_map/dot_general | solution.py:87
  100.7 3.1 %convolution_add_fusion.10 = f32[1280,384]{1,0:T(8,128)} fusion(f32[1280,384]{1,0:T(8,128)S(1)} %convolution_add_fusion.11, bf16[1280,1152]{1,0:T(8,128)(2,1)S(1)} %bitcast.167, bf16[1152,384]{1,0:T(8,128)(2,1)S(1)} %bitcast.182), kind=kOutput, calls=%fused_computation.41 | convolution fusion | flops 1132953600 | bytes 7766016 | tf_op jit(solution)/shard_map/dot_general | solution.py:87
  103.9 3.9 %all-to-all-start.1 = ((bf16[64,16,1,128]{3,0,2,1:T(8,128)(2,1)}), bf16[64,16,1,128]{3,0,2,1:T(8,128)(2,1)S(1)}, u32[]{:S(2)}, u32[]{:S(2)}) async-start(bf16[64,16,1,128]{3,0,2,1:T(8,128)(2,1)} %copy.34), calls=%async_computation.1 | async-start | bytes 524288 | tf_op jit(solution)/shard_map/all_to_all | solution.py:69
  107.8 1.9 %pad_maximum_fusion.5 = bf16[2,8,80,1152]{3,2,1,0:T(8,128)(2,1)S(1)} fusion(bf16[2,8,80,384]{3,2,1,0:T(8,128)(2,1)} %get-tuple-element.63, bf16[2,8,80,384]{3,2,1,0:T(8,128)(2,1)} %get-tuple-element.66, bf16[2,8,80,384]{3,2,1,0:T(8,128)(2,1)S(1)} %get-tuple-element.62), kind=kLoop, calls=%fused_computation.52 | loop fusion | flops 8847360 | bytes 5898240 | tf_op jit(solution)/shard_map/concatenate | solution.py:84
  110.2 3.1 %convolution_add_fusion.9 = f32[1280,384]{1,0:T(8,128)} fusion(f32[1280,384]{1,0:T(8,128)S(1)} %copy-done.20, bf16[1280,1152]{1,0:T(8,128)(2,1)S(1)} %bitcast.168, bf16[1152,384]{1,0:T(8,128)(2,1)S(1)} %bitcast.181), kind=kOutput, calls=%fused_computation.40 | convolution fusion | flops 1132953600 | bytes 7766016 | tf_op jit(solution)/shard_map/dot_general | solution.py:87
  113.4 4.5 %all-to-all-done.1 = bf16[64,16,1,128]{3,0,2,1:T(8,128)(2,1)S(1)} async-done(((bf16[64,16,1,128]{3,0,2,1:T(8,128)(2,1)}), bf16[64,16,1,128]{3,0,2,1:T(8,128)(2,1)S(1)}, u32[]{:S(2)}, u32[]{:S(2)}) %all-to-all-start.1) | async-done | bytes 262176 | tf_op jit(solution)/shard_map/all_to_all | solution.py:69
  117.9 4.2 %all-to-all-start.2 = ((bf16[64,16,1,128]{3,0,2,1:T(8,128)(2,1)}), bf16[64,16,1,128]{3,0,2,1:T(8,128)(2,1)}, u32[]{:S(2)}, u32[]{:S(2)}) async-start(bf16[64,16,1,128]{3,0,2,1:T(8,128)(2,1)} %copy.35), calls=%async_computation.2 | async-start | bytes 524288 | tf_op jit(solution)/shard_map/all_to_all | solution.py:70
  122.1 4.3 %convolution_add_fusion.8 = f32[1280,384]{1,0:T(8,128)S(1)} fusion(f32[1280,384]{1,0:T(8,128)} %convolution_add_fusion.9, bf16[1280,1152]{1,0:T(8,128)(2,1)} %bitcast.163, bf16[1152,384]{1,0:T(8,128)(2,1)S(1)} %bitcast.180), kind=kOutput, calls=%fused_computation.39 | convolution fusion | flops 1132953600 | bytes 7766016 | tf_op jit(solution)/shard_map/dot_general | solution.py:87
  126.9 5.2 %all-to-all-done.2 = bf16[64,16,1,128]{3,0,2,1:T(8,128)(2,1)} async-done(((bf16[64,16,1,128]{3,0,2,1:T(8,128)(2,1)}), bf16[64,16,1,128]{3,0,2,1:T(8,128)(2,1)}, u32[]{:S(2)}, u32[]{:S(2)}) %all-to-all-start.2) | async-done | bytes 262176 | tf_op jit(solution)/shard_map/all_to_all | solution.py:70
  132.1 6.6 %while.10 = (s32[]{:T(128)}, bf16[2,512,128]{2,1,0:T(8,128)(2,1)}, bf16[2,512,128]{2,1,0:T(8,128)(2,1)S(1)}, bf16[1024,128]{1,0:T(8,128)(2,1)S(1)}, bf16[1024,128]{1,0:T(8,128)(2,1)}, /*index=5*/s32[]{:T(128)}) while((s32[]{:T(128)}, bf16[2,512,128]{2,1,0:T(8,128)(2,1)}, bf16[2,512,128]{2,1,0:T(8,128)(2,1)S(1)}, ...), condition=%wide.region_3.4_spmd, body=%wide.region_0.3_spmd.sunk | while | flops 272759808 | bytes 9185421 | solution.py:49
  133.2 1.5 fusion.80
  136.5 1.5 fusion.80
  139.2 1.8 %reduce.2 = bf16[1024,128]{1,0:T(8,128)(2,1)S(1)} reduce(bf16[1024,1,1,128]{3,0,2,1:T(8,128)(2,1)} %bitcast.189, bf16[]{:T(256)} %broadcast.149), dimensions={1,2}, to_apply=%copy.36.reduce_sub_computation | reduce | bytes 524290 | tf_op jit(solution)/shard_map/broadcast_in_dim;stack;reshape | solution.py:55
  141.8 3.5 %all-to-all-start.3 = ((bf16[16,2,4096]{2,1,0:T(2,128)(2,1)}), bf16[16,2,4096]{2,1,0:T(2,128)(2,1)S(1)}, u32[]{:S(2)}, u32[]{:S(2)}) async-start(bf16[16,2,4096]{2,1,0:T(2,128)(2,1)} %reshape.186), calls=%async_computation.3 | async-start | bytes 524288 | tf_op jit(solution)/shard_map/all_to_all | solution.py:73
  145.4 1.6 collective-permute-start.5
  147.0 8.3 %all-to-all-done.3 = bf16[16,2,4096]{2,1,0:T(2,128)(2,1)S(1)} async-done(((bf16[16,2,4096]{2,1,0:T(2,128)(2,1)}), bf16[16,2,4096]{2,1,0:T(2,128)(2,1)S(1)}, u32[]{:S(2)}, u32[]{:S(2)}) %all-to-all-start.3) | async-done | bytes 262176 | tf_op jit(solution)/shard_map/all_to_all | solution.py:73
  155.9 1.6 collective-permute-start
  157.5 1.8 %collective-permute-done.5 = bf16[2,8,40,384]{3,2,1,0:T(8,128)(2,1)S(1)} collective-permute-done((bf16[2,8,40,384]{3,2,1,0:T(8,128)(2,1)S(1)}, bf16[2,8,40,384]{3,2,1,0:T(8,128)(2,1)S(1)}, u32[]{:S(2)}, u32[]{:S(2)}) %collective-permute-start.5) | collective-permute-done | bytes 491552 | tf_op jit(solution)/shard_map/ppermute | solution.py:27
  160.2 1.5 collective-permute-done
  (133 shorter events, 38.9 us)
Async XLA Ops:
  2.4 41.1 %copy-start.8 = (bf16[3,3,3,16,384]{4,3,2,1,0:T(8,128)(2,1)S(1)}, bf16[3,3,3,16,384]{4,3,2,1,0:T(8,128)(2,1)}, u32[]{:S(2)}) copy-start(bf16[3,3,3,16,384]{4,3,2,1,0:T(8,128)(2,1)} %param.17) | copy-start | bytes 995332
  2.4 101.5 %all-to-all-start = ((bf16[64,16,1,128]{3,0,2,1:T(8,128)(2,1)}), bf16[64,16,1,128]{3,0,2,1:T(8,128)(2,1)S(1)}, u32[]{:S(2)}, u32[]{:S(2)}) async-start(bf16[64,16,1,128]{3,0,2,1:T(8,128)(2,1)} %copy.33), calls=%async_computation | async-start | bytes 524288 | tf_op jit(solution)/shard_map/all_to_all | solution.py:68
  38.9 18.7 %collective-permute-start.2 = (bf16[2,1,80,16]{3,2,1,0:T(8,128)(2,1)S(1)}, bf16[2,1,80,16]{3,2,1,0:T(8,128)(2,1)S(1)}, u32[]{:S(2)}, u32[]{:S(2)}) collective-permute-start(bf16[2,1,80,16]{3,2,1,0:T(8,128)(2,1)S(1)} %get-tuple-element.80), channel_id=1, source_target_pairs={{1,0},{2,1},{3,2},{4,3},{5,4},{6,5},{7,6},{8,7},{9,8},{10,9},{11,1... | collective-permute-start | bytes 15368 | tf_op jit(solution)/shard_map/ppermute | solution.py:21
  40.2 17.3 %collective-permute-start.1 = (bf16[2,1,80,16]{3,2,1,0:T(8,128)(2,1)S(1)}, bf16[2,1,80,16]{3,2,1,0:T(8,128)(2,1)S(1)}, u32[]{:S(2)}, u32[]{:S(2)}) collective-permute-start(bf16[2,1,80,16]{3,2,1,0:T(8,128)(2,1)S(1)} %get-tuple-element.81), channel_id=1, source_target_pairs={{0,1},{1,2},{2,3},{3,4},{4,5},{5,6},{6,7},{7,8},{8,9},{9,10},{10,1... | collective-permute-start | bytes 15368 | tf_op jit(solution)/shard_map/ppermute | solution.py:18
  44.6 9.1 %copy-start = (bf16[2,8,80,1152]{3,2,1,0:T(8,128)(2,1)}, bf16[2,8,80,1152]{3,2,1,0:T(8,128)(2,1)S(1)}, u32[]{:S(2)}) copy-start(bf16[2,8,80,1152]{3,2,1,0:T(8,128)(2,1)S(1)} %pad_maximum_fusion) | copy-start | bytes 8847364
  61.5 1.3 copy-start.14
  62.7 0.8 copy-start.13
  63.2 0.8 copy-start.12
  64.4 0.8 copy-start.15
  64.4 0.8 copy-start.16
  64.9 1.0 copy-start.18
  65.8 5.5 %copy-start.1 = (bf16[2,8,80,1152]{3,2,1,0:T(8,128)(2,1)S(1)}, bf16[2,8,80,1152]{3,2,1,0:T(8,128)(2,1)}, u32[]{:S(2)}) copy-start(bf16[2,8,80,1152]{3,2,1,0:T(8,128)(2,1)} %copy-done) | copy-start | bytes 8847364
  67.2 13.0 %collective-permute-start.3 = (bf16[2,1,80,384]{3,2,1,0:T(8,128)(2,1)}, bf16[2,1,80,384]{3,2,1,0:T(8,128)(2,1)}, u32[]{:S(2)}, u32[]{:S(2)}) collective-permute-start(bf16[2,1,80,384]{3,2,1,0:T(8,128)(2,1)} %get-tuple-element.70), channel_id=1, source_target_pairs={{0,1},{1,2},{2,3},{3,4},{4,5},{5,6},{6,7},{7,8},{8,9},{9,10},{10,1... | collective-permute-start | bytes 368648 | tf_op jit(solution)/shard_map/ppermute | solution.py:18
  71.3 5.0 %copy-start.11 = (bf16[64,2048]{1,0:T(8,128)(2,1)S(1)}, bf16[64,2048]{1,0:T(8,128)(2,1)}, u32[]{:S(2)}) copy-start(bf16[64,2048]{1,0:T(8,128)(2,1)} %param.13) | copy-start | bytes 786436
  78.9 3.4 %collective-permute-start.4 = (bf16[2,1,80,384]{3,2,1,0:T(8,128)(2,1)}, bf16[2,1,80,384]{3,2,1,0:T(8,128)(2,1)S(1)}, u32[]{:S(2)}, u32[]{:S(2)}) collective-permute-start(bf16[2,1,80,384]{3,2,1,0:T(8,128)(2,1)} %get-tuple-element.69), channel_id=1, source_target_pairs={{1,0},{2,1},{3,2},{4,3},{5,4},{6,5},{7,6},{8,7},{9,8},{10,9},{11,1... | collective-permute-start | bytes 368648 | tf_op jit(solution)/shard_map/ppermute | solution.py:21
  90.0 1.2 copy-start.7
  90.1 1.8 %copy-start.19 = (f32[1280,384]{1,0:T(8,128)S(1)}, f32[1280,384]{1,0:T(8,128)}, u32[]{:S(2)}) copy-start(f32[1280,384]{1,0:T(8,128)} %convolution_add_fusion.14) | copy-start | bytes 5898244
  93.7 1.2 copy-start.6
  96.6 1.2 copy-start.5
  99.6 1.2 copy-start.4
  103.9 14.0 %all-to-all-start.1 = ((bf16[64,16,1,128]{3,0,2,1:T(8,128)(2,1)}), bf16[64,16,1,128]{3,0,2,1:T(8,128)(2,1)S(1)}, u32[]{:S(2)}, u32[]{:S(2)}) async-start(bf16[64,16,1,128]{3,0,2,1:T(8,128)(2,1)} %copy.34), calls=%async_computation.1 | async-start | bytes 524288 | tf_op jit(solution)/shard_map/all_to_all | solution.py:69
  107.8 1.9 %copy-start.3 = (bf16[1,1,3,384,384]{4,3,2,1,0:T(8,128)(2,1)S(1)}, bf16[1,1,3,384,384]{4,3,2,1,0:T(8,128)(2,1)}, u32[]{:S(2)}) copy-start(bf16[1,1,3,384,384]{4,3,2,1,0:T(8,128)(2,1)} %get-tuple-element.50) | copy-start | bytes 2654212
  107.8 2.4 %copy-start.20 = (f32[1280,384]{1,0:T(8,128)S(1)}, f32[1280,384]{1,0:T(8,128)}, u32[]{:S(2)}) copy-start(f32[1280,384]{1,0:T(8,128)} %convolution_add_fusion.10) | copy-start | bytes 5898244
  110.2 11.8 %copy-start.2 = (bf16[1,1,3,384,384]{4,3,2,1,0:T(8,128)(2,1)S(1)}, bf16[1,1,3,384,384]{4,3,2,1,0:T(8,128)(2,1)}, u32[]{:S(2)}) copy-start(bf16[1,1,3,384,384]{4,3,2,1,0:T(8,128)(2,1)} %get-tuple-element.42) | copy-start | bytes 2654212
  117.9 14.2 %all-to-all-start.2 = ((bf16[64,16,1,128]{3,0,2,1:T(8,128)(2,1)}), bf16[64,16,1,128]{3,0,2,1:T(8,128)(2,1)}, u32[]{:S(2)}, u32[]{:S(2)}) async-start(bf16[64,16,1,128]{3,0,2,1:T(8,128)(2,1)} %copy.35), calls=%async_computation.2 | async-start | bytes 524288 | tf_op jit(solution)/shard_map/all_to_all | solution.py:70
  122.1 4.3 %copy-start.17 = (f32[384]{0:T(512)S(1)}, f32[384]{0:T(512)}, u32[]{:S(2)}) copy-start(f32[384]{0:T(512)} %param.21) | copy-start | bytes 4612
  132.1 1.1 copy-start.9
  134.7 0.7 copy-start.10
  135.4 1.1 copy-start.9
  141.8 13.5 %all-to-all-start.3 = ((bf16[16,2,4096]{2,1,0:T(2,128)(2,1)}), bf16[16,2,4096]{2,1,0:T(2,128)(2,1)S(1)}, u32[]{:S(2)}, u32[]{:S(2)}) async-start(bf16[16,2,4096]{2,1,0:T(2,128)(2,1)} %reshape.186), calls=%async_computation.3 | async-start | bytes 524288 | tf_op jit(solution)/shard_map/all_to_all | solution.py:73
  145.4 13.9 %collective-permute-start.5 = (bf16[2,8,40,384]{3,2,1,0:T(8,128)(2,1)S(1)}, bf16[2,8,40,384]{3,2,1,0:T(8,128)(2,1)S(1)}, u32[]{:S(2)}, u32[]{:S(2)}) collective-permute-start(bf16[2,8,40,384]{3,2,1,0:T(8,128)(2,1)S(1)} %dynamic-slice_select_fusion.1), channel_id=1, source_target_pairs={{0,16},{16,0},{1,17},{17,1},{2,18},{18,2},{3,19},{19,3},{4,20},{20... | collective-permute-start | bytes 1474568 | tf_op jit(solution)/shard_map/ppermute | solution.py:27
  155.9 5.8 %collective-permute-start = (bf16[64,1024]{1,0:T(8,128)(2,1)S(1)}, bf16[64,1024]{1,0:T(8,128)(2,1)S(1)}, u32[]{:S(2)}, u32[]{:S(2)}) collective-permute-start(bf16[64,1024]{1,0:T(8,128)(2,1)S(1)} %dynamic-slice_select_fusion.2), channel_id=1, source_target_pairs={{0,16},{16,0},{1,17},{17,1},{2,18},{18,2},{3,19},{19,3},{4,20},{20... | collective-permute-start | bytes 393224 | tf_op jit(solution)/shard_map/ppermute | solution.py:27
  (1 other events, 0.7 us)
where the time goes:
time: 164 us; the launch traced here: 162 us
  matrix products  34.7 us (21%)
  local copies, waits for them, and re-layouts  33.1 us (20%)
  starting transfers between devices  32 us (20%)
  blocking collectives  22.8 us (14%)
  waiting for transfers between devices  22.3 us (14%)
  other arithmetic  15.5 us (9%)
  between operations  1.9 us (1%)
    dot_general x18, matrix products, causal_conv(): jnp.dot(stacked.reshape(-1, 3 * channels), kernel[time_tap, row_tap].resh...  30.4 us
    all_gather x1, blocking collectives, decode_tile(): piece = lax.all_gather(latent, 'seq', axis=0, tiled=True)  22.8 us
    unnamed x46, local copies, waits for them, and re-layouts  8.62 us
    all_to_all x1, waiting for transfers between devices, attend_tokens(): lax.all_to_all(per_head, 'seq', split_axis=0, concat_axis=1, tiled=True)  8.32 us
    all_to_all x1, starting transfers between devices, attend_tokens(): lax.all_to_all(query_heads, 'seq', split_axis=1, concat_axis=0, tiled=True)  7.49 us
    slice x2, local copies, waits for them, and re-layouts, causal_conv(): kernel[time_tap, row_tap].reshape(3 * channels, -1)  7.24 us
    ppermute x2, starting transfers between devices, padded_2(): lax.ppermute(lax.slice_in_dim(block, block.shape[dim] - width, None, axis...  7.15 us
    slice x4, local copies, waits for them, and re-layouts, causal_conv(): strip[:, :, col_tap:col_tap + col_count]  6.89 us
  transfers between devices with their start and end apart: 10, of which 6 were waited for; matrix products, arithmetic and copies ran while one was open for 40% of the time, Pallas kernels for 0%

commit v1 on v0

v1 whole, which is shorter than its diff:
```python
import functools
import math

import jax
import jax.numpy as jnp
from jax import lax
from jax.experimental import pallas as pl
from jax.experimental.pallas import tpu as pltpu
from jax.sharding import PartitionSpec as P

DH = 128
LF = 2
MAXT = 4
TAPS = (1, 2)
ROWS = 2 * MAXT
UNITS = 3 * LF * ROWS
VMEM_LIMIT = 56 * 1024 * 1024


def parity_groups(devices):
    return [list(range(parity, devices, 2)) for parity in range(2)]


def pack_body(section_ref, query_ref, key_ref, value_ref, out_ref):
    for head in range(out_ref.shape[0]):
        columns = slice(head * DH, (head + 1) * DH)
        for place, ref in enumerate((query_ref, key_ref, value_ref)):
            out_ref[head, place] = ref[:, columns]


def pack_heads(section, queries, key_tokens, value_tokens):
    token_rows, width = queries.shape
    heads = width // DH // lax.axis_size("sect")
    steps = 2
    block = pl.BlockSpec((token_rows, heads // steps * DH), lambda i, sec: (0, sec[0] * steps + i))
    return pl.pallas_call(
        pack_body,
        grid_spec=pltpu.PrefetchScalarGridSpec(
            num_scalar_prefetch=1,
            grid=(steps,),
            in_specs=[block] * 3,
            out_specs=pl.BlockSpec(
                (heads // steps, 3, token_rows, DH), lambda i, sec: (i, 0, 0, 0)
            ),
        ),
        out_shape=jax.ShapeDtypeStruct((heads, 3, token_rows, DH), queries.dtype),
        name="pack_heads",
    )(section, queries, key_tokens, value_tokens)


def softmax_part(query, key, value):
    scores = lax.dot_general(
        query, key, (((1,), (1,)), ((), ())), preferred_element_type=jnp.float32
    ) * (1.0 / math.sqrt(DH))
    largest = jnp.max(scores, axis=1, keepdims=True)
    exponents = jnp.exp(scores - largest)
    totals = jnp.sum(exponents, axis=1, keepdims=True)
    mixed = jnp.dot(exponents.astype(jnp.bfloat16), value, preferred_element_type=jnp.float32)
    return largest, totals, mixed


def flat(array):
    return array.reshape(-1, array.shape[-1])


def own_body(query_ref, kv_ref, mixed_ref, largest_ref, totals_ref):
    largest, totals, mixed = softmax_part(
        flat(query_ref[:, 0]), flat(kv_ref[:, 1]), flat(kv_ref[:, 2])
    )
    mixed_ref[...] = mixed
    largest_ref[...] = largest
    totals_ref[...] = totals


def merge_body(query_ref, kv_ref, mixed_ref, largest_ref, totals_ref, out_ref):
    largest, totals, mixed = softmax_part(
        flat(query_ref[:, 0]), flat(kv_ref[:, 1]), flat(kv_ref[:, 2])
    )
    top = jnp.maximum(largest, largest_ref[...])
    here = jnp.exp(largest - top)
    there = jnp.exp(largest_ref[...] - top)
    totals = totals * here + totals_ref[...] * there
    mixed = mixed * here + mixed_ref[...] * there
    out_ref[...] = (mixed / totals).astype(out_ref.dtype).reshape(out_ref.shape)


def attend(own, other_of):
    members, _, token_rows, _ = own.shape
    block = min(8, members)
    rows = block * token_rows
    total = members * token_rows
    query_spec = pl.BlockSpec((block, 1, token_rows, DH), lambda i: (i, 0, 0, 0))
    kv_spec = pl.BlockSpec(own.shape, lambda i: (0, 0, 0, 0))
    mixed_spec = pl.BlockSpec((rows, DH), lambda i: (i, 0))
    stat_spec = pl.BlockSpec((rows, 1), lambda i: (i, 0))
    flops = 4 * total * total * DH
    cost = pl.CostEstimate(flops=flops, bytes_accessed=4 * total * DH, transcendentals=total**2)
    params = pltpu.CompilerParams(vmem_limit_bytes=VMEM_LIMIT)
    stats = jax.ShapeDtypeStruct((total, 1), jnp.float32)
    mixed, largest, totals = pl.pallas_call(
        own_body,
        grid=(members // block,),
        in_specs=[query_spec, kv_spec],
        out_specs=[mixed_spec, stat_spec, stat_spec],
        out_shape=[jax.ShapeDtypeStruct((total, DH), jnp.float32), stats, stats],
        compiler_params=params,
        cost_estimate=cost,
        name="attend_own",
    )(own, own)
    other = other_of()
    return pl.pallas_call(
        merge_body,
        grid=(members // block,),
        in_specs=[query_spec, kv_spec, mixed_spec, stat_spec, stat_spec],
        out_specs=pl.BlockSpec((block, token_rows, DH), lambda i: (i, 0, 0)),
        out_shape=jax.ShapeDtypeStruct((members, token_rows, DH), own.dtype),
        compiler_params=params,
        cost_estimate=cost,
        name="attend_merge",
    )(own, other, mixed, largest, totals)


def unpack_body(in_ref, out_ref):
    for head in range(in_ref.shape[0]):
        out_ref[:, head * DH : (head + 1) * DH] = in_ref[head]


def unpack_heads(array):
    heads, token_rows, _ = array.shape
    return pl.pallas_call(
        unpack_body,
        out_shape=jax.ShapeDtypeStruct((token_rows, heads * DH), array.dtype),
        name="unpack_heads",
    )(array)


def decode_body(
    grid_rows,
    width,
    place_ref,
    latent_ref,
    in_weight_ref,
    in_bias_ref,
    gain_ref,
    mid_weight_ref,
    mid_bias_ref,
    out_ref,
    mid_weight,
    taps,
    patches,
    active,
    hidden_mid,
    summed,
    weight_sems,
):
    corners = active.shape[2] // 16
    channels = in_weight_ref.shape[3]
    features = in_weight_ref.shape[4]
    columns = out_ref.shape[2]
    first_row, filled, section = place_ref[0], place_ref[1], place_ref[2]

    def load(row_tap):
        return [
            pltpu.make_async_copy(
                mid_weight_ref.at[tap, row_tap, col_tap],
                mid_weight.at[row_tap, col_tap, pl.ds(slot * features, features)],
                weight_sems.at[row_tap, col_tap, slot],
            )
            for col_tap in range(3)
            for slot, tap in enumerate(TAPS)
        ]

    for row_tap in range(3):
        for copy in load(row_tap):
            copy.start()

    nothing = jnp.zeros((channels, features), jnp.bfloat16)
    base = 0
    for tap in TAPS:
        for row_parity in range(2):
            for i, j, p, q in [
                (i, j, p, q) for i in range(2) for j in range(2) for p in range(2) for q in range(2)
            ]:
                for col_parity in range(2):
                    row_tap, col_tap = 2 * i + p - row_parity, 2 * j + q - col_parity
                    inside = 0 <= row_tap < 3 and 0 <= col_tap < 3
                    taps[base : base + channels, col_parity * features : (col_parity + 1) * features] = (
                        in_weight_ref[tap, row_tap, col_tap] if inside else nothing
                    )
                base += channels

    held_rows = latent_ref.shape[0]
    unit = lax.broadcasted_iota(jnp.int32, (UNITS, held_rows), 0)
    held = lax.broadcasted_iota(jnp.int32, (UNITS, held_rows), 1)
    reach = (unit >> 4) + (unit & 7)
    frame = (unit >> 3) & 1
    group = 0
    for tap in TAPS:
        for row_parity in range(2):
            for i in range(2):
                token_row = first_row + (reach >> 1) - 1 + i
                source = frame + tap - 2
                wanted = (
                    ((reach & 1) == row_parity)
                    & (token_row >= 0)
                    & (token_row < grid_rows)
                    & (source >= 0)
                )
                target = jnp.where(wanted, source * grid_rows + token_row, -1)
                selector = jnp.where(held == target, 1.0, 0.0).astype(jnp.bfloat16)
                picked = jnp.dot(selector, latent_ref[...], preferred_element_type=jnp.float32)
                aside = picked[:, 64 : 64 + corners // 2 * 128]
                lanes = slice(group * 128, (group + 1) * 128)
                for corner in range(corners):
                    chunk = slice(corner // 2 * 128, corner // 2 * 128 + 128)
                    piece = (aside if corner % 2 else picked)[:, chunk]
                    patches[corner * UNITS : (corner + 1) * UNITS, lanes] = piece.astype(jnp.bfloat16)
                group += 1

    unit_row = lax.broadcasted_iota(jnp.int32, (UNITS, 1), 0)
    pixel_row = 2 * first_row + (unit_row >> 4) + (unit_row & 7) - 1
    row_inside = (pixel_row >= 0) & (pixel_row < 2 * grid_rows)
    step_corners = 3

    def first_layer(step, carried):
        start = pl.multiple_of(step * step_corners * UNITS, 16)
        block = jnp.dot(
            patches[pl.ds(start, step_corners * UNITS)],
            taps[...],
            preferred_element_type=jnp.float32,
        )
        hiddens, actives = [carried[0]], [carried[1]]
        for corner in range(step_corners):
            for col_parity in range(2):
                hidden = (
                    block[
                        corner * UNITS : (corner + 1) * UNITS,
                        col_parity * features : (col_parity + 1) * features,
                    ]
                    + in_bias_ref[...]
                )
                hidden = hidden.astype(jnp.bfloat16).astype(jnp.float32)
                scale = lax.rsqrt(jnp.mean(hidden * hidden, axis=1, keepdims=True) + 1e-06)
                scaled = hidden * scale * gain_ref[...]
                activated = scaled / (1.0 + jnp.exp(-scaled))
                pixel = section * columns + 2 * (step * step_corners + corner) + col_parity - 1
                keep = row_inside & (pixel >= 0) & (pixel < width)
                actives.append(jnp.where(keep, activated, 0.0))
                hiddens.append(hidden[16:32])
        for pair in range(step_corners):
            at = pl.ds(pl.multiple_of((step * step_corners + pair) * 16, 16), 16)
            for phase in range(2):
                left, right = actives[2 * pair + 1 - phase], actives[2 * pair + 2 - phase]
                for row_tap in range(3):
                    for field in range(LF):
                        low = row_tap * 16 + field * 8
                        joined = jnp.concatenate([left[low : low + 8], right[low : low + 8]], axis=0)
                        active[row_tap, phase, at, field * features : (field + 1) * features] = (
                            joined.astype(jnp.bfloat16)
                        )
            left, right = hiddens[2 * pair], hiddens[2 * pair + 1]
            for field in range(LF):
                low = field * 8
                joined = jnp.concatenate([left[low : low + 8], right[low : low + 8]], axis=0)
                hidden_mid[at, field * features : (field + 1) * features] = joined.astype(jnp.bfloat16)
        return hiddens[-1], actives[-1]

    lax.fori_loop(
        0,
        corners // step_corners,
        first_layer,
        (jnp.zeros((16, features), jnp.float32), jnp.zeros((UNITS, features), jnp.float32)),
    )

    rows = columns * ROWS
    for row_tap in range(3):
        for copy in load(row_tap):
            copy.wait()
        early, late = None, None
        for col_tap in range(3):
            low = 0 if col_tap == 0 else 16
            window = active[row_tap, col_tap % 2, low : low + rows]
            first = jnp.dot(
                window[:, :features],
                mid_weight[row_tap, col_tap, features:],
                preferred_element_type=jnp.float32,
            )
            second = jnp.dot(
                window, mid_weight[row_tap, col_tap], preferred_element_type=jnp.float32
            )
            early = first if early is None else early + first
            late = second if late is None else late + second
        for field, part in enumerate((early, late)):
            for lane in range(features // 128):
                lanes = slice(lane * 128, (lane + 1) * 128)
                value = part[:, lanes]
                if row_tap:
                    value = value + summed[field, lane]
                if row_tap == 2:
                    from_lane = field * features + lane * 128
                    value = (
                        value
                        + mid_bias_ref[:, lanes]
                        + hidden_mid[16 : 16 + rows, from_lane : from_lane + 128].astype(jnp.float32)
                    )
                summed[field, lane] = value

    for field in range(LF):
        for row in range(ROWS):
            for lane in range(features // 128):
                value = summed[field, lane, pl.ds(row, columns, stride=ROWS), :]
                value = jnp.where(row < 2 * filled, value, 0.0)
                out_ref[field, row, :, lane * 128 : (lane + 1) * 128] = value.astype(jnp.bfloat16)


def decode_tile(
    section,
    latent,
    tile_rows,
    conv_in_weight,
    conv_in_bias,
    norm_gain,
    conv_mid_weight,
    conv_mid_bias,
):
    devices = lax.axis_size("seq")
    sections = lax.axis_size("sect")
    position = lax.axis_index("seq")
    channels, features = conv_in_weight.shape[3:]
    token_width = 4 * channels
    tokens = latent.shape[1] // token_width
    grid_rows = latent.shape[0] * devices // LF
    width = 2 * tokens
    columns = width // sections
    span = tokens // sections
    tile_starts = jnp.cumsum(tile_rows) - tile_rows
    place = jnp.stack([tile_starts[position], tile_rows[position], section]).astype(jnp.int32)
    padded = jnp.pad(latent, ((0, 0), (token_width, token_width)))
    share = lax.dynamic_slice_in_dim(
        padded, section * span * token_width, (span + 2) * token_width, 1
    )
    gathered = lax.all_gather(share, "seq", axis=0, tiled=True)
    corners = span + 1
    vmem = pl.BlockSpec(memory_space=pltpu.VMEM)
    slots = len(TAPS)
    return pl.pallas_call(
        functools.partial(decode_body, grid_rows, width),
        in_specs=[
            pl.BlockSpec(memory_space=pltpu.SMEM),
            vmem,
            vmem,
            vmem,
            vmem,
            pl.BlockSpec(memory_space=pl.ANY),
            vmem,
        ],
        out_specs=vmem,
        out_shape=jax.ShapeDtypeStruct((LF, ROWS, columns, features), jnp.bfloat16),
        scratch_shapes=[
            pltpu.VMEM((3, 3, slots * features, features), jnp.bfloat16),
            pltpu.VMEM((slots * 2 * 4 * token_width, 2 * features), jnp.bfloat16),
            pltpu.VMEM((corners * UNITS, slots * 2 * 4 * token_width), jnp.bfloat16),
            pltpu.VMEM((3, 2, corners * 16, LF * features), jnp.bfloat16),
            pltpu.VMEM((corners * 16, LF * features), jnp.bfloat16),
            pltpu.VMEM((LF, features // 128, columns * ROWS, 128), jnp.float32),
            pltpu.SemaphoreType.DMA((3, 3, slots)),
        ],
        compiler_params=pltpu.CompilerParams(vmem_limit_bytes=VMEM_LIMIT),
        cost_estimate=pl.CostEstimate(
            flops=2 * 3 * 9 * columns * ROWS * features * features,
            bytes_accessed=slots * 9 * features * features * 2,
            transcendentals=corners * UNITS * 2 * features,
        ),
        name="decode_tile",
    )(
        place,
        gathered,
        conv_in_weight,
        conv_in_bias.reshape(1, -1),
        norm_gain.reshape(1, -1),
        conv_mid_weight,
        conv_mid_bias.reshape(1, -1),
    )


def attend_tokens(section, queries, key_tokens, value_tokens):
    devices = lax.axis_size("seq")
    groups = parity_groups(devices)
    packed = pack_heads(section.reshape(1), queries, key_tokens, value_tokens)
    own = lax.all_to_all(packed, "seq", 0, 0, axis_index_groups=groups, tiled=True)
    pairs = [(i, i ^ 1) for i in range(devices)]
    mixed = attend(own, lambda: lax.ppermute(own, "seq", pairs))
    returned = lax.all_to_all(mixed, "seq", 0, 0, axis_index_groups=groups, tiled=True)
    return unpack_heads(returned)


def on_device(
    queries,
    key_tokens,
    value_tokens,
    latent,
    tile_rows,
    conv_in_weight,
    conv_in_bias,
    norm_gain,
    conv_mid_weight,
    conv_mid_bias,
):
    section = lax.axis_index("sect").astype(jnp.int32)
    attended = attend_tokens(section, queries, key_tokens, value_tokens)
    frames = decode_tile(
        section,
        latent,
        tile_rows,
        conv_in_weight,
        conv_in_bias,
        norm_gain,
        conv_mid_weight,
        conv_mid_bias,
    )
    return (attended, frames)


def solution(mesh):
    in_specs = (
        P("seq", None),
        P("seq", None),
        P("seq", None),
        P("seq", None),
        P(),
        P(),
        P(),
        P(),
        P(),
        P(),
    )
    out_specs = (P("seq", "sect"), P(None, "seq", "sect", None))
    return jax.shard_map(
        on_device, mesh=mesh, in_specs=in_specs, out_specs=out_specs, check_vma=False
    )
```

time: 164 us -> 73.4 us (0.45)
  matrix products: 34.7 us -> 0 us
  local copies, waits for them, and re-layouts: 33.1 us -> 9.28 us
  starting transfers between devices: 32 us -> 10.6 us
  Pallas kernels: 0 us -> 21.2 us
  waiting for transfers between devices: 22.3 us -> 8.29 us
  other arithmetic: 15.5 us -> 2.64 us
  blocking collectives: 22.8 us -> 20 us
    dot_general x23 -> x0, matrix products: 34.7 us -> none  [the longest x18 30.4 us: causal_conv(): jnp.dot(stacked.reshape(-1, 3 * channels), kernel[time_tap, row_tap].resh...]
    pallas_call x0 -> x5, Pallas kernels: none -> 21.2 us  [the longest x1 11.8 us: decode_tile(): pl.pallas_call(functools.partial(decode_body, grid_rows, width), in_specs...]
    slice x8 -> x0, local copies, waits for them, and re-layouts: 14.8 us -> none  [the longest x2 7.24 us: causal_conv(): kernel[time_tap, row_tap].reshape(3 * channels, -1)]
    ppermute x6 -> x1, starting transfers between devices: 12.9 us -> 0.01 us  [attend_tokens(): mixed = attend(own, lambda: lax.ppermute(own, 'seq', pairs))]
    all_to_all x4 -> x2, waiting for transfers between devices: 18 us -> 8.29 us  [the longest x1 8.28 us: attend_tokens(): lax.all_to_all(packed, 'seq', 0, 0, axis_index_groups=groups, tiled=True)]
    all_to_all x4 -> x2, starting transfers between devices: 19.2 us -> 10.6 us  [the longest x1 7.25 us: attend_tokens(): lax.all_to_all(packed, 'seq', 0, 0, axis_index_groups=groups, tiled=True)]
    concatenate x13 -> x0, other arithmetic: 7.63 us -> none  [the longest x11 6.42 us: causal_conv(): jnp.concatenate([strip[:, :, col_tap:col_tap + col_count] for col_tap in...]
    unnamed x46 -> x8, local copies, waits for them, and re-layouts: 8.62 us -> 2.92 us
  transfers between devices with their start and end apart: 10 -> 3, of which waited for: 6 -> 1; matrix products, arithmetic and copies ran while one was open for 40% -> 14% of each run, Pallas kernels for 0% -> 20%
where the time goes in v1:
time: 73.4 us; the launch traced here: 72.7 us
  Pallas kernels  21.2 us (29%)
  blocking collectives  20 us (27%)
  starting transfers between devices  10.6 us (14%)
  local copies, waits for them, and re-layouts  9.28 us (13%)
  waiting for transfers between devices  8.29 us (11%)
  other arithmetic  2.64 us (4%)
    all_gather x1, blocking collectives, decode_tile(): gathered = lax.all_gather(share, 'seq', axis=0, tiled=True)  20 us
    pallas_call x1, Pallas kernels, decode_tile(): pl.pallas_call(functools.partial(decode_body, grid_rows, width), in_specs...  11.8 us
    all_to_all x1, waiting for transfers between devices, attend_tokens(): lax.all_to_all(packed, 'seq', 0, 0, axis_index_groups=groups, tiled=True)  8.28 us
    all_to_all x1, starting transfers between devices, attend_tokens(): lax.all_to_all(packed, 'seq', 0, 0, axis_index_groups=groups, tiled=True)  7.25 us
    pallas_call x1, Pallas kernels, attend(): pl.pallas_call(merge_body, grid=(members // block,), in_specs=[query_spec...  3.53 us
    all_to_all x1, starting transfers between devices, attend_tokens(): lax.all_to_all(mixed, 'seq', 0, 0, axis_index_groups=groups, tiled=True)  3.37 us
    unnamed x8, local copies, waits for them, and re-layouts  2.92 us
    pallas_call x1, Pallas kernels, attend(): pl.pallas_call(own_body, grid=(members // block,), in_specs=[query_spec,...  2.6 us
  transfers between devices with their start and end apart: 3, of which 1 were waited for; matrix products, arithmetic and copies ran while one was open for 14% of the time, Pallas kernels for 20%

profile of v1, /device:TPU:0, one launch (start us, length us, event | category | flops | bytes accessed | tf_op | source)
XLA Modules:
  0.0 72.7 jit_solution(14671101426914025449)
XLA Ops:
  0.6 1.7 %pack_heads.1 = bf16[8,3,64,128]{3,2,1,0:T(8,128)(2,1)} custom-call(s32[1]{0:T(128)} %bitcast.section_ref, bf16[64,2048]{1,0:T(8,128)(2,1)} %query_ref.1, bf16[64,2048]{1,0:T(8,128)(2,1)} %key_ref.1, bf16[64,2048]{1,0:T(8,128)(2,1)} %value_ref.1), custom_call_target="tpu_custom_call" | custom-call | tf_op jit(solution)/shard_map/pack_heads/pallas_call | solution.py:36
  2.4 7.3 %all-to-all-start = ((bf16[8,3,64,128]{3,2,1,0:T(8,128)(2,1)}), bf16[8,3,64,128]{3,2,1,0:T(8,128)(2,1)S(1)}, u32[]{:S(2)}, u32[]{:S(2)}) async-start(bf16[8,3,64,128]{3,2,1,0:T(8,128)(2,1)} %pack_heads.1), calls=%async_computation | async-start | bytes 786432 | tf_op jit(solution)/shard_map/all_to_all | solution.py:390
  9.6 1.3 %dynamic_slice.10 = s32[1]{0:T(128)} dynamic-slice(s32[16]{0:T(128)} %param.14, s32[]{:T(128)S(6)} %select_n.7), dynamic_slice_sizes={1} | dynamic-slice | bytes 12 | tf_op jit(solution)/shard_map/dynamic_slice | solution.py:337
  10.9 0.7 %copy.14 = s32[16,1]{1,0:T(8,128)S(1)} copy(s32[16,1]{0,1:T(1,128)} %bitcast.4) | data formatting | bytes 128 | tf_op jit(solution)/shard_map/reshape.24
  11.7 0.1 reduce
  11.8 0.7 sub.3
  12.4 0.6 dynamic_slice.9
  13.0 8.3 %all-to-all-done.query_ref.kv_ref = bf16[8,3,64,128]{3,2,1,0:T(8,128)(2,1)S(1)} async-done(((bf16[8,3,64,128]{3,2,1,0:T(8,128)(2,1)}), bf16[8,3,64,128]{3,2,1,0:T(8,128)(2,1)S(1)}, u32[]{:S(2)}, u32[]{:S(2)}) %all-to-all-start) | async-done | bytes 393248 | tf_op jit(solution)/shard_map/all_to_all | solution.py:390
  21.3 0.0 copy-start
  21.3 0.0 collective-permute-start
  21.3 0.8 %fusion = bf16[1,4,1408]{2,1,0:T(4,128)(2,1)S(1)} fusion(s32[]{:T(128)S(6)} %select_n.8, bf16[4,2560]{1,0:T(4,128)(2,1)} %param.13), kind=kLoop, calls=%fused_computation.1 | loop fusion | bytes 31748
  22.1 20.0 %all-gather = bf16[16,4,1408]{2,1,0:T(4,128)(2,1)S(1)} all-gather(bf16[1,4,1408]{2,1,0:T(4,128)(2,1)S(1)} %fusion), channel_id=1, replica_groups=mesh['sect'=2,'seq'=16] {'seq'}, dimensions={0}, use_global_device_ids=true | all-gather | bytes 191488 | tf_op jit(solution)/shard_map/all_gather | solution.py:342
  42.1 0.7 reshape.49.latent_ref
  42.9 1.3 %reshape.45.in_bias_ref = f32[1,384]{1,0:T(1,128)} reshape(f32[384]{0:T(512)} %param.16) | data formatting | bytes 3072 | tf_op jit(solution)/shard_map/reshape | solution.py:379
  44.1 1.3 %reshape.46.gain_ref = f32[1,384]{1,0:T(1,128)} reshape(f32[384]{0:T(512)} %param.17) | data formatting | bytes 3072 | tf_op jit(solution)/shard_map/reshape | solution.py:380
  45.4 1.3 %reshape.47.mid_bias_ref = f32[1,384]{1,0:T(1,128)} reshape(f32[384]{0:T(512)} %param.19) | data formatting | bytes 3072 | tf_op jit(solution)/shard_map/reshape | solution.py:382
  46.6 1.8 %pad_add_fusion.place_ref = s32[3]{0:T(128)} fusion(s32[1]{0:T(128)} %bitcast.section_ref, s32[1]{0:T(128)} %dynamic_slice.10, s32[1]{0:T(128)} %dynamic_slice.9), kind=kLoop, calls=%fused_computation.2 | loop fusion | flops 6 | bytes 24 | tf_op jit(solution)/shard_map/stack | solution.py:337
  48.5 0.0 copy-done
  48.5 2.6 %attend_own.1 = (f32[512,128]{1,0:T(8,128)}, f32[512,1]{1,0:T(8,128)}, f32[512,1]{1,0:T(8,128)}) custom-call(bf16[8,3,64,128]{3,2,1,0:T(8,128)(2,1)} %copy-done, bf16[8,3,64,128]{3,2,1,0:T(8,128)(2,1)} %copy-done), custom_call_target="tpu_custom_call" | custom-call | flops 134217728 | bytes 262144 | tf_op jit(solution)/shard_map/attend_own/pallas_call | solution.py:100
  51.1 0.0 collective-permute-done.kv_ref
  51.1 0.0 copy-start.2
  51.1 0.8 %copy-done.2 = bf16[8,3,64,128]{3,2,1,0:T(8,128)(2,1)} copy-done((bf16[8,3,64,128]{3,2,1,0:T(8,128)(2,1)}, bf16[8,3,64,128]{3,2,1,0:T(8,128)(2,1)S(1)}, u32[]{:S(2)}) %copy-start.2) | copy-done | bytes 393240
  51.8 3.5 %attend_merge.1 = bf16[8,64,128]{2,1,0:T(8,128)(2,1)} custom-call(bf16[8,3,64,128]{3,2,1,0:T(8,128)(2,1)} %copy-done, bf16[8,3,64,128]{3,2,1,0:T(8,128)(2,1)} %copy-done.2, f32[512,128]{1,0:T(8,128)} %get-tuple-element.5.mixed_ref, f32[512,1]{1,0:T(8,128)} %get-tuple-element.6.largest_ref, f32[512,1]{1,0:T(8,128)} %get-tuple-element.7.totals_ref), custom_call_target="tpu_custom_call" | custom-call | flops 134217728 | bytes 262144 | tf_op jit(solution)/shard_map/attend_merge/pallas_call | solution.py:111
  55.4 3.4 %all-to-all-start.1 = ((bf16[8,64,128]{2,1,0:T(8,128)(2,1)}), bf16[8,64,128]{2,1,0:T(8,128)(2,1)S(1)}, u32[]{:S(2)}, u32[]{:S(2)}) async-start(bf16[8,64,128]{2,1,0:T(8,128)(2,1)} %attend_merge.1), calls=%async_computation.1 | async-start | bytes 262144 | tf_op jit(solution)/shard_map/all_to_all | solution.py:393
  58.7 11.8 %decode_tile.1 = bf16[2,8,40,384]{3,2,1,0:T(8,128)(2,1)} custom-call(s32[3]{0:T(128)} %pad_add_fusion.place_ref, bf16[64,1408]{1,0:T(8,128)(2,1)} %reshape.49.latent_ref, bf16[3,3,3,16,384]{4,3,2,1,0:T(8,128)(2,1)} %in_weight_ref.1, f32[1,384]{1,0:T(1,128)} %reshape.45.in_bias_ref, f32[1,384]{1,0:T(1,128)} %reshape.46.gain_ref, ...), custom_call_target="tpu_custom_call" | custom-call | flops 2548039680 | bytes 5308416 | tf_op jit(solution)/shard_map/decode_tile/pallas_call | solution.py:346
  70.5 0.0 all-to-all-done.1.in_ref
  70.5 0.0 copy-start.1
  70.5 0.6 copy-done.1
  71.1 1.6 %unpack_heads.1 = bf16[64,1024]{1,0:T(8,128)(2,1)} custom-call(bf16[8,64,128]{2,1,0:T(8,128)(2,1)} %copy-done.1), custom_call_target="tpu_custom_call" | custom-call | tf_op jit(solution)/shard_map/unpack_heads/pallas_call | solution.py:130
  (1 shorter events, 0.0 us)
Async XLA Ops:
  2.4 18.9 %all-to-all-start = ((bf16[8,3,64,128]{3,2,1,0:T(8,128)(2,1)}), bf16[8,3,64,128]{3,2,1,0:T(8,128)(2,1)S(1)}, u32[]{:S(2)}, u32[]{:S(2)}) async-start(bf16[8,3,64,128]{3,2,1,0:T(8,128)(2,1)} %pack_heads.1), calls=%async_computation | async-start | bytes 786432 | tf_op jit(solution)/shard_map/all_to_all | solution.py:390
  21.3 27.1 %copy-start = (bf16[8,3,64,128]{3,2,1,0:T(8,128)(2,1)}, bf16[8,3,64,128]{3,2,1,0:T(8,128)(2,1)S(1)}, u32[]{:S(2)}) copy-start(bf16[8,3,64,128]{3,2,1,0:T(8,128)(2,1)S(1)} %all-to-all-done.query_ref.kv_ref) | copy-start | bytes 1179652
  21.3 29.7 %collective-permute-start = (bf16[8,3,64,128]{3,2,1,0:T(8,128)(2,1)S(1)}, bf16[8,3,64,128]{3,2,1,0:T(8,128)(2,1)S(1)}, u32[]{:S(2)}, u32[]{:S(2)}) collective-permute-start(bf16[8,3,64,128]{3,2,1,0:T(8,128)(2,1)S(1)} %all-to-all-done.query_ref.kv_ref), channel_id=1, source_target_pairs={{0,1},{1,0},{2,3},{3,2},{4,5},{5,4},{6,7},{7,6},{8,9},{9,8},{10,11... | collective-permute-start | bytes 1179656 | tf_op jit(solution)/shard_map/ppermute | solution.py:392
  51.1 0.8 %copy-start.2 = (bf16[8,3,64,128]{3,2,1,0:T(8,128)(2,1)}, bf16[8,3,64,128]{3,2,1,0:T(8,128)(2,1)S(1)}, u32[]{:S(2)}) copy-start(bf16[8,3,64,128]{3,2,1,0:T(8,128)(2,1)S(1)} %collective-permute-done.kv_ref) | copy-start | bytes 1179652
  55.4 15.1 %all-to-all-start.1 = ((bf16[8,64,128]{2,1,0:T(8,128)(2,1)}), bf16[8,64,128]{2,1,0:T(8,128)(2,1)S(1)}, u32[]{:S(2)}, u32[]{:S(2)}) async-start(bf16[8,64,128]{2,1,0:T(8,128)(2,1)} %attend_merge.1), calls=%async_computation.1 | async-start | bytes 262144 | tf_op jit(solution)/shard_map/all_to_all | solution.py:393
  70.5 0.6 copy-start.1

commit v2 on v1

v2 whole, which is shorter than its diff:
```python
import functools
import math

import jax
import jax.numpy as jnp
from jax import lax
from jax.experimental import pallas as pl
from jax.experimental.pallas import tpu as pltpu
from jax.sharding import PartitionSpec as P

DH = 128
LF = 2
MAXT = 4
TAPS = (1, 2)
ROWS = 2 * MAXT
UNITS = 3 * LF * ROWS
ATTEND_VMEM = 32 * 1024 * 1024
DECODE_VMEM = 48 * 1024 * 1024


def parity_groups(devices):
    return [list(range(parity, devices, 2)) for parity in range(2)]


def pack_body(query_ref, key_ref, value_ref, latent_ref, packed_ref, share_ref, sems):
    heads = packed_ref.shape[0]
    section = lax.axis_index("sect")
    copies = []
    for head in range(heads):
        columns = pl.ds(pl.multiple_of((section * heads + head) * DH, DH), DH)
        for place, ref in enumerate((query_ref, key_ref, value_ref)):
            copy = pltpu.make_async_copy(
                ref.at[:, columns], packed_ref.at[head, place], sems.at[head, place]
            )
            copy.start()
            copies.append(copy)
    rows, width = latent_ref.shape
    span = share_ref.shape[2]
    rim = (2 * span - width) // 4
    wide = latent_ref[...].astype(jnp.float32)
    rim_zeros = jnp.zeros((rows, rim), jnp.float32)
    lower = jnp.concatenate([rim_zeros, wide[:, : span - rim]], axis=1)
    upper = jnp.concatenate([wide[:, width - span + rim :], rim_zeros], axis=1)
    share = jnp.where(section == 0, lower, upper).astype(share_ref.dtype)
    for member in range(share_ref.shape[0]):
        share_ref[member] = share
    for copy in copies:
        copy.wait()


def pack_heads(queries, key_tokens, value_tokens, latent, token_width):
    token_rows, width = queries.shape
    sections = lax.axis_size("sect")
    heads = width // DH // sections
    span = latent.shape[1] // sections + 2 * token_width
    hbm = pl.BlockSpec(memory_space=pl.ANY)
    vmem = pl.BlockSpec(memory_space=pltpu.VMEM)
    return pl.pallas_call(
        pack_body,
        in_specs=[hbm, hbm, hbm, vmem],
        out_specs=[vmem, vmem],
        out_shape=[
            jax.ShapeDtypeStruct((heads, 3, token_rows, DH), queries.dtype),
            jax.ShapeDtypeStruct((lax.axis_size("seq"), latent.shape[0], span), latent.dtype),
        ],
        scratch_shapes=[pltpu.SemaphoreType.DMA((heads, 3))],
        name="pack_heads",
    )(queries, key_tokens, value_tokens, latent)


def flat(array):
    return array.reshape(-1, array.shape[-1])


def attend_body(block, own_ref, other_ref, out_ref):
    members, _, token_rows, _ = own_ref.shape
    keys = jnp.concatenate([flat(own_ref[:, 1]), flat(other_ref[:, 1])], axis=0)
    values = jnp.concatenate([flat(own_ref[:, 2]), flat(other_ref[:, 2])], axis=0)

    def one_block(step):
        at = pl.ds(step * block, block)
        scores = lax.dot_general(
            flat(own_ref[at, 0]),
            keys,
            (((1,), (1,)), ((), ())),
            preferred_element_type=jnp.float32,
        ) * (1.0 / math.sqrt(DH))
        exponents = jnp.exp(scores - jnp.max(scores, axis=1, keepdims=True))
        totals = jnp.sum(exponents, axis=1, keepdims=True)
        mixed = jnp.dot(
            exponents.astype(jnp.bfloat16), values, preferred_element_type=jnp.float32
        )
        out_ref[at] = (mixed / totals).astype(out_ref.dtype).reshape(block, token_rows, DH)

    if members <= 8:
        for step in range(members // block):
            one_block(step)
    else:
        pl.loop(0, members // block)(one_block)


def attend(own, other):
    members, _, token_rows, _ = own.shape
    total = members * token_rows
    vmem = pl.BlockSpec(memory_space=pltpu.VMEM)
    return pl.pallas_call(
        functools.partial(attend_body, min(4, members)),
        in_specs=[vmem, vmem],
        out_specs=vmem,
        out_shape=jax.ShapeDtypeStruct((members, token_rows, DH), own.dtype),
        compiler_params=pltpu.CompilerParams(vmem_limit_bytes=ATTEND_VMEM),
        cost_estimate=pl.CostEstimate(
            flops=8 * total * total * DH,
            bytes_accessed=7 * total * DH * 2,
            transcendentals=2 * total * total,
        ),
        name="attend",
    )(own, other)


def unpack_body(in_ref, out_ref):
    for head in range(in_ref.shape[0]):
        out_ref[:, head * DH : (head + 1) * DH] = in_ref[head]


def unpack_heads(array):
    heads, token_rows, _ = array.shape
    return pl.pallas_call(
        unpack_body,
        in_specs=[pl.BlockSpec(memory_space=pltpu.VMEM)],
        out_shape=jax.ShapeDtypeStruct((token_rows, heads * DH), array.dtype),
        name="unpack_heads",
    )(array)


def decode_body(
    grid_rows,
    width,
    tile_ref,
    latent_ref,
    in_weight_ref,
    in_bias_ref,
    gain_ref,
    mid_weight_ref,
    mid_bias_ref,
    out_ref,
    mid_weight,
    taps,
    rows_held,
    patches,
    active,
    hidden_mid,
    summed,
    weight_sems,
):
    corners = active.shape[1] // 16
    channels = in_weight_ref.shape[3]
    features = in_weight_ref.shape[4]
    columns = out_ref.shape[2]
    position = lax.axis_index("seq")
    section = lax.axis_index("sect")
    filled = tile_ref[position]
    first_row = lax.fori_loop(0, position, lambda d, total: total + tile_ref[d], jnp.int32(0))

    def load(col_tap):
        return [
            pltpu.make_async_copy(
                mid_weight_ref.at[tap, row_tap, col_tap],
                mid_weight.at[col_tap, pl.ds((slot * 3 + row_tap) * features, features)],
                weight_sems.at[col_tap, row_tap, slot],
            )
            for row_tap in range(3)
            for slot, tap in enumerate(TAPS)
        ]

    for col_tap in range(3):
        for copy in load(col_tap):
            copy.start()

    nothing = jnp.zeros((channels, features), jnp.bfloat16)
    base = 0
    for tap in TAPS:
        for row_parity in range(2):
            for i, j, p, q in [
                (i, j, p, q) for i in range(2) for j in range(2) for p in range(2) for q in range(2)
            ]:
                for col_parity in range(2):
                    row_tap, col_tap = 2 * i + p - row_parity, 2 * j + q - col_parity
                    inside = 0 <= row_tap < 3 and 0 <= col_tap < 3
                    taps[base : base + channels, col_parity * features : (col_parity + 1) * features] = (
                        in_weight_ref[tap, row_tap, col_tap] if inside else nothing
                    )
                base += channels

    members, share_rows, _ = latent_ref.shape
    for member in range(members):
        rows_held[member * share_rows : (member + 1) * share_rows] = latent_ref[member].astype(
            jnp.float32
        )
    latent = rows_held[...]
    held_rows = latent.shape[0]
    aside = pltpu.roll(latent, latent.shape[1] - 64, 1).astype(jnp.bfloat16)
    latent = latent.astype(jnp.bfloat16)
    unit = lax.broadcasted_iota(jnp.int32, (UNITS, held_rows), 0)
    held = lax.broadcasted_iota(jnp.int32, (UNITS, held_rows), 1)
    reach = (unit >> 4) + (unit & 7)
    frame = (unit >> 3) & 1
    selectors = []
    for tap in TAPS:
        for row_parity in range(2):
            for i in range(2):
                token_row = first_row + (reach >> 1) - 1 + i
                source = frame + tap - 2
                wanted = (
                    ((reach & 1) == row_parity)
                    & (token_row >= 0)
                    & (token_row < grid_rows)
                    & (source >= 0)
                )
                target = jnp.where(wanted, source * grid_rows + token_row, -1)
                selectors.append(jnp.where(held == target, 1.0, 0.0).astype(jnp.bfloat16))
    selector = jnp.concatenate(selectors, axis=0)
    even = jnp.dot(selector, latent, preferred_element_type=jnp.float32).astype(jnp.bfloat16)
    odd = jnp.dot(
        selector, aside[:, : corners // 2 * 128], preferred_element_type=jnp.float32
    ).astype(jnp.bfloat16)
    for corner in range(corners):
        chunk = slice(corner // 2 * 128, corner // 2 * 128 + 128)
        for group in range(len(selectors)):
            patches[corner * UNITS : (corner + 1) * UNITS, group * 128 : (group + 1) * 128] = (
                odd if corner % 2 else even
            )[group * UNITS : (group + 1) * UNITS, chunk]

    unit_row = lax.broadcasted_iota(jnp.int32, (UNITS, 1), 0)
    pixel_row = 2 * first_row + (unit_row >> 4) + (unit_row & 7) - 1
    row_inside = (pixel_row >= 0) & (pixel_row < 2 * grid_rows)
    step_corners = 3
    in_bias = in_bias_ref[...].reshape(1, features)
    half_gain = gain_ref[...].reshape(1, features) * 0.5

    def first_layer(step, carried):
        start = pl.multiple_of(step * step_corners * UNITS, 16)
        block = jnp.dot(
            patches[pl.ds(start, step_corners * UNITS)],
            taps[...],
            preferred_element_type=jnp.float32,
        )
        hiddens, actives = [carried[0]], [carried[1]]
        for corner in range(step_corners):
            for col_parity in range(2):
                hidden = (
                    block[
                        corner * UNITS : (corner + 1) * UNITS,
                        col_parity * features : (col_parity + 1) * features,
                    ]
                    + in_bias
                )
                hidden = hidden.astype(jnp.bfloat16).astype(jnp.float32)
                scale = lax.rsqrt(jnp.mean(hidden * hidden, axis=1, keepdims=True) + 1e-06)
                pixel = section * columns + 2 * (step * step_corners + corner) + col_parity - 1
                keep = row_inside & (pixel >= 0) & (pixel < width)
                half = hidden * jnp.where(keep, scale, 0.0) * half_gain
                actives.append(half + half * jnp.tanh(half))
                hiddens.append(hidden[16:32])
        for pair in range(step_corners):
            at = pl.ds(pl.multiple_of((step * step_corners + pair) * 16, 16), 16)
            for phase in range(2):
                left, right = actives[2 * pair + 1 - phase], actives[2 * pair + 2 - phase]
                for field in range(LF):
                    for row_tap in range(3):
                        low = row_tap * 16 + field * 8
                        lane = (field * 3 + row_tap) * features
                        joined = jnp.concatenate([left[low : low + 8], right[low : low + 8]], axis=0)
                        active[phase, at, lane : lane + features] = joined.astype(jnp.bfloat16)
            left, right = hiddens[2 * pair], hiddens[2 * pair + 1]
            for field in range(LF):
                low = field * 8
                joined = jnp.concatenate([left[low : low + 8], right[low : low + 8]], axis=0)
                hidden_mid[at, field * features : (field + 1) * features] = joined.astype(jnp.bfloat16)
        return hiddens[-1], actives[-1]

    lax.fori_loop(
        0,
        corners // step_corners,
        first_layer,
        (jnp.zeros((16, features), jnp.float32), jnp.zeros((UNITS, features), jnp.float32)),
    )

    rows = columns * ROWS
    depth = 3 * features
    mid_bias = mid_bias_ref[...].reshape(1, features)
    for col_tap in range(3):
        for copy in load(col_tap):
            copy.wait()
        low = 0 if col_tap == 0 else 16
        window = active[col_tap % 2, low : low + rows]
        early = jnp.dot(
            window[:, :depth], mid_weight[col_tap, depth:], preferred_element_type=jnp.float32
        )
        late = jnp.dot(window, mid_weight[col_tap], preferred_element_type=jnp.float32)
        for field, part in enumerate((early, late)):
            for lane in range(features // 128):
                lanes = slice(lane * 128, (lane + 1) * 128)
                value = part[:, lanes]
                if col_tap:
                    value = value + summed[field, lane]
                if col_tap == 2:
                    from_lane = field * features + lane * 128
                    value = (
                        value
                        + mid_bias[:, lanes]
                        + hidden_mid[16 : 16 + rows, from_lane : from_lane + 128].astype(jnp.float32)
                    )
                summed[field, lane] = value

    for field in range(LF):
        for row in range(ROWS):
            for lane in range(features // 128):
                value = summed[field, lane, pl.ds(row, columns, stride=ROWS), :]
                value = jnp.where(row < 2 * filled, value, 0.0)
                out_ref[field, row, :, lane * 128 : (lane + 1) * 128] = value.astype(jnp.bfloat16)


def decode_tile(
    latent,
    grid_rows,
    tile_rows,
    conv_in_weight,
    conv_in_bias,
    norm_gain,
    conv_mid_weight,
    conv_mid_bias,
):
    sections = lax.axis_size("sect")
    channels, features = conv_in_weight.shape[3:]
    token_width = 4 * channels
    span = latent.shape[2] // token_width - 2
    columns = 2 * span
    corners = span + 1
    vmem = pl.BlockSpec(memory_space=pltpu.VMEM)
    slots = len(TAPS)
    depth = slots * 2 * 4 * token_width
    return pl.pallas_call(
        functools.partial(decode_body, grid_rows, columns * sections),
        in_specs=[
            pl.BlockSpec(memory_space=pltpu.SMEM),
            vmem,
            vmem,
            vmem,
            vmem,
            pl.BlockSpec(memory_space=pl.ANY),
            vmem,
        ],
        out_specs=vmem,
        out_shape=jax.ShapeDtypeStruct((LF, ROWS, columns, features), jnp.bfloat16),
        scratch_shapes=[
            pltpu.VMEM((3, slots * 3 * features, features), jnp.bfloat16),
            pltpu.VMEM((depth, 2 * features), jnp.bfloat16),
            pltpu.VMEM((latent.shape[0] * latent.shape[1], latent.shape[2]), jnp.float32),
            pltpu.VMEM((corners * UNITS, depth), jnp.bfloat16),
            pltpu.VMEM((2, corners * 16, LF * 3 * features), jnp.bfloat16),
            pltpu.VMEM((corners * 16, LF * features), jnp.bfloat16),
            pltpu.VMEM((LF, features // 128, columns * ROWS, 128), jnp.float32),
            pltpu.SemaphoreType.DMA((3, 3, slots)),
        ],
        compiler_params=pltpu.CompilerParams(vmem_limit_bytes=DECODE_VMEM),
        cost_estimate=pl.CostEstimate(
            flops=2 * 3 * 9 * columns * ROWS * features * features,
            bytes_accessed=slots * 9 * features * features * 2,
            transcendentals=corners * UNITS * 2 * features,
        ),
        name="decode_tile",
    )(
        tile_rows,
        latent,
        conv_in_weight,
        conv_in_bias,
        norm_gain,
        conv_mid_weight,
        conv_mid_bias,
    )


def on_device(
    queries,
    key_tokens,
    value_tokens,
    latent,
    tile_rows,
    conv_in_weight,
    conv_in_bias,
    norm_gain,
    conv_mid_weight,
    conv_mid_bias,
):
    devices = lax.axis_size("seq")
    groups = parity_groups(devices)
    grid_rows = latent.shape[0] * devices // LF
    packed, share = pack_heads(
        queries, key_tokens, value_tokens, latent, 4 * conv_in_weight.shape[3]
    )
    own = lax.all_to_all(packed, "seq", 0, 0, axis_index_groups=groups, tiled=True)
    gathered = lax.all_to_all(share, "seq", 0, 0, tiled=True)
    frames = decode_tile(
        gathered,
        grid_rows,
        tile_rows,
        conv_in_weight,
        conv_in_bias,
        norm_gain,
        conv_mid_weight,
        conv_mid_bias,
    )
    own, frames = lax.optimization_barrier((own, frames))
    other = lax.ppermute(own, "seq", [(i, i ^ 1) for i in range(devices)])
    mixed = attend(own, other)
    returned = lax.all_to_all(mixed, "seq", 0, 0, axis_index_groups=groups, tiled=True)
    return (unpack_heads(returned), frames)


def solution(mesh):
    in_specs = (
        P("seq", None),
        P("seq", None),
        P("seq", None),
        P("seq", None),
        P(),
        P(),
        P(),
        P(),
        P(),
        P(),
    )
    out_specs = (P("seq", "sect"), P(None, "seq", "sect", None))
    return jax.shard_map(
        on_device, mesh=mesh, in_specs=in_specs, out_specs=out_specs, check_vma=False
    )
```

time: 73.4 us -> 55.6 us (0.76)
  blocking collectives: 20 us -> 29.4 us
  starting transfers between devices: 10.6 us -> 3.52 us
  waiting for transfers between devices: 8.29 us -> 1.71 us
  local copies, waits for them, and re-layouts: 9.28 us -> 3.67 us
  Pallas kernels: 21.2 us -> 16.1 us
  other arithmetic: 2.64 us -> 0 us
    all_to_all x0 -> x2, blocking collectives: none -> 29.4 us  [the longest x1 16.1 us: on_device(): gathered = lax.all_to_all(share, 'seq', 0, 0, tiled=True)]
    all_gather x1 -> x0, blocking collectives: 20 us -> none  [decode_tile(): gathered = lax.all_gather(share, 'seq', axis=0, tiled=True)]
    all_to_all x2 -> x1, waiting for transfers between devices: 8.29 us -> 0.01 us  [on_device(): lax.all_to_all(packed, 'seq', 0, 0, axis_index_groups=groups, tiled=True)]
    all_to_all x2 -> x1, starting transfers between devices: 10.6 us -> 3.45 us  [on_device(): lax.all_to_all(packed, 'seq', 0, 0, axis_index_groups=groups, tiled=True)]
    pallas_call x5 -> x4, Pallas kernels: 21.2 us -> 16.1 us  [the longest x1 10.6 us: decode_tile(): pl.pallas_call(functools.partial(decode_body, grid_rows, columns * sectio...]
    reshape x3 -> x0, local copies, waits for them, and re-layouts: 3.77 us -> none  [the longest x1 1.26 us: decode_tile(): conv_mid_bias.reshape(1, -1)]
    another operation x3 -> x0, other arithmetic: 1.98 us -> none  [the longest x1 1.83 us: decode_tile(): jnp.stack([tile_starts[position], tile_rows[position], section])]
    dynamic_slice x2 -> x0, local copies, waits for them, and re-layouts: 1.86 us -> none  [the longest x1 1.27 us: decode_tile(): tile_rows[position]]
  transfers between devices with their start and end apart: 3 -> 2, of which waited for: 1 -> 1; matrix products, arithmetic and copies ran while one was open for 14% -> 0% of each run, Pallas kernels for 20% -> 19%
where the time goes in v2:
time: 55.6 us; the launch traced here: 55 us
  blocking collectives  29.4 us (53%)
  Pallas kernels  16.1 us (29%)
  local copies, waits for them, and re-layouts  3.67 us (7%)
  starting transfers between devices  3.52 us (6%)
  waiting for transfers between devices  1.71 us (3%)
  between operations  0.69 us (1%)
    all_to_all x1, blocking collectives, on_device(): gathered = lax.all_to_all(share, 'seq', 0, 0, tiled=True)  16.1 us
    all_to_all x1, blocking collectives, on_device(): lax.all_to_all(mixed, 'seq', 0, 0, axis_index_groups=groups, tiled=True)  13.2 us
    pallas_call x1, Pallas kernels, decode_tile(): pl.pallas_call(functools.partial(decode_body, grid_rows, columns * sectio...  10.6 us
    unnamed x10, local copies, waits for them, and re-layouts  3.67 us
    all_to_all x1, starting transfers between devices, on_device(): lax.all_to_all(packed, 'seq', 0, 0, axis_index_groups=groups, tiled=True)  3.45 us
    pallas_call x1, Pallas kernels, pack_heads(): pl.pallas_call(pack_body, in_specs=[hbm, hbm, hbm, vmem], out_specs=[vmem...  2.7 us
    ppermute x1, waiting for transfers between devices, on_device(): other = lax.ppermute(own, 'seq', [(i, i ^ 1) for i in range(devices)])  1.71 us
    pallas_call x1, Pallas kernels, unpack_heads(): pl.pallas_call(unpack_body, in_specs=[pl.BlockSpec(memory_space=pltpu.VME...  1.58 us
  transfers between devices with their start and end apart: 2, of which 1 were waited for; matrix products, arithmetic and copies ran while one was open for 0% of the time, Pallas kernels for 19%

profile of v2, /device:TPU:0, one launch (start us, length us, event | category | flops | bytes accessed | tf_op | source)
XLA Modules:
  0.0 55.0 jit_solution(12268313045150314393)
XLA Ops:
  0.6 2.7 %pack_heads.1 = (bf16[8,3,64,128]{3,2,1,0:T(8,128)(2,1)}, bf16[16,4,1408]{2,1,0:T(4,128)(2,1)}) custom-call(bf16[64,2048]{1,0:T(8,128)(2,1)} %query_ref.1, bf16[64,2048]{1,0:T(8,128)(2,1)} %key_ref.1, bf16[64,2048]{1,0:T(8,128)(2,1)} %value_ref.1, bf16[4,2560]{1,0:T(4,128)(2,1)} %latent_ref.1), custom_call_target="tpu_custom_call" | custom-call | tf_op jit(solution)/shard_map/pack_heads/pallas_call | solution.py:58
  3.3 16.1 %all_to_all.15.latent_ref = bf16[16,4,1408]{2,1,0:T(4,128)(2,1)S(1)} all-to-all(bf16[16,4,1408]{2,1,0:T(4,128)(2,1)} %get-tuple-element.7), channel_id=1, replica_groups=mesh['sect'=2,'seq'=16] {'seq'}, dimensions={0} | all-to-all | bytes 360448 | tf_op jit(solution)/shard_map/all_to_all | solution.py:403
  19.4 3.5 %all-to-all-start = ((bf16[8,3,64,128]{3,2,1,0:T(8,128)(2,1)}), bf16[8,3,64,128]{3,2,1,0:T(8,128)(2,1)S(1)}, u32[]{:S(2)}, u32[]{:S(2)}) async-start(bf16[8,3,64,128]{3,2,1,0:T(8,128)(2,1)} %get-tuple-element.6), calls=%async_computation | async-start | bytes 786432 | tf_op jit(solution)/shard_map/all_to_all | solution.py:402
  22.9 0.0 copy-start
  22.9 1.0 %copy-done = bf16[3,3,3,16,384]{4,3,2,1,0:T(8,128)(2,1)S(1)} copy-done((bf16[3,3,3,16,384]{4,3,2,1,0:T(8,128)(2,1)S(1)}, bf16[3,3,3,16,384]{4,3,2,1,0:T(8,128)(2,1)}, u32[]{:S(2)}) %copy-start) | copy-done | bytes 331800
  23.9 0.0 copy-start.1
  23.9 0.7 %copy-done.1 = f32[384]{0:T(512)S(1)} copy-done((f32[384]{0:T(512)S(1)}, f32[384]{0:T(512)}, u32[]{:S(2)}) %copy-start.1) | copy-done | bytes 1560
  24.6 0.0 copy-start.2
  24.6 0.7 %copy-done.2 = f32[384]{0:T(512)S(1)} copy-done((f32[384]{0:T(512)S(1)}, f32[384]{0:T(512)}, u32[]{:S(2)}) %copy-start.2) | copy-done | bytes 1560
  25.2 0.0 copy-start.3
  25.2 0.7 %copy-done.3 = f32[384]{0:T(512)S(1)} copy-done((f32[384]{0:T(512)S(1)}, f32[384]{0:T(512)}, u32[]{:S(2)}) %copy-start.3) | copy-done | bytes 1560
  25.9 0.0 copy-start.4
  25.9 0.7 %copy-done.4 = s32[16]{0:T(128)S(1)} copy-done((s32[16]{0:T(128)S(1)}, s32[16]{0:T(128)}, u32[]{:S(2)}) %copy-start.4) | copy-done | bytes 88
  26.6 10.6 %decode_tile.1 = bf16[2,8,40,384]{3,2,1,0:T(8,128)(2,1)} custom-call(s32[16]{0:T(128)S(1)} %copy-done.4, bf16[16,4,1408]{2,1,0:T(4,128)(2,1)S(1)} %all_to_all.15.latent_ref, bf16[3,3,3,16,384]{4,3,2,1,0:T(8,128)(2,1)S(1)} %copy-done, f32[384]{0:T(512)S(1)} %copy-done.1, f32[384]{0:T(512)S(1)} %copy-done.2, bf16[3,3,3,384,384]{4,3,2,1,0:T(8,128)(2,1)} %mid_weight_ref.1, ...), custom_call_target="tpu_custom_call" | custom-call | flops 2548039680 | bytes 5308416 | tf_op jit(solution)/shard_map/decode_tile/pallas_call | solution.py:343
  37.2 0.0 all-to-all-done.own_ref
  37.2 0.1 collective-permute-start
  37.3 1.7 %collective-permute-done.other_ref = bf16[8,3,64,128]{3,2,1,0:T(8,128)(2,1)S(1)} collective-permute-done((bf16[8,3,64,128]{3,2,1,0:T(8,128)(2,1)S(1)}, bf16[8,3,64,128]{3,2,1,0:T(8,128)(2,1)S(1)}, u32[]{:S(2)}, u32[]{:S(2)}) %collective-permute-start) | collective-permute-done | bytes 393248 | tf_op jit(solution)/shard_map/ppermute | solution.py:415
  39.0 1.2 %attend.1 = bf16[8,64,128]{2,1,0:T(8,128)(2,1)S(1)} custom-call(bf16[8,3,64,128]{3,2,1,0:T(8,128)(2,1)S(1)} %all-to-all-done.own_ref, bf16[8,3,64,128]{3,2,1,0:T(8,128)(2,1)S(1)} %collective-permute-done.other_ref), custom_call_target="tpu_custom_call" | custom-call | flops 268435456 | bytes 917504 | tf_op jit(solution)/shard_map/attend/pallas_call | solution.py:106
  40.2 13.2 %all_to_all.16.in_ref = bf16[8,64,128]{2,1,0:T(8,128)(2,1)} all-to-all(bf16[8,64,128]{2,1,0:T(8,128)(2,1)S(1)} %attend.1), channel_id=1, replica_groups={{0,2,4,6,8,10,12,14},{1,3,5,7,9,11,13,15},{16,18,20,22,24,26,28,30},{17..., dimensions={0} | all-to-all | bytes 262144 | tf_op jit(solution)/shard_map/all_to_all | solution.py:417
  53.4 1.6 %unpack_heads.1 = bf16[64,1024]{1,0:T(8,128)(2,1)} custom-call(bf16[8,64,128]{2,1,0:T(8,128)(2,1)} %all_to_all.16.in_ref), custom_call_target="tpu_custom_call" | custom-call | tf_op jit(solution)/shard_map/unpack_heads/pallas_call | solution.py:128
Async XLA Ops:
  19.4 17.8 %all-to-all-start = ((bf16[8,3,64,128]{3,2,1,0:T(8,128)(2,1)}), bf16[8,3,64,128]{3,2,1,0:T(8,128)(2,1)S(1)}, u32[]{:S(2)}, u32[]{:S(2)}) async-start(bf16[8,3,64,128]{3,2,1,0:T(8,128)(2,1)} %get-tuple-element.6), calls=%async_computation | async-start | bytes 786432 | tf_op jit(solution)/shard_map/all_to_all | solution.py:402
  22.9 1.0 %copy-start = (bf16[3,3,3,16,384]{4,3,2,1,0:T(8,128)(2,1)S(1)}, bf16[3,3,3,16,384]{4,3,2,1,0:T(8,128)(2,1)}, u32[]{:S(2)}) copy-start(bf16[3,3,3,16,384]{4,3,2,1,0:T(8,128)(2,1)} %in_weight_ref.1) | copy-start | bytes 995332
  23.9 0.7 %copy-start.1 = (f32[384]{0:T(512)S(1)}, f32[384]{0:T(512)}, u32[]{:S(2)}) copy-start(f32[384]{0:T(512)} %in_bias_ref.1) | copy-start | bytes 4612
  24.6 0.7 %copy-start.2 = (f32[384]{0:T(512)S(1)}, f32[384]{0:T(512)}, u32[]{:S(2)}) copy-start(f32[384]{0:T(512)} %gain_ref.1) | copy-start | bytes 4612
  25.2 0.7 %copy-start.3 = (f32[384]{0:T(512)S(1)}, f32[384]{0:T(512)}, u32[]{:S(2)}) copy-start(f32[384]{0:T(512)} %mid_bias_ref.1) | copy-start | bytes 4612
  25.9 0.7 %copy-start.4 = (s32[16]{0:T(128)S(1)}, s32[16]{0:T(128)}, u32[]{:S(2)}) copy-start(s32[16]{0:T(128)} %tile_ref.1) | copy-start | bytes 196
  37.2 1.8 %collective-permute-start = (bf16[8,3,64,128]{3,2,1,0:T(8,128)(2,1)S(1)}, bf16[8,3,64,128]{3,2,1,0:T(8,128)(2,1)S(1)}, u32[]{:S(2)}, u32[]{:S(2)}) collective-permute-start(bf16[8,3,64,128]{3,2,1,0:T(8,128)(2,1)S(1)} %all-to-all-done.own_ref), channel_id=1, source_target_pairs={{0,1},{1,0},{2,3},{3,2},{4,5},{5,4},{6,7},{7,6},{8,9},{9,8},{10,11... | collective-permute-start | bytes 1179656 | tf_op jit(solution)/shard_map/ppermute | solution.py:415

commit v3 on v2

--- a/solution.py
+++ b/solution.py
@@ -14,8 +14,9 @@
 TAPS = (1, 2)
 ROWS = 2 * MAXT
 UNITS = 3 * LF * ROWS
+DECODE_VMEM = 44 * 1024 * 1024
 ATTEND_VMEM = 32 * 1024 * 1024
-DECODE_VMEM = 48 * 1024 * 1024
+COPY_VMEM = 16 * 1024 * 1024
 
 
 def parity_groups(devices):
@@ -35,15 +36,13 @@
             copy.start()
             copies.append(copy)
     rows, width = latent_ref.shape
-    span = share_ref.shape[2]
+    span = share_ref.shape[1]
     rim = (2 * span - width) // 4
     wide = latent_ref[...].astype(jnp.float32)
     rim_zeros = jnp.zeros((rows, rim), jnp.float32)
     lower = jnp.concatenate([rim_zeros, wide[:, : span - rim]], axis=1)
     upper = jnp.concatenate([wide[:, width - span + rim :], rim_zeros], axis=1)
-    share = jnp.where(section == 0, lower, upper).astype(share_ref.dtype)
-    for member in range(share_ref.shape[0]):
-        share_ref[member] = share
+    share_ref[...] = jnp.where(section == 0, lower, upper).astype(share_ref.dtype)
     for copy in copies:
         copy.wait()
 
@@ -53,50 +52,65 @@
     sections = lax.axis_size("sect")
     heads = width // DH // sections
     span = latent.shape[1] // sections + 2 * token_width
-    hbm = pl.BlockSpec(memory_space=pl.ANY)
+    hbm = pl.BlockSpec(memory_space=pltpu.HBM)
     vmem = pl.BlockSpec(memory_space=pltpu.VMEM)
     return pl.pallas_call(
         pack_body,
         in_specs=[hbm, hbm, hbm, vmem],
-        out_specs=[vmem, vmem],
+        out_specs=[hbm, vmem],
         out_shape=[
             jax.ShapeDtypeStruct((heads, 3, token_rows, DH), queries.dtype),
-            jax.ShapeDtypeStruct((lax.axis_size("seq"), latent.shape[0], span), latent.dtype),
+            jax.ShapeDtypeStruct((latent.shape[0], span), latent.dtype),
         ],
         scratch_shapes=[pltpu.SemaphoreType.DMA((heads, 3))],
+        compiler_params=pltpu.CompilerParams(vmem_limit_bytes=COPY_VMEM),
         name="pack_heads",
-    )(queries, key_tokens, value_tokens, latent)
+    )(*in_hbm(queries, key_tokens, value_tokens, latent))
+
+
+def in_hbm(*arrays):
+    return [pltpu.with_memory_space_constraint(array, pltpu.HBM) for array in arrays]
+
+
+def gather_rows(array):
+    devices = lax.axis_size("seq")
+    reach = 1
+    parts = [array]
+    while reach < devices:
+        block = parts[0] if len(parts) == 1 else jnp.concatenate(parts, axis=0)
+        parts = [block]
+        for step in range(1, min(4, devices // reach)):
+            parts.append(lax.ppermute(block, "seq", xor_pairs(step * reach)))
+        reach *= 4
+    return parts
+
+
+def xor_pairs(distance):
+    return [(i, i ^ distance) for i in range(lax.axis_size("seq"))]
 
 
 def flat(array):
     return array.reshape(-1, array.shape[-1])
 
 
-def attend_body(block, own_ref, other_ref, out_ref):
+def attend_body(block, own_ref, other_ref, *out_refs):
     members, _, token_rows, _ = own_ref.shape
+    chip = lax.axis_index("seq") // 2
     keys = jnp.concatenate([flat(own_ref[:, 1]), flat(other_ref[:, 1])], axis=0)
     values = jnp.concatenate([flat(own_ref[:, 2]), flat(other_ref[:, 2])], axis=0)
-
-    def one_block(step):
-        at = pl.ds(step * block, block)
+    for step in range(0, members, block):
+        query = jnp.concatenate([own_ref[chip ^ m, 0] for m in range(step, step + block)], axis=0)
         scores = lax.dot_general(
-            flat(own_ref[at, 0]),
-            keys,
-            (((1,), (1,)), ((), ())),
-            preferred_element_type=jnp.float32,
+            query, keys, (((1,), (1,)), ((), ())), preferred_element_type=jnp.float32
         ) * (1.0 / math.sqrt(DH))
         exponents = jnp.exp(scores - jnp.max(scores, axis=1, keepdims=True))
         totals = jnp.sum(exponents, axis=1, keepdims=True)
         mixed = jnp.dot(
             exponents.astype(jnp.bfloat16), values, preferred_element_type=jnp.float32
         )
-        out_ref[at] = (mixed / totals).astype(out_ref.dtype).reshape(block, token_rows, DH)
-
-    if members <= 8:
-        for step in range(members // block):
-            one_block(step)
-    else:
-        pl.loop(0, members // block)(one_block)
+        mixed = (mixed / totals).astype(jnp.bfloat16)
+        for m in range(block):
+            out_refs[step + m][...] = mixed[m * token_rows : (m + 1) * token_rows]
 
 
 def attend(own, other):
@@ -106,8 +120,8 @@
     return pl.pallas_call(
         functools.partial(attend_body, min(4, members)),
         in_specs=[vmem, vmem],
-        out_specs=vmem,
-        out_shape=jax.ShapeDtypeStruct((members, token_rows, DH), own.dtype),
+        out_specs=[vmem] * members,
+        out_shape=[jax.ShapeDtypeStruct((token_rows, DH), own.dtype)] * members,
         compiler_params=pltpu.CompilerParams(vmem_limit_bytes=ATTEND_VMEM),
         cost_estimate=pl.CostEstimate(
             flops=8 * total * total * DH,
@@ -118,41 +132,76 @@
     )(own, other)
 
 
-def unpack_body(in_ref, out_ref):
-    for head in range(in_ref.shape[0]):
-        out_ref[:, head * DH : (head + 1) * DH] = in_ref[head]
-
-
-def unpack_heads(array):
-    heads, token_rows, _ = array.shape
+def unpack_body(*refs):
+    in_refs, out_ref, sems = refs[:-2], refs[-2], refs[-1]
+    chip = lax.axis_index("seq") // 2
+    copies = []
+    for m, ref in enumerate(in_refs):
+        columns = pl.ds(pl.multiple_of((chip ^ m) * DH, DH), DH)
+        copy = pltpu.make_async_copy(ref, out_ref.at[:, columns], sems.at[m])
+        copy.start()
+        copies.append(copy)
+    for copy in copies:
+        copy.wait()
+
+
+def unpack_heads(pieces):
+    heads = len(pieces)
+    token_rows = pieces[0].shape[0]
+    hbm = pl.BlockSpec(memory_space=pltpu.HBM)
+    vmem = pl.BlockSpec(memory_space=pltpu.VMEM)
     return pl.pallas_call(
         unpack_body,
-        in_specs=[pl.BlockSpec(memory_space=pltpu.VMEM)],
-        out_shape=jax.ShapeDtypeStruct((token_rows, heads * DH), array.dtype),
+        in_specs=[vmem] * heads,
+        out_specs=hbm,
+        out_shape=jax.ShapeDtypeStruct((token_rows, heads * DH), pieces[0].dtype),
+        scratch_shapes=[pltpu.SemaphoreType.DMA((heads,))],
+        compiler_params=pltpu.CompilerParams(vmem_limit_bytes=COPY_VMEM),
         name="unpack_heads",
-    )(array)
+    )(*pieces)
 
 
 def decode_body(
     grid_rows,
     width,
-    tile_ref,
-    latent_ref,
-    in_weight_ref,
-    in_bias_ref,
-    gain_ref,
-    mid_weight_ref,
-    mid_bias_ref,
-    out_ref,
-    mid_weight,
-    taps,
-    rows_held,
-    patches,
-    active,
-    hidden_mid,
-    summed,
-    weight_sems,
+    blocks,
+    *refs,
 ):
+    latent_refs, refs = refs[:blocks], refs[blocks:]
+    (
+        tile_ref,
+        in_weight_hbm,
+        in_bias_hbm,
+        gain_hbm,
+        mid_weight_ref,
+        mid_bias_hbm,
+        out_ref,
+        mid_weight,
+        in_weight_ref,
+        in_bias_ref,
+        gain_ref,
+        mid_bias_ref,
+        taps,
+        patches,
+        active,
+        hidden_mid,
+        summed,
+        weight_sems,
+        small_sems,
+    ) = refs
+    small = [
+        pltpu.make_async_copy(source, target, small_sems.at[place])
+        for place, (source, target) in enumerate(
+            (
+                (in_weight_hbm, in_weight_ref),
+                (in_bias_hbm, in_bias_ref),
+                (gain_hbm, gain_ref),
+                (mid_bias_hbm, mid_bias_ref),
+            )
+        )
+    ]
+    for copy in small:
+        copy.start()
     corners = active.shape[1] // 16
     channels = in_weight_ref.shape[3]
     features = in_weight_ref.shape[4]
@@ -177,6 +226,8 @@
         for copy in load(col_tap):
             copy.start()
 
+    for copy in small:
+        copy.wait()
     nothing = jnp.zeros((channels, features), jnp.bfloat16)
     base = 0
     for tap in TAPS:
@@ -192,17 +243,14 @@
                     )
                 base += channels
 
-    members, share_rows, _ = latent_ref.shape
-    for member in range(members):
-        rows_held[member * share_rows : (member + 1) * share_rows] = latent_ref[member].astype(
-            jnp.float32
-        )
-    latent = rows_held[...]
+    latent = jnp.concatenate([ref[...] for ref in latent_refs], axis=0).astype(jnp.float32)
     held_rows = latent.shape[0]
+    share_rows = held_rows // lax.axis_size("seq")
     aside = pltpu.roll(latent, latent.shape[1] - 64, 1).astype(jnp.bfloat16)
     latent = latent.astype(jnp.bfloat16)
     unit = lax.broadcasted_iota(jnp.int32, (UNITS, held_rows), 0)
     held = lax.broadcasted_iota(jnp.int32, (UNITS, held_rows), 1)
+    held = ((held // share_rows) ^ position) * share_rows + held % share_rows
     reach = (unit >> 4) + (unit & 7)
     frame = (unit >> 3) & 1
     selectors = []
@@ -322,7 +370,7 @@
 
 
 def decode_tile(
-    latent,
+    latents,
     grid_rows,
     tile_rows,
     conv_in_weight,
@@ -334,34 +382,31 @@
     sections = lax.axis_size("sect")
     channels, features = conv_in_weight.shape[3:]
     token_width = 4 * channels
-    span = latent.shape[2] // token_width - 2
+    span = latents[0].shape[1] // token_width - 2
     columns = 2 * span
     corners = span + 1
     vmem = pl.BlockSpec(memory_space=pltpu.VMEM)
+    hbm = pl.BlockSpec(memory_space=pltpu.HBM)
     slots = len(TAPS)
     depth = slots * 2 * 4 * token_width
     return pl.pallas_call(
-        functools.partial(decode_body, grid_rows, columns * sections),
-        in_specs=[
-            pl.BlockSpec(memory_space=pltpu.SMEM),
-            vmem,
-            vmem,
-            vmem,
-            vmem,
-            pl.BlockSpec(memory_space=pl.ANY),
-            vmem,
-        ],
+        functools.partial(decode_body, grid_rows, columns * sections, len(latents)),
+        in_specs=[vmem] * len(latents) + [pl.BlockSpec(memory_space=pltpu.SMEM)] + [hbm] * 5,
         out_specs=vmem,
         out_shape=jax.ShapeDtypeStruct((LF, ROWS, columns, features), jnp.bfloat16),
         scratch_shapes=[
             pltpu.VMEM((3, slots * 3 * features, features), jnp.bfloat16),
+            pltpu.VMEM(conv_in_weight.shape, jnp.bfloat16),
+            pltpu.VMEM(conv_in_bias.shape, jnp.float32),
+            pltpu.VMEM(norm_gain.shape, jnp.float32),
+            pltpu.VMEM(conv_mid_bias.shape, jnp.float32),
             pltpu.VMEM((depth, 2 * features), jnp.bfloat16),
-            pltpu.VMEM((latent.shape[0] * latent.shape[1], latent.shape[2]), jnp.float32),
             pltpu.VMEM((corners * UNITS, depth), jnp.bfloat16),
             pltpu.VMEM((2, corners * 16, LF * 3 * features), jnp.bfloat16),
             pltpu.VMEM((corners * 16, LF * features), jnp.bfloat16),
             pltpu.VMEM((LF, features // 128, columns * ROWS, 128), jnp.float32),
             pltpu.SemaphoreType.DMA((3, 3, slots)),
+            pltpu.SemaphoreType.DMA((4,)),
         ],
         compiler_params=pltpu.CompilerParams(vmem_limit_bytes=DECODE_VMEM),
         cost_estimate=pl.CostEstimate(
@@ -371,13 +416,10 @@
         ),
         name="decode_tile",
     )(
-        tile_rows,
-        latent,
-        conv_in_weight,
-        conv_in_bias,
-        norm_gain,
-        conv_mid_weight,
-        conv_mid_bias,
+        *latents,
+        *in_hbm(
+            tile_rows, conv_in_weight, conv_in_bias, norm_gain, conv_mid_weight, conv_mid_bias
+        ),
     )
 
 
@@ -399,10 +441,10 @@
     packed, share = pack_heads(
         queries, key_tokens, value_tokens, latent, 4 * conv_in_weight.shape[3]
     )
+    latents = gather_rows(share)
     own = lax.all_to_all(packed, "seq", 0, 0, axis_index_groups=groups, tiled=True)
-    gathered = lax.all_to_all(share, "seq", 0, 0, tiled=True)
     frames = decode_tile(
-        gathered,
+        latents,
         grid_rows,
         tile_rows,
         conv_in_weight,
@@ -412,9 +454,11 @@
         conv_mid_bias,
     )
     own, frames = lax.optimization_barrier((own, frames))
-    other = lax.ppermute(own, "seq", [(i, i ^ 1) for i in range(devices)])
-    mixed = attend(own, other)
-    returned = lax.all_to_all(mixed, "seq", 0, 0, axis_index_groups=groups, tiled=True)
+    other = lax.ppermute(own, "seq", xor_pairs(1))
+    pieces = attend(own, other)
+    returned = [pieces[0]] + [
+        lax.ppermute(pieces[m], "seq", xor_pairs(2 * m)) for m in range(1, len(pieces))
+    ]
     return (unpack_heads(returned), frames)
 
 

time: 55.6 us -> 68.4 us (1.23)
  blocking collectives: 29.4 us -> 0 us
  starting transfers between devices: 3.52 us -> 25.1 us
  waiting for transfers between devices: 1.71 us -> 14.7 us
  Pallas kernels: 16.1 us -> 27.6 us
  local copies, waits for them, and re-layouts: 3.67 us -> 0 us
    all_to_all x2 -> x0, blocking collectives: 29.4 us -> none  [the longest x1 16.1 us: on_device(): gathered = lax.all_to_all(share, 'seq', 0, 0, tiled=True)]
    ppermute x1 -> x14, starting transfers between devices: 0.07 us -> 17.9 us  [the longest x7 11.2 us: on_device(): lax.ppermute(pieces[m], 'seq', xor_pairs(2 * m))]
    ppermute x1 -> x14, waiting for transfers between devices: 1.71 us -> 14.7 us  [the longest x6 8.92 us: gather_rows(): parts.append(lax.ppermute(block, 'seq', xor_pairs(step * reach)))]
    pallas_call x2, Pallas kernels: 4.28 us -> 14.7 us  [the longest x1 14 us: pack_heads(): pl.pallas_call(pack_body, in_specs=[hbm, hbm, hbm, vmem], out_specs=[hbm,...]
    all_to_all x1, starting transfers between devices: 3.45 us -> 7.26 us  [on_device(): lax.all_to_all(packed, 'seq', 0, 0, axis_index_groups=groups, tiled=True)]
    unnamed x10 -> x0, local copies, waits for them, and re-layouts: 3.67 us -> none
    pallas_call x1, Pallas kernels: 10.6 us -> 11.7 us  [decode_tile(): pl.pallas_call(functools.partial(decode_body, grid_rows, columns * sectio...]
  transfers between devices with their start and end apart: 2 -> 15, of which waited for: 1 -> 7; matrix products, arithmetic and copies ran while one was open for 0% -> 0% of each run, Pallas kernels for 19% -> 17%
where the time goes in v3:
time: 68.4 us; the launch traced here: 68.1 us
  Pallas kernels  27.6 us (40%)
  starting transfers between devices  25.1 us (37%)
  waiting for transfers between devices  14.7 us (21%)
  between operations  0.69 us (1%)
    pallas_call x1, Pallas kernels, pack_heads(): pl.pallas_call(pack_body, in_specs=[hbm, hbm, hbm, vmem], out_specs=[hbm,...  14 us
    pallas_call x1, Pallas kernels, decode_tile(): pl.pallas_call(functools.partial(decode_body, grid_rows, columns * sectio...  11.7 us
    ppermute x7, starting transfers between devices, on_device(): lax.ppermute(pieces[m], 'seq', xor_pairs(2 * m))  11.2 us
    ppermute x6, waiting for transfers between devices, gather_rows(): parts.append(lax.ppermute(block, 'seq', xor_pairs(step * reach)))  8.92 us
    all_to_all x1, starting transfers between devices, on_device(): lax.all_to_all(packed, 'seq', 0, 0, axis_index_groups=groups, tiled=True)  7.26 us
    ppermute x6, starting transfers between devices, gather_rows(): parts.append(lax.ppermute(block, 'seq', xor_pairs(step * reach)))  6.59 us
    ppermute x7, waiting for transfers between devices, on_device(): lax.ppermute(pieces[m], 'seq', xor_pairs(2 * m))  4.06 us
    ppermute x1, waiting for transfers between devices, on_device(): other = lax.ppermute(own, 'seq', xor_pairs(1))  1.71 us
  transfers between devices with their start and end apart: 15, of which 7 were waited for; matrix products, arithmetic and copies ran while one was open for 0% of the time, Pallas kernels for 17%

profile of v3, /device:TPU:0, one launch (start us, length us, event | category | flops | bytes accessed | tf_op | source)
XLA Modules:
  0.0 68.1 jit_solution(4150631920169823202)
XLA Ops:
  0.6 14.0 %pack_heads.1 = (bf16[8,3,64,128]{3,2,1,0:T(8,128)(2,1)}, bf16[4,1408]{1,0:T(4,128)(2,1)S(1)}) custom-call(bf16[64,2048]{1,0:T(8,128)(2,1)} %query_ref.1, bf16[64,2048]{1,0:T(8,128)(2,1)} %key_ref.1, bf16[64,2048]{1,0:T(8,128)(2,1)} %value_ref.1, bf16[4,2560]{1,0:T(4,128)(2,1)} %latent_ref.1), custom_call_target="tpu_custom_call" | custom-call | tf_op jit(solution)/shard_map/pack_heads/pallas_call | solution.py:57
  14.6 7.3 %all-to-all-start = ((bf16[8,3,64,128]{3,2,1,0:T(8,128)(2,1)}), bf16[8,3,64,128]{3,2,1,0:T(8,128)(2,1)S(1)}, u32[]{:S(2)}, u32[]{:S(2)}) async-start(bf16[8,3,64,128]{3,2,1,0:T(8,128)(2,1)} %get-tuple-element.14), calls=%async_computation | async-start | bytes 786432 | tf_op jit(solution)/shard_map/all_to_all | solution.py:445
  21.9 0.9 %collective-permute-start.2 = (bf16[4,1408]{1,0:T(4,128)(2,1)S(1)}, bf16[4,1408]{1,0:T(4,128)(2,1)S(1)}, u32[]{:S(2)}, u32[]{:S(2)}) collective-permute-start(bf16[4,1408]{1,0:T(4,128)(2,1)S(1)} %get-tuple-element.15), channel_id=1, source_target_pairs={{0,3},{1,2},{2,1},{3,0},{4,7},{5,6},{6,5},{7,4},{8,11},{9,10},{10,... | collective-permute-start | bytes 33800 | tf_op jit(solution)/shard_map/ppermute | solution.py:83
  22.8 1.2 %collective-permute-start.1 = (bf16[4,1408]{1,0:T(4,128)(2,1)S(1)}, bf16[4,1408]{1,0:T(4,128)(2,1)S(1)}, u32[]{:S(2)}, u32[]{:S(2)}) collective-permute-start(bf16[4,1408]{1,0:T(4,128)(2,1)S(1)} %get-tuple-element.15), channel_id=1, source_target_pairs={{0,2},{1,3},{2,0},{3,1},{4,6},{5,7},{6,4},{7,5},{8,10},{9,11},{10,... | collective-permute-start | bytes 33800 | tf_op jit(solution)/shard_map/ppermute | solution.py:83
  23.9 0.1 collective-permute-start
  24.0 1.0 %collective-permute-done.2 = bf16[4,1408]{1,0:T(4,128)(2,1)S(1)} collective-permute-done((bf16[4,1408]{1,0:T(4,128)(2,1)S(1)}, bf16[4,1408]{1,0:T(4,128)(2,1)S(1)}, u32[]{:S(2)}, u32[]{:S(2)}) %collective-permute-start.2) | collective-permute-done | bytes 11296 | tf_op jit(solution)/shard_map/ppermute | solution.py:83
  25.0 3.3 %collective-permute-done.1 = bf16[4,1408]{1,0:T(4,128)(2,1)S(1)} collective-permute-done((bf16[4,1408]{1,0:T(4,128)(2,1)S(1)}, bf16[4,1408]{1,0:T(4,128)(2,1)S(1)}, u32[]{:S(2)}, u32[]{:S(2)}) %collective-permute-start.1) | collective-permute-done | bytes 11296 | tf_op jit(solution)/shard_map/ppermute | solution.py:83
  28.3 0.0 collective-permute-done
  28.3 3.3 %collective-permute-start.5 = (bf16[16,1408]{1,0:T(8,128)(2,1)S(1)}, bf16[16,1408]{1,0:T(8,128)(2,1)S(1)}, u32[]{:S(2)}, u32[]{:S(2)}) collective-permute-start(bf16[16,1408]{1,0:T(8,128)(2,1)S(1)} %pad_maximum_fusion.refs_0_), channel_id=1, source_target_pairs={{0,12},{1,13},{2,14},{3,15},{4,8},{5,9},{6,10},{7,11},{8,4},{9,5},... | collective-permute-start | bytes 135176 | tf_op jit(solution)/shard_map/ppermute | solution.py:83
  31.6 0.0 collective-permute-start.4
  31.6 1.2 %collective-permute-start.3 = (bf16[16,1408]{1,0:T(8,128)(2,1)S(1)}, bf16[16,1408]{1,0:T(8,128)(2,1)S(1)}, u32[]{:S(2)}, u32[]{:S(2)}) collective-permute-start(bf16[16,1408]{1,0:T(8,128)(2,1)S(1)} %pad_maximum_fusion.refs_0_), channel_id=1, source_target_pairs={{0,4},{1,5},{2,6},{3,7},{4,0},{5,1},{6,2},{7,3},{8,12},{9,13},{10,... | collective-permute-start | bytes 135176 | tf_op jit(solution)/shard_map/ppermute | solution.py:83
  32.8 1.6 %collective-permute-done.5.refs_3_ = bf16[16,1408]{1,0:T(8,128)(2,1)S(1)} collective-permute-done((bf16[16,1408]{1,0:T(8,128)(2,1)S(1)}, bf16[16,1408]{1,0:T(8,128)(2,1)S(1)}, u32[]{:S(2)}, u32[]{:S(2)}) %collective-permute-start.5) | collective-permute-done | bytes 45088 | tf_op jit(solution)/shard_map/ppermute | solution.py:83
  34.3 3.1 %collective-permute-done.4.refs_2_ = bf16[16,1408]{1,0:T(8,128)(2,1)S(1)} collective-permute-done((bf16[16,1408]{1,0:T(8,128)(2,1)S(1)}, bf16[16,1408]{1,0:T(8,128)(2,1)S(1)}, u32[]{:S(2)}, u32[]{:S(2)}) %collective-permute-start.4) | collective-permute-done | bytes 45088 | tf_op jit(solution)/shard_map/ppermute | solution.py:83
  37.4 0.0 collective-permute-done.3.refs_1_
  37.4 11.7 %decode_tile.1 = bf16[2,8,40,384]{3,2,1,0:T(8,128)(2,1)} custom-call(bf16[16,1408]{1,0:T(8,128)(2,1)S(1)} %pad_maximum_fusion.refs_0_, bf16[16,1408]{1,0:T(8,128)(2,1)S(1)} %collective-permute-done.3.refs_1_, bf16[16,1408]{1,0:T(8,128)(2,1)S(1)} %collective-permute-done.4.refs_2_, bf16[16,1408]{1,0:T(8,128)(2,1)S(1)} %collective-permute-done.5.refs_3_, ...), custom_call_target="tpu_custom_call" | custom-call | flops 2548039680 | bytes 5308416 | tf_op jit(solution)/shard_map/decode_tile/pallas_call | solution.py:392
  49.2 0.0 all-to-all-done.own_ref
  49.2 0.1 collective-permute-start.6
  49.2 1.7 %collective-permute-done.6.other_ref = bf16[8,3,64,128]{3,2,1,0:T(8,128)(2,1)S(1)} collective-permute-done((bf16[8,3,64,128]{3,2,1,0:T(8,128)(2,1)S(1)}, bf16[8,3,64,128]{3,2,1,0:T(8,128)(2,1)S(1)}, u32[]{:S(2)}, u32[]{:S(2)}) %collective-permute-start.6) | collective-permute-done | bytes 393248 | tf_op jit(solution)/shard_map/ppermute | solution.py:457
  51.0 1.2 %attend.1 = (bf16[64,128]{1,0:T(8,128)(2,1)S(1)}, bf16[64,128]{1,0:T(8,128)(2,1)S(1)}, bf16[64,128]{1,0:T(8,128)(2,1)S(1)}, bf16[64,128]{1,0:T(8,128)(2,1)S(1)},...) custom-call(bf16[8,3,64,128]{3,2,1,0:T(8,128)(2,1)S(1)} %all-to-all-, ...), custom_call_target="tpu_custom_call" | custom-call | flops 268435456 | bytes 917504 | tf_op jit(solution)/shard_map/attend/pallas_call | solution.py:120
  52.1 1.5 %collective-permute-start.7 = (bf16[64,128]{1,0:T(8,128)(2,1)S(1)}, bf16[64,128]{1,0:T(8,128)(2,1)S(1)}, u32[]{:S(2)}, u32[]{:S(2)}) collective-permute-start(bf16[64,128]{1,0:T(8,128)(2,1)S(1)} %get-tuple-element.18), channel_id=1, source_target_pairs={{0,2},{1,3},{2,0},{3,1},{4,6},{5,7},{6,4},{7,5},{8,10},{9,11},{10,... | collective-permute-start | bytes 49160 | tf_op jit(solution)/shard_map/ppermute | solution.py:460
  53.6 0.1 collective-permute-start.8
  53.7 2.0 %collective-permute-start.9 = (bf16[64,128]{1,0:T(8,128)(2,1)S(1)}, bf16[64,128]{1,0:T(8,128)(2,1)S(1)}, u32[]{:S(2)}, u32[]{:S(2)}) collective-permute-start(bf16[64,128]{1,0:T(8,128)(2,1)S(1)} %get-tuple-element.20), channel_id=1, source_target_pairs={{0,6},{1,7},{2,4},{3,5},{4,2},{5,3},{6,0},{7,1},{8,14},{9,15},{10,... | collective-permute-start | bytes 49160 | tf_op jit(solution)/shard_map/ppermute | solution.py:460
  55.7 1.1 %collective-permute-start.10 = (bf16[64,128]{1,0:T(8,128)(2,1)S(1)}, bf16[64,128]{1,0:T(8,128)(2,1)S(1)}, u32[]{:S(2)}, u32[]{:S(2)}) collective-permute-start(bf16[64,128]{1,0:T(8,128)(2,1)S(1)} %get-tuple-element.21), channel_id=1, source_target_pairs={{0,8},{1,9},{2,10},{3,11},{4,12},{5,13},{6,14},{7,15},{8,0},{9,1},... | collective-permute-start | bytes 49160 | tf_op jit(solution)/shard_map/ppermute | solution.py:460
  56.8 2.7 %collective-permute-start.11 = (bf16[64,128]{1,0:T(8,128)(2,1)S(1)}, bf16[64,128]{1,0:T(8,128)(2,1)S(1)}, u32[]{:S(2)}, u32[]{:S(2)}) collective-permute-start(bf16[64,128]{1,0:T(8,128)(2,1)S(1)} %get-tuple-element.22), channel_id=1, source_target_pairs={{0,10},{1,11},{2,8},{3,9},{4,14},{5,15},{6,12},{7,13},{8,2},{9,3},... | collective-permute-start | bytes 49160 | tf_op jit(solution)/shard_map/ppermute | solution.py:460
  59.5 0.0 collective-permute-done.7.refs_1_
  59.5 1.5 %collective-permute-start.12 = (bf16[64,128]{1,0:T(8,128)(2,1)S(1)}, bf16[64,128]{1,0:T(8,128)(2,1)S(1)}, u32[]{:S(2)}, u32[]{:S(2)}) collective-permute-start(bf16[64,128]{1,0:T(8,128)(2,1)S(1)} %get-tuple-element.23), channel_id=1, source_target_pairs={{0,12},{1,13},{2,14},{3,15},{4,8},{5,9},{6,10},{7,11},{8,4},{9,5},... | collective-permute-start | bytes 49160 | tf_op jit(solution)/shard_map/ppermute | solution.py:460
  61.0 0.0 collective-permute-done.8.refs_2_
  61.0 2.4 %collective-permute-start.13 = (bf16[64,128]{1,0:T(8,128)(2,1)S(1)}, bf16[64,128]{1,0:T(8,128)(2,1)S(1)}, u32[]{:S(2)}, u32[]{:S(2)}) collective-permute-start(bf16[64,128]{1,0:T(8,128)(2,1)S(1)} %get-tuple-element.24), channel_id=1, source_target_pairs={{0,14},{1,15},{2,12},{3,13},{4,10},{5,11},{6,8},{7,9},{8,6},{9,7},... | collective-permute-start | bytes 49160 | tf_op jit(solution)/shard_map/ppermute | solution.py:460
  63.4 0.0 collective-permute-done.11.refs_5_
  63.4 1.7 %collective-permute-done.12.refs_6_ = bf16[64,128]{1,0:T(8,128)(2,1)S(1)} collective-permute-done((bf16[64,128]{1,0:T(8,128)(2,1)S(1)}, bf16[64,128]{1,0:T(8,128)(2,1)S(1)}, u32[]{:S(2)}, u32[]{:S(2)}) %collective-permute-start.12) | collective-permute-done | bytes 16416 | tf_op jit(solution)/shard_map/ppermute | solution.py:460
  65.0 2.4 %collective-permute-done.13.refs_7_ = bf16[64,128]{1,0:T(8,128)(2,1)S(1)} collective-permute-done((bf16[64,128]{1,0:T(8,128)(2,1)S(1)}, bf16[64,128]{1,0:T(8,128)(2,1)S(1)}, u32[]{:S(2)}, u32[]{:S(2)}) %collective-permute-start.13) | collective-permute-done | bytes 16416 | tf_op jit(solution)/shard_map/ppermute | solution.py:460
  67.4 0.7 %unpack_heads.1 = bf16[64,1024]{1,0:T(8,128)(2,1)} custom-call(bf16[64,128]{1,0:T(8,128)(2,1)S(1)} %get-tuple-element.17.refs_0_, bf16[64,128]{1,0:T(8,128)(2,1)S(1)} %collective-permute-done.7.refs_1_, bf16[64,128]{1,0:T(8,128)(2,1)S(1)} %collective-permute-done.8.refs_2_, bf16[64,128]{1,0:T(8,128)(2,1)S(1)} %collective-permute-done.9.refs_3_, ...), custom_call_target="tpu_custom_call" | custom-call | tf_op jit(solution)/shard_map/unpack_heads/pallas_call | solution.py:153
  (3 shorter events, 0.0 us)
Async XLA Ops:
  14.6 34.6 %all-to-all-start = ((bf16[8,3,64,128]{3,2,1,0:T(8,128)(2,1)}), bf16[8,3,64,128]{3,2,1,0:T(8,128)(2,1)S(1)}, u32[]{:S(2)}, u32[]{:S(2)}) async-start(bf16[8,3,64,128]{3,2,1,0:T(8,128)(2,1)} %get-tuple-element.14), calls=%async_computation | async-start | bytes 786432 | tf_op jit(solution)/shard_map/all_to_all | solution.py:445
  21.9 3.1 %collective-permute-start.2 = (bf16[4,1408]{1,0:T(4,128)(2,1)S(1)}, bf16[4,1408]{1,0:T(4,128)(2,1)S(1)}, u32[]{:S(2)}, u32[]{:S(2)}) collective-permute-start(bf16[4,1408]{1,0:T(4,128)(2,1)S(1)} %get-tuple-element.15), channel_id=1, source_target_pairs={{0,3},{1,2},{2,1},{3,0},{4,7},{5,6},{6,5},{7,4},{8,11},{9,10},{10,... | collective-permute-start | bytes 33800 | tf_op jit(solution)/shard_map/ppermute | solution.py:83
  22.8 5.5 %collective-permute-start.1 = (bf16[4,1408]{1,0:T(4,128)(2,1)S(1)}, bf16[4,1408]{1,0:T(4,128)(2,1)S(1)}, u32[]{:S(2)}, u32[]{:S(2)}) collective-permute-start(bf16[4,1408]{1,0:T(4,128)(2,1)S(1)} %get-tuple-element.15), channel_id=1, source_target_pairs={{0,2},{1,3},{2,0},{3,1},{4,6},{5,7},{6,4},{7,5},{8,10},{9,11},{10,... | collective-permute-start | bytes 33800 | tf_op jit(solution)/shard_map/ppermute | solution.py:83
  23.9 4.4 %collective-permute-start = (bf16[4,1408]{1,0:T(4,128)(2,1)S(1)}, bf16[4,1408]{1,0:T(4,128)(2,1)S(1)}, u32[]{:S(2)}, u32[]{:S(2)}) collective-permute-start(bf16[4,1408]{1,0:T(4,128)(2,1)S(1)} %get-tuple-element.15), channel_id=1, source_target_pairs={{0,1},{1,0},{2,3},{3,2},{4,5},{5,4},{6,7},{7,6},{8,9},{9,8},{10,11... | collective-permute-start | bytes 33800 | tf_op jit(solution)/shard_map/ppermute | solution.py:83
  28.3 6.0 %collective-permute-start.5 = (bf16[16,1408]{1,0:T(8,128)(2,1)S(1)}, bf16[16,1408]{1,0:T(8,128)(2,1)S(1)}, u32[]{:S(2)}, u32[]{:S(2)}) collective-permute-start(bf16[16,1408]{1,0:T(8,128)(2,1)S(1)} %pad_maximum_fusion.refs_0_), channel_id=1, source_target_pairs={{0,12},{1,13},{2,14},{3,15},{4,8},{5,9},{6,10},{7,11},{8,4},{9,5},... | collective-permute-start | bytes 135176 | tf_op jit(solution)/shard_map/ppermute | solution.py:83
  31.6 5.8 %collective-permute-start.4 = (bf16[16,1408]{1,0:T(8,128)(2,1)S(1)}, bf16[16,1408]{1,0:T(8,128)(2,1)S(1)}, u32[]{:S(2)}, u32[]{:S(2)}) collective-permute-start(bf16[16,1408]{1,0:T(8,128)(2,1)S(1)} %pad_maximum_fusion.refs_0_), channel_id=1, source_target_pairs={{0,8},{1,9},{2,10},{3,11},{4,12},{5,13},{6,14},{7,15},{8,0},{9,1},... | collective-permute-start | bytes 135176 | tf_op jit(solution)/shard_map/ppermute | solution.py:83
  31.6 5.8 %collective-permute-start.3 = (bf16[16,1408]{1,0:T(8,128)(2,1)S(1)}, bf16[16,1408]{1,0:T(8,128)(2,1)S(1)}, u32[]{:S(2)}, u32[]{:S(2)}) collective-permute-start(bf16[16,1408]{1,0:T(8,128)(2,1)S(1)} %pad_maximum_fusion.refs_0_), channel_id=1, source_target_pairs={{0,4},{1,5},{2,6},{3,7},{4,0},{5,1},{6,2},{7,3},{8,12},{9,13},{10,... | collective-permute-start | bytes 135176 | tf_op jit(solution)/shard_map/ppermute | solution.py:83
  49.2 1.8 %collective-permute-start.6 = (bf16[8,3,64,128]{3,2,1,0:T(8,128)(2,1)S(1)}, bf16[8,3,64,128]{3,2,1,0:T(8,128)(2,1)S(1)}, u32[]{:S(2)}, u32[]{:S(2)}) collective-permute-start(bf16[8,3,64,128]{3,2,1,0:T(8,128)(2,1)S(1)} %all-to-all-done.own_ref), channel_id=1, source_target_pairs={{0,1},{1,0},{2,3},{3,2},{4,5},{5,4},{6,7},{7,6},{8,9},{9,8},{10,11... | collective-permute-start | bytes 1179656 | tf_op jit(solution)/shard_map/ppermute | solution.py:457
  52.1 7.4 %collective-permute-start.7 = (bf16[64,128]{1,0:T(8,128)(2,1)S(1)}, bf16[64,128]{1,0:T(8,128)(2,1)S(1)}, u32[]{:S(2)}, u32[]{:S(2)}) collective-permute-start(bf16[64,128]{1,0:T(8,128)(2,1)S(1)} %get-tuple-element.18), channel_id=1, source_target_pairs={{0,2},{1,3},{2,0},{3,1},{4,6},{5,7},{6,4},{7,5},{8,10},{9,11},{10,... | collective-permute-start | bytes 49160 | tf_op jit(solution)/shard_map/ppermute | solution.py:460
  53.6 7.3 %collective-permute-start.8 = (bf16[64,128]{1,0:T(8,128)(2,1)S(1)}, bf16[64,128]{1,0:T(8,128)(2,1)S(1)}, u32[]{:S(2)}, u32[]{:S(2)}) collective-permute-start(bf16[64,128]{1,0:T(8,128)(2,1)S(1)} %get-tuple-element.19), channel_id=1, source_target_pairs={{0,4},{1,5},{2,6},{3,7},{4,0},{5,1},{6,2},{7,3},{8,12},{9,13},{10,... | collective-permute-start | bytes 49160 | tf_op jit(solution)/shard_map/ppermute | solution.py:460
  53.7 9.6 %collective-permute-start.9 = (bf16[64,128]{1,0:T(8,128)(2,1)S(1)}, bf16[64,128]{1,0:T(8,128)(2,1)S(1)}, u32[]{:S(2)}, u32[]{:S(2)}) collective-permute-start(bf16[64,128]{1,0:T(8,128)(2,1)S(1)} %get-tuple-element.20), channel_id=1, source_target_pairs={{0,6},{1,7},{2,4},{3,5},{4,2},{5,3},{6,0},{7,1},{8,14},{9,15},{10,... | collective-permute-start | bytes 49160 | tf_op jit(solution)/shard_map/ppermute | solution.py:460
  55.7 7.7 %collective-permute-start.10 = (bf16[64,128]{1,0:T(8,128)(2,1)S(1)}, bf16[64,128]{1,0:T(8,128)(2,1)S(1)}, u32[]{:S(2)}, u32[]{:S(2)}) collective-permute-start(bf16[64,128]{1,0:T(8,128)(2,1)S(1)} %get-tuple-element.21), channel_id=1, source_target_pairs={{0,8},{1,9},{2,10},{3,11},{4,12},{5,13},{6,14},{7,15},{8,0},{9,1},... | collective-permute-start | bytes 49160 | tf_op jit(solution)/shard_map/ppermute | solution.py:460
  56.8 6.5 %collective-permute-start.11 = (bf16[64,128]{1,0:T(8,128)(2,1)S(1)}, bf16[64,128]{1,0:T(8,128)(2,1)S(1)}, u32[]{:S(2)}, u32[]{:S(2)}) collective-permute-start(bf16[64,128]{1,0:T(8,128)(2,1)S(1)} %get-tuple-element.22), channel_id=1, source_target_pairs={{0,10},{1,11},{2,8},{3,9},{4,14},{5,15},{6,12},{7,13},{8,2},{9,3},... | collective-permute-start | bytes 49160 | tf_op jit(solution)/shard_map/ppermute | solution.py:460
  59.5 5.5 %collective-permute-start.12 = (bf16[64,128]{1,0:T(8,128)(2,1)S(1)}, bf16[64,128]{1,0:T(8,128)(2,1)S(1)}, u32[]{:S(2)}, u32[]{:S(2)}) collective-permute-start(bf16[64,128]{1,0:T(8,128)(2,1)S(1)} %get-tuple-element.23), channel_id=1, source_target_pairs={{0,12},{1,13},{2,14},{3,15},{4,8},{5,9},{6,10},{7,11},{8,4},{9,5},... | collective-permute-start | bytes 49160 | tf_op jit(solution)/shard_map/ppermute | solution.py:460
  61.0 6.4 %collective-permute-start.13 = (bf16[64,128]{1,0:T(8,128)(2,1)S(1)}, bf16[64,128]{1,0:T(8,128)(2,1)S(1)}, u32[]{:S(2)}, u32[]{:S(2)}) collective-permute-start(bf16[64,128]{1,0:T(8,128)(2,1)S(1)} %get-tuple-element.24), channel_id=1, source_target_pairs={{0,14},{1,15},{2,12},{3,13},{4,10},{5,11},{6,8},{7,9},{8,6},{9,7},... | collective-permute-start | bytes 49160 | tf_op jit(solution)/shard_map/ppermute | solution.py:460

commit v4 on v2

v4 whole, which is shorter than its diff:
```python
import functools
import math

import jax
import jax.numpy as jnp
from jax import lax
from jax.experimental import pallas as pl
from jax.experimental.pallas import tpu as pltpu
from jax.sharding import PartitionSpec as P

DH = 128
LF = 2
MAXT = 4
TAPS = (1, 2)
ROWS = 2 * MAXT
REACH = ROWS + 2
UNITS = -(-LF * REACH // 8) * 8
DECODE_VMEM = 32 * 1024 * 1024
ATTEND_VMEM = 32 * 1024 * 1024
COPY_VMEM = 16 * 1024 * 1024


def parity_groups(devices):
    return [list(range(parity, devices, 2)) for parity in range(2)]


def in_hbm(*arrays):
    return [pltpu.with_memory_space_constraint(array, pltpu.HBM) for array in arrays]


def pack_body(query_ref, key_ref, value_ref, latent_ref, packed_ref, spread_ref, held, sems):
    heads = packed_ref.shape[0]
    section = lax.axis_index("sect")
    position = lax.axis_index("seq")
    wide_columns = pl.ds(pl.multiple_of(section * heads * DH, DH), heads * DH)
    copies = [
        pltpu.make_async_copy(ref.at[:, wide_columns], held.at[place], sems.at[place])
        for place, ref in enumerate((query_ref, key_ref, value_ref))
    ]
    for copy in copies:
        copy.start()
    rows, width = latent_ref.shape
    held_rows, span = spread_ref.shape
    rim = (2 * span - width) // 4
    wide = latent_ref[...].astype(jnp.float32)
    rim_zeros = jnp.zeros((rows, rim), jnp.float32)
    lower = jnp.concatenate([rim_zeros, wide[:, : span - rim]], axis=1)
    upper = jnp.concatenate([wide[:, width - span + rim :], rim_zeros], axis=1)
    share = jnp.where(section == 0, lower, upper).astype(jnp.bfloat16)
    place = lax.broadcasted_iota(jnp.int32, (held_rows, rows), 0)
    own = lax.broadcasted_iota(jnp.int32, (held_rows, rows), 1) + position * rows
    selector = jnp.where(place == own, 1.0, 0.0).astype(jnp.bfloat16)
    spread = jnp.dot(selector, share, preferred_element_type=jnp.float32)
    spread_ref[...] = spread.astype(spread_ref.dtype)
    for place, copy in enumerate(copies):
        copy.wait()
        for head in range(heads):
            packed_ref[head, place] = held[place, :, head * DH : (head + 1) * DH]


def pack_heads(queries, key_tokens, value_tokens, latent, token_width):
    token_rows, width = queries.shape
    sections = lax.axis_size("sect")
    heads = width // DH // sections
    span = latent.shape[1] // sections + 2 * token_width
    held_rows = latent.shape[0] * lax.axis_size("seq")
    hbm = pl.BlockSpec(memory_space=pltpu.HBM)
    vmem = pl.BlockSpec(memory_space=pltpu.VMEM)
    return pl.pallas_call(
        pack_body,
        in_specs=[hbm, hbm, hbm, vmem],
        out_specs=[vmem, vmem],
        out_shape=[
            jax.ShapeDtypeStruct((heads, 3, token_rows, DH), queries.dtype),
            jax.ShapeDtypeStruct((held_rows, span), latent.dtype),
        ],
        scratch_shapes=[
            pltpu.VMEM((3, token_rows, heads * DH), queries.dtype),
            pltpu.SemaphoreType.DMA((3,)),
        ],
        compiler_params=pltpu.CompilerParams(vmem_limit_bytes=COPY_VMEM),
        name="pack_heads",
    )(*in_hbm(queries, key_tokens, value_tokens, latent))


def xor_pairs(distance):
    return [(i, i ^ distance) for i in range(lax.axis_size("seq"))]


def flat(array):
    return array.reshape(-1, array.shape[-1])


def attend_body(block, own_ref, other_ref, out_ref):
    members, _, token_rows, _ = own_ref.shape
    keys = jnp.concatenate([flat(own_ref[:, 1]), flat(other_ref[:, 1])], axis=0)
    values = jnp.concatenate([flat(own_ref[:, 2]), flat(other_ref[:, 2])], axis=0)

    def one_block(step):
        at = pl.ds(step * block, block)
        scores = lax.dot_general(
            flat(own_ref[at, 0]),
            keys,
            (((1,), (1,)), ((), ())),
            preferred_element_type=jnp.float32,
        ) * (1.0 / math.sqrt(DH))
        exponents = jnp.exp(scores - jnp.max(scores, axis=1, keepdims=True))
        totals = jnp.sum(exponents, axis=1, keepdims=True)
        mixed = jnp.dot(
            exponents.astype(jnp.bfloat16), values, preferred_element_type=jnp.float32
        )
        out_ref[at] = (mixed / totals).astype(out_ref.dtype).reshape(block, token_rows, DH)

    if members <= 8:
        for step in range(members // block):
            one_block(step)
    else:
        pl.loop(0, members // block)(one_block)


def attend(own, other):
    members, _, token_rows, _ = own.shape
    total = members * token_rows
    vmem = pl.BlockSpec(memory_space=pltpu.VMEM)
    return pl.pallas_call(
        functools.partial(attend_body, min(4, members)),
        in_specs=[vmem, vmem],
        out_specs=vmem,
        out_shape=jax.ShapeDtypeStruct((members, token_rows, DH), own.dtype),
        compiler_params=pltpu.CompilerParams(vmem_limit_bytes=ATTEND_VMEM),
        cost_estimate=pl.CostEstimate(
            flops=8 * total * total * DH,
            bytes_accessed=7 * total * DH * 2,
            transcendentals=2 * total * total,
        ),
        name="attend",
    )(own, other)


def unpack_body(in_ref, out_ref, sems):
    copies = [
        pltpu.make_async_copy(
            in_ref.at[head], out_ref.at[:, pl.ds(head * DH, DH)], sems.at[head]
        )
        for head in range(in_ref.shape[0])
    ]
    for copy in copies:
        copy.start()
    for copy in copies:
        copy.wait()


def unpack_heads(array):
    heads, token_rows, _ = array.shape
    return pl.pallas_call(
        unpack_body,
        in_specs=[pl.BlockSpec(memory_space=pltpu.VMEM)],
        out_specs=pl.BlockSpec(memory_space=pltpu.HBM),
        out_shape=jax.ShapeDtypeStruct((token_rows, heads * DH), array.dtype),
        scratch_shapes=[pltpu.SemaphoreType.DMA((heads,))],
        compiler_params=pltpu.CompilerParams(vmem_limit_bytes=COPY_VMEM),
        name="unpack_heads",
    )(array)


def decode_body(
    grid_rows,
    width,
    latent_ref,
    tile_ref,
    in_weight_hbm,
    in_bias_hbm,
    gain_hbm,
    mid_weight_hbm,
    mid_bias_hbm,
    out_ref,
    mid_weight,
    in_weight_ref,
    in_bias_ref,
    gain_ref,
    mid_bias_ref,
    taps,
    patches,
    raw,
    hidden,
    activated,
    active,
    summed,
    weight_sems,
    small_sems,
):
    pairs = active.shape[1] // 16
    channels, features = in_weight_ref.shape[3:]
    columns = out_ref.shape[2]
    lane_tiles = features // 128
    position = lax.axis_index("seq")
    section = lax.axis_index("sect")
    small = [
        pltpu.make_async_copy(source, target, small_sems.at[place])
        for place, (source, target) in enumerate(
            (
                (in_weight_hbm, in_weight_ref),
                (in_bias_hbm, in_bias_ref),
                (gain_hbm, gain_ref),
                (mid_bias_hbm, mid_bias_ref),
            )
        )
    ]
    for copy in small:
        copy.start()

    def load(col_tap):
        return [
            pltpu.make_async_copy(
                mid_weight_hbm.at[tap, row_tap, col_tap],
                mid_weight.at[
                    col_tap,
                    pl.ds(row_tap * features, features),
                    pl.ds((2 - tap) * features, features),
                ],
                weight_sems.at[col_tap, row_tap, slot],
            )
            for row_tap in range(3)
            for slot, tap in enumerate(TAPS)
        ]

    for col_tap in range(3):
        for copy in load(col_tap):
            copy.start()

    filled = tile_ref[position]
    first_row = lax.fori_loop(0, position, lambda d, total: total + tile_ref[d], jnp.int32(0))

    latent = latent_ref[...].astype(jnp.float32)
    aside = pltpu.roll(latent, latent.shape[1] - 64, 1).astype(jnp.bfloat16)
    latent = latent_ref[...]
    held_rows = latent.shape[0]
    unit = lax.broadcasted_iota(jnp.int32, (UNITS, held_rows), 0)
    held = lax.broadcasted_iota(jnp.int32, (UNITS, held_rows), 1)
    frame = sum((unit >= (k + 1) * REACH).astype(jnp.int32) for k in range(LF))
    reach = unit - frame * REACH
    selectors = []
    for tap in TAPS:
        for row_parity in range(2):
            for i in range(2):
                token_row = first_row + (reach >> 1) - 1 + i
                source = frame + tap - 2
                wanted = (
                    ((reach & 1) == row_parity)
                    & (token_row >= 0)
                    & (token_row < grid_rows)
                    & (source >= 0)
                    & (source < LF)
                )
                target = jnp.where(wanted, source * grid_rows + token_row, -1)
                selectors.append(jnp.where(held == target, 1.0, 0.0).astype(jnp.bfloat16))
    selector = jnp.concatenate(selectors, axis=0)
    even = jnp.dot(selector, latent, preferred_element_type=jnp.float32)
    odd = jnp.dot(selector, aside, preferred_element_type=jnp.float32)
    chunks = latent.shape[1] // 128
    for chunk in range(chunks):
        lanes = slice(chunk * 128, (chunk + 1) * 128)
        for group in range(len(selectors)):
            rows = slice(group * UNITS, (group + 1) * UNITS)
            piece = jnp.concatenate([even[rows, lanes], odd[rows, lanes]], axis=0)
            patches[
                chunk * 2 * UNITS : (chunk + 1) * 2 * UNITS, group * 128 : (group + 1) * 128
            ] = piece.astype(jnp.bfloat16)

    for copy in small:
        copy.wait()
    nothing = jnp.zeros((channels, features), jnp.bfloat16)
    base = 0
    for tap in TAPS:
        for row_parity in range(2):
            for i, j, p, q in [
                (i, j, p, q) for i in range(2) for j in range(2) for p in range(2) for q in range(2)
            ]:
                for col_parity in range(2):
                    row_tap, col_tap = 2 * i + p - row_parity, 2 * j + q - col_parity
                    inside = 0 <= row_tap < 3 and 0 <= col_tap < 3
                    taps[base : base + channels, col_parity * features : (col_parity + 1) * features] = (
                        in_weight_ref[tap, row_tap, col_tap] if inside else nothing
                    )
                base += channels

    raw[...] = jnp.dot(patches[...], taps[...], preferred_element_type=jnp.float32)

    unit_row = lax.broadcasted_iota(jnp.int32, (UNITS, 1), 0)
    row_frame = sum((unit_row >= (k + 1) * REACH).astype(jnp.int32) for k in range(LF))
    pixel_row = 2 * first_row + unit_row - row_frame * REACH - 1
    row_inside = (pixel_row >= 0) & (pixel_row < 2 * grid_rows)
    in_bias = in_bias_ref[...].reshape(1, features)
    half_gain = gain_ref[...].reshape(1, features) * 0.5

    @pl.loop(0, chunks)
    def _(chunk):
        for corner in range(2):
            start = pl.multiple_of((chunk * 2 + corner) * UNITS, 8)
            for col_parity in range(2):
                value = (
                    raw[pl.ds(start, UNITS), col_parity * features : (col_parity + 1) * features]
                    + in_bias
                )
                value = value.astype(jnp.bfloat16).astype(jnp.float32)
                scale = lax.rsqrt(jnp.mean(value * value, axis=1, keepdims=True) + 1e-06)
                column = chunk * 4 + corner * 2 + col_parity
                pixel = section * columns + column - 1
                keep = row_inside & (pixel >= 0) & (pixel < width)
                half = value * jnp.where(keep, scale, 0.0) * half_gain
                result = half + half * jnp.tanh(half)
                at = pl.ds(pl.multiple_of(column * UNITS, 8), UNITS)
                for lane in range(lane_tiles):
                    lanes = slice(lane * 128, (lane + 1) * 128)
                    hidden[lane, at] = value[:, lanes]
                    activated[lane, at] = result[:, lanes]

    @pl.loop(0, pairs)
    def _(pair):
        at = pl.ds(pl.multiple_of(pair * 16, 16), 16)
        for lane in range(lane_tiles):
            for field in range(LF):
                for row_tap in range(3):
                    units = [
                        activated[
                            lane, pl.ds((2 * pair + k) * UNITS + field * REACH + row_tap, ROWS)
                        ]
                        for k in range(3)
                    ]
                    to_lane = (field * 3 + row_tap) * features + lane * 128
                    for phase in range(2):
                        joined = jnp.concatenate(units[phase : phase + 2], axis=0)
                        active[phase, at, to_lane : to_lane + 128] = joined.astype(jnp.bfloat16)

    rows = columns * ROWS
    depth = 3 * features
    for col_tap in range(3):
        for copy in load(col_tap):
            copy.wait()
        low = 16 * (col_tap // 2)
        window = active[col_tap % 2, low : low + rows]
        both = jnp.dot(window[:, :depth], mid_weight[col_tap], preferred_element_type=jnp.float32)
        late = jnp.dot(
            window[:, depth:], mid_weight[col_tap, :, :features], preferred_element_type=jnp.float32
        )
        for lane in range(lane_tiles):
            lanes = slice(lane * 128, (lane + 1) * 128)
            further = slice(features + lane * 128, features + (lane + 1) * 128)
            for field, value in enumerate((both[:, lanes], both[:, further] + late[:, lanes])):
                summed[field, lane] = value + summed[field, lane] if col_tap else value

    mid_bias = mid_bias_ref[...].reshape(1, features)
    for field in range(LF):
        for row in range(ROWS):
            for lane in range(lane_tiles):
                lanes = slice(lane * 128, (lane + 1) * 128)
                skip = hidden[lane, pl.ds(UNITS + field * REACH + 1 + row, columns, stride=UNITS), :]
                value = summed[field, lane, pl.ds(row, columns, stride=ROWS), :]
                value = value + skip + mid_bias[:, lanes]
                value = jnp.where(row < 2 * filled, value, 0.0)
                out_ref[field, row, :, lanes] = value.astype(jnp.bfloat16)


def decode_tile(
    latent,
    grid_rows,
    tile_rows,
    conv_in_weight,
    conv_in_bias,
    norm_gain,
    conv_mid_weight,
    conv_mid_bias,
):
    sections = lax.axis_size("sect")
    channels, features = conv_in_weight.shape[3:]
    token_width = 4 * channels
    span = latent.shape[1] // token_width - 2
    columns = 2 * span
    pairs = span + 1
    chunks = latent.shape[1] // 128
    lane_tiles = features // 128
    vmem = pl.BlockSpec(memory_space=pltpu.VMEM)
    hbm = pl.BlockSpec(memory_space=pltpu.HBM)
    slots = len(TAPS)
    depth = slots * 2 * 4 * token_width
    held = chunks * 4 * UNITS
    return pl.pallas_call(
        functools.partial(decode_body, grid_rows, columns * sections),
        in_specs=[vmem, pl.BlockSpec(memory_space=pltpu.SMEM)] + [hbm] * 5,
        out_specs=vmem,
        out_shape=jax.ShapeDtypeStruct((LF, ROWS, columns, features), jnp.bfloat16),
        scratch_shapes=[
            pltpu.VMEM((3, 3 * features, slots * features), jnp.bfloat16),
            pltpu.VMEM(conv_in_weight.shape, jnp.bfloat16),
            pltpu.VMEM(conv_in_bias.shape, jnp.float32),
            pltpu.VMEM(norm_gain.shape, jnp.float32),
            pltpu.VMEM(conv_mid_bias.shape, jnp.float32),
            pltpu.VMEM((depth, 2 * features), jnp.bfloat16),
            pltpu.VMEM((chunks * 2 * UNITS, depth), jnp.bfloat16),
            pltpu.VMEM((chunks * 2 * UNITS, 2 * features), jnp.float32),
            pltpu.VMEM((lane_tiles, held, 128), jnp.float32),
            pltpu.VMEM((lane_tiles, held, 128), jnp.float32),
            pltpu.VMEM((2, pairs * 16, LF * 3 * features), jnp.bfloat16),
            pltpu.VMEM((LF, lane_tiles, columns * ROWS, 128), jnp.float32),
            pltpu.SemaphoreType.DMA((3, 3, slots)),
            pltpu.SemaphoreType.DMA((4,)),
        ],
        compiler_params=pltpu.CompilerParams(vmem_limit_bytes=DECODE_VMEM),
        cost_estimate=pl.CostEstimate(
            flops=2 * 3 * 9 * columns * ROWS * features * features,
            bytes_accessed=slots * 9 * features * features * 2,
            transcendentals=held * features,
        ),
        name="decode_tile",
    )(
        latent,
        *in_hbm(
            tile_rows, conv_in_weight, conv_in_bias, norm_gain, conv_mid_weight, conv_mid_bias
        ),
    )


def on_device(
    queries,
    key_tokens,
    value_tokens,
    latent,
    tile_rows,
    conv_in_weight,
    conv_in_bias,
    norm_gain,
    conv_mid_weight,
    conv_mid_bias,
):
    devices = lax.axis_size("seq")
    groups = parity_groups(devices)
    grid_rows = latent.shape[0] * devices // LF
    packed, spread = pack_heads(
        queries, key_tokens, value_tokens, latent, 4 * conv_in_weight.shape[3]
    )
    own = lax.all_to_all(packed, "seq", 0, 0, axis_index_groups=groups, tiled=True)
    gathered = lax.psum(spread, "seq")
    other = lax.ppermute(own, "seq", xor_pairs(1))
    mixed = attend(own, other)
    returned = lax.all_to_all(mixed, "seq", 0, 0, axis_index_groups=groups, tiled=True)
    frames = decode_tile(
        gathered,
        grid_rows,
        tile_rows,
        conv_in_weight,
        conv_in_bias,
        norm_gain,
        conv_mid_weight,
        conv_mid_bias,
    )
    return (unpack_heads(returned), frames)


def solution(mesh):
    in_specs = (
        P("seq", None),
        P("seq", None),
        P("seq", None),
        P("seq", None),
        P(),
        P(),
        P(),
        P(),
        P(),
        P(),
    )
    out_specs = (P("seq", "sect"), P(None, "seq", "sect", None))
    return jax.shard_map(
        on_device, mesh=mesh, in_specs=in_specs, out_specs=out_specs, check_vma=False
    )
```

time: 55.6 us -> 137 us (2.46)
  waiting for transfers between devices: 1.71 us -> 82.7 us
  between operations: 0.69 us -> 14.1 us
  blocking collectives: 29.4 us -> 19.1 us
  local copies, waits for them, and re-layouts: 3.67 us -> 0.92 us
    psum x0 -> x1, waiting for transfers between devices: none -> 81 us  [on_device(): gathered = lax.psum(spread, 'seq')]
    all_to_all x2 -> x1, blocking collectives: 29.4 us -> 19.1 us  [on_device(): lax.all_to_all(packed, 'seq', 0, 0, axis_index_groups=groups, tiled=True)]
    unnamed x10 -> x2, local copies, waits for them, and re-layouts: 3.67 us -> 0.92 us
  transfers between devices with their start and end apart: 2 -> 3, of which waited for: 1 -> 2; matrix products, arithmetic and copies ran while one was open for 0% -> 0% of each run, Pallas kernels for 19% -> 10%
where the time goes in v4:
time: 137 us
  waiting for transfers between devices  82.7 us (60%)
  blocking collectives  19.1 us (14%)
  Pallas kernels  16.6 us (12%)
  between operations  14.1 us (10%)
  starting transfers between devices  3.41 us (2%)
    psum x1, waiting for transfers between devices, on_device(): gathered = lax.psum(spread, 'seq')  81 us
    all_to_all x1, blocking collectives, on_device(): lax.all_to_all(packed, 'seq', 0, 0, axis_index_groups=groups, tiled=True)  19.1 us
    pallas_call x1, Pallas kernels, decode_tile(): pl.pallas_call(functools.partial(decode_body, grid_rows, columns * sectio...  11.6 us
    all_to_all x1, starting transfers between devices, on_device(): lax.all_to_all(mixed, 'seq', 0, 0, axis_index_groups=groups, tiled=True)  3.37 us
  transfers between devices with their start and end apart: 3, of which 2 were waited for; matrix products, arithmetic and copies ran while one was open for 0% of the time, Pallas kernels for 10%

profile of v4, /device:TPU:0, one launch (start us, length us, event | category | flops | bytes accessed | tf_op | source)
XLA Modules:
  0.0 136.9 jit_solution(15151096328755521332)
XLA Ops:
  7.2 0.0 all-reduce.2.cloned.1.call-start
  7.2 2.5 %pack_heads.1 = (bf16[8,3,64,128]{3,2,1,0:T(8,128)(2,1)S(1)}, bf16[64,1408]{1,0:T(8,128)(2,1)}) custom-call(bf16[64,2048]{1,0:T(8,128)(2,1)} %query_ref.1, bf16[64,2048]{1,0:T(8,128)(2,1)} %key_ref.1, bf16[64,2048]{1,0:T(8,128)(2,1)} %value_ref.1, bf16[4,2560]{1,0:T(4,128)(2,1)} %latent_ref.1), custom_call_target="tpu_custom_call" | custom-call | tf_op jit(solution)/shard_map/pack_heads/pallas_call | solution.py:69
  9.7 19.1 %all_to_all.10.own_ref = bf16[8,3,64,128]{3,2,1,0:T(8,128)(2,1)S(1)} all-to-all(bf16[8,3,64,128]{3,2,1,0:T(8,128)(2,1)S(1)} %get-tuple-element.4), channel_id=1, replica_groups={{0,2,4,6,8,10,12,14},{1,3,5,7,9,11,13,15},{16,18,20,22,24,26,28,30},{17..., dimensions={0} | all-to-all | bytes 786432 | tf_op jit(solution)/shard_map/all_to_all | solution.py:441
  28.8 0.0 collective-permute-start
  28.8 0.0 all-reduce.2.cloned.1.call-update
  28.9 1.7 %collective-permute-done.other_ref = bf16[8,3,64,128]{3,2,1,0:T(8,128)(2,1)S(1)} collective-permute-done((bf16[8,3,64,128]{3,2,1,0:T(8,128)(2,1)S(1)}, bf16[8,3,64,128]{3,2,1,0:T(8,128)(2,1)S(1)}, u32[]{:S(2)}, u32[]{:S(2)}) %collective-permute-start) | collective-permute-done | bytes 393248 | tf_op jit(solution)/shard_map/ppermute | solution.py:443
  30.6 1.8 %attend.1 = bf16[8,64,128]{2,1,0:T(8,128)(2,1)} custom-call(bf16[8,3,64,128]{3,2,1,0:T(8,128)(2,1)S(1)} %all_to_all.10.own_ref, bf16[8,3,64,128]{3,2,1,0:T(8,128)(2,1)S(1)} %collective-permute-done.other_ref), custom_call_target="tpu_custom_call" | custom-call | flops 268435456 | bytes 917504 | tf_op jit(solution)/shard_map/attend/pallas_call | solution.py:125
  32.4 3.4 %all-to-all-start.1 = ((bf16[8,64,128]{2,1,0:T(8,128)(2,1)}), bf16[8,64,128]{2,1,0:T(8,128)(2,1)S(1)}, u32[]{:S(2)}, u32[]{:S(2)}) async-start(bf16[8,64,128]{2,1,0:T(8,128)(2,1)} %attend.1), calls=%async_computation.1 | async-start | bytes 262144 | tf_op jit(solution)/shard_map/all_to_all | solution.py:445
  35.8 81.0 %all-reduce.2.cloned.1.call-done.latent_ref = bf16[64,1408]{1,0:T(8,128)(2,1)} async-done(((bf16[64,1408]{1,0:T(8,128)(2,1)}), bf16[64,1408]{1,0:T(8,128)(2,1)}) %all-reduce.2.cloned.1.call-update) | async-done | bytes 180240 | tf_op jit(solution)/shard_map/psum | solution.py:442
  116.7 0.0 copy-start
  116.7 0.9 copy-done
  117.7 11.6 %decode_tile.1 = bf16[2,8,40,384]{3,2,1,0:T(8,128)(2,1)} custom-call(bf16[64,1408]{1,0:T(8,128)(2,1)S(1)} %copy-done, s32[16]{0:T(128)} %tile_ref.1, bf16[3,3,3,16,384]{4,3,2,1,0:T(8,128)(2,1)} %in_weight_hbm.1, f32[384]{0:T(512)} %in_bias_hbm.1, f32[384]{0:T(512)} %gain_hbm.1, bf16[3,3,3,384,384]{4,3,2,1,0:T(8,128)(2,1)} %mid_weight_hbm.1, f32[384]{0:T(512)} %mid_bias_hbm.1), custom_call_target="tpu_custom_call" | custom-call | flops 2548039680 | bytes 5308416 | tf_op jit(solution)/shard_map/decode_tile/pallas_call | solution.py:387
  129.3 0.0 all-to-all-done.1.in_ref
  129.3 0.7 unpack_heads.1
Async XLA Ops:
  7.2 109.6 %all-reduce.2.cloned.1.call-start = ((), (), s32[]{:S(2)}) async-start(), calls=%async_computation.2 | async-start | bytes 360448 | tf_op jit(solution)/shard_map/psum | solution.py:442
  28.8 1.7 %collective-permute-start = (bf16[8,3,64,128]{3,2,1,0:T(8,128)(2,1)S(1)}, bf16[8,3,64,128]{3,2,1,0:T(8,128)(2,1)S(1)}, u32[]{:S(2)}, u32[]{:S(2)}) collective-permute-start(bf16[8,3,64,128]{3,2,1,0:T(8,128)(2,1)S(1)} %all_to_all.10.own_ref), channel_id=1, source_target_pairs={{0,1},{1,0},{2,3},{3,2},{4,5},{5,4},{6,7},{7,6},{8,9},{9,8},{10,11... | collective-permute-start | bytes 1179656 | tf_op jit(solution)/shard_map/ppermute | solution.py:443
  32.4 96.9 %all-to-all-start.1 = ((bf16[8,64,128]{2,1,0:T(8,128)(2,1)}), bf16[8,64,128]{2,1,0:T(8,128)(2,1)S(1)}, u32[]{:S(2)}, u32[]{:S(2)}) async-start(bf16[8,64,128]{2,1,0:T(8,128)(2,1)} %attend.1), calls=%async_computation.1 | async-start | bytes 262144 | tf_op jit(solution)/shard_map/all_to_all | solution.py:445
  116.7 0.9 copy-start
Sparse Core Ops, SparseCore 0:
  29.0 87.7 all-reduce.1

commit v5 on v4

--- a/solution.py
+++ b/solution.py
@@ -11,6 +11,7 @@
 DH = 128
 LF = 2
 MAXT = 4
+RIM = 64
 TAPS = (1, 2)
 ROWS = 2 * MAXT
 REACH = ROWS + 2
@@ -28,10 +29,10 @@
     return [pltpu.with_memory_space_constraint(array, pltpu.HBM) for array in arrays]
 
 
-def pack_body(query_ref, key_ref, value_ref, latent_ref, packed_ref, spread_ref, held, sems):
+def pack_body(query_ref, key_ref, value_ref, latent_ref, packed_ref, held, sems):
     heads = packed_ref.shape[0]
+    token_rows = query_ref.shape[0]
     section = lax.axis_index("sect")
-    position = lax.axis_index("seq")
     wide_columns = pl.ds(pl.multiple_of(section * heads * DH, DH), heads * DH)
     copies = [
         pltpu.make_async_copy(ref.at[:, wide_columns], held.at[place], sems.at[place])
@@ -40,22 +41,25 @@
     for copy in copies:
         copy.start()
     rows, width = latent_ref.shape
-    held_rows, span = spread_ref.shape
-    rim = (2 * span - width) // 4
+    half, rim = width // 2, RIM
     wide = latent_ref[...].astype(jnp.float32)
     rim_zeros = jnp.zeros((rows, rim), jnp.float32)
-    lower = jnp.concatenate([rim_zeros, wide[:, : span - rim]], axis=1)
-    upper = jnp.concatenate([wide[:, width - span + rim :], rim_zeros], axis=1)
-    share = jnp.where(section == 0, lower, upper).astype(jnp.bfloat16)
-    place = lax.broadcasted_iota(jnp.int32, (held_rows, rows), 0)
-    own = lax.broadcasted_iota(jnp.int32, (held_rows, rows), 1) + position * rows
-    selector = jnp.where(place == own, 1.0, 0.0).astype(jnp.bfloat16)
-    spread = jnp.dot(selector, share, preferred_element_type=jnp.float32)
-    spread_ref[...] = spread.astype(spread_ref.dtype)
+    lower = jnp.concatenate([rim_zeros, wide[:, : half + rim]], axis=1)
+    upper = jnp.concatenate([wide[:, half - rim :], rim_zeros], axis=1)
+    share = jnp.where(section == 0, lower, upper)
+    chunks = share.shape[1] // DH
+    lines = [share[:, chunk * DH : (chunk + 1) * DH] for chunk in range(chunks)]
+    spare = packed_ref.shape[1] - 3 * token_rows - chunks * rows
+    lines.append(jnp.zeros((spare, DH), jnp.float32))
+    share = jnp.concatenate(lines, axis=0).astype(packed_ref.dtype)
+    for head in range(heads):
+        packed_ref[head, 3 * token_rows :] = share
     for place, copy in enumerate(copies):
         copy.wait()
         for head in range(heads):
-            packed_ref[head, place] = held[place, :, head * DH : (head + 1) * DH]
+            packed_ref[head, place * token_rows : (place + 1) * token_rows] = held[
+                place, :, head * DH : (head + 1) * DH
+            ]
 
 
 def pack_heads(queries, key_tokens, value_tokens, latent, token_width):
@@ -63,17 +67,14 @@
     sections = lax.axis_size("sect")
     heads = width // DH // sections
     span = latent.shape[1] // sections + 2 * token_width
-    held_rows = latent.shape[0] * lax.axis_size("seq")
+    extra = -(-latent.shape[0] * (span // DH) // 16) * 16
     hbm = pl.BlockSpec(memory_space=pltpu.HBM)
     vmem = pl.BlockSpec(memory_space=pltpu.VMEM)
     return pl.pallas_call(
         pack_body,
         in_specs=[hbm, hbm, hbm, vmem],
-        out_specs=[vmem, vmem],
-        out_shape=[
-            jax.ShapeDtypeStruct((heads, 3, token_rows, DH), queries.dtype),
-            jax.ShapeDtypeStruct((held_rows, span), latent.dtype),
-        ],
+        out_specs=vmem,
+        out_shape=jax.ShapeDtypeStruct((heads, 3 * token_rows + extra, DH), queries.dtype),
         scratch_shapes=[
             pltpu.VMEM((3, token_rows, heads * DH), queries.dtype),
             pltpu.SemaphoreType.DMA((3,)),
@@ -92,14 +93,16 @@
 
 
 def attend_body(block, own_ref, other_ref, out_ref):
-    members, _, token_rows, _ = own_ref.shape
-    keys = jnp.concatenate([flat(own_ref[:, 1]), flat(other_ref[:, 1])], axis=0)
-    values = jnp.concatenate([flat(own_ref[:, 2]), flat(other_ref[:, 2])], axis=0)
+    members, token_rows, _ = out_ref.shape
+    at_keys = slice(token_rows, 2 * token_rows)
+    at_values = slice(2 * token_rows, 3 * token_rows)
+    keys = jnp.concatenate([flat(own_ref[:, at_keys]), flat(other_ref[:, at_keys])], axis=0)
+    values = jnp.concatenate([flat(own_ref[:, at_values]), flat(other_ref[:, at_values])], axis=0)
 
     def one_block(step):
         at = pl.ds(step * block, block)
         scores = lax.dot_general(
-            flat(own_ref[at, 0]),
+            flat(own_ref[at, :token_rows]),
             keys,
             (((1,), (1,)), ((), ())),
             preferred_element_type=jnp.float32,
@@ -118,8 +121,8 @@
         pl.loop(0, members // block)(one_block)
 
 
-def attend(own, other):
-    members, _, token_rows, _ = own.shape
+def attend(own, other, token_rows):
+    members = own.shape[0]
     total = members * token_rows
     vmem = pl.BlockSpec(memory_space=pltpu.VMEM)
     return pl.pallas_call(
@@ -166,7 +169,9 @@
 def decode_body(
     grid_rows,
     width,
-    latent_ref,
+    share_rows,
+    own_ref,
+    other_ref,
     tile_ref,
     in_weight_hbm,
     in_bias_hbm,
@@ -180,6 +185,7 @@
     gain_ref,
     mid_bias_ref,
     taps,
+    rows_held,
     patches,
     raw,
     hidden,
@@ -231,12 +237,26 @@
     filled = tile_ref[position]
     first_row = lax.fori_loop(0, position, lambda d, total: total + tile_ref[d], jnp.int32(0))
 
-    latent = latent_ref[...].astype(jnp.float32)
-    aside = pltpu.roll(latent, latent.shape[1] - 64, 1).astype(jnp.bfloat16)
-    latent = latent_ref[...]
+    members, message, _ = own_ref.shape
+    chunks = rows_held.shape[1] // 128
+    extra = -(-share_rows * chunks // 16) * 16
+    for side, ref in enumerate((own_ref, other_ref)):
+        for member in range(members):
+            lines = ref[member, message - extra :].astype(jnp.float32)
+            low = (side * members + member) * share_rows
+            for chunk in range(chunks):
+                rows_held[low : low + share_rows, chunk * 128 : (chunk + 1) * 128] = lines[
+                    chunk * share_rows : (chunk + 1) * share_rows
+                ]
+    latent = rows_held[...]
+    aside = pltpu.roll(latent, latent.shape[1] - RIM, 1).astype(jnp.bfloat16)
+    latent = latent.astype(jnp.bfloat16)
     held_rows = latent.shape[0]
     unit = lax.broadcasted_iota(jnp.int32, (UNITS, held_rows), 0)
     held = lax.broadcasted_iota(jnp.int32, (UNITS, held_rows), 1)
+    side = (held >= members * share_rows).astype(jnp.int32)
+    member = held // share_rows - side * members
+    held = (2 * member + ((position & 1) ^ side)) * share_rows + held % share_rows
     frame = sum((unit >= (k + 1) * REACH).astype(jnp.int32) for k in range(LF))
     reach = unit - frame * REACH
     selectors = []
@@ -257,7 +277,6 @@
     selector = jnp.concatenate(selectors, axis=0)
     even = jnp.dot(selector, latent, preferred_element_type=jnp.float32)
     odd = jnp.dot(selector, aside, preferred_element_type=jnp.float32)
-    chunks = latent.shape[1] // 128
     for chunk in range(chunks):
         lanes = slice(chunk * 128, (chunk + 1) * 128)
         for group in range(len(selectors)):
@@ -293,10 +312,9 @@
     in_bias = in_bias_ref[...].reshape(1, features)
     half_gain = gain_ref[...].reshape(1, features) * 0.5
 
-    @pl.loop(0, chunks)
-    def _(chunk):
+    for chunk in range(chunks):
         for corner in range(2):
-            start = pl.multiple_of((chunk * 2 + corner) * UNITS, 8)
+            start = (chunk * 2 + corner) * UNITS
             for col_parity in range(2):
                 value = (
                     raw[pl.ds(start, UNITS), col_parity * features : (col_parity + 1) * features]
@@ -309,45 +327,43 @@
                 keep = row_inside & (pixel >= 0) & (pixel < width)
                 half = value * jnp.where(keep, scale, 0.0) * half_gain
                 result = half + half * jnp.tanh(half)
-                at = pl.ds(pl.multiple_of(column * UNITS, 8), UNITS)
+                at = pl.ds(column * UNITS, UNITS)
                 for lane in range(lane_tiles):
                     lanes = slice(lane * 128, (lane + 1) * 128)
                     hidden[lane, at] = value[:, lanes]
                     activated[lane, at] = result[:, lanes]
 
-    @pl.loop(0, pairs)
-    def _(pair):
-        at = pl.ds(pl.multiple_of(pair * 16, 16), 16)
+    def pair_up(phase, pair):
+        at = slice(pair * 16, pair * 16 + 16)
         for lane in range(lane_tiles):
             for field in range(LF):
                 for row_tap in range(3):
-                    units = [
-                        activated[
-                            lane, pl.ds((2 * pair + k) * UNITS + field * REACH + row_tap, ROWS)
-                        ]
-                        for k in range(3)
-                    ]
+                    start = (2 * pair + phase) * UNITS + field * REACH + row_tap
+                    joined = jnp.concatenate(
+                        [activated[lane, pl.ds(start + k * UNITS, ROWS)] for k in range(2)], axis=0
+                    )
                     to_lane = (field * 3 + row_tap) * features + lane * 128
-                    for phase in range(2):
-                        joined = jnp.concatenate(units[phase : phase + 2], axis=0)
-                        active[phase, at, to_lane : to_lane + 128] = joined.astype(jnp.bfloat16)
+                    active[phase, at, to_lane : to_lane + 128] = joined.astype(jnp.bfloat16)
+
+    for phase in range(2):
+        for pair in range(pairs - phase):
+            pair_up(phase, pair)
 
     rows = columns * ROWS
     depth = 3 * features
+    windows = [active[col_tap % 2, 16 * (col_tap // 2) : 16 * (col_tap // 2) + rows] for col_tap in range(3)]
     for col_tap in range(3):
         for copy in load(col_tap):
             copy.wait()
-        low = 16 * (col_tap // 2)
-        window = active[col_tap % 2, low : low + rows]
-        both = jnp.dot(window[:, :depth], mid_weight[col_tap], preferred_element_type=jnp.float32)
-        late = jnp.dot(
-            window[:, depth:], mid_weight[col_tap, :, :features], preferred_element_type=jnp.float32
-        )
-        for lane in range(lane_tiles):
-            lanes = slice(lane * 128, (lane + 1) * 128)
-            further = slice(features + lane * 128, features + (lane + 1) * 128)
-            for field, value in enumerate((both[:, lanes], both[:, further] + late[:, lanes])):
-                summed[field, lane] = value + summed[field, lane] if col_tap else value
+    early = jnp.concatenate([window[:, :depth] for window in windows], axis=1)
+    both = jnp.dot(early, flat(mid_weight[...]), preferred_element_type=jnp.float32)
+    late = jnp.concatenate([window[:, depth:] for window in windows], axis=1)
+    late = jnp.dot(late, flat(mid_weight[:, :, :features]), preferred_element_type=jnp.float32)
+    for lane in range(lane_tiles):
+        lanes = slice(lane * 128, (lane + 1) * 128)
+        further = slice(features + lane * 128, features + (lane + 1) * 128)
+        summed[0, lane] = both[:, lanes]
+        summed[1, lane] = both[:, further] + late[:, lanes]
 
     mid_bias = mid_bias_ref[...].reshape(1, features)
     for field in range(LF):
@@ -362,8 +378,11 @@
 
 
 def decode_tile(
-    latent,
+    own,
+    other,
+    share_rows,
     grid_rows,
+    width,
     tile_rows,
     conv_in_weight,
     conv_in_bias,
@@ -374,10 +393,10 @@
     sections = lax.axis_size("sect")
     channels, features = conv_in_weight.shape[3:]
     token_width = 4 * channels
-    span = latent.shape[1] // token_width - 2
-    columns = 2 * span
+    columns = width // sections
+    span = columns // 2
     pairs = span + 1
-    chunks = latent.shape[1] // 128
+    chunks = (span + 2) * token_width // 128
     lane_tiles = features // 128
     vmem = pl.BlockSpec(memory_space=pltpu.VMEM)
     hbm = pl.BlockSpec(memory_space=pltpu.HBM)
@@ -385,8 +404,8 @@
     depth = slots * 2 * 4 * token_width
     held = chunks * 4 * UNITS
     return pl.pallas_call(
-        functools.partial(decode_body, grid_rows, columns * sections),
-        in_specs=[vmem, pl.BlockSpec(memory_space=pltpu.SMEM)] + [hbm] * 5,
+        functools.partial(decode_body, grid_rows, width, share_rows),
+        in_specs=[vmem, vmem, pl.BlockSpec(memory_space=pltpu.SMEM)] + [hbm] * 5,
         out_specs=vmem,
         out_shape=jax.ShapeDtypeStruct((LF, ROWS, columns, features), jnp.bfloat16),
         scratch_shapes=[
@@ -396,6 +415,7 @@
             pltpu.VMEM(norm_gain.shape, jnp.float32),
             pltpu.VMEM(conv_mid_bias.shape, jnp.float32),
             pltpu.VMEM((depth, 2 * features), jnp.bfloat16),
+            pltpu.VMEM((2 * own.shape[0] * share_rows, chunks * 128), jnp.float32),
             pltpu.VMEM((chunks * 2 * UNITS, depth), jnp.bfloat16),
             pltpu.VMEM((chunks * 2 * UNITS, 2 * features), jnp.float32),
             pltpu.VMEM((lane_tiles, held, 128), jnp.float32),
@@ -413,7 +433,8 @@
         ),
         name="decode_tile",
     )(
-        latent,
+        own,
+        other,
         *in_hbm(
             tile_rows, conv_in_weight, conv_in_bias, norm_gain, conv_mid_weight, conv_mid_bias
         ),
@@ -435,17 +456,18 @@
     devices = lax.axis_size("seq")
     groups = parity_groups(devices)
     grid_rows = latent.shape[0] * devices // LF
-    packed, spread = pack_heads(
-        queries, key_tokens, value_tokens, latent, 4 * conv_in_weight.shape[3]
-    )
+    token_width = 4 * conv_in_weight.shape[3]
+    packed = pack_heads(queries, key_tokens, value_tokens, latent, token_width)
     own = lax.all_to_all(packed, "seq", 0, 0, axis_index_groups=groups, tiled=True)
-    gathered = lax.psum(spread, "seq")
     other = lax.ppermute(own, "seq", xor_pairs(1))
-    mixed = attend(own, other)
+    mixed = attend(own, other, queries.shape[0])
     returned = lax.all_to_all(mixed, "seq", 0, 0, axis_index_groups=groups, tiled=True)
     frames = decode_tile(
-        gathered,
+        own,
+        other,
+        latent.shape[0],
         grid_rows,
+        2 * latent.shape[1] // token_width,
         tile_rows,
         conv_in_weight,
         conv_in_bias,

time: 137 us -> 41.7 us (0.30)
  waiting for transfers between devices: 82.7 us -> 1.86 us
  between operations: 14.1 us -> 0.66 us
  Pallas kernels: 16.6 us -> 14.4 us
  blocking collectives: 19.1 us -> 20.9 us
    psum x1 -> x0, waiting for transfers between devices: 81 us -> none  [on_device(): gathered = lax.psum(spread, 'seq')]
    pallas_call x2, Pallas kernels: 14.1 us -> 11.9 us  [the longest x1 10 us: decode_tile(): pl.pallas_call(functools.partial(decode_body, grid_rows, width, share_row...]
    all_to_all x1, blocking collectives: 19.1 us -> 20.9 us  [on_device(): lax.all_to_all(packed, 'seq', 0, 0, axis_index_groups=groups, tiled=True)]
  transfers between devices with their start and end apart: 3 -> 2, of which waited for: 2 -> 1; matrix products, arithmetic and copies ran while one was open for 0% -> 0% of each run, Pallas kernels for 10% -> 24%
where the time goes in v5:
time: 41.7 us; the launch traced here: 41.4 us
  blocking collectives  20.9 us (50%)
  Pallas kernels  14.4 us (35%)
  starting transfers between devices  3.59 us (9%)
  waiting for transfers between devices  1.86 us (4%)
  between operations  0.66 us (2%)
    all_to_all x1, blocking collectives, on_device(): lax.all_to_all(packed, 'seq', 0, 0, axis_index_groups=groups, tiled=True)  20.9 us
    pallas_call x1, Pallas kernels, decode_tile(): pl.pallas_call(functools.partial(decode_body, grid_rows, width, share_row...  10 us
    all_to_all x1, starting transfers between devices, on_device(): lax.all_to_all(mixed, 'seq', 0, 0, axis_index_groups=groups, tiled=True)  3.58 us
    ppermute x1, waiting for transfers between devices, on_device(): other = lax.ppermute(own, 'seq', xor_pairs(1))  1.86 us
    pallas_call x1, Pallas kernels, attend(): pl.pallas_call(functools.partial(attend_body, min(4, members)), in_specs=...  1.83 us
    pallas_call x1, Pallas kernels, pack_heads(): pl.pallas_call(pack_body, in_specs=[hbm, hbm, hbm, vmem], out_specs=vmem,...  1.82 us
  transfers between devices with their start and end apart: 2, of which 1 were waited for; matrix products, arithmetic and copies ran while one was open for 0% of the time, Pallas kernels for 24%

profile of v5, /device:TPU:0, one launch (start us, length us, event | category | flops | bytes accessed | tf_op | source)
XLA Modules:
  0.0 41.4 jit_solution(1594490114467071737)
XLA Ops:
  0.6 1.8 %pack_heads.1 = bf16[8,240,128]{2,1,0:T(8,128)(2,1)S(1)} custom-call(bf16[64,2048]{1,0:T(8,128)(2,1)} %query_ref.1, bf16[64,2048]{1,0:T(8,128)(2,1)} %key_ref.1, bf16[64,2048]{1,0:T(8,128)(2,1)} %value_ref.1, bf16[4,2560]{1,0:T(4,128)(2,1)} %latent_ref.1), custom_call_target="tpu_custom_call" | custom-call | tf_op jit(solution)/shard_map/pack_heads/pallas_call | solution.py:73
  2.5 20.9 %all_to_all.10.own_ref = bf16[8,240,128]{2,1,0:T(8,128)(2,1)S(1)} all-to-all(bf16[8,240,128]{2,1,0:T(8,128)(2,1)S(1)} %pack_heads.1), channel_id=1, replica_groups={{0,2,4,6,8,10,12,14},{1,3,5,7,9,11,13,15},{16,18,20,22,24,26,28,30},{17..., dimensions={0} | all-to-all | bytes 983040 | tf_op jit(solution)/shard_map/all_to_all | solution.py:461
  23.3 0.0 collective-permute-start
  23.3 1.9 %collective-permute-done.other_ref = bf16[8,240,128]{2,1,0:T(8,128)(2,1)S(1)} collective-permute-done((bf16[8,240,128]{2,1,0:T(8,128)(2,1)S(1)}, bf16[8,240,128]{2,1,0:T(8,128)(2,1)S(1)}, u32[]{:S(2)}, u32[]{:S(2)}) %collective-permute-start) | collective-permute-done | bytes 491552 | tf_op jit(solution)/shard_map/ppermute | solution.py:462
  25.2 1.8 %attend.1 = bf16[8,64,128]{2,1,0:T(8,128)(2,1)} custom-call(bf16[8,240,128]{2,1,0:T(8,128)(2,1)S(1)} %all_to_all.10.own_ref, bf16[8,240,128]{2,1,0:T(8,128)(2,1)S(1)} %collective-permute-done.other_ref), custom_call_target="tpu_custom_call" | custom-call | flops 268435456 | bytes 917504 | tf_op jit(solution)/shard_map/attend/pallas_call | solution.py:128
  27.0 3.6 %all-to-all-start.1 = ((bf16[8,64,128]{2,1,0:T(8,128)(2,1)}), bf16[8,64,128]{2,1,0:T(8,128)(2,1)S(1)}, u32[]{:S(2)}, u32[]{:S(2)}) async-start(bf16[8,64,128]{2,1,0:T(8,128)(2,1)} %attend.1), calls=%async_computation.1 | async-start | bytes 262144 | tf_op jit(solution)/shard_map/all_to_all | solution.py:464
  30.6 10.0 %decode_tile.1 = bf16[2,8,40,384]{3,2,1,0:T(8,128)(2,1)} custom-call(bf16[8,240,128]{2,1,0:T(8,128)(2,1)S(1)} %all_to_all.10.own_ref, bf16[8,240,128]{2,1,0:T(8,128)(2,1)S(1)} %collective-permute-done.other_ref, s32[16]{0:T(128)} %tile_ref.1, bf16[3,3,3,16,384]{4,3,2,1,0:T(8,128)(2,1)} %in_weight_hbm.1, f32[384]{0:T(512)} %in_bias_hbm.1, f32[384]{0:T(512)} %gain_hbm.1, ...), custom_call_target="tpu_custom_call" | custom-call | flops 2548039680 | bytes 5308416 | tf_op jit(solution)/shard_map/decode_tile/pallas_call | solution.py:406
  40.7 0.0 all-to-all-done.1.in_ref
  40.7 0.7 %unpack_heads.1 = bf16[64,1024]{1,0:T(8,128)(2,1)} custom-call(bf16[8,64,128]{2,1,0:T(8,128)(2,1)S(1)} %all-to-all-done.1.in_ref), custom_call_target="tpu_custom_call" | custom-call | tf_op jit(solution)/shard_map/unpack_heads/pallas_call | solution.py:158
Async XLA Ops:
  23.3 1.9 %collective-permute-start = (bf16[8,240,128]{2,1,0:T(8,128)(2,1)S(1)}, bf16[8,240,128]{2,1,0:T(8,128)(2,1)S(1)}, u32[]{:S(2)}, u32[]{:S(2)}) collective-permute-start(bf16[8,240,128]{2,1,0:T(8,128)(2,1)S(1)} %all_to_all.10.own_ref), channel_id=1, source_target_pairs={{0,1},{1,0},{2,3},{3,2},{4,5},{5,4},{6,7},{7,6},{8,9},{9,8},{10,11... | collective-permute-start | bytes 1474568 | tf_op jit(solution)/shard_map/ppermute | solution.py:462
  27.0 13.6 %all-to-all-start.1 = ((bf16[8,64,128]{2,1,0:T(8,128)(2,1)}), bf16[8,64,128]{2,1,0:T(8,128)(2,1)S(1)}, u32[]{:S(2)}, u32[]{:S(2)}) async-start(bf16[8,64,128]{2,1,0:T(8,128)(2,1)} %attend.1), calls=%async_computation.1 | async-start | bytes 262144 | tf_op jit(solution)/shard_map/all_to_all | solution.py:464

commit v6 on v5

--- a/solution.py
+++ b/solution.py
@@ -303,8 +303,6 @@
                     )
                 base += channels
 
-    raw[...] = jnp.dot(patches[...], taps[...], preferred_element_type=jnp.float32)
-
     unit_row = lax.broadcasted_iota(jnp.int32, (UNITS, 1), 0)
     row_frame = sum((unit_row >= (k + 1) * REACH).astype(jnp.int32) for k in range(LF))
     pixel_row = 2 * first_row + unit_row - row_frame * REACH - 1
@@ -312,7 +310,7 @@
     in_bias = in_bias_ref[...].reshape(1, features)
     half_gain = gain_ref[...].reshape(1, features) * 0.5
 
-    for chunk in range(chunks):
+    def first_layer(chunk):
         for corner in range(2):
             start = (chunk * 2 + corner) * UNITS
             for col_parity in range(2):
@@ -333,6 +331,15 @@
                     hidden[lane, at] = value[:, lanes]
                     activated[lane, at] = result[:, lanes]
 
+    middle = (chunks + 1) // 2
+    groups = ((0, middle), (middle, chunks))
+    for low, high in groups:
+        rows = slice(low * 2 * UNITS, high * 2 * UNITS)
+        raw[rows] = jnp.dot(patches[rows], taps[...], preferred_element_type=jnp.float32)
+    for low, high in groups:
+        for chunk in range(low, high):
+            first_layer(chunk)
+
     def pair_up(phase, pair):
         at = slice(pair * 16, pair * 16 + 16)
         for lane in range(lane_tiles):
@@ -345,28 +352,27 @@
                     to_lane = (field * 3 + row_tap) * features + lane * 128
                     active[phase, at, to_lane : to_lane + 128] = joined.astype(jnp.bfloat16)
 
-    for phase in range(2):
-        for pair in range(pairs - phase):
-            pair_up(phase, pair)
-
     rows = columns * ROWS
     depth = 3 * features
-    windows = [active[col_tap % 2, 16 * (col_tap // 2) : 16 * (col_tap // 2) + rows] for col_tap in range(3)]
-    for col_tap in range(3):
-        for copy in load(col_tap):
-            copy.wait()
-    early = jnp.concatenate([window[:, :depth] for window in windows], axis=1)
-    both = jnp.dot(early, flat(mid_weight[...]), preferred_element_type=jnp.float32)
-    late = jnp.concatenate([window[:, depth:] for window in windows], axis=1)
-    late = jnp.dot(late, flat(mid_weight[:, :, :features]), preferred_element_type=jnp.float32)
-    for lane in range(lane_tiles):
-        lanes = slice(lane * 128, (lane + 1) * 128)
-        further = slice(features + lane * 128, features + (lane + 1) * 128)
-        summed[0, lane] = both[:, lanes]
-        summed[1, lane] = both[:, further] + late[:, lanes]
+
+    def second_layer(col_taps):
+        windows = []
+        for col_tap in col_taps:
+            for copy in load(col_tap):
+                copy.wait()
+            low = 16 * (col_tap // 2)
+            windows.append(active[col_tap % 2, low : low + rows])
+        weights = jnp.concatenate([mid_weight[col_tap] for col_tap in col_taps], axis=0)
+        early = jnp.concatenate([window[:, :depth] for window in windows], axis=1)
+        late = jnp.concatenate([window[:, depth:] for window in windows], axis=1)
+        return (
+            jnp.dot(early, weights, preferred_element_type=jnp.float32),
+            jnp.dot(late, weights[:, :features], preferred_element_type=jnp.float32),
+        )
 
     mid_bias = mid_bias_ref[...].reshape(1, features)
-    for field in range(LF):
+
+    def finish(field):
         for row in range(ROWS):
             for lane in range(lane_tiles):
                 lanes = slice(lane * 128, (lane + 1) * 128)
@@ -375,6 +381,25 @@
                 value = value + skip + mid_bias[:, lanes]
                 value = jnp.where(row < 2 * filled, value, 0.0)
                 out_ref[field, row, :, lanes] = value.astype(jnp.bfloat16)
+
+    for pair in range(pairs):
+        pair_up(0, pair)
+    both, late = second_layer((0, 2))
+    for lane in range(lane_tiles):
+        lanes = slice(lane * 128, (lane + 1) * 128)
+        further = slice(features + lane * 128, features + (lane + 1) * 128)
+        summed[0, lane] = both[:, lanes]
+        summed[1, lane] = both[:, further] + late[:, lanes]
+    for pair in range(pairs - 1):
+        pair_up(1, pair)
+    both, late = second_layer((1,))
+    for lane in range(lane_tiles):
+        lanes = slice(lane * 128, (lane + 1) * 128)
+        further = slice(features + lane * 128, features + (lane + 1) * 128)
+        summed[0, lane] = summed[0, lane] + both[:, lanes]
+        summed[1, lane] = summed[1, lane] + (both[:, further] + late[:, lanes])
+    for field in range(LF):
+        finish(field)
 
 
 def decode_tile(

time: 41.7 us -> 41.4 us (level)
  no operation moved by 1% of the time
where the time goes in v6:
time: 41.4 us; the launch traced here: 41.1 us
  blocking collectives  20.9 us (50%)
  Pallas kernels  14.1 us (34%)
  starting transfers between devices  3.59 us (9%)
  waiting for transfers between devices  1.86 us (4%)
  between operations  0.66 us (2%)
    all_to_all x1, blocking collectives, on_device(): lax.all_to_all(packed, 'seq', 0, 0, axis_index_groups=groups, tiled=True)  20.9 us
    pallas_call x1, Pallas kernels, decode_tile(): pl.pallas_call(functools.partial(decode_body, grid_rows, width, share_row...  9.71 us
    all_to_all x1, starting transfers between devices, on_device(): lax.all_to_all(mixed, 'seq', 0, 0, axis_index_groups=groups, tiled=True)  3.58 us
    ppermute x1, waiting for transfers between devices, on_device(): other = lax.ppermute(own, 'seq', xor_pairs(1))  1.86 us
    pallas_call x1, Pallas kernels, attend(): pl.pallas_call(functools.partial(attend_body, min(4, members)), in_specs=...  1.83 us
    pallas_call x1, Pallas kernels, pack_heads(): pl.pallas_call(pack_body, in_specs=[hbm, hbm, hbm, vmem], out_specs=vmem,...  1.82 us
  transfers between devices with their start and end apart: 2, of which 1 were waited for; matrix products, arithmetic and copies ran while one was open for 0% of the time, Pallas kernels for 24%

profile of v6, /device:TPU:0, one launch (start us, length us, event | category | flops | bytes accessed | tf_op | source)
XLA Modules:
  0.0 41.1 jit_solution(8012788176809441556)
XLA Ops:
  0.6 1.8 %pack_heads.1 = bf16[8,240,128]{2,1,0:T(8,128)(2,1)S(1)} custom-call(bf16[64,2048]{1,0:T(8,128)(2,1)} %query_ref.1, bf16[64,2048]{1,0:T(8,128)(2,1)} %key_ref.1, bf16[64,2048]{1,0:T(8,128)(2,1)} %value_ref.1, bf16[4,2560]{1,0:T(4,128)(2,1)} %latent_ref.1), custom_call_target="tpu_custom_call" | custom-call | tf_op jit(solution)/shard_map/pack_heads/pallas_call | solution.py:73
  2.5 20.9 %all_to_all.10.own_ref = bf16[8,240,128]{2,1,0:T(8,128)(2,1)S(1)} all-to-all(bf16[8,240,128]{2,1,0:T(8,128)(2,1)S(1)} %pack_heads.1), channel_id=1, replica_groups={{0,2,4,6,8,10,12,14},{1,3,5,7,9,11,13,15},{16,18,20,22,24,26,28,30},{17..., dimensions={0} | all-to-all | bytes 983040 | tf_op jit(solution)/shard_map/all_to_all | solution.py:486
  23.3 0.0 collective-permute-start
  23.3 1.9 %collective-permute-done.other_ref = bf16[8,240,128]{2,1,0:T(8,128)(2,1)S(1)} collective-permute-done((bf16[8,240,128]{2,1,0:T(8,128)(2,1)S(1)}, bf16[8,240,128]{2,1,0:T(8,128)(2,1)S(1)}, u32[]{:S(2)}, u32[]{:S(2)}) %collective-permute-start) | collective-permute-done | bytes 491552 | tf_op jit(solution)/shard_map/ppermute | solution.py:487
  25.2 1.8 %attend.1 = bf16[8,64,128]{2,1,0:T(8,128)(2,1)} custom-call(bf16[8,240,128]{2,1,0:T(8,128)(2,1)S(1)} %all_to_all.10.own_ref, bf16[8,240,128]{2,1,0:T(8,128)(2,1)S(1)} %collective-permute-done.other_ref), custom_call_target="tpu_custom_call" | custom-call | flops 268435456 | bytes 917504 | tf_op jit(solution)/shard_map/attend/pallas_call | solution.py:128
  27.0 3.6 %all-to-all-start.1 = ((bf16[8,64,128]{2,1,0:T(8,128)(2,1)}), bf16[8,64,128]{2,1,0:T(8,128)(2,1)S(1)}, u32[]{:S(2)}, u32[]{:S(2)}) async-start(bf16[8,64,128]{2,1,0:T(8,128)(2,1)} %attend.1), calls=%async_computation.1 | async-start | bytes 262144 | tf_op jit(solution)/shard_map/all_to_all | solution.py:489
  30.6 9.7 %decode_tile.1 = bf16[2,8,40,384]{3,2,1,0:T(8,128)(2,1)} custom-call(bf16[8,240,128]{2,1,0:T(8,128)(2,1)S(1)} %all_to_all.10.own_ref, bf16[8,240,128]{2,1,0:T(8,128)(2,1)S(1)} %collective-permute-done.other_ref, s32[16]{0:T(128)} %tile_ref.1, bf16[3,3,3,16,384]{4,3,2,1,0:T(8,128)(2,1)} %in_weight_hbm.1, f32[384]{0:T(512)} %in_bias_hbm.1, f32[384]{0:T(512)} %gain_hbm.1, ...), custom_call_target="tpu_custom_call" | custom-call | flops 2548039680 | bytes 5308416 | tf_op jit(solution)/shard_map/decode_tile/pallas_call | solution.py:431
  40.3 0.0 all-to-all-done.1.in_ref
  40.3 0.7 %unpack_heads.1 = bf16[64,1024]{1,0:T(8,128)(2,1)} custom-call(bf16[8,64,128]{2,1,0:T(8,128)(2,1)S(1)} %all-to-all-done.1.in_ref), custom_call_target="tpu_custom_call" | custom-call | tf_op jit(solution)/shard_map/unpack_heads/pallas_call | solution.py:158
Async XLA Ops:
  23.3 1.9 %collective-permute-start = (bf16[8,240,128]{2,1,0:T(8,128)(2,1)S(1)}, bf16[8,240,128]{2,1,0:T(8,128)(2,1)S(1)}, u32[]{:S(2)}, u32[]{:S(2)}) collective-permute-start(bf16[8,240,128]{2,1,0:T(8,128)(2,1)S(1)} %all_to_all.10.own_ref), channel_id=1, source_target_pairs={{0,1},{1,0},{2,3},{3,2},{4,5},{5,4},{6,7},{7,6},{8,9},{9,8},{10,11... | collective-permute-start | bytes 1474568 | tf_op jit(solution)/shard_map/ppermute | solution.py:487
  27.0 13.3 %all-to-all-start.1 = ((bf16[8,64,128]{2,1,0:T(8,128)(2,1)}), bf16[8,64,128]{2,1,0:T(8,128)(2,1)S(1)}, u32[]{:S(2)}, u32[]{:S(2)}) async-start(bf16[8,64,128]{2,1,0:T(8,128)(2,1)} %attend.1), calls=%async_computation.1 | async-start | bytes 262144 | tf_op jit(solution)/shard_map/all_to_all | solution.py:489

commit v7 on v6

--- a/solution.py
+++ b/solution.py
@@ -355,20 +355,17 @@
     rows = columns * ROWS
     depth = 3 * features
 
-    def second_layer(col_taps):
-        windows = []
-        for col_tap in col_taps:
-            for copy in load(col_tap):
-                copy.wait()
-            low = 16 * (col_tap // 2)
-            windows.append(active[col_tap % 2, low : low + rows])
-        weights = jnp.concatenate([mid_weight[col_tap] for col_tap in col_taps], axis=0)
-        early = jnp.concatenate([window[:, :depth] for window in windows], axis=1)
-        late = jnp.concatenate([window[:, depth:] for window in windows], axis=1)
-        return (
-            jnp.dot(early, weights, preferred_element_type=jnp.float32),
-            jnp.dot(late, weights[:, :features], preferred_element_type=jnp.float32),
+    def windows(low, high, lanes):
+        return jnp.concatenate(
+            [
+                active[tap % 2, 16 * (tap // 2) + low : 16 * (tap // 2) + high, lanes]
+                for tap in range(3)
+            ],
+            axis=1,
         )
+
+    def weights(lanes):
+        return jnp.concatenate([mid_weight[tap, :, lanes] for tap in range(3)], axis=0)
 
     mid_bias = mid_bias_ref[...].reshape(1, features)
 
@@ -382,22 +379,34 @@
                 value = jnp.where(row < 2 * filled, value, 0.0)
                 out_ref[field, row, :, lanes] = value.astype(jnp.bfloat16)
 
-    for pair in range(pairs):
-        pair_up(0, pair)
-    both, late = second_layer((0, 2))
-    for lane in range(lane_tiles):
-        lanes = slice(lane * 128, (lane + 1) * 128)
-        further = slice(features + lane * 128, features + (lane + 1) * 128)
-        summed[0, lane] = both[:, lanes]
-        summed[1, lane] = both[:, further] + late[:, lanes]
-    for pair in range(pairs - 1):
-        pair_up(1, pair)
-    both, late = second_layer((1,))
-    for lane in range(lane_tiles):
-        lanes = slice(lane * 128, (lane + 1) * 128)
-        further = slice(features + lane * 128, features + (lane + 1) * 128)
-        summed[0, lane] = summed[0, lane] + both[:, lanes]
-        summed[1, lane] = summed[1, lane] + (both[:, further] + late[:, lanes])
+    for phase in range(2):
+        for pair in range(pairs - phase):
+            pair_up(phase, pair)
+    for tap in range(3):
+        for copy in load(tap):
+            copy.wait()
+    step = rows // 2
+    for low in (0, step):
+        at = slice(low, low + step)
+        early = windows(low, low + step, slice(0, depth))
+        late = windows(low, low + step, slice(depth, 2 * depth))
+        for left in range(0, 2 * features, 256):
+            block = jnp.dot(
+                early, weights(slice(left, left + 256)), preferred_element_type=jnp.float32
+            )
+            for lane in range(2):
+                field, tile = divmod(left // 128 + lane, lane_tiles)
+                summed[field, tile, at] = block[:, lane * 128 : (lane + 1) * 128]
+        for left in range(0, features, 256):
+            right = min(left + 256, features)
+            block = jnp.dot(
+                late, weights(slice(left, right)), preferred_element_type=jnp.float32
+            )
+            for lane in range((right - left) // 128):
+                tile = left // 128 + lane
+                summed[1, tile, at] = (
+                    summed[1, tile, at] + block[:, lane * 128 : (lane + 1) * 128]
+                )
     for field in range(LF):
         finish(field)
 

time: 41.4 us -> 40.6 us (0.981)
  Pallas kernels: 14.1 us -> 13.2 us
    pallas_call x1, Pallas kernels: 9.71 us -> 8.86 us  [decode_tile(): pl.pallas_call(functools.partial(decode_body, grid_rows, width, share_row...]
  transfers between devices with their start and end apart: 2 -> 2, of which waited for: 1 -> 1; matrix products, arithmetic and copies ran while one was open for 0% -> 0% of each run, Pallas kernels for 24% -> 22%
where the time goes in v7:
time: 40.6 us; the launch traced here: 40.2 us
  blocking collectives  20.9 us (51%)
  Pallas kernels  13.2 us (33%)
  starting transfers between devices  3.59 us (9%)
  waiting for transfers between devices  1.86 us (5%)
  between operations  0.66 us (2%)
    all_to_all x1, blocking collectives, on_device(): lax.all_to_all(packed, 'seq', 0, 0, axis_index_groups=groups, tiled=True)  20.9 us
    pallas_call x1, Pallas kernels, decode_tile(): pl.pallas_call(functools.partial(decode_body, grid_rows, width, share_row...  8.86 us
    all_to_all x1, starting transfers between devices, on_device(): lax.all_to_all(mixed, 'seq', 0, 0, axis_index_groups=groups, tiled=True)  3.58 us
    ppermute x1, waiting for transfers between devices, on_device(): other = lax.ppermute(own, 'seq', xor_pairs(1))  1.86 us
    pallas_call x1, Pallas kernels, attend(): pl.pallas_call(functools.partial(attend_body, min(4, members)), in_specs=...  1.83 us
    pallas_call x1, Pallas kernels, pack_heads(): pl.pallas_call(pack_body, in_specs=[hbm, hbm, hbm, vmem], out_specs=vmem,...  1.82 us
  transfers between devices with their start and end apart: 2, of which 1 were waited for; matrix products, arithmetic and copies ran while one was open for 0% of the time, Pallas kernels for 22%

profile of v7, /device:TPU:0, one launch (start us, length us, event | category | flops | bytes accessed | tf_op | source)
XLA Modules:
  0.0 40.2 jit_solution(9420440740781968600)
XLA Ops:
  0.6 1.8 %pack_heads.1 = bf16[8,240,128]{2,1,0:T(8,128)(2,1)S(1)} custom-call(bf16[64,2048]{1,0:T(8,128)(2,1)} %query_ref.1, bf16[64,2048]{1,0:T(8,128)(2,1)} %key_ref.1, bf16[64,2048]{1,0:T(8,128)(2,1)} %value_ref.1, bf16[4,2560]{1,0:T(4,128)(2,1)} %latent_ref.1), custom_call_target="tpu_custom_call" | custom-call | tf_op jit(solution)/shard_map/pack_heads/pallas_call | solution.py:73
  2.5 20.9 %all_to_all.10.own_ref = bf16[8,240,128]{2,1,0:T(8,128)(2,1)S(1)} all-to-all(bf16[8,240,128]{2,1,0:T(8,128)(2,1)S(1)} %pack_heads.1), channel_id=1, replica_groups={{0,2,4,6,8,10,12,14},{1,3,5,7,9,11,13,15},{16,18,20,22,24,26,28,30},{17..., dimensions={0} | all-to-all | bytes 983040 | tf_op jit(solution)/shard_map/all_to_all | solution.py:495
  23.3 0.0 collective-permute-start
  23.3 1.9 %collective-permute-done.other_ref = bf16[8,240,128]{2,1,0:T(8,128)(2,1)S(1)} collective-permute-done((bf16[8,240,128]{2,1,0:T(8,128)(2,1)S(1)}, bf16[8,240,128]{2,1,0:T(8,128)(2,1)S(1)}, u32[]{:S(2)}, u32[]{:S(2)}) %collective-permute-start) | collective-permute-done | bytes 491552 | tf_op jit(solution)/shard_map/ppermute | solution.py:496
  25.2 1.8 %attend.1 = bf16[8,64,128]{2,1,0:T(8,128)(2,1)} custom-call(bf16[8,240,128]{2,1,0:T(8,128)(2,1)S(1)} %all_to_all.10.own_ref, bf16[8,240,128]{2,1,0:T(8,128)(2,1)S(1)} %collective-permute-done.other_ref), custom_call_target="tpu_custom_call" | custom-call | flops 268435456 | bytes 917504 | tf_op jit(solution)/shard_map/attend/pallas_call | solution.py:128
  27.0 3.6 %all-to-all-start.1 = ((bf16[8,64,128]{2,1,0:T(8,128)(2,1)}), bf16[8,64,128]{2,1,0:T(8,128)(2,1)S(1)}, u32[]{:S(2)}, u32[]{:S(2)}) async-start(bf16[8,64,128]{2,1,0:T(8,128)(2,1)} %attend.1), calls=%async_computation.1 | async-start | bytes 262144 | tf_op jit(solution)/shard_map/all_to_all | solution.py:498
  30.6 8.9 %decode_tile.1 = bf16[2,8,40,384]{3,2,1,0:T(8,128)(2,1)} custom-call(bf16[8,240,128]{2,1,0:T(8,128)(2,1)S(1)} %all_to_all.10.own_ref, bf16[8,240,128]{2,1,0:T(8,128)(2,1)S(1)} %collective-permute-done.other_ref, s32[16]{0:T(128)} %tile_ref.1, bf16[3,3,3,16,384]{4,3,2,1,0:T(8,128)(2,1)} %in_weight_hbm.1, f32[384]{0:T(512)} %in_bias_hbm.1, f32[384]{0:T(512)} %gain_hbm.1, ...), custom_call_target="tpu_custom_call" | custom-call | flops 2548039680 | bytes 5308416 | tf_op jit(solution)/shard_map/decode_tile/pallas_call | solution.py:440
  39.5 0.0 all-to-all-done.1.in_ref
  39.5 0.7 %unpack_heads.1 = bf16[64,1024]{1,0:T(8,128)(2,1)} custom-call(bf16[8,64,128]{2,1,0:T(8,128)(2,1)S(1)} %all-to-all-done.1.in_ref), custom_call_target="tpu_custom_call" | custom-call | tf_op jit(solution)/shard_map/unpack_heads/pallas_call | solution.py:158
Async XLA Ops:
  23.3 1.9 %collective-permute-start = (bf16[8,240,128]{2,1,0:T(8,128)(2,1)S(1)}, bf16[8,240,128]{2,1,0:T(8,128)(2,1)S(1)}, u32[]{:S(2)}, u32[]{:S(2)}) collective-permute-start(bf16[8,240,128]{2,1,0:T(8,128)(2,1)S(1)} %all_to_all.10.own_ref), channel_id=1, source_target_pairs={{0,1},{1,0},{2,3},{3,2},{4,5},{5,4},{6,7},{7,6},{8,9},{9,8},{10,11... | collective-permute-start | bytes 1474568 | tf_op jit(solution)/shard_map/ppermute | solution.py:496
  27.0 12.5 %all-to-all-start.1 = ((bf16[8,64,128]{2,1,0:T(8,128)(2,1)}), bf16[8,64,128]{2,1,0:T(8,128)(2,1)S(1)}, u32[]{:S(2)}, u32[]{:S(2)}) async-start(bf16[8,64,128]{2,1,0:T(8,128)(2,1)} %attend.1), calls=%async_computation.1 | async-start | bytes 262144 | tf_op jit(solution)/shard_map/all_to_all | solution.py:498

commit v8 on v7

--- a/solution.py
+++ b/solution.py
@@ -92,7 +92,7 @@
     return array.reshape(-1, array.shape[-1])
 
 
-def attend_body(block, own_ref, other_ref, out_ref):
+def attend_body(block, own_ref, other_ref, out_ref, mixed_ref, sems):
     members, token_rows, _ = out_ref.shape
     at_keys = slice(token_rows, 2 * token_rows)
     at_values = slice(2 * token_rows, 3 * token_rows)
@@ -112,24 +112,38 @@
         mixed = jnp.dot(
             exponents.astype(jnp.bfloat16), values, preferred_element_type=jnp.float32
         )
-        out_ref[at] = (mixed / totals).astype(out_ref.dtype).reshape(block, token_rows, DH)
-
+        mixed = (mixed / totals).astype(out_ref.dtype)
+        mixed_ref[at] = mixed.reshape(block, token_rows, DH)
+        move(step).start()
+
+    def move(step):
+        at = pl.ds(step * block, block)
+        return pltpu.make_async_copy(mixed_ref.at[at], out_ref.at[at], sems.at[step])
+
+    steps = members // block
     if members <= 8:
-        for step in range(members // block):
+        for step in range(steps):
             one_block(step)
     else:
-        pl.loop(0, members // block)(one_block)
+        pl.loop(0, steps)(one_block)
+    for step in range(steps):
+        move(step).wait()
 
 
 def attend(own, other, token_rows):
     members = own.shape[0]
     total = members * token_rows
+    block = 2 if members <= 8 else 4
     vmem = pl.BlockSpec(memory_space=pltpu.VMEM)
     return pl.pallas_call(
-        functools.partial(attend_body, min(4, members)),
+        functools.partial(attend_body, block),
         in_specs=[vmem, vmem],
-        out_specs=vmem,
+        out_specs=pl.BlockSpec(memory_space=pltpu.HBM),
         out_shape=jax.ShapeDtypeStruct((members, token_rows, DH), own.dtype),
+        scratch_shapes=[
+            pltpu.VMEM((members, token_rows, DH), own.dtype),
+            pltpu.SemaphoreType.DMA((members // block,)),
+        ],
         compiler_params=pltpu.CompilerParams(vmem_limit_bytes=ATTEND_VMEM),
         cost_estimate=pl.CostEstimate(
             flops=8 * total * total * DH,
@@ -331,12 +345,14 @@
                     hidden[lane, at] = value[:, lanes]
                     activated[lane, at] = result[:, lanes]
 
-    middle = (chunks + 1) // 2
-    groups = ((0, middle), (middle, chunks))
+    groups = [(low, min(low + 4, chunks)) for low in range(0, chunks, 4)]
     for low, high in groups:
         rows = slice(low * 2 * UNITS, high * 2 * UNITS)
-        raw[rows] = jnp.dot(patches[rows], taps[...], preferred_element_type=jnp.float32)
-    for low, high in groups:
+        for left in range(0, 2 * features, 256):
+            lanes = slice(left, left + 256)
+            raw[rows, lanes] = jnp.dot(
+                patches[rows], taps[:, lanes], preferred_element_type=jnp.float32
+            )
         for chunk in range(low, high):
             first_layer(chunk)
 

time: 40.6 us -> 41.1 us (1.012)
  Pallas kernels: 13.2 us -> 13.8 us
    pallas_call x1, Pallas kernels: 1.83 us -> 2.25 us  [attend(): pl.pallas_call(functools.partial(attend_body, block), in_specs=[vmem, vme...]
where the time goes in v8:
time: 41.1 us; the launch traced here: 40.8 us
  blocking collectives  20.9 us (51%)
  Pallas kernels  13.8 us (34%)
  starting transfers between devices  3.61 us (9%)
  waiting for transfers between devices  1.86 us (5%)
  between operations  0.66 us (2%)
    all_to_all x1, blocking collectives, on_device(): lax.all_to_all(packed, 'seq', 0, 0, axis_index_groups=groups, tiled=True)  20.9 us
    pallas_call x1, Pallas kernels, decode_tile(): pl.pallas_call(functools.partial(decode_body, grid_rows, width, share_row...  8.98 us
    all_to_all x1, starting transfers between devices, on_device(): lax.all_to_all(mixed, 'seq', 0, 0, axis_index_groups=groups, tiled=True)  3.6 us
    pallas_call x1, Pallas kernels, attend(): pl.pallas_call(functools.partial(attend_body, block), in_specs=[vmem, vme...  2.25 us
    ppermute x1, waiting for transfers between devices, on_device(): other = lax.ppermute(own, 'seq', xor_pairs(1))  1.86 us
    pallas_call x1, Pallas kernels, pack_heads(): pl.pallas_call(pack_body, in_specs=[hbm, hbm, hbm, vmem], out_specs=vmem,...  1.82 us
  transfers between devices with their start and end apart: 2, of which 1 were waited for; matrix products, arithmetic and copies ran while one was open for 0% of the time, Pallas kernels for 22%

profile of v8, /device:TPU:0, one launch (start us, length us, event | category | flops | bytes accessed | tf_op | source)
XLA Modules:
  0.0 40.8 jit_solution(18165452858191185892)
XLA Ops:
  0.6 1.8 %pack_heads.1 = bf16[8,240,128]{2,1,0:T(8,128)(2,1)S(1)} custom-call(bf16[64,2048]{1,0:T(8,128)(2,1)} %query_ref.1, bf16[64,2048]{1,0:T(8,128)(2,1)} %key_ref.1, bf16[64,2048]{1,0:T(8,128)(2,1)} %value_ref.1, bf16[4,2560]{1,0:T(4,128)(2,1)} %latent_ref.1), custom_call_target="tpu_custom_call" | custom-call | tf_op jit(solution)/shard_map/pack_heads/pallas_call | solution.py:73
  2.5 20.9 %all_to_all.10.own_ref = bf16[8,240,128]{2,1,0:T(8,128)(2,1)S(1)} all-to-all(bf16[8,240,128]{2,1,0:T(8,128)(2,1)S(1)} %pack_heads.1), channel_id=1, replica_groups={{0,2,4,6,8,10,12,14},{1,3,5,7,9,11,13,15},{16,18,20,22,24,26,28,30},{17..., dimensions={0} | all-to-all | bytes 983040 | tf_op jit(solution)/shard_map/all_to_all | solution.py:511
  23.3 0.0 collective-permute-start
  23.3 1.9 %collective-permute-done.other_ref = bf16[8,240,128]{2,1,0:T(8,128)(2,1)S(1)} collective-permute-done((bf16[8,240,128]{2,1,0:T(8,128)(2,1)S(1)}, bf16[8,240,128]{2,1,0:T(8,128)(2,1)S(1)}, u32[]{:S(2)}, u32[]{:S(2)}) %collective-permute-start) | collective-permute-done | bytes 491552 | tf_op jit(solution)/shard_map/ppermute | solution.py:512
  25.2 2.2 %attend.1 = bf16[8,64,128]{2,1,0:T(8,128)(2,1)} custom-call(bf16[8,240,128]{2,1,0:T(8,128)(2,1)S(1)} %all_to_all.10.own_ref, bf16[8,240,128]{2,1,0:T(8,128)(2,1)S(1)} %collective-permute-done.other_ref), custom_call_target="tpu_custom_call" | custom-call | flops 268435456 | bytes 917504 | tf_op jit(solution)/shard_map/attend/pallas_call | solution.py:138
  27.5 3.6 %all-to-all-start.1 = ((bf16[8,64,128]{2,1,0:T(8,128)(2,1)}), bf16[8,64,128]{2,1,0:T(8,128)(2,1)S(1)}, u32[]{:S(2)}, u32[]{:S(2)}) async-start(bf16[8,64,128]{2,1,0:T(8,128)(2,1)} %attend.1), calls=%async_computation.1 | async-start | bytes 262144 | tf_op jit(solution)/shard_map/all_to_all | solution.py:514
  31.1 9.0 %decode_tile.1 = bf16[2,8,40,384]{3,2,1,0:T(8,128)(2,1)} custom-call(bf16[8,240,128]{2,1,0:T(8,128)(2,1)S(1)} %all_to_all.10.own_ref, bf16[8,240,128]{2,1,0:T(8,128)(2,1)S(1)} %collective-permute-done.other_ref, s32[16]{0:T(128)} %tile_ref.1, bf16[3,3,3,16,384]{4,3,2,1,0:T(8,128)(2,1)} %in_weight_hbm.1, f32[384]{0:T(512)} %in_bias_hbm.1, f32[384]{0:T(512)} %gain_hbm.1, ...), custom_call_target="tpu_custom_call" | custom-call | flops 2548039680 | bytes 5308416 | tf_op jit(solution)/shard_map/decode_tile/pallas_call | solution.py:456
  40.0 0.0 all-to-all-done.1.in_ref
  40.1 0.7 %unpack_heads.1 = bf16[64,1024]{1,0:T(8,128)(2,1)} custom-call(bf16[8,64,128]{2,1,0:T(8,128)(2,1)S(1)} %all-to-all-done.1.in_ref), custom_call_target="tpu_custom_call" | custom-call | tf_op jit(solution)/shard_map/unpack_heads/pallas_call | solution.py:172
Async XLA Ops:
  23.3 1.9 %collective-permute-start = (bf16[8,240,128]{2,1,0:T(8,128)(2,1)S(1)}, bf16[8,240,128]{2,1,0:T(8,128)(2,1)S(1)}, u32[]{:S(2)}, u32[]{:S(2)}) collective-permute-start(bf16[8,240,128]{2,1,0:T(8,128)(2,1)S(1)} %all_to_all.10.own_ref), channel_id=1, source_target_pairs={{0,1},{1,0},{2,3},{3,2},{4,5},{5,4},{6,7},{7,6},{8,9},{9,8},{10,11... | collective-permute-start | bytes 1474568 | tf_op jit(solution)/shard_map/ppermute | solution.py:512
  27.5 12.6 %all-to-all-start.1 = ((bf16[8,64,128]{2,1,0:T(8,128)(2,1)}), bf16[8,64,128]{2,1,0:T(8,128)(2,1)S(1)}, u32[]{:S(2)}, u32[]{:S(2)}) async-start(bf16[8,64,128]{2,1,0:T(8,128)(2,1)} %attend.1), calls=%async_computation.1 | async-start | bytes 262144 | tf_op jit(solution)/shard_map/all_to_all | solution.py:514

commit v9 on v7

--- a/solution.py
+++ b/solution.py
@@ -385,28 +385,21 @@
     for tap in range(3):
         for copy in load(tap):
             copy.wait()
-    step = rows // 2
-    for low in (0, step):
-        at = slice(low, low + step)
-        early = windows(low, low + step, slice(0, depth))
-        late = windows(low, low + step, slice(depth, 2 * depth))
-        for left in range(0, 2 * features, 256):
-            block = jnp.dot(
-                early, weights(slice(left, left + 256)), preferred_element_type=jnp.float32
-            )
-            for lane in range(2):
-                field, tile = divmod(left // 128 + lane, lane_tiles)
-                summed[field, tile, at] = block[:, lane * 128 : (lane + 1) * 128]
-        for left in range(0, features, 256):
-            right = min(left + 256, features)
-            block = jnp.dot(
-                late, weights(slice(left, right)), preferred_element_type=jnp.float32
-            )
-            for lane in range((right - left) // 128):
-                tile = left // 128 + lane
-                summed[1, tile, at] = (
-                    summed[1, tile, at] + block[:, lane * 128 : (lane + 1) * 128]
-                )
+    early = windows(0, rows, slice(0, depth))
+    late = windows(0, rows, slice(depth, 2 * depth))
+    for left in range(0, 2 * features, 256):
+        block = jnp.dot(
+            early, weights(slice(left, left + 256)), preferred_element_type=jnp.float32
+        )
+        for lane in range(2):
+            field, tile = divmod(left // 128 + lane, lane_tiles)
+            summed[field, tile] = block[:, lane * 128 : (lane + 1) * 128]
+    for left in range(0, features, 256):
+        right = min(left + 256, features)
+        block = jnp.dot(late, weights(slice(left, right)), preferred_element_type=jnp.float32)
+        for lane in range((right - left) // 128):
+            tile = left // 128 + lane
+            summed[1, tile] = summed[1, tile] + block[:, lane * 128 : (lane + 1) * 128]
     for field in range(LF):
         finish(field)
 

time: 40.6 us -> 40.5 us (level)
  no operation moved by 1% of the time
where the time goes in v9:
time: 40.5 us; the launch traced here: 40.1 us
  blocking collectives  20.9 us (52%)
  Pallas kernels  13.1 us (32%)
  starting transfers between devices  3.59 us (9%)
  waiting for transfers between devices  1.86 us (5%)
  between operations  0.66 us (2%)
    all_to_all x1, blocking collectives, on_device(): lax.all_to_all(packed, 'seq', 0, 0, axis_index_groups=groups, tiled=True)  20.9 us
    pallas_call x1, Pallas kernels, decode_tile(): pl.pallas_call(functools.partial(decode_body, grid_rows, width, share_row...  8.78 us
    all_to_all x1, starting transfers between devices, on_device(): lax.all_to_all(mixed, 'seq', 0, 0, axis_index_groups=groups, tiled=True)  3.58 us
    ppermute x1, waiting for transfers between devices, on_device(): other = lax.ppermute(own, 'seq', xor_pairs(1))  1.86 us
    pallas_call x1, Pallas kernels, attend(): pl.pallas_call(functools.partial(attend_body, min(4, members)), in_specs=...  1.83 us
    pallas_call x1, Pallas kernels, pack_heads(): pl.pallas_call(pack_body, in_specs=[hbm, hbm, hbm, vmem], out_specs=vmem,...  1.82 us
  transfers between devices with their start and end apart: 2, of which 1 were waited for; matrix products, arithmetic and copies ran while one was open for 0% of the time, Pallas kernels for 22%

profile of v9, /device:TPU:0, one launch (start us, length us, event | category | flops | bytes accessed | tf_op | source)
XLA Modules:
  0.0 40.1 jit_solution(15568280808484396485)
XLA Ops:
  0.6 1.8 %pack_heads.1 = bf16[8,240,128]{2,1,0:T(8,128)(2,1)S(1)} custom-call(bf16[64,2048]{1,0:T(8,128)(2,1)} %query_ref.1, bf16[64,2048]{1,0:T(8,128)(2,1)} %key_ref.1, bf16[64,2048]{1,0:T(8,128)(2,1)} %value_ref.1, bf16[4,2560]{1,0:T(4,128)(2,1)} %latent_ref.1), custom_call_target="tpu_custom_call" | custom-call | tf_op jit(solution)/shard_map/pack_heads/pallas_call | solution.py:73
  2.5 20.9 %all_to_all.10.own_ref = bf16[8,240,128]{2,1,0:T(8,128)(2,1)S(1)} all-to-all(bf16[8,240,128]{2,1,0:T(8,128)(2,1)S(1)} %pack_heads.1), channel_id=1, replica_groups={{0,2,4,6,8,10,12,14},{1,3,5,7,9,11,13,15},{16,18,20,22,24,26,28,30},{17..., dimensions={0} | all-to-all | bytes 983040 | tf_op jit(solution)/shard_map/all_to_all | solution.py:488
  23.3 0.0 collective-permute-start
  23.3 1.9 %collective-permute-done.other_ref = bf16[8,240,128]{2,1,0:T(8,128)(2,1)S(1)} collective-permute-done((bf16[8,240,128]{2,1,0:T(8,128)(2,1)S(1)}, bf16[8,240,128]{2,1,0:T(8,128)(2,1)S(1)}, u32[]{:S(2)}, u32[]{:S(2)}) %collective-permute-start) | collective-permute-done | bytes 491552 | tf_op jit(solution)/shard_map/ppermute | solution.py:489
  25.2 1.8 %attend.1 = bf16[8,64,128]{2,1,0:T(8,128)(2,1)} custom-call(bf16[8,240,128]{2,1,0:T(8,128)(2,1)S(1)} %all_to_all.10.own_ref, bf16[8,240,128]{2,1,0:T(8,128)(2,1)S(1)} %collective-permute-done.other_ref), custom_call_target="tpu_custom_call" | custom-call | flops 268435456 | bytes 917504 | tf_op jit(solution)/shard_map/attend/pallas_call | solution.py:128
  27.0 3.6 %all-to-all-start.1 = ((bf16[8,64,128]{2,1,0:T(8,128)(2,1)}), bf16[8,64,128]{2,1,0:T(8,128)(2,1)S(1)}, u32[]{:S(2)}, u32[]{:S(2)}) async-start(bf16[8,64,128]{2,1,0:T(8,128)(2,1)} %attend.1), calls=%async_computation.1 | async-start | bytes 262144 | tf_op jit(solution)/shard_map/all_to_all | solution.py:491
  30.6 8.8 %decode_tile.1 = bf16[2,8,40,384]{3,2,1,0:T(8,128)(2,1)} custom-call(bf16[8,240,128]{2,1,0:T(8,128)(2,1)S(1)} %all_to_all.10.own_ref, bf16[8,240,128]{2,1,0:T(8,128)(2,1)S(1)} %collective-permute-done.other_ref, s32[16]{0:T(128)} %tile_ref.1, bf16[3,3,3,16,384]{4,3,2,1,0:T(8,128)(2,1)} %in_weight_hbm.1, f32[384]{0:T(512)} %in_bias_hbm.1, f32[384]{0:T(512)} %gain_hbm.1, ...), custom_call_target="tpu_custom_call" | custom-call | flops 2548039680 | bytes 5308416 | tf_op jit(solution)/shard_map/decode_tile/pallas_call | solution.py:433
  39.4 0.0 all-to-all-done.1.in_ref
  39.4 0.7 %unpack_heads.1 = bf16[64,1024]{1,0:T(8,128)(2,1)} custom-call(bf16[8,64,128]{2,1,0:T(8,128)(2,1)S(1)} %all-to-all-done.1.in_ref), custom_call_target="tpu_custom_call" | custom-call | tf_op jit(solution)/shard_map/unpack_heads/pallas_call | solution.py:158
Async XLA Ops:
  23.3 1.9 %collective-permute-start = (bf16[8,240,128]{2,1,0:T(8,128)(2,1)S(1)}, bf16[8,240,128]{2,1,0:T(8,128)(2,1)S(1)}, u32[]{:S(2)}, u32[]{:S(2)}) collective-permute-start(bf16[8,240,128]{2,1,0:T(8,128)(2,1)S(1)} %all_to_all.10.own_ref), channel_id=1, source_target_pairs={{0,1},{1,0},{2,3},{3,2},{4,5},{5,4},{6,7},{7,6},{8,9},{9,8},{10,11... | collective-permute-start | bytes 1474568 | tf_op jit(solution)/shard_map/ppermute | solution.py:489
  27.0 12.4 %all-to-all-start.1 = ((bf16[8,64,128]{2,1,0:T(8,128)(2,1)}), bf16[8,64,128]{2,1,0:T(8,128)(2,1)S(1)}, u32[]{:S(2)}, u32[]{:S(2)}) async-start(bf16[8,64,128]{2,1,0:T(8,128)(2,1)} %attend.1), calls=%async_computation.1 | async-start | bytes 262144 | tf_op jit(solution)/shard_map/all_to_all | solution.py:491

commit v10 on v7

--- a/solution.py
+++ b/solution.py
@@ -230,7 +230,7 @@
             for slot, tap in enumerate(TAPS)
         ]
 
-    for col_tap in range(3):
+    for col_tap in (0, 2, 1):
         for copy in load(col_tap):
             copy.start()
 
@@ -355,18 +355,6 @@
     rows = columns * ROWS
     depth = 3 * features
 
-    def windows(low, high, lanes):
-        return jnp.concatenate(
-            [
-                active[tap % 2, 16 * (tap // 2) + low : 16 * (tap // 2) + high, lanes]
-                for tap in range(3)
-            ],
-            axis=1,
-        )
-
-    def weights(lanes):
-        return jnp.concatenate([mid_weight[tap, :, lanes] for tap in range(3)], axis=0)
-
     mid_bias = mid_bias_ref[...].reshape(1, features)
 
     def finish(field):
@@ -379,34 +367,32 @@
                 value = jnp.where(row < 2 * filled, value, 0.0)
                 out_ref[field, row, :, lanes] = value.astype(jnp.bfloat16)
 
-    for phase in range(2):
-        for pair in range(pairs - phase):
-            pair_up(phase, pair)
-    for tap in range(3):
+    for place, tap in enumerate((0, 2, 1)):
+        if place != 1:
+            phase = tap % 2
+            for pair in range(pairs - phase):
+                pair_up(phase, pair)
         for copy in load(tap):
             copy.wait()
-    step = rows // 2
-    for low in (0, step):
-        at = slice(low, low + step)
-        early = windows(low, low + step, slice(0, depth))
-        late = windows(low, low + step, slice(depth, 2 * depth))
+        low = 16 * (tap // 2)
+        early = active[tap % 2, low : low + rows, :depth]
+        late = active[tap % 2, low : low + rows, depth:]
         for left in range(0, 2 * features, 256):
             block = jnp.dot(
-                early, weights(slice(left, left + 256)), preferred_element_type=jnp.float32
+                early, mid_weight[tap, :, left : left + 256], preferred_element_type=jnp.float32
             )
             for lane in range(2):
                 field, tile = divmod(left // 128 + lane, lane_tiles)
-                summed[field, tile, at] = block[:, lane * 128 : (lane + 1) * 128]
+                value = block[:, lane * 128 : (lane + 1) * 128]
+                summed[field, tile] = summed[field, tile] + value if place else value
         for left in range(0, features, 256):
             right = min(left + 256, features)
             block = jnp.dot(
-                late, weights(slice(left, right)), preferred_element_type=jnp.float32
+                late, mid_weight[tap, :, left:right], preferred_element_type=jnp.float32
             )
             for lane in range((right - left) // 128):
                 tile = left // 128 + lane
-                summed[1, tile, at] = (
-                    summed[1, tile, at] + block[:, lane * 128 : (lane + 1) * 128]
-                )
+                summed[1, tile] = summed[1, tile] + block[:, lane * 128 : (lane + 1) * 128]
     for field in range(LF):
         finish(field)
 

time: 40.6 us -> 41.5 us (1.022)
  Pallas kernels: 13.2 us -> 14.2 us
    pallas_call x1, Pallas kernels: 8.86 us -> 9.8 us  [decode_tile(): pl.pallas_call(functools.partial(decode_body, grid_rows, width, share_row...]
  transfers between devices with their start and end apart: 2 -> 2, of which waited for: 1 -> 1; matrix products, arithmetic and copies ran while one was open for 0% -> 0% of each run, Pallas kernels for 22% -> 24%
where the time goes in v10:
time: 41.5 us; the launch traced here: 41.1 us
  blocking collectives  20.9 us (50%)
  Pallas kernels  14.2 us (34%)
  starting transfers between devices  3.59 us (9%)
  waiting for transfers between devices  1.86 us (4%)
  between operations  0.66 us (2%)
    all_to_all x1, blocking collectives, on_device(): lax.all_to_all(packed, 'seq', 0, 0, axis_index_groups=groups, tiled=True)  20.9 us
    pallas_call x1, Pallas kernels, decode_tile(): pl.pallas_call(functools.partial(decode_body, grid_rows, width, share_row...  9.8 us
    all_to_all x1, starting transfers between devices, on_device(): lax.all_to_all(mixed, 'seq', 0, 0, axis_index_groups=groups, tiled=True)  3.58 us
    ppermute x1, waiting for transfers between devices, on_device(): other = lax.ppermute(own, 'seq', xor_pairs(1))  1.86 us
    pallas_call x1, Pallas kernels, attend(): pl.pallas_call(functools.partial(attend_body, min(4, members)), in_specs=...  1.83 us
    pallas_call x1, Pallas kernels, pack_heads(): pl.pallas_call(pack_body, in_specs=[hbm, hbm, hbm, vmem], out_specs=vmem,...  1.82 us
  transfers between devices with their start and end apart: 2, of which 1 were waited for; matrix products, arithmetic and copies ran while one was open for 0% of the time, Pallas kernels for 24%

profile of v10, /device:TPU:0, one launch (start us, length us, event | category | flops | bytes accessed | tf_op | source)
XLA Modules:
  0.0 41.1 jit_solution(12356501129965364214)
XLA Ops:
  0.6 1.8 %pack_heads.1 = bf16[8,240,128]{2,1,0:T(8,128)(2,1)S(1)} custom-call(bf16[64,2048]{1,0:T(8,128)(2,1)} %query_ref.1, bf16[64,2048]{1,0:T(8,128)(2,1)} %key_ref.1, bf16[64,2048]{1,0:T(8,128)(2,1)} %value_ref.1, bf16[4,2560]{1,0:T(4,128)(2,1)} %latent_ref.1), custom_call_target="tpu_custom_call" | custom-call | tf_op jit(solution)/shard_map/pack_heads/pallas_call | solution.py:73
  2.5 20.9 %all_to_all.10.own_ref = bf16[8,240,128]{2,1,0:T(8,128)(2,1)S(1)} all-to-all(bf16[8,240,128]{2,1,0:T(8,128)(2,1)S(1)} %pack_heads.1), channel_id=1, replica_groups={{0,2,4,6,8,10,12,14},{1,3,5,7,9,11,13,15},{16,18,20,22,24,26,28,30},{17..., dimensions={0} | all-to-all | bytes 983040 | tf_op jit(solution)/shard_map/all_to_all | solution.py:481
  23.3 0.0 collective-permute-start
  23.3 1.9 %collective-permute-done.other_ref = bf16[8,240,128]{2,1,0:T(8,128)(2,1)S(1)} collective-permute-done((bf16[8,240,128]{2,1,0:T(8,128)(2,1)S(1)}, bf16[8,240,128]{2,1,0:T(8,128)(2,1)S(1)}, u32[]{:S(2)}, u32[]{:S(2)}) %collective-permute-start) | collective-permute-done | bytes 491552 | tf_op jit(solution)/shard_map/ppermute | solution.py:482
  25.2 1.8 %attend.1 = bf16[8,64,128]{2,1,0:T(8,128)(2,1)} custom-call(bf16[8,240,128]{2,1,0:T(8,128)(2,1)S(1)} %all_to_all.10.own_ref, bf16[8,240,128]{2,1,0:T(8,128)(2,1)S(1)} %collective-permute-done.other_ref), custom_call_target="tpu_custom_call" | custom-call | flops 268435456 | bytes 917504 | tf_op jit(solution)/shard_map/attend/pallas_call | solution.py:128
  27.0 3.6 %all-to-all-start.1 = ((bf16[8,64,128]{2,1,0:T(8,128)(2,1)}), bf16[8,64,128]{2,1,0:T(8,128)(2,1)S(1)}, u32[]{:S(2)}, u32[]{:S(2)}) async-start(bf16[8,64,128]{2,1,0:T(8,128)(2,1)} %attend.1), calls=%async_computation.1 | async-start | bytes 262144 | tf_op jit(solution)/shard_map/all_to_all | solution.py:484
  30.6 9.8 %decode_tile.1 = bf16[2,8,40,384]{3,2,1,0:T(8,128)(2,1)} custom-call(bf16[8,240,128]{2,1,0:T(8,128)(2,1)S(1)} %all_to_all.10.own_ref, bf16[8,240,128]{2,1,0:T(8,128)(2,1)S(1)} %collective-permute-done.other_ref, s32[16]{0:T(128)} %tile_ref.1, bf16[3,3,3,16,384]{4,3,2,1,0:T(8,128)(2,1)} %in_weight_hbm.1, f32[384]{0:T(512)} %in_bias_hbm.1, f32[384]{0:T(512)} %gain_hbm.1, ...), custom_call_target="tpu_custom_call" | custom-call | flops 2548039680 | bytes 5308416 | tf_op jit(solution)/shard_map/decode_tile/pallas_call | solution.py:426
  40.4 0.0 all-to-all-done.1.in_ref
  40.4 0.7 %unpack_heads.1 = bf16[64,1024]{1,0:T(8,128)(2,1)} custom-call(bf16[8,64,128]{2,1,0:T(8,128)(2,1)S(1)} %all-to-all-done.1.in_ref), custom_call_target="tpu_custom_call" | custom-call | tf_op jit(solution)/shard_map/unpack_heads/pallas_call | solution.py:158
Async XLA Ops:
  23.3 1.9 %collective-permute-start = (bf16[8,240,128]{2,1,0:T(8,128)(2,1)S(1)}, bf16[8,240,128]{2,1,0:T(8,128)(2,1)S(1)}, u32[]{:S(2)}, u32[]{:S(2)}) collective-permute-start(bf16[8,240,128]{2,1,0:T(8,128)(2,1)S(1)} %all_to_all.10.own_ref), channel_id=1, source_target_pairs={{0,1},{1,0},{2,3},{3,2},{4,5},{5,4},{6,7},{7,6},{8,9},{9,8},{10,11... | collective-permute-start | bytes 1474568 | tf_op jit(solution)/shard_map/ppermute | solution.py:482
  27.0 13.4 %all-to-all-start.1 = ((bf16[8,64,128]{2,1,0:T(8,128)(2,1)}), bf16[8,64,128]{2,1,0:T(8,128)(2,1)S(1)}, u32[]{:S(2)}, u32[]{:S(2)}) async-start(bf16[8,64,128]{2,1,0:T(8,128)(2,1)} %attend.1), calls=%async_computation.1 | async-start | bytes 262144 | tf_op jit(solution)/shard_map/all_to_all | solution.py:484

commit v11 on v9

--- a/solution.py
+++ b/solution.py
@@ -370,14 +370,20 @@
     mid_bias = mid_bias_ref[...].reshape(1, features)
 
     def finish(field):
-        for row in range(ROWS):
-            for lane in range(lane_tiles):
-                lanes = slice(lane * 128, (lane + 1) * 128)
-                skip = hidden[lane, pl.ds(UNITS + field * REACH + 1 + row, columns, stride=UNITS), :]
-                value = summed[field, lane, pl.ds(row, columns, stride=ROWS), :]
-                value = value + skip + mid_bias[:, lanes]
-                value = jnp.where(row < 2 * filled, value, 0.0)
-                out_ref[field, row, :, lanes] = value.astype(jnp.bfloat16)
+        tile_row = lax.broadcasted_iota(jnp.int32, (columns * ROWS, 128), 0) & (ROWS - 1)
+        for lane in range(lane_tiles):
+            lanes = slice(lane * 128, (lane + 1) * 128)
+            skip = jnp.concatenate(
+                [
+                    hidden[lane, pl.ds((column + 1) * UNITS + field * REACH + 1, ROWS)]
+                    for column in range(columns)
+                ],
+                axis=0,
+            )
+            value = summed[field, lane] + skip + mid_bias[:, lanes]
+            value = jnp.where(tile_row < 2 * filled, value, 0.0)
+            value = jnp.swapaxes(value.reshape(columns, ROWS, 128), 0, 1)
+            out_ref[field, :, :, lanes] = value.astype(jnp.bfloat16)
 
     for phase in range(2):
         for pair in range(pairs - phase):

time: 40.5 us -> 40.4 us (level)
  no operation moved by 1% of the time
where the time goes in v11:
time: 40.4 us; the launch traced here: 40 us
  blocking collectives  20.9 us (52%)
  Pallas kernels  13 us (32%)
  starting transfers between devices  3.59 us (9%)
  waiting for transfers between devices  1.86 us (5%)
  between operations  0.66 us (2%)
    all_to_all x1, blocking collectives, on_device(): lax.all_to_all(packed, 'seq', 0, 0, axis_index_groups=groups, tiled=True)  20.9 us
    pallas_call x1, Pallas kernels, decode_tile(): pl.pallas_call(functools.partial(decode_body, grid_rows, width, share_row...  8.67 us
    all_to_all x1, starting transfers between devices, on_device(): lax.all_to_all(mixed, 'seq', 0, 0, axis_index_groups=groups, tiled=True)  3.58 us
    ppermute x1, waiting for transfers between devices, on_device(): other = lax.ppermute(own, 'seq', xor_pairs(1))  1.86 us
    pallas_call x1, Pallas kernels, attend(): pl.pallas_call(functools.partial(attend_body, min(4, members)), in_specs=...  1.83 us
    pallas_call x1, Pallas kernels, pack_heads(): pl.pallas_call(pack_body, in_specs=[hbm, hbm, hbm, vmem], out_specs=vmem,...  1.82 us
  transfers between devices with their start and end apart: 2, of which 1 were waited for; matrix products, arithmetic and copies ran while one was open for 0% of the time, Pallas kernels for 22%

profile of v11, /device:TPU:0, one launch (start us, length us, event | category | flops | bytes accessed | tf_op | source)
XLA Modules:
  0.0 40.0 jit_solution(1919745275406478483)
XLA Ops:
  0.6 1.8 %pack_heads.1 = bf16[8,240,128]{2,1,0:T(8,128)(2,1)S(1)} custom-call(bf16[64,2048]{1,0:T(8,128)(2,1)} %query_ref.1, bf16[64,2048]{1,0:T(8,128)(2,1)} %key_ref.1, bf16[64,2048]{1,0:T(8,128)(2,1)} %value_ref.1, bf16[4,2560]{1,0:T(4,128)(2,1)} %latent_ref.1), custom_call_target="tpu_custom_call" | custom-call | tf_op jit(solution)/shard_map/pack_heads/pallas_call | solution.py:73
  2.5 20.9 %all_to_all.10.own_ref = bf16[8,240,128]{2,1,0:T(8,128)(2,1)S(1)} all-to-all(bf16[8,240,128]{2,1,0:T(8,128)(2,1)S(1)} %pack_heads.1), channel_id=1, replica_groups={{0,2,4,6,8,10,12,14},{1,3,5,7,9,11,13,15},{16,18,20,22,24,26,28,30},{17..., dimensions={0} | all-to-all | bytes 983040 | tf_op jit(solution)/shard_map/all_to_all | solution.py:494
  23.3 0.0 collective-permute-start
  23.3 1.9 %collective-permute-done.other_ref = bf16[8,240,128]{2,1,0:T(8,128)(2,1)S(1)} collective-permute-done((bf16[8,240,128]{2,1,0:T(8,128)(2,1)S(1)}, bf16[8,240,128]{2,1,0:T(8,128)(2,1)S(1)}, u32[]{:S(2)}, u32[]{:S(2)}) %collective-permute-start) | collective-permute-done | bytes 491552 | tf_op jit(solution)/shard_map/ppermute | solution.py:495
  25.2 1.8 %attend.1 = bf16[8,64,128]{2,1,0:T(8,128)(2,1)} custom-call(bf16[8,240,128]{2,1,0:T(8,128)(2,1)S(1)} %all_to_all.10.own_ref, bf16[8,240,128]{2,1,0:T(8,128)(2,1)S(1)} %collective-permute-done.other_ref), custom_call_target="tpu_custom_call" | custom-call | flops 268435456 | bytes 917504 | tf_op jit(solution)/shard_map/attend/pallas_call | solution.py:128
  27.0 3.6 %all-to-all-start.1 = ((bf16[8,64,128]{2,1,0:T(8,128)(2,1)}), bf16[8,64,128]{2,1,0:T(8,128)(2,1)S(1)}, u32[]{:S(2)}, u32[]{:S(2)}) async-start(bf16[8,64,128]{2,1,0:T(8,128)(2,1)} %attend.1), calls=%async_computation.1 | async-start | bytes 262144 | tf_op jit(solution)/shard_map/all_to_all | solution.py:497
  30.6 8.7 %decode_tile.1 = bf16[2,8,40,384]{3,2,1,0:T(8,128)(2,1)} custom-call(bf16[8,240,128]{2,1,0:T(8,128)(2,1)S(1)} %all_to_all.10.own_ref, bf16[8,240,128]{2,1,0:T(8,128)(2,1)S(1)} %collective-permute-done.other_ref, s32[16]{0:T(128)} %tile_ref.1, bf16[3,3,3,16,384]{4,3,2,1,0:T(8,128)(2,1)} %in_weight_hbm.1, f32[384]{0:T(512)} %in_bias_hbm.1, f32[384]{0:T(512)} %gain_hbm.1, ...), custom_call_target="tpu_custom_call" | custom-call | flops 2548039680 | bytes 5308416 | tf_op jit(solution)/shard_map/decode_tile/pallas_call | solution.py:439
  39.3 0.0 all-to-all-done.1.in_ref
  39.3 0.7 %unpack_heads.1 = bf16[64,1024]{1,0:T(8,128)(2,1)} custom-call(bf16[8,64,128]{2,1,0:T(8,128)(2,1)S(1)} %all-to-all-done.1.in_ref), custom_call_target="tpu_custom_call" | custom-call | tf_op jit(solution)/shard_map/unpack_heads/pallas_call | solution.py:158
Async XLA Ops:
  23.3 1.9 %collective-permute-start = (bf16[8,240,128]{2,1,0:T(8,128)(2,1)S(1)}, bf16[8,240,128]{2,1,0:T(8,128)(2,1)S(1)}, u32[]{:S(2)}, u32[]{:S(2)}) collective-permute-start(bf16[8,240,128]{2,1,0:T(8,128)(2,1)S(1)} %all_to_all.10.own_ref), channel_id=1, source_target_pairs={{0,1},{1,0},{2,3},{3,2},{4,5},{5,4},{6,7},{7,6},{8,9},{9,8},{10,11... | collective-permute-start | bytes 1474568 | tf_op jit(solution)/shard_map/ppermute | solution.py:495
  27.0 12.3 %all-to-all-start.1 = ((bf16[8,64,128]{2,1,0:T(8,128)(2,1)}), bf16[8,64,128]{2,1,0:T(8,128)(2,1)S(1)}, u32[]{:S(2)}, u32[]{:S(2)}) async-start(bf16[8,64,128]{2,1,0:T(8,128)(2,1)} %attend.1), calls=%async_computation.1 | async-start | bytes 262144 | tf_op jit(solution)/shard_map/all_to_all | solution.py:497

commit v12 on v11

--- a/solution.py
+++ b/solution.py
@@ -29,8 +29,10 @@
     return [pltpu.with_memory_space_constraint(array, pltpu.HBM) for array in arrays]
 
 
-def pack_body(query_ref, key_ref, value_ref, latent_ref, packed_ref, held, sems):
-    heads = packed_ref.shape[0]
+def pack_body(query_ref, key_ref, value_ref, latent_ref, *refs):
+    packed_refs, (held, sems) = refs[:-2], refs[-2:]
+    heads = len(packed_refs)
+    chip = lax.axis_index("seq") // 2
     token_rows = query_ref.shape[0]
     section = lax.axis_index("sect")
     wide_columns = pl.ds(pl.multiple_of(section * heads * DH, DH), heads * DH)
@@ -49,17 +51,16 @@
     share = jnp.where(section == 0, lower, upper)
     chunks = share.shape[1] // DH
     lines = [share[:, chunk * DH : (chunk + 1) * DH] for chunk in range(chunks)]
-    spare = packed_ref.shape[1] - 3 * token_rows - chunks * rows
+    spare = packed_refs[0].shape[0] - 3 * token_rows - chunks * rows
     lines.append(jnp.zeros((spare, DH), jnp.float32))
-    share = jnp.concatenate(lines, axis=0).astype(packed_ref.dtype)
-    for head in range(heads):
-        packed_ref[head, 3 * token_rows :] = share
+    share = jnp.concatenate(lines, axis=0).astype(jnp.bfloat16)
+    for packed_ref in packed_refs:
+        packed_ref[3 * token_rows :] = share
     for place, copy in enumerate(copies):
         copy.wait()
-        for head in range(heads):
-            packed_ref[head, place * token_rows : (place + 1) * token_rows] = held[
-                place, :, head * DH : (head + 1) * DH
-            ]
+        for m, packed_ref in enumerate(packed_refs):
+            columns = pl.ds(pl.multiple_of((chip ^ m) * DH, DH), DH)
+            packed_ref[place * token_rows : (place + 1) * token_rows] = held[place, :, columns]
 
 
 def pack_heads(queries, key_tokens, value_tokens, latent, token_width):
@@ -73,8 +74,8 @@
     return pl.pallas_call(
         pack_body,
         in_specs=[hbm, hbm, hbm, vmem],
-        out_specs=vmem,
-        out_shape=jax.ShapeDtypeStruct((heads, 3 * token_rows + extra, DH), queries.dtype),
+        out_specs=[vmem] * heads,
+        out_shape=[jax.ShapeDtypeStruct((3 * token_rows + extra, DH), queries.dtype)] * heads,
         scratch_shapes=[
             pltpu.VMEM((3, token_rows, heads * DH), queries.dtype),
             pltpu.SemaphoreType.DMA((3,)),
@@ -92,17 +93,21 @@
     return array.reshape(-1, array.shape[-1])
 
 
-def attend_body(block, own_ref, other_ref, out_ref):
+def attend_body(*refs):
+    out_ref = refs[-1]
     members, token_rows, _ = out_ref.shape
-    at_keys = slice(token_rows, 2 * token_rows)
-    at_values = slice(2 * token_rows, 3 * token_rows)
-    keys = jnp.concatenate([flat(own_ref[:, at_keys]), flat(other_ref[:, at_keys])], axis=0)
-    values = jnp.concatenate([flat(own_ref[:, at_values]), flat(other_ref[:, at_values])], axis=0)
-
-    def one_block(step):
-        at = pl.ds(step * block, block)
+    block = min(4, members)
+    chip = lax.axis_index("seq") // 2
+    pieces = refs[:-1]
+
+    def rows(place, chosen):
+        at = slice(place * token_rows, (place + 1) * token_rows)
+        return jnp.concatenate([ref[at] for ref in chosen], axis=0)
+
+    keys, values = rows(1, pieces), rows(2, pieces)
+    for step in range(0, members, block):
         scores = lax.dot_general(
-            flat(own_ref[at, :token_rows]),
+            rows(0, pieces[step : step + block]),
             keys,
             (((1,), (1,)), ((), ())),
             preferred_element_type=jnp.float32,
@@ -112,24 +117,20 @@
         mixed = jnp.dot(
             exponents.astype(jnp.bfloat16), values, preferred_element_type=jnp.float32
         )
-        out_ref[at] = (mixed / totals).astype(out_ref.dtype).reshape(block, token_rows, DH)
-
-    if members <= 8:
-        for step in range(members // block):
-            one_block(step)
-    else:
-        pl.loop(0, members // block)(one_block)
+        mixed = (mixed / totals).astype(out_ref.dtype)
+        for m in range(block):
+            out_ref[chip ^ (step + m)] = mixed[m * token_rows : (m + 1) * token_rows]
 
 
 def attend(own, other, token_rows):
-    members = own.shape[0]
+    members = len(own)
     total = members * token_rows
     vmem = pl.BlockSpec(memory_space=pltpu.VMEM)
     return pl.pallas_call(
-        functools.partial(attend_body, min(4, members)),
-        in_specs=[vmem, vmem],
+        attend_body,
+        in_specs=[vmem] * (2 * members),
         out_specs=vmem,
-        out_shape=jax.ShapeDtypeStruct((members, token_rows, DH), own.dtype),
+        out_shape=jax.ShapeDtypeStruct((members, token_rows, DH), own[0].dtype),
         compiler_params=pltpu.CompilerParams(vmem_limit_bytes=ATTEND_VMEM),
         cost_estimate=pl.CostEstimate(
             flops=8 * total * total * DH,
@@ -137,7 +138,7 @@
             transcendentals=2 * total * total,
         ),
         name="attend",
-    )(own, other)
+    )(*own, *other)
 
 
 def unpack_body(in_ref, out_ref, sems):
@@ -170,8 +171,11 @@
     grid_rows,
     width,
     share_rows,
-    own_ref,
-    other_ref,
+    members,
+    *refs,
+):
+    pieces, refs = refs[: 2 * members], refs[2 * members :]
+    (
     tile_ref,
     in_weight_hbm,
     in_bias_hbm,
@@ -194,7 +198,7 @@
     summed,
     weight_sems,
     small_sems,
-):
+    ) = refs
     pairs = active.shape[1] // 16
     channels, features = in_weight_ref.shape[3:]
     columns = out_ref.shape[2]
@@ -237,17 +241,15 @@
     filled = tile_ref[position]
     first_row = lax.fori_loop(0, position, lambda d, total: total + tile_ref[d], jnp.int32(0))
 
-    members, message, _ = own_ref.shape
     chunks = rows_held.shape[1] // 128
     extra = -(-share_rows * chunks // 16) * 16
-    for side, ref in enumerate((own_ref, other_ref)):
-        for member in range(members):
-            lines = ref[member, message - extra :].astype(jnp.float32)
-            low = (side * members + member) * share_rows
-            for chunk in range(chunks):
-                rows_held[low : low + share_rows, chunk * 128 : (chunk + 1) * 128] = lines[
-                    chunk * share_rows : (chunk + 1) * share_rows
-                ]
+    for place, ref in enumerate(pieces):
+        lines = ref[ref.shape[0] - extra :].astype(jnp.float32)
+        low = place * share_rows
+        for chunk in range(chunks):
+            rows_held[low : low + share_rows, chunk * 128 : (chunk + 1) * 128] = lines[
+                chunk * share_rows : (chunk + 1) * share_rows
+            ]
     latent = rows_held[...]
     aside = pltpu.roll(latent, latent.shape[1] - RIM, 1).astype(jnp.bfloat16)
     latent = latent.astype(jnp.bfloat16)
@@ -255,7 +257,7 @@
     unit = lax.broadcasted_iota(jnp.int32, (UNITS, held_rows), 0)
     held = lax.broadcasted_iota(jnp.int32, (UNITS, held_rows), 1)
     side = (held >= members * share_rows).astype(jnp.int32)
-    member = held // share_rows - side * members
+    member = (held // share_rows - side * members) ^ (position // 2)
     held = (2 * member + ((position & 1) ^ side)) * share_rows + held % share_rows
     frame = sum((unit >= (k + 1) * REACH).astype(jnp.int32) for k in range(LF))
     reach = unit - frame * REACH
@@ -437,8 +439,8 @@
     depth = slots * 2 * 4 * token_width
     held = chunks * 4 * UNITS
     return pl.pallas_call(
-        functools.partial(decode_body, grid_rows, width, share_rows),
-        in_specs=[vmem, vmem, pl.BlockSpec(memory_space=pltpu.SMEM)] + [hbm] * 5,
+        functools.partial(decode_body, grid_rows, width, share_rows, len(own)),
+        in_specs=[vmem] * (2 * len(own)) + [pl.BlockSpec(memory_space=pltpu.SMEM)] + [hbm] * 5,
         out_specs=vmem,
         out_shape=jax.ShapeDtypeStruct((LF, ROWS, columns, features), jnp.bfloat16),
         scratch_shapes=[
@@ -448,7 +450,7 @@
             pltpu.VMEM(norm_gain.shape, jnp.float32),
             pltpu.VMEM(conv_mid_bias.shape, jnp.float32),
             pltpu.VMEM((depth, 2 * features), jnp.bfloat16),
-            pltpu.VMEM((2 * own.shape[0] * share_rows, chunks * 128), jnp.float32),
+            pltpu.VMEM((2 * len(own) * share_rows, chunks * 128), jnp.float32),
             pltpu.VMEM((chunks * 2 * UNITS, depth), jnp.bfloat16),
             pltpu.VMEM((chunks * 2 * UNITS, 2 * features), jnp.float32),
             pltpu.VMEM((lane_tiles, held, 128), jnp.float32),
@@ -466,8 +468,8 @@
         ),
         name="decode_tile",
     )(
-        own,
-        other,
+        *own,
+        *other,
         *in_hbm(
             tile_rows, conv_in_weight, conv_in_bias, norm_gain, conv_mid_weight, conv_mid_bias
         ),
@@ -491,8 +493,11 @@
     grid_rows = latent.shape[0] * devices // LF
     token_width = 4 * conv_in_weight.shape[3]
     packed = pack_heads(queries, key_tokens, value_tokens, latent, token_width)
-    own = lax.all_to_all(packed, "seq", 0, 0, axis_index_groups=groups, tiled=True)
-    other = lax.ppermute(own, "seq", xor_pairs(1))
+    chips = len(packed)
+    own = list(packed)
+    for m in [1, 2, *range(chips // 2, chips), *range(3, chips // 2)]:
+        own[m] = lax.ppermute(packed[m], "seq", xor_pairs(2 * m))
+    other = [lax.ppermute(piece, "seq", xor_pairs(1)) for piece in own]
     mixed = attend(own, other, queries.shape[0])
     returned = lax.all_to_all(mixed, "seq", 0, 0, axis_index_groups=groups, tiled=True)
     frames = decode_tile(

time: 40.4 us -> 38.8 us (0.960)
  blocking collectives: 20.9 us -> 0 us
  starting transfers between devices: 3.59 us -> 17.9 us
  waiting for transfers between devices: 1.86 us -> 6.83 us
    all_to_all x1 -> x0, blocking collectives: 20.9 us -> none  [on_device(): lax.all_to_all(packed, 'seq', 0, 0, axis_index_groups=groups, tiled=True)]
    ppermute x1 -> x15, starting transfers between devices: 0.01 us -> 14.6 us  [the longest x7 12.5 us: on_device(): own[m] = lax.ppermute(packed[m], 'seq', xor_pairs(2 * m))]
    ppermute x1 -> x15, waiting for transfers between devices: 1.86 us -> 6.83 us  [the longest x7 5.93 us: on_device(): own[m] = lax.ppermute(packed[m], 'seq', xor_pairs(2 * m))]
  transfers between devices with their start and end apart: 2 -> 16, of which waited for: 1 -> 6; matrix products, arithmetic and copies ran while one was open for 0% -> 0% of each run, Pallas kernels for 22% -> 23%
where the time goes in v12:
time: 38.8 us; the launch traced here: 38.5 us
  starting transfers between devices  17.9 us (46%)
  Pallas kernels  13.1 us (34%)
  waiting for transfers between devices  6.83 us (18%)
  between operations  0.69 us (2%)
    ppermute x7, starting transfers between devices, on_device(): own[m] = lax.ppermute(packed[m], 'seq', xor_pairs(2 * m))  12.5 us
    pallas_call x1, Pallas kernels, decode_tile(): pl.pallas_call(functools.partial(decode_body, grid_rows, width, share_row...  8.69 us
    ppermute x7, waiting for transfers between devices, on_device(): own[m] = lax.ppermute(packed[m], 'seq', xor_pairs(2 * m))  5.93 us
    all_to_all x1, starting transfers between devices, on_device(): lax.all_to_all(mixed, 'seq', 0, 0, axis_index_groups=groups, tiled=True)  3.37 us
    ppermute x8, starting transfers between devices, on_device(): other = [lax.ppermute(piece, 'seq', xor_pairs(1)) for piece in own]  2.06 us
    pallas_call x1, Pallas kernels, attend(): pl.pallas_call(attend_body, in_specs=[vmem] * (2 * members), out_specs=vm...  1.85 us
    pallas_call x1, Pallas kernels, pack_heads(): pl.pallas_call(pack_body, in_specs=[hbm, hbm, hbm, vmem], out_specs=[vmem...  1.83 us
    ppermute x8, waiting for transfers between devices, on_device(): other = [lax.ppermute(piece, 'seq', xor_pairs(1)) for piece in own]  0.9 us
  transfers between devices with their start and end apart: 16, of which 6 were waited for; matrix products, arithmetic and copies ran while one was open for 0% of the time, Pallas kernels for 23%

profile of v12, /device:TPU:0, one launch (start us, length us, event | category | flops | bytes accessed | tf_op | source)
XLA Modules:
  0.0 38.5 jit_solution(15052624834413318899)
XLA Ops:
  0.6 1.8 %pack_heads.1 = (bf16[240,128]{1,0:T(8,128)(2,1)S(1)}, bf16[240,128]{1,0:T(8,128)(2,1)S(1)}, bf16[240,128]{1,0:T(8,128)(2,1)S(1)}, bf16[240,128]{1,0:T(8,128)(2,...) custom-call(bf16[64,2048]{1,0:T(8,128)(2,1)} %query_ref.1, ...), custom_call_target="tpu_custom_call" | custom-call | tf_op jit(solution)/shard_map/pack_heads/pallas_call | solution.py:74
  2.5 3.0 %collective-permute-start = (bf16[240,128]{1,0:T(8,128)(2,1)S(1)}, bf16[240,128]{1,0:T(8,128)(2,1)S(1)}, u32[]{:S(2)}, u32[]{:S(2)}) collective-permute-start(bf16[240,128]{1,0:T(8,128)(2,1)S(1)} %get-tuple-element.11), channel_id=1, source_target_pairs={{0,2},{1,3},{2,0},{3,1},{4,6},{5,7},{6,4},{7,5},{8,10},{9,11},{10,... | collective-permute-start | bytes 184328 | tf_op jit(solution)/shard_map/ppermute | solution.py:499
  5.5 1.6 %collective-permute-start.1 = (bf16[240,128]{1,0:T(8,128)(2,1)S(1)}, bf16[240,128]{1,0:T(8,128)(2,1)S(1)}, u32[]{:S(2)}, u32[]{:S(2)}) collective-permute-start(bf16[240,128]{1,0:T(8,128)(2,1)S(1)} %get-tuple-element.12), channel_id=1, source_target_pairs={{0,4},{1,5},{2,6},{3,7},{4,0},{5,1},{6,2},{7,3},{8,12},{9,13},{10,... | collective-permute-start | bytes 184328 | tf_op jit(solution)/shard_map/ppermute | solution.py:499
  7.0 0.0 collective-permute-start.2
  7.1 3.0 %collective-permute-start.3 = (bf16[240,128]{1,0:T(8,128)(2,1)S(1)}, bf16[240,128]{1,0:T(8,128)(2,1)S(1)}, u32[]{:S(2)}, u32[]{:S(2)}) collective-permute-start(bf16[240,128]{1,0:T(8,128)(2,1)S(1)} %get-tuple-element.14), channel_id=1, source_target_pairs={{0,8},{1,9},{2,10},{3,11},{4,12},{5,13},{6,14},{7,15},{8,0},{9,1},... | collective-permute-start | bytes 184328 | tf_op jit(solution)/shard_map/ppermute | solution.py:499
  10.1 1.3 %collective-permute-start.4 = (bf16[240,128]{1,0:T(8,128)(2,1)S(1)}, bf16[240,128]{1,0:T(8,128)(2,1)S(1)}, u32[]{:S(2)}, u32[]{:S(2)}) collective-permute-start(bf16[240,128]{1,0:T(8,128)(2,1)S(1)} %get-tuple-element.15), channel_id=1, source_target_pairs={{0,10},{1,11},{2,8},{3,9},{4,14},{5,15},{6,12},{7,13},{8,2},{9,3},... | collective-permute-start | bytes 184328 | tf_op jit(solution)/shard_map/ppermute | solution.py:499
  11.3 0.0 collective-permute-done.refs_1_
  11.3 3.6 %collective-permute-start.5 = (bf16[240,128]{1,0:T(8,128)(2,1)S(1)}, bf16[240,128]{1,0:T(8,128)(2,1)S(1)}, u32[]{:S(2)}, u32[]{:S(2)}) collective-permute-start(bf16[240,128]{1,0:T(8,128)(2,1)S(1)} %get-tuple-element.16), channel_id=1, source_target_pairs={{0,12},{1,13},{2,14},{3,15},{4,8},{5,9},{6,10},{7,11},{8,4},{9,5},... | collective-permute-start | bytes 184328 | tf_op jit(solution)/shard_map/ppermute | solution.py:499
  14.9 0.0 collective-permute-done.1.refs_2_
  14.9 0.0 collective-permute-start.6
  15.0 0.0 collective-permute-done.2.refs_3_
  15.0 0.0 collective-permute-start.7
  15.0 0.0 collective-permute-done.3.refs_4_
  15.0 0.5 %collective-permute-start.8 = (bf16[240,128]{1,0:T(8,128)(2,1)S(1)}, bf16[240,128]{1,0:T(8,128)(2,1)S(1)}, u32[]{:S(2)}, u32[]{:S(2)}) collective-permute-start(bf16[240,128]{1,0:T(8,128)(2,1)S(1)} %collective-permute-done.refs_1_), channel_id=1, source_target_pairs={{0,1},{1,0},{2,3},{3,2},{4,5},{5,4},{6,7},{7,6},{8,9},{9,8},{10,11... | collective-permute-start | bytes 184328 | tf_op jit(solution)/shard_map/ppermute | solution.py:500
  15.5 4.2 %collective-permute-done.4.refs_5_ = bf16[240,128]{1,0:T(8,128)(2,1)S(1)} collective-permute-done((bf16[240,128]{1,0:T(8,128)(2,1)S(1)}, bf16[240,128]{1,0:T(8,128)(2,1)S(1)}, u32[]{:S(2)}, u32[]{:S(2)}) %collective-permute-start.4) | collective-permute-done | bytes 61472 | tf_op jit(solution)/shard_map/ppermute | solution.py:499
  19.7 0.0 collective-permute-start.9
  19.7 0.0 collective-permute-done.5.refs_6_
  19.7 0.5 %collective-permute-start.10 = (bf16[240,128]{1,0:T(8,128)(2,1)S(1)}, bf16[240,128]{1,0:T(8,128)(2,1)S(1)}, u32[]{:S(2)}, u32[]{:S(2)}) collective-permute-start(bf16[240,128]{1,0:T(8,128)(2,1)S(1)} %collective-permute-done.2.refs_3_), channel_id=1, source_target_pairs={{0,1},{1,0},{2,3},{3,2},{4,5},{5,4},{6,7},{7,6},{8,9},{9,8},{10,11... | collective-permute-start | bytes 184328 | tf_op jit(solution)/shard_map/ppermute | solution.py:500
  20.2 1.7 %collective-permute-done.6.refs_7_ = bf16[240,128]{1,0:T(8,128)(2,1)S(1)} collective-permute-done((bf16[240,128]{1,0:T(8,128)(2,1)S(1)}, bf16[240,128]{1,0:T(8,128)(2,1)S(1)}, u32[]{:S(2)}, u32[]{:S(2)}) %collective-permute-start.6) | collective-permute-done | bytes 61472 | tf_op jit(solution)/shard_map/ppermute | solution.py:499
  22.0 0.0 collective-permute-start.11
  22.0 0.5 %collective-permute-start.12 = (bf16[240,128]{1,0:T(8,128)(2,1)S(1)}, bf16[240,128]{1,0:T(8,128)(2,1)S(1)}, u32[]{:S(2)}, u32[]{:S(2)}) collective-permute-start(bf16[240,128]{1,0:T(8,128)(2,1)S(1)} %collective-permute-done.4.refs_5_), channel_id=1, source_target_pairs={{0,1},{1,0},{2,3},{3,2},{4,5},{5,4},{6,7},{7,6},{8,9},{9,8},{10,11... | collective-permute-start | bytes 184328 | tf_op jit(solution)/shard_map/ppermute | solution.py:500
  22.5 0.1 collective-permute-start.13
  22.5 0.0 collective-permute-done.9.refs_10_
  22.5 0.4 %collective-permute-start.14 = (bf16[240,128]{1,0:T(8,128)(2,1)S(1)}, bf16[240,128]{1,0:T(8,128)(2,1)S(1)}, u32[]{:S(2)}, u32[]{:S(2)}) collective-permute-start(bf16[240,128]{1,0:T(8,128)(2,1)S(1)} %collective-permute-done.6.refs_7_), channel_id=1, source_target_pairs={{0,1},{1,0},{2,3},{3,2},{4,5},{5,4},{6,7},{7,6},{8,9},{9,8},{10,11... | collective-permute-start | bytes 184328 | tf_op jit(solution)/shard_map/ppermute | solution.py:500
  23.0 0.2 collective-permute-done.11.refs_12_
  23.2 0.2 collective-permute-done.12.refs_13_
  23.4 0.4 collective-permute-done.13.refs_14_
  23.7 0.2 collective-permute-done.14.refs_15_
  23.9 1.9 %attend.1 = bf16[8,64,128]{2,1,0:T(8,128)(2,1)} custom-call(bf16[240,128]{1,0:T(8,128)(2,1)S(1)} %get-tuple-element.10.refs_0_, bf16[240,128]{1,0:T(8,128)(2,1)S(1)} %collective-permute-done.refs_1_, bf16[240,128]{1,0:T(8,128)(2,1)S(1)} %collective-permute-done.1.refs_2_, bf16[240,128]{1,0:T(8,128)(2,1)S(1)} %collective-permute-done.2.refs_3_, ...), custom_call_target="tpu_custom_call" | custom-call | flops 268435456 | bytes 917504 | tf_op jit(solution)/shard_map/attend/pallas_call | solution.py:129
  25.7 3.4 %all-to-all-start = ((bf16[8,64,128]{2,1,0:T(8,128)(2,1)}), bf16[8,64,128]{2,1,0:T(8,128)(2,1)S(1)}, u32[]{:S(2)}, u32[]{:S(2)}) async-start(bf16[8,64,128]{2,1,0:T(8,128)(2,1)} %attend.1), calls=%async_computation | async-start | bytes 262144 | tf_op jit(solution)/shard_map/all_to_all | solution.py:502
  29.1 8.7 %decode_tile.1 = bf16[2,8,40,384]{3,2,1,0:T(8,128)(2,1)} custom-call(bf16[240,128]{1,0:T(8,128)(2,1)S(1)} %get-tuple-element.10.refs_0_, bf16[240,128]{1,0:T(8,128)(2,1)S(1)} %collective-permute-done.refs_1_, bf16[240,128]{1,0:T(8,128)(2,1)S(1)} %collective-permute-done.1.refs_2_, bf16[240,128]{1,0:T(8,128)(2,1)S(1)} %collective-permute-done.2.refs_3_, ...), custom_call_target="tpu_custom_call" | custom-call | flops 2548039680 | bytes 5308416 | tf_op jit(solution)/shard_map/decode_tile/pallas_call | solution.py:441
  37.8 0.7 %unpack_heads.1 = bf16[64,1024]{1,0:T(8,128)(2,1)} custom-call(bf16[8,64,128]{2,1,0:T(8,128)(2,1)S(1)} %all-to-all-done.in_ref), custom_call_target="tpu_custom_call" | custom-call | tf_op jit(solution)/shard_map/unpack_heads/pallas_call | solution.py:159
  (4 shorter events, 0.0 us)
Async XLA Ops:
  2.5 8.9 %collective-permute-start = (bf16[240,128]{1,0:T(8,128)(2,1)S(1)}, bf16[240,128]{1,0:T(8,128)(2,1)S(1)}, u32[]{:S(2)}, u32[]{:S(2)}) collective-permute-start(bf16[240,128]{1,0:T(8,128)(2,1)S(1)} %get-tuple-element.11), channel_id=1, source_target_pairs={{0,2},{1,3},{2,0},{3,1},{4,6},{5,7},{6,4},{7,5},{8,10},{9,11},{10,... | collective-permute-start | bytes 184328 | tf_op jit(solution)/shard_map/ppermute | solution.py:499
  5.5 9.5 %collective-permute-start.1 = (bf16[240,128]{1,0:T(8,128)(2,1)S(1)}, bf16[240,128]{1,0:T(8,128)(2,1)S(1)}, u32[]{:S(2)}, u32[]{:S(2)}) collective-permute-start(bf16[240,128]{1,0:T(8,128)(2,1)S(1)} %get-tuple-element.12), channel_id=1, source_target_pairs={{0,4},{1,5},{2,6},{3,7},{4,0},{5,1},{6,2},{7,3},{8,12},{9,13},{10,... | collective-permute-start | bytes 184328 | tf_op jit(solution)/shard_map/ppermute | solution.py:499
  7.0 7.9 %collective-permute-start.2 = (bf16[240,128]{1,0:T(8,128)(2,1)S(1)}, bf16[240,128]{1,0:T(8,128)(2,1)S(1)}, u32[]{:S(2)}, u32[]{:S(2)}) collective-permute-start(bf16[240,128]{1,0:T(8,128)(2,1)S(1)} %get-tuple-element.13), channel_id=1, source_target_pairs={{0,6},{1,7},{2,4},{3,5},{4,2},{5,3},{6,0},{7,1},{8,14},{9,15},{10,... | collective-permute-start | bytes 184328 | tf_op jit(solution)/shard_map/ppermute | solution.py:499
  7.1 8.0 %collective-permute-start.3 = (bf16[240,128]{1,0:T(8,128)(2,1)S(1)}, bf16[240,128]{1,0:T(8,128)(2,1)S(1)}, u32[]{:S(2)}, u32[]{:S(2)}) collective-permute-start(bf16[240,128]{1,0:T(8,128)(2,1)S(1)} %get-tuple-element.14), channel_id=1, source_target_pairs={{0,8},{1,9},{2,10},{3,11},{4,12},{5,13},{6,14},{7,15},{8,0},{9,1},... | collective-permute-start | bytes 184328 | tf_op jit(solution)/shard_map/ppermute | solution.py:499
  10.1 9.7 %collective-permute-start.4 = (bf16[240,128]{1,0:T(8,128)(2,1)S(1)}, bf16[240,128]{1,0:T(8,128)(2,1)S(1)}, u32[]{:S(2)}, u32[]{:S(2)}) collective-permute-start(bf16[240,128]{1,0:T(8,128)(2,1)S(1)} %get-tuple-element.15), channel_id=1, source_target_pairs={{0,10},{1,11},{2,8},{3,9},{4,14},{5,15},{6,12},{7,13},{8,2},{9,3},... | collective-permute-start | bytes 184328 | tf_op jit(solution)/shard_map/ppermute | solution.py:499
  11.3 8.4 %collective-permute-start.5 = (bf16[240,128]{1,0:T(8,128)(2,1)S(1)}, bf16[240,128]{1,0:T(8,128)(2,1)S(1)}, u32[]{:S(2)}, u32[]{:S(2)}) collective-permute-start(bf16[240,128]{1,0:T(8,128)(2,1)S(1)} %get-tuple-element.16), channel_id=1, source_target_pairs={{0,12},{1,13},{2,14},{3,15},{4,8},{5,9},{6,10},{7,11},{8,4},{9,5},... | collective-permute-start | bytes 184328 | tf_op jit(solution)/shard_map/ppermute | solution.py:499
  14.9 7.0 %collective-permute-start.6 = (bf16[240,128]{1,0:T(8,128)(2,1)S(1)}, bf16[240,128]{1,0:T(8,128)(2,1)S(1)}, u32[]{:S(2)}, u32[]{:S(2)}) collective-permute-start(bf16[240,128]{1,0:T(8,128)(2,1)S(1)} %get-tuple-element.17), channel_id=1, source_target_pairs={{0,14},{1,15},{2,12},{3,13},{4,10},{5,11},{6,8},{7,9},{8,6},{9,7},... | collective-permute-start | bytes 184328 | tf_op jit(solution)/shard_map/ppermute | solution.py:499
  15.0 7.0 %collective-permute-start.7 = (bf16[240,128]{1,0:T(8,128)(2,1)S(1)}, bf16[240,128]{1,0:T(8,128)(2,1)S(1)}, u32[]{:S(2)}, u32[]{:S(2)}) collective-permute-start(bf16[240,128]{1,0:T(8,128)(2,1)S(1)} %get-tuple-element.10.refs_0_), channel_id=1, source_target_pairs={{0,1},{1,0},{2,3},{3,2},{4,5},{5,4},{6,7},{7,6},{8,9},{9,8},{10,11... | collective-permute-start | bytes 184328 | tf_op jit(solution)/shard_map/ppermute | solution.py:500
  15.0 7.4 %collective-permute-start.8 = (bf16[240,128]{1,0:T(8,128)(2,1)S(1)}, bf16[240,128]{1,0:T(8,128)(2,1)S(1)}, u32[]{:S(2)}, u32[]{:S(2)}) collective-permute-start(bf16[240,128]{1,0:T(8,128)(2,1)S(1)} %collective-permute-done.refs_1_), channel_id=1, source_target_pairs={{0,1},{1,0},{2,3},{3,2},{4,5},{5,4},{6,7},{7,6},{8,9},{9,8},{10,11... | collective-permute-start | bytes 184328 | tf_op jit(solution)/shard_map/ppermute | solution.py:500
  19.7 2.8 %collective-permute-start.9 = (bf16[240,128]{1,0:T(8,128)(2,1)S(1)}, bf16[240,128]{1,0:T(8,128)(2,1)S(1)}, u32[]{:S(2)}, u32[]{:S(2)}) collective-permute-start(bf16[240,128]{1,0:T(8,128)(2,1)S(1)} %collective-permute-done.1.refs_2_), channel_id=1, source_target_pairs={{0,1},{1,0},{2,3},{3,2},{4,5},{5,4},{6,7},{7,6},{8,9},{9,8},{10,11... | collective-permute-start | bytes 184328 | tf_op jit(solution)/shard_map/ppermute | solution.py:500
  19.7 3.3 %collective-permute-start.10 = (bf16[240,128]{1,0:T(8,128)(2,1)S(1)}, bf16[240,128]{1,0:T(8,128)(2,1)S(1)}, u32[]{:S(2)}, u32[]{:S(2)}) collective-permute-start(bf16[240,128]{1,0:T(8,128)(2,1)S(1)} %collective-permute-done.2.refs_3_), channel_id=1, source_target_pairs={{0,1},{1,0},{2,3},{3,2},{4,5},{5,4},{6,7},{7,6},{8,9},{9,8},{10,11... | collective-permute-start | bytes 184328 | tf_op jit(solution)/shard_map/ppermute | solution.py:500
  22.0 1.2 %collective-permute-start.11 = (bf16[240,128]{1,0:T(8,128)(2,1)S(1)}, bf16[240,128]{1,0:T(8,128)(2,1)S(1)}, u32[]{:S(2)}, u32[]{:S(2)}) collective-permute-start(bf16[240,128]{1,0:T(8,128)(2,1)S(1)} %collective-permute-done.3.refs_4_), channel_id=1, source_target_pairs={{0,1},{1,0},{2,3},{3,2},{4,5},{5,4},{6,7},{7,6},{8,9},{9,8},{10,11... | collective-permute-start | bytes 184328 | tf_op jit(solution)/shard_map/ppermute | solution.py:500
  22.0 1.4 %collective-permute-start.12 = (bf16[240,128]{1,0:T(8,128)(2,1)S(1)}, bf16[240,128]{1,0:T(8,128)(2,1)S(1)}, u32[]{:S(2)}, u32[]{:S(2)}) collective-permute-start(bf16[240,128]{1,0:T(8,128)(2,1)S(1)} %collective-permute-done.4.refs_5_), channel_id=1, source_target_pairs={{0,1},{1,0},{2,3},{3,2},{4,5},{5,4},{6,7},{7,6},{8,9},{9,8},{10,11... | collective-permute-start | bytes 184328 | tf_op jit(solution)/shard_map/ppermute | solution.py:500
  22.5 1.2 %collective-permute-start.13 = (bf16[240,128]{1,0:T(8,128)(2,1)S(1)}, bf16[240,128]{1,0:T(8,128)(2,1)S(1)}, u32[]{:S(2)}, u32[]{:S(2)}) collective-permute-start(bf16[240,128]{1,0:T(8,128)(2,1)S(1)} %collective-permute-done.5.refs_6_), channel_id=1, source_target_pairs={{0,1},{1,0},{2,3},{3,2},{4,5},{5,4},{6,7},{7,6},{8,9},{9,8},{10,11... | collective-permute-start | bytes 184328 | tf_op jit(solution)/shard_map/ppermute | solution.py:500
  22.5 1.3 %collective-permute-start.14 = (bf16[240,128]{1,0:T(8,128)(2,1)S(1)}, bf16[240,128]{1,0:T(8,128)(2,1)S(1)}, u32[]{:S(2)}, u32[]{:S(2)}) collective-permute-start(bf16[240,128]{1,0:T(8,128)(2,1)S(1)} %collective-permute-done.6.refs_7_), channel_id=1, source_target_pairs={{0,1},{1,0},{2,3},{3,2},{4,5},{5,4},{6,7},{7,6},{8,9},{9,8},{10,11... | collective-permute-start | bytes 184328 | tf_op jit(solution)/shard_map/ppermute | solution.py:500
  25.7 12.1 %all-to-all-start = ((bf16[8,64,128]{2,1,0:T(8,128)(2,1)}), bf16[8,64,128]{2,1,0:T(8,128)(2,1)S(1)}, u32[]{:S(2)}, u32[]{:S(2)}) async-start(bf16[8,64,128]{2,1,0:T(8,128)(2,1)} %attend.1), calls=%async_computation | async-start | bytes 262144 | tf_op jit(solution)/shard_map/all_to_all | solution.py:502

commit v13 on v12

--- a/solution.py
+++ b/solution.py
@@ -30,7 +30,7 @@
 
 
 def pack_body(query_ref, key_ref, value_ref, latent_ref, *refs):
-    packed_refs, (held, sems) = refs[:-2], refs[-2:]
+    packed_refs, (held, latent_held, sems) = refs[:-3], refs[-3:]
     heads = len(packed_refs)
     chip = lax.axis_index("seq") // 2
     token_rows = query_ref.shape[0]
@@ -40,11 +40,14 @@
         pltpu.make_async_copy(ref.at[:, wide_columns], held.at[place], sems.at[place])
         for place, ref in enumerate((query_ref, key_ref, value_ref))
     ]
+    latent_copy = pltpu.make_async_copy(latent_ref, latent_held, sems.at[3])
+    latent_copy.start()
     for copy in copies:
         copy.start()
     rows, width = latent_ref.shape
+    latent_copy.wait()
     half, rim = width // 2, RIM
-    wide = latent_ref[...].astype(jnp.float32)
+    wide = latent_held[...].astype(jnp.float32)
     rim_zeros = jnp.zeros((rows, rim), jnp.float32)
     lower = jnp.concatenate([rim_zeros, wide[:, : half + rim]], axis=1)
     upper = jnp.concatenate([wide[:, half - rim :], rim_zeros], axis=1)
@@ -73,12 +76,13 @@
     vmem = pl.BlockSpec(memory_space=pltpu.VMEM)
     return pl.pallas_call(
         pack_body,
-        in_specs=[hbm, hbm, hbm, vmem],
+        in_specs=[hbm] * 4,
         out_specs=[vmem] * heads,
         out_shape=[jax.ShapeDtypeStruct((3 * token_rows + extra, DH), queries.dtype)] * heads,
         scratch_shapes=[
             pltpu.VMEM((3, token_rows, heads * DH), queries.dtype),
-            pltpu.SemaphoreType.DMA((3,)),
+            pltpu.VMEM(latent.shape, latent.dtype),
+            pltpu.SemaphoreType.DMA((4,)),
         ],
         compiler_params=pltpu.CompilerParams(vmem_limit_bytes=COPY_VMEM),
         name="pack_heads",
@@ -176,12 +180,14 @@
 ):
     pieces, refs = refs[: 2 * members], refs[2 * members :]
     (
-    tile_ref,
+    tile_hbm,
     in_weight_hbm,
     in_bias_hbm,
     gain_hbm,
     mid_weight_hbm,
     mid_bias_hbm,
+    out_hbm,
+    tile_ref,
     out_ref,
     mid_weight,
     in_weight_ref,
@@ -198,6 +204,7 @@
     summed,
     weight_sems,
     small_sems,
+    out_sems,
     ) = refs
     pairs = active.shape[1] // 16
     channels, features = in_weight_ref.shape[3:]
@@ -205,6 +212,8 @@
     lane_tiles = features // 128
     position = lax.axis_index("seq")
     section = lax.axis_index("sect")
+    tile_copy = pltpu.make_async_copy(tile_hbm, tile_ref, small_sems.at[4])
+    tile_copy.start()
     small = [
         pltpu.make_async_copy(source, target, small_sems.at[place])
         for place, (source, target) in enumerate(
@@ -238,6 +247,7 @@
         for copy in load(col_tap):
             copy.start()
 
+    tile_copy.wait()
     filled = tile_ref[position]
     first_row = lax.fori_loop(0, position, lambda d, total: total + tile_ref[d], jnp.int32(0))
 
@@ -386,6 +396,10 @@
             value = jnp.where(tile_row < 2 * filled, value, 0.0)
             value = jnp.swapaxes(value.reshape(columns, ROWS, 128), 0, 1)
             out_ref[field, :, :, lanes] = value.astype(jnp.bfloat16)
+        leave(field).start()
+
+    def leave(field):
+        return pltpu.make_async_copy(out_ref.at[field], out_hbm.at[field], out_sems.at[field])
 
     for phase in range(2):
         for pair in range(pairs - phase):
@@ -402,14 +416,16 @@
         for lane in range(2):
             field, tile = divmod(left // 128 + lane, lane_tiles)
             summed[field, tile] = block[:, lane * 128 : (lane + 1) * 128]
+    finish(0)
     for left in range(0, features, 256):
         right = min(left + 256, features)
         block = jnp.dot(late, weights(slice(left, right)), preferred_element_type=jnp.float32)
         for lane in range((right - left) // 128):
             tile = left // 128 + lane
             summed[1, tile] = summed[1, tile] + block[:, lane * 128 : (lane + 1) * 128]
+    finish(1)
     for field in range(LF):
-        finish(field)
+        leave(field).wait()
 
 
 def decode_tile(
@@ -440,10 +456,12 @@
     held = chunks * 4 * UNITS
     return pl.pallas_call(
         functools.partial(decode_body, grid_rows, width, share_rows, len(own)),
-        in_specs=[vmem] * (2 * len(own)) + [pl.BlockSpec(memory_space=pltpu.SMEM)] + [hbm] * 5,
-        out_specs=vmem,
+        in_specs=[vmem] * (2 * len(own)) + [hbm] * 6,
+        out_specs=hbm,
         out_shape=jax.ShapeDtypeStruct((LF, ROWS, columns, features), jnp.bfloat16),
         scratch_shapes=[
+            pltpu.SMEM(tile_rows.shape, tile_rows.dtype),
+            pltpu.VMEM((LF, ROWS, columns, features), jnp.bfloat16),
             pltpu.VMEM((3, 3 * features, slots * features), jnp.bfloat16),
             pltpu.VMEM(conv_in_weight.shape, jnp.bfloat16),
             pltpu.VMEM(conv_in_bias.shape, jnp.float32),
@@ -458,7 +476,8 @@
             pltpu.VMEM((2, pairs * 16, LF * 3 * features), jnp.bfloat16),
             pltpu.VMEM((LF, lane_tiles, columns * ROWS, 128), jnp.float32),
             pltpu.SemaphoreType.DMA((3, 3, slots)),
-            pltpu.SemaphoreType.DMA((4,)),
+            pltpu.SemaphoreType.DMA((5,)),
+            pltpu.SemaphoreType.DMA((LF,)),
         ],
         compiler_params=pltpu.CompilerParams(vmem_limit_bytes=DECODE_VMEM),
         cost_estimate=pl.CostEstimate(
@@ -495,7 +514,8 @@
     packed = pack_heads(queries, key_tokens, value_tokens, latent, token_width)
     chips = len(packed)
     own = list(packed)
-    for m in [1, 2, *range(chips // 2, chips), *range(3, chips // 2)]:
+    far, near = list(range(chips // 2, chips)), list(range(1, chips // 2))
+    for m in [*far[:2], *near[1:2], *far[2:], *near[2:], *near[:1]]:
         own[m] = lax.ppermute(packed[m], "seq", xor_pairs(2 * m))
     other = [lax.ppermute(piece, "seq", xor_pairs(1)) for piece in own]
     mixed = attend(own, other, queries.shape[0])

time: 38.8 us -> 37.4 us (0.964)
  Pallas kernels: 13.1 us -> 11.6 us
    pallas_call x1, Pallas kernels: 8.69 us -> 7.96 us  [decode_tile(): pl.pallas_call(functools.partial(decode_body, grid_rows, width, share_row...]
    pallas_call x1, Pallas kernels: 1.83 us -> 1.12 us  [pack_heads(): pl.pallas_call(pack_body, in_specs=[hbm] * 4, out_specs=[vmem] * heads, o...]
  transfers between devices with their start and end apart: 16 -> 16, of which waited for: 6 -> 6; matrix products, arithmetic and copies ran while one was open for 0% -> 0% of each run, Pallas kernels for 23% -> 21%
where the time goes in v13:
time: 37.4 us; the launch traced here: 37.1 us
  starting transfers between devices  17.9 us (48%)
  Pallas kernels  11.6 us (31%)
  waiting for transfers between devices  6.83 us (18%)
  between operations  0.69 us (2%)
    ppermute x7, starting transfers between devices, on_device(): own[m] = lax.ppermute(packed[m], 'seq', xor_pairs(2 * m))  12.5 us
    pallas_call x1, Pallas kernels, decode_tile(): pl.pallas_call(functools.partial(decode_body, grid_rows, width, share_row...  7.96 us
    ppermute x7, waiting for transfers between devices, on_device(): own[m] = lax.ppermute(packed[m], 'seq', xor_pairs(2 * m))  5.93 us
    all_to_all x1, starting transfers between devices, on_device(): lax.all_to_all(mixed, 'seq', 0, 0, axis_index_groups=groups, tiled=True)  3.37 us
    ppermute x8, starting transfers between devices, on_device(): other = [lax.ppermute(piece, 'seq', xor_pairs(1)) for piece in own]  2.06 us
    pallas_call x1, Pallas kernels, attend(): pl.pallas_call(attend_body, in_specs=[vmem] * (2 * members), out_specs=vm...  1.85 us
    pallas_call x1, Pallas kernels, pack_heads(): pl.pallas_call(pack_body, in_specs=[hbm] * 4, out_specs=[vmem] * heads, o...  1.12 us
    ppermute x8, waiting for transfers between devices, on_device(): other = [lax.ppermute(piece, 'seq', xor_pairs(1)) for piece in own]  0.9 us
  transfers between devices with their start and end apart: 16, of which 6 were waited for; matrix products, arithmetic and copies ran while one was open for 0% of the time, Pallas kernels for 21%

profile of v13, /device:TPU:0, one launch (start us, length us, event | category | flops | bytes accessed | tf_op | source)
XLA Modules:
  0.0 37.1 jit_solution(11052932330803646595)
XLA Ops:
  0.6 1.1 %pack_heads.1 = (bf16[240,128]{1,0:T(8,128)(2,1)S(1)}, bf16[240,128]{1,0:T(8,128)(2,1)S(1)}, bf16[240,128]{1,0:T(8,128)(2,1)S(1)}, bf16[240,128]{1,0:T(8,128)(2,...) custom-call(bf16[64,2048]{1,0:T(8,128)(2,1)} %query_ref.1, ...), custom_call_target="tpu_custom_call" | custom-call | tf_op jit(solution)/shard_map/pack_heads/pallas_call | solution.py:77
  1.8 3.0 %collective-permute-start = (bf16[240,128]{1,0:T(8,128)(2,1)S(1)}, bf16[240,128]{1,0:T(8,128)(2,1)S(1)}, u32[]{:S(2)}, u32[]{:S(2)}) collective-permute-start(bf16[240,128]{1,0:T(8,128)(2,1)S(1)} %get-tuple-element.11), channel_id=1, source_target_pairs={{0,2},{1,3},{2,0},{3,1},{4,6},{5,7},{6,4},{7,5},{8,10},{9,11},{10,... | collective-permute-start | bytes 184328 | tf_op jit(solution)/shard_map/ppermute | solution.py:519
  4.8 1.6 %collective-permute-start.1 = (bf16[240,128]{1,0:T(8,128)(2,1)S(1)}, bf16[240,128]{1,0:T(8,128)(2,1)S(1)}, u32[]{:S(2)}, u32[]{:S(2)}) collective-permute-start(bf16[240,128]{1,0:T(8,128)(2,1)S(1)} %get-tuple-element.12), channel_id=1, source_target_pairs={{0,4},{1,5},{2,6},{3,7},{4,0},{5,1},{6,2},{7,3},{8,12},{9,13},{10,... | collective-permute-start | bytes 184328 | tf_op jit(solution)/shard_map/ppermute | solution.py:519
  6.3 0.0 collective-permute-start.2
  6.3 3.0 %collective-permute-start.3 = (bf16[240,128]{1,0:T(8,128)(2,1)S(1)}, bf16[240,128]{1,0:T(8,128)(2,1)S(1)}, u32[]{:S(2)}, u32[]{:S(2)}) collective-permute-start(bf16[240,128]{1,0:T(8,128)(2,1)S(1)} %get-tuple-element.14), channel_id=1, source_target_pairs={{0,8},{1,9},{2,10},{3,11},{4,12},{5,13},{6,14},{7,15},{8,0},{9,1},... | collective-permute-start | bytes 184328 | tf_op jit(solution)/shard_map/ppermute | solution.py:519
  9.3 1.3 %collective-permute-start.4 = (bf16[240,128]{1,0:T(8,128)(2,1)S(1)}, bf16[240,128]{1,0:T(8,128)(2,1)S(1)}, u32[]{:S(2)}, u32[]{:S(2)}) collective-permute-start(bf16[240,128]{1,0:T(8,128)(2,1)S(1)} %get-tuple-element.15), channel_id=1, source_target_pairs={{0,10},{1,11},{2,8},{3,9},{4,14},{5,15},{6,12},{7,13},{8,2},{9,3},... | collective-permute-start | bytes 184328 | tf_op jit(solution)/shard_map/ppermute | solution.py:519
  10.6 0.0 collective-permute-done.refs_1_
  10.6 3.6 %collective-permute-start.5 = (bf16[240,128]{1,0:T(8,128)(2,1)S(1)}, bf16[240,128]{1,0:T(8,128)(2,1)S(1)}, u32[]{:S(2)}, u32[]{:S(2)}) collective-permute-start(bf16[240,128]{1,0:T(8,128)(2,1)S(1)} %get-tuple-element.16), channel_id=1, source_target_pairs={{0,12},{1,13},{2,14},{3,15},{4,8},{5,9},{6,10},{7,11},{8,4},{9,5},... | collective-permute-start | bytes 184328 | tf_op jit(solution)/shard_map/ppermute | solution.py:519
  14.2 0.0 collective-permute-start.6
  14.3 0.0 collective-permute-done.2.refs_3_
  14.3 0.0 collective-permute-start.7
  14.3 0.0 collective-permute-done.3.refs_4_
  14.3 0.5 %collective-permute-start.8 = (bf16[240,128]{1,0:T(8,128)(2,1)S(1)}, bf16[240,128]{1,0:T(8,128)(2,1)S(1)}, u32[]{:S(2)}, u32[]{:S(2)}) collective-permute-start(bf16[240,128]{1,0:T(8,128)(2,1)S(1)} %collective-permute-done.refs_1_), channel_id=1, source_target_pairs={{0,1},{1,0},{2,3},{3,2},{4,5},{5,4},{6,7},{7,6},{8,9},{9,8},{10,11... | collective-permute-start | bytes 184328 | tf_op jit(solution)/shard_map/ppermute | solution.py:520
  14.8 4.2 %collective-permute-done.4.refs_5_ = bf16[240,128]{1,0:T(8,128)(2,1)S(1)} collective-permute-done((bf16[240,128]{1,0:T(8,128)(2,1)S(1)}, bf16[240,128]{1,0:T(8,128)(2,1)S(1)}, u32[]{:S(2)}, u32[]{:S(2)}) %collective-permute-start.4) | collective-permute-done | bytes 61472 | tf_op jit(solution)/shard_map/ppermute | solution.py:519
  19.0 0.0 collective-permute-start.9
  19.0 0.0 collective-permute-done.5.refs_6_
  19.0 0.5 %collective-permute-start.10 = (bf16[240,128]{1,0:T(8,128)(2,1)S(1)}, bf16[240,128]{1,0:T(8,128)(2,1)S(1)}, u32[]{:S(2)}, u32[]{:S(2)}) collective-permute-start(bf16[240,128]{1,0:T(8,128)(2,1)S(1)} %collective-permute-done.2.refs_3_), channel_id=1, source_target_pairs={{0,1},{1,0},{2,3},{3,2},{4,5},{5,4},{6,7},{7,6},{8,9},{9,8},{10,11... | collective-permute-start | bytes 184328 | tf_op jit(solution)/shard_map/ppermute | solution.py:520
  19.5 1.7 %collective-permute-done.6.refs_7_ = bf16[240,128]{1,0:T(8,128)(2,1)S(1)} collective-permute-done((bf16[240,128]{1,0:T(8,128)(2,1)S(1)}, bf16[240,128]{1,0:T(8,128)(2,1)S(1)}, u32[]{:S(2)}, u32[]{:S(2)}) %collective-permute-start.6) | collective-permute-done | bytes 61472 | tf_op jit(solution)/shard_map/ppermute | solution.py:519
  21.2 0.0 collective-permute-start.11
  21.2 0.0 collective-permute-done.7.refs_8_
  21.2 0.5 %collective-permute-start.12 = (bf16[240,128]{1,0:T(8,128)(2,1)S(1)}, bf16[240,128]{1,0:T(8,128)(2,1)S(1)}, u32[]{:S(2)}, u32[]{:S(2)}) collective-permute-start(bf16[240,128]{1,0:T(8,128)(2,1)S(1)} %collective-permute-done.4.refs_5_), channel_id=1, source_target_pairs={{0,1},{1,0},{2,3},{3,2},{4,5},{5,4},{6,7},{7,6},{8,9},{9,8},{10,11... | collective-permute-start | bytes 184328 | tf_op jit(solution)/shard_map/ppermute | solution.py:520
  21.8 0.0 collective-permute-done.8.refs_9_
  21.8 0.1 collective-permute-start.13
  21.8 0.4 %collective-permute-start.14 = (bf16[240,128]{1,0:T(8,128)(2,1)S(1)}, bf16[240,128]{1,0:T(8,128)(2,1)S(1)}, u32[]{:S(2)}, u32[]{:S(2)}) collective-permute-start(bf16[240,128]{1,0:T(8,128)(2,1)S(1)} %collective-permute-done.6.refs_7_), channel_id=1, source_target_pairs={{0,1},{1,0},{2,3},{3,2},{4,5},{5,4},{6,7},{7,6},{8,9},{9,8},{10,11... | collective-permute-start | bytes 184328 | tf_op jit(solution)/shard_map/ppermute | solution.py:520
  22.3 0.2 collective-permute-done.11.refs_12_
  22.5 0.2 collective-permute-done.12.refs_13_
  22.7 0.4 collective-permute-done.13.refs_14_
  23.0 0.2 collective-permute-done.14.refs_15_
  23.2 1.8 %attend.1 = bf16[8,64,128]{2,1,0:T(8,128)(2,1)} custom-call(bf16[240,128]{1,0:T(8,128)(2,1)S(1)} %get-tuple-element.10.refs_0_, bf16[240,128]{1,0:T(8,128)(2,1)S(1)} %collective-permute-done.refs_1_, bf16[240,128]{1,0:T(8,128)(2,1)S(1)} %collective-permute-done.1.refs_2_, bf16[240,128]{1,0:T(8,128)(2,1)S(1)} %collective-permute-done.2.refs_3_, ...), custom_call_target="tpu_custom_call" | custom-call | flops 268435456 | bytes 917504 | tf_op jit(solution)/shard_map/attend/pallas_call | solution.py:133
  25.0 3.4 %all-to-all-start = ((bf16[8,64,128]{2,1,0:T(8,128)(2,1)}), bf16[8,64,128]{2,1,0:T(8,128)(2,1)S(1)}, u32[]{:S(2)}, u32[]{:S(2)}) async-start(bf16[8,64,128]{2,1,0:T(8,128)(2,1)} %attend.1), calls=%async_computation | async-start | bytes 262144 | tf_op jit(solution)/shard_map/all_to_all | solution.py:522
  28.4 8.0 %decode_tile.1 = bf16[2,8,40,384]{3,2,1,0:T(8,128)(2,1)} custom-call(bf16[240,128]{1,0:T(8,128)(2,1)S(1)} %get-tuple-element.10.refs_0_, bf16[240,128]{1,0:T(8,128)(2,1)S(1)} %collective-permute-done.refs_1_, bf16[240,128]{1,0:T(8,128)(2,1)S(1)} %collective-permute-done.1.refs_2_, bf16[240,128]{1,0:T(8,128)(2,1)S(1)} %collective-permute-done.2.refs_3_, ...), custom_call_target="tpu_custom_call" | custom-call | flops 2548039680 | bytes 5308416 | tf_op jit(solution)/shard_map/decode_tile/pallas_call | solution.py:457
  36.4 0.7 %unpack_heads.1 = bf16[64,1024]{1,0:T(8,128)(2,1)} custom-call(bf16[8,64,128]{2,1,0:T(8,128)(2,1)S(1)} %all-to-all-done.in_ref), custom_call_target="tpu_custom_call" | custom-call | tf_op jit(solution)/shard_map/unpack_heads/pallas_call | solution.py:163
  (4 shorter events, 0.0 us)
Async XLA Ops:
  1.8 8.9 %collective-permute-start = (bf16[240,128]{1,0:T(8,128)(2,1)S(1)}, bf16[240,128]{1,0:T(8,128)(2,1)S(1)}, u32[]{:S(2)}, u32[]{:S(2)}) collective-permute-start(bf16[240,128]{1,0:T(8,128)(2,1)S(1)} %get-tuple-element.11), channel_id=1, source_target_pairs={{0,2},{1,3},{2,0},{3,1},{4,6},{5,7},{6,4},{7,5},{8,10},{9,11},{10,... | collective-permute-start | bytes 184328 | tf_op jit(solution)/shard_map/ppermute | solution.py:519
  4.8 9.5 %collective-permute-start.1 = (bf16[240,128]{1,0:T(8,128)(2,1)S(1)}, bf16[240,128]{1,0:T(8,128)(2,1)S(1)}, u32[]{:S(2)}, u32[]{:S(2)}) collective-permute-start(bf16[240,128]{1,0:T(8,128)(2,1)S(1)} %get-tuple-element.12), channel_id=1, source_target_pairs={{0,4},{1,5},{2,6},{3,7},{4,0},{5,1},{6,2},{7,3},{8,12},{9,13},{10,... | collective-permute-start | bytes 184328 | tf_op jit(solution)/shard_map/ppermute | solution.py:519
  6.3 7.9 %collective-permute-start.2 = (bf16[240,128]{1,0:T(8,128)(2,1)S(1)}, bf16[240,128]{1,0:T(8,128)(2,1)S(1)}, u32[]{:S(2)}, u32[]{:S(2)}) collective-permute-start(bf16[240,128]{1,0:T(8,128)(2,1)S(1)} %get-tuple-element.13), channel_id=1, source_target_pairs={{0,6},{1,7},{2,4},{3,5},{4,2},{5,3},{6,0},{7,1},{8,14},{9,15},{10,... | collective-permute-start | bytes 184328 | tf_op jit(solution)/shard_map/ppermute | solution.py:519
  6.3 8.0 %collective-permute-start.3 = (bf16[240,128]{1,0:T(8,128)(2,1)S(1)}, bf16[240,128]{1,0:T(8,128)(2,1)S(1)}, u32[]{:S(2)}, u32[]{:S(2)}) collective-permute-start(bf16[240,128]{1,0:T(8,128)(2,1)S(1)} %get-tuple-element.14), channel_id=1, source_target_pairs={{0,8},{1,9},{2,10},{3,11},{4,12},{5,13},{6,14},{7,15},{8,0},{9,1},... | collective-permute-start | bytes 184328 | tf_op jit(solution)/shard_map/ppermute | solution.py:519
  9.3 9.7 %collective-permute-start.4 = (bf16[240,128]{1,0:T(8,128)(2,1)S(1)}, bf16[240,128]{1,0:T(8,128)(2,1)S(1)}, u32[]{:S(2)}, u32[]{:S(2)}) collective-permute-start(bf16[240,128]{1,0:T(8,128)(2,1)S(1)} %get-tuple-element.15), channel_id=1, source_target_pairs={{0,10},{1,11},{2,8},{3,9},{4,14},{5,15},{6,12},{7,13},{8,2},{9,3},... | collective-permute-start | bytes 184328 | tf_op jit(solution)/shard_map/ppermute | solution.py:519
  10.6 8.4 %collective-permute-start.5 = (bf16[240,128]{1,0:T(8,128)(2,1)S(1)}, bf16[240,128]{1,0:T(8,128)(2,1)S(1)}, u32[]{:S(2)}, u32[]{:S(2)}) collective-permute-start(bf16[240,128]{1,0:T(8,128)(2,1)S(1)} %get-tuple-element.16), channel_id=1, source_target_pairs={{0,12},{1,13},{2,14},{3,15},{4,8},{5,9},{6,10},{7,11},{8,4},{9,5},... | collective-permute-start | bytes 184328 | tf_op jit(solution)/shard_map/ppermute | solution.py:519
  14.2 7.0 %collective-permute-start.6 = (bf16[240,128]{1,0:T(8,128)(2,1)S(1)}, bf16[240,128]{1,0:T(8,128)(2,1)S(1)}, u32[]{:S(2)}, u32[]{:S(2)}) collective-permute-start(bf16[240,128]{1,0:T(8,128)(2,1)S(1)} %get-tuple-element.17), channel_id=1, source_target_pairs={{0,14},{1,15},{2,12},{3,13},{4,10},{5,11},{6,8},{7,9},{8,6},{9,7},... | collective-permute-start | bytes 184328 | tf_op jit(solution)/shard_map/ppermute | solution.py:519
  14.3 7.0 %collective-permute-start.7 = (bf16[240,128]{1,0:T(8,128)(2,1)S(1)}, bf16[240,128]{1,0:T(8,128)(2,1)S(1)}, u32[]{:S(2)}, u32[]{:S(2)}) collective-permute-start(bf16[240,128]{1,0:T(8,128)(2,1)S(1)} %get-tuple-element.10.refs_0_), channel_id=1, source_target_pairs={{0,1},{1,0},{2,3},{3,2},{4,5},{5,4},{6,7},{7,6},{8,9},{9,8},{10,11... | collective-permute-start | bytes 184328 | tf_op jit(solution)/shard_map/ppermute | solution.py:520
  14.3 7.4 %collective-permute-start.8 = (bf16[240,128]{1,0:T(8,128)(2,1)S(1)}, bf16[240,128]{1,0:T(8,128)(2,1)S(1)}, u32[]{:S(2)}, u32[]{:S(2)}) collective-permute-start(bf16[240,128]{1,0:T(8,128)(2,1)S(1)} %collective-permute-done.refs_1_), channel_id=1, source_target_pairs={{0,1},{1,0},{2,3},{3,2},{4,5},{5,4},{6,7},{7,6},{8,9},{9,8},{10,11... | collective-permute-start | bytes 184328 | tf_op jit(solution)/shard_map/ppermute | solution.py:520
  19.0 2.8 %collective-permute-start.9 = (bf16[240,128]{1,0:T(8,128)(2,1)S(1)}, bf16[240,128]{1,0:T(8,128)(2,1)S(1)}, u32[]{:S(2)}, u32[]{:S(2)}) collective-permute-start(bf16[240,128]{1,0:T(8,128)(2,1)S(1)} %collective-permute-done.1.refs_2_), channel_id=1, source_target_pairs={{0,1},{1,0},{2,3},{3,2},{4,5},{5,4},{6,7},{7,6},{8,9},{9,8},{10,11... | collective-permute-start | bytes 184328 | tf_op jit(solution)/shard_map/ppermute | solution.py:520
  19.0 3.3 %collective-permute-start.10 = (bf16[240,128]{1,0:T(8,128)(2,1)S(1)}, bf16[240,128]{1,0:T(8,128)(2,1)S(1)}, u32[]{:S(2)}, u32[]{:S(2)}) collective-permute-start(bf16[240,128]{1,0:T(8,128)(2,1)S(1)} %collective-permute-done.2.refs_3_), channel_id=1, source_target_pairs={{0,1},{1,0},{2,3},{3,2},{4,5},{5,4},{6,7},{7,6},{8,9},{9,8},{10,11... | collective-permute-start | bytes 184328 | tf_op jit(solution)/shard_map/ppermute | solution.py:520
  21.2 1.2 %collective-permute-start.11 = (bf16[240,128]{1,0:T(8,128)(2,1)S(1)}, bf16[240,128]{1,0:T(8,128)(2,1)S(1)}, u32[]{:S(2)}, u32[]{:S(2)}) collective-permute-start(bf16[240,128]{1,0:T(8,128)(2,1)S(1)} %collective-permute-done.3.refs_4_), channel_id=1, source_target_pairs={{0,1},{1,0},{2,3},{3,2},{4,5},{5,4},{6,7},{7,6},{8,9},{9,8},{10,11... | collective-permute-start | bytes 184328 | tf_op jit(solution)/shard_map/ppermute | solution.py:520
  21.2 1.4 %collective-permute-start.12 = (bf16[240,128]{1,0:T(8,128)(2,1)S(1)}, bf16[240,128]{1,0:T(8,128)(2,1)S(1)}, u32[]{:S(2)}, u32[]{:S(2)}) collective-permute-start(bf16[240,128]{1,0:T(8,128)(2,1)S(1)} %collective-permute-done.4.refs_5_), channel_id=1, source_target_pairs={{0,1},{1,0},{2,3},{3,2},{4,5},{5,4},{6,7},{7,6},{8,9},{9,8},{10,11... | collective-permute-start | bytes 184328 | tf_op jit(solution)/shard_map/ppermute | solution.py:520
  21.8 1.2 %collective-permute-start.13 = (bf16[240,128]{1,0:T(8,128)(2,1)S(1)}, bf16[240,128]{1,0:T(8,128)(2,1)S(1)}, u32[]{:S(2)}, u32[]{:S(2)}) collective-permute-start(bf16[240,128]{1,0:T(8,128)(2,1)S(1)} %collective-permute-done.5.refs_6_), channel_id=1, source_target_pairs={{0,1},{1,0},{2,3},{3,2},{4,5},{5,4},{6,7},{7,6},{8,9},{9,8},{10,11... | collective-permute-start | bytes 184328 | tf_op jit(solution)/shard_map/ppermute | solution.py:520
  21.8 1.3 %collective-permute-start.14 = (bf16[240,128]{1,0:T(8,128)(2,1)S(1)}, bf16[240,128]{1,0:T(8,128)(2,1)S(1)}, u32[]{:S(2)}, u32[]{:S(2)}) collective-permute-start(bf16[240,128]{1,0:T(8,128)(2,1)S(1)} %collective-permute-done.6.refs_7_), channel_id=1, source_target_pairs={{0,1},{1,0},{2,3},{3,2},{4,5},{5,4},{6,7},{7,6},{8,9},{9,8},{10,11... | collective-permute-start | bytes 184328 | tf_op jit(solution)/shard_map/ppermute | solution.py:520
  25.0 11.4 %all-to-all-start = ((bf16[8,64,128]{2,1,0:T(8,128)(2,1)}), bf16[8,64,128]{2,1,0:T(8,128)(2,1)S(1)}, u32[]{:S(2)}, u32[]{:S(2)}) async-start(bf16[8,64,128]{2,1,0:T(8,128)(2,1)} %attend.1), calls=%async_computation | async-start | bytes 262144 | tf_op jit(solution)/shard_map/all_to_all | solution.py:522

commit v14 on v13

--- a/solution.py
+++ b/solution.py
@@ -61,7 +61,7 @@
         packed_ref[3 * token_rows :] = share
     for place, copy in enumerate(copies):
         copy.wait()
-        for m, packed_ref in enumerate(packed_refs):
+        for m, packed_ref in zip(sending_order(heads), packed_refs):
             columns = pl.ds(pl.multiple_of((chip ^ m) * DH, DH), DH)
             packed_ref[place * token_rows : (place + 1) * token_rows] = held[place, :, columns]
 
@@ -89,6 +89,11 @@
     )(*in_hbm(queries, key_tokens, value_tokens, latent))
 
 
+def sending_order(chips):
+    far, near = list(range(chips // 2, chips)), list(range(1, chips // 2))
+    return [0, *far[:2], *near[1:2], *far[2:], *near[2:], *near[:1]]
+
+
 def xor_pairs(distance):
     return [(i, i ^ distance) for i in range(lax.axis_size("seq"))]
 
@@ -102,6 +107,7 @@
     members, token_rows, _ = out_ref.shape
     block = min(4, members)
     chip = lax.axis_index("seq") // 2
+    order = sending_order(members)
     pieces = refs[:-1]
 
     def rows(place, chosen):
@@ -123,7 +129,7 @@
         )
         mixed = (mixed / totals).astype(out_ref.dtype)
         for m in range(block):
-            out_ref[chip ^ (step + m)] = mixed[m * token_rows : (m + 1) * token_rows]
+            out_ref[chip ^ order[step + m]] = mixed[m * token_rows : (m + 1) * token_rows]
 
 
 def attend(own, other, token_rows):
@@ -179,6 +185,7 @@
     *refs,
 ):
     pieces, refs = refs[: 2 * members], refs[2 * members :]
+    order = sending_order(members)
     (
     tile_hbm,
     in_weight_hbm,
@@ -255,7 +262,7 @@
     extra = -(-share_rows * chunks // 16) * 16
     for place, ref in enumerate(pieces):
         lines = ref[ref.shape[0] - extra :].astype(jnp.float32)
-        low = place * share_rows
+        low = (place // members * members + order[place % members]) * share_rows
         for chunk in range(chunks):
             rows_held[low : low + share_rows, chunk * 128 : (chunk + 1) * 128] = lines[
                 chunk * share_rows : (chunk + 1) * share_rows
@@ -512,11 +519,10 @@
     grid_rows = latent.shape[0] * devices // LF
     token_width = 4 * conv_in_weight.shape[3]
     packed = pack_heads(queries, key_tokens, value_tokens, latent, token_width)
-    chips = len(packed)
-    own = list(packed)
-    far, near = list(range(chips // 2, chips)), list(range(1, chips // 2))
-    for m in [*far[:2], *near[1:2], *far[2:], *near[2:], *near[:1]]:
-        own[m] = lax.ppermute(packed[m], "seq", xor_pairs(2 * m))
+    own = [
+        lax.ppermute(piece, "seq", xor_pairs(2 * m)) if m else piece
+        for m, piece in zip(sending_order(len(packed)), packed)
+    ]
     other = [lax.ppermute(piece, "seq", xor_pairs(1)) for piece in own]
     mixed = attend(own, other, queries.shape[0])
     returned = lax.all_to_all(mixed, "seq", 0, 0, axis_index_groups=groups, tiled=True)

time: 37.4 us -> 36.8 us (0.984)
  waiting for transfers between devices: 6.83 us -> 5.75 us
  starting transfers between devices: 17.9 us -> 18.4 us
    all_to_all x1, starting transfers between devices: 3.37 us -> 4.81 us  [on_device(): lax.all_to_all(mixed, 'seq', 0, 0, axis_index_groups=groups, tiled=True)]
    ppermute x7, waiting for transfers between devices: 5.93 us -> 4.84 us  [on_device(): lax.ppermute(piece, 'seq', xor_pairs(2 * m))]
    ppermute x7, starting transfers between devices: 12.5 us -> 11.6 us  [on_device(): lax.ppermute(piece, 'seq', xor_pairs(2 * m))]
  transfers between devices with their start and end apart: 16 -> 16, of which waited for: 6 -> 8; matrix products, arithmetic and copies ran while one was open for 0% -> 0% of each run, Pallas kernels for 21% -> 22%
where the time goes in v14:
time: 36.8 us; the launch traced here: 36.5 us
  starting transfers between devices  18.4 us (50%)
  Pallas kernels  11.6 us (32%)
  waiting for transfers between devices  5.75 us (16%)
  between operations  0.67 us (2%)
    ppermute x7, starting transfers between devices, on_device(): lax.ppermute(piece, 'seq', xor_pairs(2 * m))  11.6 us
    pallas_call x1, Pallas kernels, decode_tile(): pl.pallas_call(functools.partial(decode_body, grid_rows, width, share_row...  7.95 us
    ppermute x7, waiting for transfers between devices, on_device(): lax.ppermute(piece, 'seq', xor_pairs(2 * m))  4.84 us
    all_to_all x1, starting transfers between devices, on_device(): lax.all_to_all(mixed, 'seq', 0, 0, axis_index_groups=groups, tiled=True)  4.81 us
    ppermute x8, starting transfers between devices, on_device(): other = [lax.ppermute(piece, 'seq', xor_pairs(1)) for piece in own]  1.97 us
    pallas_call x1, Pallas kernels, attend(): pl.pallas_call(attend_body, in_specs=[vmem] * (2 * members), out_specs=vm...  1.85 us
    pallas_call x1, Pallas kernels, pack_heads(): pl.pallas_call(pack_body, in_specs=[hbm] * 4, out_specs=[vmem] * heads, o...  1.12 us
    ppermute x8, waiting for transfers between devices, on_device(): other = [lax.ppermute(piece, 'seq', xor_pairs(1)) for piece in own]  0.9 us
  transfers between devices with their start and end apart: 16, of which 8 were waited for; matrix products, arithmetic and copies ran while one was open for 0% of the time, Pallas kernels for 22%

profile of v14, /device:TPU:0, one launch (start us, length us, event | category | flops | bytes accessed | tf_op | source)
XLA Modules:
  0.0 36.5 jit_solution(12409811395065592837)
XLA Ops:
  0.6 1.1 %pack_heads.1 = (bf16[240,128]{1,0:T(8,128)(2,1)S(1)}, bf16[240,128]{1,0:T(8,128)(2,1)S(1)}, bf16[240,128]{1,0:T(8,128)(2,1)S(1)}, bf16[240,128]{1,0:T(8,128)(2,...) custom-call(bf16[64,2048]{1,0:T(8,128)(2,1)} %query_ref.1, ...), custom_call_target="tpu_custom_call" | custom-call | tf_op jit(solution)/shard_map/pack_heads/pallas_call | solution.py:77
  1.8 4.1 %collective-permute-start = (bf16[240,128]{1,0:T(8,128)(2,1)S(1)}, bf16[240,128]{1,0:T(8,128)(2,1)S(1)}, u32[]{:S(2)}, u32[]{:S(2)}) collective-permute-start(bf16[240,128]{1,0:T(8,128)(2,1)S(1)} %get-tuple-element.11), channel_id=1, source_target_pairs={{0,8},{1,9},{2,10},{3,11},{4,12},{5,13},{6,14},{7,15},{8,0},{9,1},... | collective-permute-start | bytes 184328 | tf_op jit(solution)/shard_map/ppermute | solution.py:523
  5.9 1.3 %collective-permute-start.1 = (bf16[240,128]{1,0:T(8,128)(2,1)S(1)}, bf16[240,128]{1,0:T(8,128)(2,1)S(1)}, u32[]{:S(2)}, u32[]{:S(2)}) collective-permute-start(bf16[240,128]{1,0:T(8,128)(2,1)S(1)} %get-tuple-element.12), channel_id=1, source_target_pairs={{0,10},{1,11},{2,8},{3,9},{4,14},{5,15},{6,12},{7,13},{8,2},{9,3},... | collective-permute-start | bytes 184328 | tf_op jit(solution)/shard_map/ppermute | solution.py:523
  7.1 1.6 %collective-permute-start.2 = (bf16[240,128]{1,0:T(8,128)(2,1)S(1)}, bf16[240,128]{1,0:T(8,128)(2,1)S(1)}, u32[]{:S(2)}, u32[]{:S(2)}) collective-permute-start(bf16[240,128]{1,0:T(8,128)(2,1)S(1)} %get-tuple-element.13), channel_id=1, source_target_pairs={{0,4},{1,5},{2,6},{3,7},{4,0},{5,1},{6,2},{7,3},{8,12},{9,13},{10,... | collective-permute-start | bytes 184328 | tf_op jit(solution)/shard_map/ppermute | solution.py:523
  8.7 2.5 %collective-permute-start.3 = (bf16[240,128]{1,0:T(8,128)(2,1)S(1)}, bf16[240,128]{1,0:T(8,128)(2,1)S(1)}, u32[]{:S(2)}, u32[]{:S(2)}) collective-permute-start(bf16[240,128]{1,0:T(8,128)(2,1)S(1)} %get-tuple-element.14), channel_id=1, source_target_pairs={{0,12},{1,13},{2,14},{3,15},{4,8},{5,9},{6,10},{7,11},{8,4},{9,5},... | collective-permute-start | bytes 184328 | tf_op jit(solution)/shard_map/ppermute | solution.py:523
  11.2 1.3 %collective-permute-start.4 = (bf16[240,128]{1,0:T(8,128)(2,1)S(1)}, bf16[240,128]{1,0:T(8,128)(2,1)S(1)}, u32[]{:S(2)}, u32[]{:S(2)}) collective-permute-start(bf16[240,128]{1,0:T(8,128)(2,1)S(1)} %get-tuple-element.15), channel_id=1, source_target_pairs={{0,14},{1,15},{2,12},{3,13},{4,10},{5,11},{6,8},{7,9},{8,6},{9,7},... | collective-permute-start | bytes 184328 | tf_op jit(solution)/shard_map/ppermute | solution.py:523
  12.5 0.0 collective-permute-done.refs_1_
  12.5 0.3 collective-permute-start.5
  12.8 2.2 %collective-permute-done.1.refs_2_ = bf16[240,128]{1,0:T(8,128)(2,1)S(1)} collective-permute-done((bf16[240,128]{1,0:T(8,128)(2,1)S(1)}, bf16[240,128]{1,0:T(8,128)(2,1)S(1)}, u32[]{:S(2)}, u32[]{:S(2)}) %collective-permute-start.1) | collective-permute-done | bytes 61472 | tf_op jit(solution)/shard_map/ppermute | solution.py:523
  15.0 0.6 %collective-permute-start.6 = (bf16[240,128]{1,0:T(8,128)(2,1)S(1)}, bf16[240,128]{1,0:T(8,128)(2,1)S(1)}, u32[]{:S(2)}, u32[]{:S(2)}) collective-permute-start(bf16[240,128]{1,0:T(8,128)(2,1)S(1)} %get-tuple-element.17), channel_id=1, source_target_pairs={{0,2},{1,3},{2,0},{3,1},{4,6},{5,7},{6,4},{7,5},{8,10},{9,11},{10,... | collective-permute-start | bytes 184328 | tf_op jit(solution)/shard_map/ppermute | solution.py:523
  15.6 0.0 collective-permute-done.2.refs_3_
  15.6 0.0 collective-permute-start.7
  15.6 0.5 %collective-permute-start.8 = (bf16[240,128]{1,0:T(8,128)(2,1)S(1)}, bf16[240,128]{1,0:T(8,128)(2,1)S(1)}, u32[]{:S(2)}, u32[]{:S(2)}) collective-permute-start(bf16[240,128]{1,0:T(8,128)(2,1)S(1)} %collective-permute-done.refs_1_), channel_id=1, source_target_pairs={{0,1},{1,0},{2,3},{3,2},{4,5},{5,4},{6,7},{7,6},{8,9},{9,8},{10,11... | collective-permute-start | bytes 184328 | tf_op jit(solution)/shard_map/ppermute | solution.py:526
  16.1 2.1 %collective-permute-done.4.refs_5_ = bf16[240,128]{1,0:T(8,128)(2,1)S(1)} collective-permute-done((bf16[240,128]{1,0:T(8,128)(2,1)S(1)}, bf16[240,128]{1,0:T(8,128)(2,1)S(1)}, u32[]{:S(2)}, u32[]{:S(2)}) %collective-permute-start.4) | collective-permute-done | bytes 61472 | tf_op jit(solution)/shard_map/ppermute | solution.py:523
  18.2 0.0 collective-permute-start.9
  18.2 0.1 collective-permute-done.5.refs_6_
  18.3 0.4 %collective-permute-start.10 = (bf16[240,128]{1,0:T(8,128)(2,1)S(1)}, bf16[240,128]{1,0:T(8,128)(2,1)S(1)}, u32[]{:S(2)}, u32[]{:S(2)}) collective-permute-start(bf16[240,128]{1,0:T(8,128)(2,1)S(1)} %collective-permute-done.2.refs_3_), channel_id=1, source_target_pairs={{0,1},{1,0},{2,3},{3,2},{4,5},{5,4},{6,7},{7,6},{8,9},{9,8},{10,11... | collective-permute-start | bytes 184328 | tf_op jit(solution)/shard_map/ppermute | solution.py:526
  18.7 0.5 %collective-permute-done.6.refs_7_ = bf16[240,128]{1,0:T(8,128)(2,1)S(1)} collective-permute-done((bf16[240,128]{1,0:T(8,128)(2,1)S(1)}, bf16[240,128]{1,0:T(8,128)(2,1)S(1)}, u32[]{:S(2)}, u32[]{:S(2)}) %collective-permute-start.6) | collective-permute-done | bytes 61472 | tf_op jit(solution)/shard_map/ppermute | solution.py:523
  19.2 0.0 collective-permute-start.11
  19.2 0.5 %collective-permute-start.12 = (bf16[240,128]{1,0:T(8,128)(2,1)S(1)}, bf16[240,128]{1,0:T(8,128)(2,1)S(1)}, u32[]{:S(2)}, u32[]{:S(2)}) collective-permute-start(bf16[240,128]{1,0:T(8,128)(2,1)S(1)} %collective-permute-done.4.refs_5_), channel_id=1, source_target_pairs={{0,1},{1,0},{2,3},{3,2},{4,5},{5,4},{6,7},{7,6},{8,9},{9,8},{10,11... | collective-permute-start | bytes 184328 | tf_op jit(solution)/shard_map/ppermute | solution.py:526
  19.7 0.1 collective-permute-start.13
  19.8 0.0 collective-permute-done.9.refs_10_
  19.8 0.4 %collective-permute-start.14 = (bf16[240,128]{1,0:T(8,128)(2,1)S(1)}, bf16[240,128]{1,0:T(8,128)(2,1)S(1)}, u32[]{:S(2)}, u32[]{:S(2)}) collective-permute-start(bf16[240,128]{1,0:T(8,128)(2,1)S(1)} %collective-permute-done.6.refs_7_), channel_id=1, source_target_pairs={{0,1},{1,0},{2,3},{3,2},{4,5},{5,4},{6,7},{7,6},{8,9},{9,8},{10,11... | collective-permute-start | bytes 184328 | tf_op jit(solution)/shard_map/ppermute | solution.py:526
  20.2 0.2 collective-permute-done.11.refs_12_
  20.4 0.2 collective-permute-done.12.refs_13_
  20.6 0.4 collective-permute-done.13.refs_14_
  21.0 0.2 collective-permute-done.14.refs_15_
  21.1 1.9 %attend.1 = bf16[8,64,128]{2,1,0:T(8,128)(2,1)} custom-call(bf16[240,128]{1,0:T(8,128)(2,1)S(1)} %get-tuple-element.10.refs_0_, bf16[240,128]{1,0:T(8,128)(2,1)S(1)} %collective-permute-done.refs_1_, bf16[240,128]{1,0:T(8,128)(2,1)S(1)} %collective-permute-done.1.refs_2_, bf16[240,128]{1,0:T(8,128)(2,1)S(1)} %collective-permute-done.2.refs_3_, ...), custom_call_target="tpu_custom_call" | custom-call | flops 268435456 | bytes 917504 | tf_op jit(solution)/shard_map/attend/pallas_call | solution.py:139
  23.0 4.8 %all-to-all-start = ((bf16[8,64,128]{2,1,0:T(8,128)(2,1)}), bf16[8,64,128]{2,1,0:T(8,128)(2,1)S(1)}, u32[]{:S(2)}, u32[]{:S(2)}) async-start(bf16[8,64,128]{2,1,0:T(8,128)(2,1)} %attend.1), calls=%async_computation | async-start | bytes 262144 | tf_op jit(solution)/shard_map/all_to_all | solution.py:528
  27.8 7.9 %decode_tile.1 = bf16[2,8,40,384]{3,2,1,0:T(8,128)(2,1)} custom-call(bf16[240,128]{1,0:T(8,128)(2,1)S(1)} %get-tuple-element.10.refs_0_, bf16[240,128]{1,0:T(8,128)(2,1)S(1)} %collective-permute-done.refs_1_, bf16[240,128]{1,0:T(8,128)(2,1)S(1)} %collective-permute-done.1.refs_2_, bf16[240,128]{1,0:T(8,128)(2,1)S(1)} %collective-permute-done.2.refs_3_, ...), custom_call_target="tpu_custom_call" | custom-call | flops 2548039680 | bytes 5308416 | tf_op jit(solution)/shard_map/decode_tile/pallas_call | solution.py:464
  35.7 0.0 all-to-all-done.in_ref
  35.8 0.7 %unpack_heads.1 = bf16[64,1024]{1,0:T(8,128)(2,1)} custom-call(bf16[8,64,128]{2,1,0:T(8,128)(2,1)S(1)} %all-to-all-done.in_ref), custom_call_target="tpu_custom_call" | custom-call | tf_op jit(solution)/shard_map/unpack_heads/pallas_call | solution.py:169
  (4 shorter events, 0.0 us)
Async XLA Ops:
  1.8 10.7 %collective-permute-start = (bf16[240,128]{1,0:T(8,128)(2,1)S(1)}, bf16[240,128]{1,0:T(8,128)(2,1)S(1)}, u32[]{:S(2)}, u32[]{:S(2)}) collective-permute-start(bf16[240,128]{1,0:T(8,128)(2,1)S(1)} %get-tuple-element.11), channel_id=1, source_target_pairs={{0,8},{1,9},{2,10},{3,11},{4,12},{5,13},{6,14},{7,15},{8,0},{9,1},... | collective-permute-start | bytes 184328 | tf_op jit(solution)/shard_map/ppermute | solution.py:523
  5.9 9.1 %collective-permute-start.1 = (bf16[240,128]{1,0:T(8,128)(2,1)S(1)}, bf16[240,128]{1,0:T(8,128)(2,1)S(1)}, u32[]{:S(2)}, u32[]{:S(2)}) collective-permute-start(bf16[240,128]{1,0:T(8,128)(2,1)S(1)} %get-tuple-element.12), channel_id=1, source_target_pairs={{0,10},{1,11},{2,8},{3,9},{4,14},{5,15},{6,12},{7,13},{8,2},{9,3},... | collective-permute-start | bytes 184328 | tf_op jit(solution)/shard_map/ppermute | solution.py:523
  7.1 8.5 %collective-permute-start.2 = (bf16[240,128]{1,0:T(8,128)(2,1)S(1)}, bf16[240,128]{1,0:T(8,128)(2,1)S(1)}, u32[]{:S(2)}, u32[]{:S(2)}) collective-permute-start(bf16[240,128]{1,0:T(8,128)(2,1)S(1)} %get-tuple-element.13), channel_id=1, source_target_pairs={{0,4},{1,5},{2,6},{3,7},{4,0},{5,1},{6,2},{7,3},{8,12},{9,13},{10,... | collective-permute-start | bytes 184328 | tf_op jit(solution)/shard_map/ppermute | solution.py:523
  8.7 6.9 %collective-permute-start.3 = (bf16[240,128]{1,0:T(8,128)(2,1)S(1)}, bf16[240,128]{1,0:T(8,128)(2,1)S(1)}, u32[]{:S(2)}, u32[]{:S(2)}) collective-permute-start(bf16[240,128]{1,0:T(8,128)(2,1)S(1)} %get-tuple-element.14), channel_id=1, source_target_pairs={{0,12},{1,13},{2,14},{3,15},{4,8},{5,9},{6,10},{7,11},{8,4},{9,5},... | collective-permute-start | bytes 184328 | tf_op jit(solution)/shard_map/ppermute | solution.py:523
  11.2 7.0 %collective-permute-start.4 = (bf16[240,128]{1,0:T(8,128)(2,1)S(1)}, bf16[240,128]{1,0:T(8,128)(2,1)S(1)}, u32[]{:S(2)}, u32[]{:S(2)}) collective-permute-start(bf16[240,128]{1,0:T(8,128)(2,1)S(1)} %get-tuple-element.15), channel_id=1, source_target_pairs={{0,14},{1,15},{2,12},{3,13},{4,10},{5,11},{6,8},{7,9},{8,6},{9,7},... | collective-permute-start | bytes 184328 | tf_op jit(solution)/shard_map/ppermute | solution.py:523
  12.5 5.8 %collective-permute-start.5 = (bf16[240,128]{1,0:T(8,128)(2,1)S(1)}, bf16[240,128]{1,0:T(8,128)(2,1)S(1)}, u32[]{:S(2)}, u32[]{:S(2)}) collective-permute-start(bf16[240,128]{1,0:T(8,128)(2,1)S(1)} %get-tuple-element.16), channel_id=1, source_target_pairs={{0,6},{1,7},{2,4},{3,5},{4,2},{5,3},{6,0},{7,1},{8,14},{9,15},{10,... | collective-permute-start | bytes 184328 | tf_op jit(solution)/shard_map/ppermute | solution.py:523
  15.0 4.2 %collective-permute-start.6 = (bf16[240,128]{1,0:T(8,128)(2,1)S(1)}, bf16[240,128]{1,0:T(8,128)(2,1)S(1)}, u32[]{:S(2)}, u32[]{:S(2)}) collective-permute-start(bf16[240,128]{1,0:T(8,128)(2,1)S(1)} %get-tuple-element.17), channel_id=1, source_target_pairs={{0,2},{1,3},{2,0},{3,1},{4,6},{5,7},{6,4},{7,5},{8,10},{9,11},{10,... | collective-permute-start | bytes 184328 | tf_op jit(solution)/shard_map/ppermute | solution.py:523
  15.6 3.6 %collective-permute-start.7 = (bf16[240,128]{1,0:T(8,128)(2,1)S(1)}, bf16[240,128]{1,0:T(8,128)(2,1)S(1)}, u32[]{:S(2)}, u32[]{:S(2)}) collective-permute-start(bf16[240,128]{1,0:T(8,128)(2,1)S(1)} %get-tuple-element.10.refs_0_), channel_id=1, source_target_pairs={{0,1},{1,0},{2,3},{3,2},{4,5},{5,4},{6,7},{7,6},{8,9},{9,8},{10,11... | collective-permute-start | bytes 184328 | tf_op jit(solution)/shard_map/ppermute | solution.py:526
  15.6 4.1 %collective-permute-start.8 = (bf16[240,128]{1,0:T(8,128)(2,1)S(1)}, bf16[240,128]{1,0:T(8,128)(2,1)S(1)}, u32[]{:S(2)}, u32[]{:S(2)}) collective-permute-start(bf16[240,128]{1,0:T(8,128)(2,1)S(1)} %collective-permute-done.refs_1_), channel_id=1, source_target_pairs={{0,1},{1,0},{2,3},{3,2},{4,5},{5,4},{6,7},{7,6},{8,9},{9,8},{10,11... | collective-permute-start | bytes 184328 | tf_op jit(solution)/shard_map/ppermute | solution.py:526
  18.2 1.6 %collective-permute-start.9 = (bf16[240,128]{1,0:T(8,128)(2,1)S(1)}, bf16[240,128]{1,0:T(8,128)(2,1)S(1)}, u32[]{:S(2)}, u32[]{:S(2)}) collective-permute-start(bf16[240,128]{1,0:T(8,128)(2,1)S(1)} %collective-permute-done.1.refs_2_), channel_id=1, source_target_pairs={{0,1},{1,0},{2,3},{3,2},{4,5},{5,4},{6,7},{7,6},{8,9},{9,8},{10,11... | collective-permute-start | bytes 184328 | tf_op jit(solution)/shard_map/ppermute | solution.py:526
  18.3 2.0 %collective-permute-start.10 = (bf16[240,128]{1,0:T(8,128)(2,1)S(1)}, bf16[240,128]{1,0:T(8,128)(2,1)S(1)}, u32[]{:S(2)}, u32[]{:S(2)}) collective-permute-start(bf16[240,128]{1,0:T(8,128)(2,1)S(1)} %collective-permute-done.2.refs_3_), channel_id=1, source_target_pairs={{0,1},{1,0},{2,3},{3,2},{4,5},{5,4},{6,7},{7,6},{8,9},{9,8},{10,11... | collective-permute-start | bytes 184328 | tf_op jit(solution)/shard_map/ppermute | solution.py:526
  19.2 1.2 %collective-permute-start.11 = (bf16[240,128]{1,0:T(8,128)(2,1)S(1)}, bf16[240,128]{1,0:T(8,128)(2,1)S(1)}, u32[]{:S(2)}, u32[]{:S(2)}) collective-permute-start(bf16[240,128]{1,0:T(8,128)(2,1)S(1)} %collective-permute-done.3.refs_4_), channel_id=1, source_target_pairs={{0,1},{1,0},{2,3},{3,2},{4,5},{5,4},{6,7},{7,6},{8,9},{9,8},{10,11... | collective-permute-start | bytes 184328 | tf_op jit(solution)/shard_map/ppermute | solution.py:526
  19.2 1.4 %collective-permute-start.12 = (bf16[240,128]{1,0:T(8,128)(2,1)S(1)}, bf16[240,128]{1,0:T(8,128)(2,1)S(1)}, u32[]{:S(2)}, u32[]{:S(2)}) collective-permute-start(bf16[240,128]{1,0:T(8,128)(2,1)S(1)} %collective-permute-done.4.refs_5_), channel_id=1, source_target_pairs={{0,1},{1,0},{2,3},{3,2},{4,5},{5,4},{6,7},{7,6},{8,9},{9,8},{10,11... | collective-permute-start | bytes 184328 | tf_op jit(solution)/shard_map/ppermute | solution.py:526
  19.7 1.2 %collective-permute-start.13 = (bf16[240,128]{1,0:T(8,128)(2,1)S(1)}, bf16[240,128]{1,0:T(8,128)(2,1)S(1)}, u32[]{:S(2)}, u32[]{:S(2)}) collective-permute-start(bf16[240,128]{1,0:T(8,128)(2,1)S(1)} %collective-permute-done.5.refs_6_), channel_id=1, source_target_pairs={{0,1},{1,0},{2,3},{3,2},{4,5},{5,4},{6,7},{7,6},{8,9},{9,8},{10,11... | collective-permute-start | bytes 184328 | tf_op jit(solution)/shard_map/ppermute | solution.py:526
  19.8 1.3 %collective-permute-start.14 = (bf16[240,128]{1,0:T(8,128)(2,1)S(1)}, bf16[240,128]{1,0:T(8,128)(2,1)S(1)}, u32[]{:S(2)}, u32[]{:S(2)}) collective-permute-start(bf16[240,128]{1,0:T(8,128)(2,1)S(1)} %collective-permute-done.6.refs_7_), channel_id=1, source_target_pairs={{0,1},{1,0},{2,3},{3,2},{4,5},{5,4},{6,7},{7,6},{8,9},{9,8},{10,11... | collective-permute-start | bytes 184328 | tf_op jit(solution)/shard_map/ppermute | solution.py:526
  23.0 12.8 %all-to-all-start = ((bf16[8,64,128]{2,1,0:T(8,128)(2,1)}), bf16[8,64,128]{2,1,0:T(8,128)(2,1)S(1)}, u32[]{:S(2)}, u32[]{:S(2)}) async-start(bf16[8,64,128]{2,1,0:T(8,128)(2,1)} %attend.1), calls=%async_computation | async-start | bytes 262144 | tf_op jit(solution)/shard_map/all_to_all | solution.py:528

commit v15 on v14

--- a/solution.py
+++ b/solution.py
@@ -98,26 +98,53 @@
     return [(i, i ^ distance) for i in range(lax.axis_size("seq"))]
 
 
+def join_body(count, *refs):
+    out_ref = refs[-1]
+    for place, ref in enumerate(refs[:count]):
+        out_ref[place] = ref[ref.shape[0] - out_ref.shape[1] :]
+
+
+def join(pieces, earlier, skipped):
+    rows, width = pieces[0].shape
+    vmem = pl.BlockSpec(memory_space=pltpu.VMEM)
+    return pl.pallas_call(
+        functools.partial(join_body, len(pieces)),
+        in_specs=[vmem] * len(pieces) + [pl.BlockSpec(memory_space=pl.ANY)] * len(earlier),
+        out_specs=vmem,
+        out_shape=jax.ShapeDtypeStruct((len(pieces), rows - skipped, width), pieces[0].dtype),
+        compiler_params=pltpu.CompilerParams(vmem_limit_bytes=COPY_VMEM),
+        name="join",
+    )(*pieces, *earlier)
+
+
 def flat(array):
     return array.reshape(-1, array.shape[-1])
 
 
 def attend_body(*refs):
-    out_ref = refs[-1]
+    out_hbm, out_ref, sems = refs[-3:]
     members, token_rows, _ = out_ref.shape
     block = min(4, members)
     chip = lax.axis_index("seq") // 2
     order = sending_order(members)
-    pieces = refs[:-1]
+    own, other = refs[:members], refs[members:-3]
 
     def rows(place, chosen):
         at = slice(place * token_rows, (place + 1) * token_rows)
         return jnp.concatenate([ref[at] for ref in chosen], axis=0)
 
-    keys, values = rows(1, pieces), rows(2, pieces)
+    def both(place):
+        at = slice((place - 1) * token_rows, place * token_rows)
+        return jnp.concatenate([rows(place, own)] + [flat(ref[:, at]) for ref in other], axis=0)
+
+    def leave(m):
+        target = out_hbm.at[chip ^ order[m]]
+        return pltpu.make_async_copy(out_ref.at[m], target, sems.at[m])
+
+    keys, values = both(1), both(2)
     for step in range(0, members, block):
         scores = lax.dot_general(
-            rows(0, pieces[step : step + block]),
+            rows(0, own[step : step + block]),
             keys,
             (((1,), (1,)), ((), ())),
             preferred_element_type=jnp.float32,
@@ -129,7 +156,10 @@
         )
         mixed = (mixed / totals).astype(out_ref.dtype)
         for m in range(block):
-            out_ref[chip ^ order[step + m]] = mixed[m * token_rows : (m + 1) * token_rows]
+            out_ref[step + m] = mixed[m * token_rows : (m + 1) * token_rows]
+            leave(step + m).start()
+    for m in range(members):
+        leave(m).wait()
 
 
 def attend(own, other, token_rows):
@@ -138,9 +168,13 @@
     vmem = pl.BlockSpec(memory_space=pltpu.VMEM)
     return pl.pallas_call(
         attend_body,
-        in_specs=[vmem] * (2 * members),
-        out_specs=vmem,
+        in_specs=[vmem] * (members + len(other)),
+        out_specs=pl.BlockSpec(memory_space=pltpu.HBM),
         out_shape=jax.ShapeDtypeStruct((members, token_rows, DH), own[0].dtype),
+        scratch_shapes=[
+            pltpu.VMEM((members, token_rows, DH), own[0].dtype),
+            pltpu.SemaphoreType.DMA((members,)),
+        ],
         compiler_params=pltpu.CompilerParams(vmem_limit_bytes=ATTEND_VMEM),
         cost_estimate=pl.CostEstimate(
             flops=8 * total * total * DH,
@@ -182,9 +216,10 @@
     width,
     share_rows,
     members,
+    halves,
     *refs,
 ):
-    pieces, refs = refs[: 2 * members], refs[2 * members :]
+    own, other, refs = refs[:members], refs[members : members + halves], refs[members + halves :]
     order = sending_order(members)
     (
     tile_hbm,
@@ -260,8 +295,10 @@
 
     chunks = rows_held.shape[1] // 128
     extra = -(-share_rows * chunks // 16) * 16
-    for place, ref in enumerate(pieces):
-        lines = ref[ref.shape[0] - extra :].astype(jnp.float32)
+    shares = [ref[ref.shape[0] - extra :] for ref in own]
+    shares += [ref[m, ref.shape[1] - extra :] for ref in other for m in range(ref.shape[0])]
+    for place, share in enumerate(shares):
+        lines = share.astype(jnp.float32)
         low = (place // members * members + order[place % members]) * share_rows
         for chunk in range(chunks):
             rows_held[low : low + share_rows, chunk * 128 : (chunk + 1) * 128] = lines[
@@ -462,8 +499,8 @@
     depth = slots * 2 * 4 * token_width
     held = chunks * 4 * UNITS
     return pl.pallas_call(
-        functools.partial(decode_body, grid_rows, width, share_rows, len(own)),
-        in_specs=[vmem] * (2 * len(own)) + [hbm] * 6,
+        functools.partial(decode_body, grid_rows, width, share_rows, len(own), len(other)),
+        in_specs=[vmem] * (len(own) + len(other)) + [hbm] * 6,
         out_specs=hbm,
         out_shape=jax.ShapeDtypeStruct((LF, ROWS, columns, features), jnp.bfloat16),
         scratch_shapes=[
@@ -523,7 +560,10 @@
         lax.ppermute(piece, "seq", xor_pairs(2 * m)) if m else piece
         for m, piece in zip(sending_order(len(packed)), packed)
     ]
-    other = [lax.ppermute(piece, "seq", xor_pairs(1)) for piece in own]
+    half, other = len(own) // 2, []
+    for low in (0, half):
+        joined = join(own[low : low + half], other[-1:], queries.shape[0])
+        other.append(lax.ppermute(joined, "seq", xor_pairs(1)))
     mixed = attend(own, other, queries.shape[0])
     returned = lax.all_to_all(mixed, "seq", 0, 0, axis_index_groups=groups, tiled=True)
     frames = decode_tile(

time: 36.8 us -> 41 us (1.11)
  waiting for transfers between devices: 5.75 us -> 11.3 us
  starting transfers between devices: 18.4 us -> 17.1 us
    ppermute x7, waiting for transfers between devices: 4.84 us -> 9.84 us  [on_device(): lax.ppermute(piece, 'seq', xor_pairs(2 * m))]
    ppermute x8 -> x2, starting transfers between devices: 1.97 us -> 0.14 us  [on_device(): other.append(lax.ppermute(joined, 'seq', xor_pairs(1)))]
    ppermute x7, starting transfers between devices: 11.6 us -> 12.3 us  [on_device(): lax.ppermute(piece, 'seq', xor_pairs(2 * m))]
    ppermute x8 -> x2, waiting for transfers between devices: 0.9 us -> 1.41 us  [on_device(): other.append(lax.ppermute(joined, 'seq', xor_pairs(1)))]
    pallas_call x1 -> x3, Pallas kernels: 1.85 us -> 1.89 us  [the longest x1 1.86 us: attend(): pl.pallas_call(attend_body, in_specs=[vmem] * (members + len(other)), out...]
  transfers between devices with their start and end apart: 16 -> 10, of which waited for: 8 -> 4; matrix products, arithmetic and copies ran while one was open for 0% -> 0% of each run, Pallas kernels for 22% -> 19%
where the time goes in v15:
time: 41 us; the launch traced here: 40.8 us
  starting transfers between devices  17.1 us (42%)
  Pallas kernels  11.7 us (29%)
  waiting for transfers between devices  11.3 us (28%)
  between operations  0.7 us (2%)
    ppermute x7, starting transfers between devices, on_device(): lax.ppermute(piece, 'seq', xor_pairs(2 * m))  12.3 us
    ppermute x7, waiting for transfers between devices, on_device(): lax.ppermute(piece, 'seq', xor_pairs(2 * m))  9.84 us
    pallas_call x1, Pallas kernels, decode_tile(): pl.pallas_call(functools.partial(decode_body, grid_rows, width, share_row...  7.95 us
    all_to_all x1, starting transfers between devices, on_device(): lax.all_to_all(mixed, 'seq', 0, 0, axis_index_groups=groups, tiled=True)  4.69 us
    pallas_call x1, Pallas kernels, attend(): pl.pallas_call(attend_body, in_specs=[vmem] * (members + len(other)), out...  1.86 us
    ppermute x2, waiting for transfers between devices, on_device(): other.append(lax.ppermute(joined, 'seq', xor_pairs(1)))  1.41 us
    pallas_call x1, Pallas kernels, pack_heads(): pl.pallas_call(pack_body, in_specs=[hbm] * 4, out_specs=[vmem] * heads, o...  1.12 us
  transfers between devices with their start and end apart: 10, of which 4 were waited for; matrix products, arithmetic and copies ran while one was open for 0% of the time, Pallas kernels for 19%

profile of v15, /device:TPU:0, one launch (start us, length us, event | category | flops | bytes accessed | tf_op | source)
XLA Modules:
  0.0 40.8 jit_solution(10056597722329916531)
XLA Ops:
  0.6 1.1 %pack_heads.1 = (bf16[240,128]{1,0:T(8,128)(2,1)S(1)}, bf16[240,128]{1,0:T(8,128)(2,1)S(1)}, bf16[240,128]{1,0:T(8,128)(2,1)S(1)}, bf16[240,128]{1,0:T(8,128)(2,...) custom-call(bf16[64,2048]{1,0:T(8,128)(2,1)} %query_ref.1, ...), custom_call_target="tpu_custom_call" | custom-call | tf_op jit(solution)/shard_map/pack_heads/pallas_call | solution.py:77
  1.8 4.1 %collective-permute-start = (bf16[240,128]{1,0:T(8,128)(2,1)S(1)}, bf16[240,128]{1,0:T(8,128)(2,1)S(1)}, u32[]{:S(2)}, u32[]{:S(2)}) collective-permute-start(bf16[240,128]{1,0:T(8,128)(2,1)S(1)} %get-tuple-element.11), channel_id=1, source_target_pairs={{0,8},{1,9},{2,10},{3,11},{4,12},{5,13},{6,14},{7,15},{8,0},{9,1},... | collective-permute-start | bytes 184328 | tf_op jit(solution)/shard_map/ppermute | solution.py:560
  5.9 1.3 %collective-permute-start.1 = (bf16[240,128]{1,0:T(8,128)(2,1)S(1)}, bf16[240,128]{1,0:T(8,128)(2,1)S(1)}, u32[]{:S(2)}, u32[]{:S(2)}) collective-permute-start(bf16[240,128]{1,0:T(8,128)(2,1)S(1)} %get-tuple-element.12), channel_id=1, source_target_pairs={{0,10},{1,11},{2,8},{3,9},{4,14},{5,15},{6,12},{7,13},{8,2},{9,3},... | collective-permute-start | bytes 184328 | tf_op jit(solution)/shard_map/ppermute | solution.py:560
  7.1 1.6 %collective-permute-start.2 = (bf16[240,128]{1,0:T(8,128)(2,1)S(1)}, bf16[240,128]{1,0:T(8,128)(2,1)S(1)}, u32[]{:S(2)}, u32[]{:S(2)}) collective-permute-start(bf16[240,128]{1,0:T(8,128)(2,1)S(1)} %get-tuple-element.13), channel_id=1, source_target_pairs={{0,4},{1,5},{2,6},{3,7},{4,0},{5,1},{6,2},{7,3},{8,12},{9,13},{10,... | collective-permute-start | bytes 184328 | tf_op jit(solution)/shard_map/ppermute | solution.py:560
  8.7 0.0 collective-permute-done.refs_1_
  8.7 4.4 %collective-permute-done.1.refs_2_ = bf16[240,128]{1,0:T(8,128)(2,1)S(1)} collective-permute-done((bf16[240,128]{1,0:T(8,128)(2,1)S(1)}, bf16[240,128]{1,0:T(8,128)(2,1)S(1)}, u32[]{:S(2)}, u32[]{:S(2)}) %collective-permute-start.1) | collective-permute-done | bytes 61472 | tf_op jit(solution)/shard_map/ppermute | solution.py:560
  13.1 0.0 collective-permute-done.2.refs_3_
  13.2 0.1 collective-permute-start.7
  13.2 3.3 %collective-permute-start.3 = (bf16[240,128]{1,0:T(8,128)(2,1)S(1)}, bf16[240,128]{1,0:T(8,128)(2,1)S(1)}, u32[]{:S(2)}, u32[]{:S(2)}) collective-permute-start(bf16[240,128]{1,0:T(8,128)(2,1)S(1)} %get-tuple-element.14), channel_id=1, source_target_pairs={{0,12},{1,13},{2,14},{3,15},{4,8},{5,9},{6,10},{7,11},{8,4},{9,5},... | collective-permute-start | bytes 184328 | tf_op jit(solution)/shard_map/ppermute | solution.py:560
  16.6 0.6 %collective-permute-start.4 = (bf16[240,128]{1,0:T(8,128)(2,1)S(1)}, bf16[240,128]{1,0:T(8,128)(2,1)S(1)}, u32[]{:S(2)}, u32[]{:S(2)}) collective-permute-start(bf16[240,128]{1,0:T(8,128)(2,1)S(1)} %get-tuple-element.15), channel_id=1, source_target_pairs={{0,14},{1,15},{2,12},{3,13},{4,10},{5,11},{6,8},{7,9},{8,6},{9,7},... | collective-permute-start | bytes 184328 | tf_op jit(solution)/shard_map/ppermute | solution.py:560
  17.1 0.0 collective-permute-start.5
  17.1 1.5 %collective-permute-start.6 = (bf16[240,128]{1,0:T(8,128)(2,1)S(1)}, bf16[240,128]{1,0:T(8,128)(2,1)S(1)}, u32[]{:S(2)}, u32[]{:S(2)}) collective-permute-start(bf16[240,128]{1,0:T(8,128)(2,1)S(1)} %get-tuple-element.17), channel_id=1, source_target_pairs={{0,2},{1,3},{2,0},{3,1},{4,6},{5,7},{6,4},{7,5},{8,10},{9,11},{10,... | collective-permute-start | bytes 184328 | tf_op jit(solution)/shard_map/ppermute | solution.py:560
  18.6 1.0 %collective-permute-done.3.refs_0_.refs_4_ = bf16[240,128]{1,0:T(8,128)(2,1)S(1)} collective-permute-done((bf16[240,128]{1,0:T(8,128)(2,1)S(1)}, bf16[240,128]{1,0:T(8,128)(2,1)S(1)}, u32[]{:S(2)}, u32[]{:S(2)}) %collective-permute-start.3) | collective-permute-done | bytes 61472 | tf_op jit(solution)/shard_map/ppermute | solution.py:560
  19.6 4.4 %collective-permute-done.4.refs_1_.refs_5_ = bf16[240,128]{1,0:T(8,128)(2,1)S(1)} collective-permute-done((bf16[240,128]{1,0:T(8,128)(2,1)S(1)}, bf16[240,128]{1,0:T(8,128)(2,1)S(1)}, u32[]{:S(2)}, u32[]{:S(2)}) %collective-permute-start.4) | collective-permute-done | bytes 61472 | tf_op jit(solution)/shard_map/ppermute | solution.py:560
  24.0 0.0 collective-permute-done.5.refs_2_.refs_6_
  24.0 0.0 collective-permute-done.6.refs_3_.refs_7_
  24.0 0.0 collective-permute-done.7.refs_4_.refs_8_
  24.0 0.1 collective-permute-start.8
  24.1 1.4 %collective-permute-done.8.refs_9_ = bf16[4,176,128]{2,1,0:T(8,128)(2,1)S(1)} collective-permute-done((bf16[4,176,128]{2,1,0:T(8,128)(2,1)S(1)}, bf16[4,176,128]{2,1,0:T(8,128)(2,1)S(1)}, u32[]{:S(2)}, u32[]{:S(2)}) %collective-permute-start.8) | collective-permute-done | bytes 180256 | tf_op jit(solution)/shard_map/ppermute | solution.py:566
  25.5 1.9 %attend.1 = bf16[8,64,128]{2,1,0:T(8,128)(2,1)} custom-call(bf16[240,128]{1,0:T(8,128)(2,1)S(1)} %get-tuple-element.10.refs_0_, bf16[240,128]{1,0:T(8,128)(2,1)S(1)} %collective-permute-done.refs_1_, bf16[240,128]{1,0:T(8,128)(2,1)S(1)} %collective-permute-done.1.refs_2_, bf16[240,128]{1,0:T(8,128)(2,1)S(1)} %collective-permute-done.2.refs_3_, ...), custom_call_target="tpu_custom_call" | custom-call | flops 268435456 | bytes 917504 | tf_op jit(solution)/shard_map/attend/pallas_call | solution.py:169
  27.4 4.7 %all-to-all-start = ((bf16[8,64,128]{2,1,0:T(8,128)(2,1)}), bf16[8,64,128]{2,1,0:T(8,128)(2,1)S(1)}, u32[]{:S(2)}, u32[]{:S(2)}) async-start(bf16[8,64,128]{2,1,0:T(8,128)(2,1)} %attend.1), calls=%async_computation | async-start | bytes 262144 | tf_op jit(solution)/shard_map/all_to_all | solution.py:568
  32.1 7.9 %decode_tile.1 = bf16[2,8,40,384]{3,2,1,0:T(8,128)(2,1)} custom-call(bf16[240,128]{1,0:T(8,128)(2,1)S(1)} %get-tuple-element.10.refs_0_, bf16[240,128]{1,0:T(8,128)(2,1)S(1)} %collective-permute-done.refs_1_, bf16[240,128]{1,0:T(8,128)(2,1)S(1)} %collective-permute-done.1.refs_2_, bf16[240,128]{1,0:T(8,128)(2,1)S(1)} %collective-permute-done.2.refs_3_, ...), custom_call_target="tpu_custom_call" | custom-call | flops 2548039680 | bytes 5308416 | tf_op jit(solution)/shard_map/decode_tile/pallas_call | solution.py:501
  40.0 0.0 all-to-all-done.in_ref
  40.0 0.7 %unpack_heads.1 = bf16[64,1024]{1,0:T(8,128)(2,1)} custom-call(bf16[8,64,128]{2,1,0:T(8,128)(2,1)S(1)} %all-to-all-done.in_ref), custom_call_target="tpu_custom_call" | custom-call | tf_op jit(solution)/shard_map/unpack_heads/pallas_call | solution.py:203
  (2 shorter events, 0.0 us)
Async XLA Ops:
  1.8 7.0 %collective-permute-start = (bf16[240,128]{1,0:T(8,128)(2,1)S(1)}, bf16[240,128]{1,0:T(8,128)(2,1)S(1)}, u32[]{:S(2)}, u32[]{:S(2)}) collective-permute-start(bf16[240,128]{1,0:T(8,128)(2,1)S(1)} %get-tuple-element.11), channel_id=1, source_target_pairs={{0,8},{1,9},{2,10},{3,11},{4,12},{5,13},{6,14},{7,15},{8,0},{9,1},... | collective-permute-start | bytes 184328 | tf_op jit(solution)/shard_map/ppermute | solution.py:560
  5.9 7.3 %collective-permute-start.1 = (bf16[240,128]{1,0:T(8,128)(2,1)S(1)}, bf16[240,128]{1,0:T(8,128)(2,1)S(1)}, u32[]{:S(2)}, u32[]{:S(2)}) collective-permute-start(bf16[240,128]{1,0:T(8,128)(2,1)S(1)} %get-tuple-element.12), channel_id=1, source_target_pairs={{0,10},{1,11},{2,8},{3,9},{4,14},{5,15},{6,12},{7,13},{8,2},{9,3},... | collective-permute-start | bytes 184328 | tf_op jit(solution)/shard_map/ppermute | solution.py:560
  7.1 6.0 %collective-permute-start.2 = (bf16[240,128]{1,0:T(8,128)(2,1)S(1)}, bf16[240,128]{1,0:T(8,128)(2,1)S(1)}, u32[]{:S(2)}, u32[]{:S(2)}) collective-permute-start(bf16[240,128]{1,0:T(8,128)(2,1)S(1)} %get-tuple-element.13), channel_id=1, source_target_pairs={{0,4},{1,5},{2,6},{3,7},{4,0},{5,1},{6,2},{7,3},{8,12},{9,13},{10,... | collective-permute-start | bytes 184328 | tf_op jit(solution)/shard_map/ppermute | solution.py:560
  13.2 10.8 %collective-permute-start.7 = (bf16[4,176,128]{2,1,0:T(8,128)(2,1)S(1)}, bf16[4,176,128]{2,1,0:T(8,128)(2,1)S(1)}, u32[]{:S(2)}, u32[]{:S(2)}) collective-permute-start(bf16[4,176,128]{2,1,0:T(8,128)(2,1)S(1)} %join.2), channel_id=1, source_target_pairs={{0,1},{1,0},{2,3},{3,2},{4,5},{5,4},{6,7},{7,6},{8,9},{9,8},{10,11... | collective-permute-start | bytes 540680 | tf_op jit(solution)/shard_map/ppermute | solution.py:566
  13.2 6.3 %collective-permute-start.3 = (bf16[240,128]{1,0:T(8,128)(2,1)S(1)}, bf16[240,128]{1,0:T(8,128)(2,1)S(1)}, u32[]{:S(2)}, u32[]{:S(2)}) collective-permute-start(bf16[240,128]{1,0:T(8,128)(2,1)S(1)} %get-tuple-element.14), channel_id=1, source_target_pairs={{0,12},{1,13},{2,14},{3,15},{4,8},{5,9},{6,10},{7,11},{8,4},{9,5},... | collective-permute-start | bytes 184328 | tf_op jit(solution)/shard_map/ppermute | solution.py:560
  16.6 7.4 %collective-permute-start.4 = (bf16[240,128]{1,0:T(8,128)(2,1)S(1)}, bf16[240,128]{1,0:T(8,128)(2,1)S(1)}, u32[]{:S(2)}, u32[]{:S(2)}) collective-permute-start(bf16[240,128]{1,0:T(8,128)(2,1)S(1)} %get-tuple-element.15), channel_id=1, source_target_pairs={{0,14},{1,15},{2,12},{3,13},{4,10},{5,11},{6,8},{7,9},{8,6},{9,7},... | collective-permute-start | bytes 184328 | tf_op jit(solution)/shard_map/ppermute | solution.py:560
  17.1 6.9 %collective-permute-start.5 = (bf16[240,128]{1,0:T(8,128)(2,1)S(1)}, bf16[240,128]{1,0:T(8,128)(2,1)S(1)}, u32[]{:S(2)}, u32[]{:S(2)}) collective-permute-start(bf16[240,128]{1,0:T(8,128)(2,1)S(1)} %get-tuple-element.16), channel_id=1, source_target_pairs={{0,6},{1,7},{2,4},{3,5},{4,2},{5,3},{6,0},{7,1},{8,14},{9,15},{10,... | collective-permute-start | bytes 184328 | tf_op jit(solution)/shard_map/ppermute | solution.py:560
  17.1 6.9 %collective-permute-start.6 = (bf16[240,128]{1,0:T(8,128)(2,1)S(1)}, bf16[240,128]{1,0:T(8,128)(2,1)S(1)}, u32[]{:S(2)}, u32[]{:S(2)}) collective-permute-start(bf16[240,128]{1,0:T(8,128)(2,1)S(1)} %get-tuple-element.17), channel_id=1, source_target_pairs={{0,2},{1,3},{2,0},{3,1},{4,6},{5,7},{6,4},{7,5},{8,10},{9,11},{10,... | collective-permute-start | bytes 184328 | tf_op jit(solution)/shard_map/ppermute | solution.py:560
  24.0 1.5 %collective-permute-start.8 = (bf16[4,176,128]{2,1,0:T(8,128)(2,1)S(1)}, bf16[4,176,128]{2,1,0:T(8,128)(2,1)S(1)}, u32[]{:S(2)}, u32[]{:S(2)}) collective-permute-start(bf16[4,176,128]{2,1,0:T(8,128)(2,1)S(1)} %join.3), channel_id=1, source_target_pairs={{0,1},{1,0},{2,3},{3,2},{4,5},{5,4},{6,7},{7,6},{8,9},{9,8},{10,11... | collective-permute-start | bytes 540680 | tf_op jit(solution)/shard_map/ppermute | solution.py:566
  27.4 12.6 %all-to-all-start = ((bf16[8,64,128]{2,1,0:T(8,128)(2,1)}), bf16[8,64,128]{2,1,0:T(8,128)(2,1)S(1)}, u32[]{:S(2)}, u32[]{:S(2)}) async-start(bf16[8,64,128]{2,1,0:T(8,128)(2,1)} %attend.1), calls=%async_computation | async-start | bytes 262144 | tf_op jit(solution)/shard_map/all_to_all | solution.py:568

commit v16 on v15

--- a/solution.py
+++ b/solution.py
@@ -98,23 +98,23 @@
     return [(i, i ^ distance) for i in range(lax.axis_size("seq"))]
 
 
-def join_body(count, *refs):
+def join_body(*refs):
     out_ref = refs[-1]
-    for place, ref in enumerate(refs[:count]):
+    for place, ref in enumerate(refs[:-1]):
         out_ref[place] = ref[ref.shape[0] - out_ref.shape[1] :]
 
 
-def join(pieces, earlier, skipped):
+def join(pieces, skipped):
     rows, width = pieces[0].shape
     vmem = pl.BlockSpec(memory_space=pltpu.VMEM)
     return pl.pallas_call(
-        functools.partial(join_body, len(pieces)),
-        in_specs=[vmem] * len(pieces) + [pl.BlockSpec(memory_space=pl.ANY)] * len(earlier),
+        join_body,
+        in_specs=[vmem] * len(pieces),
         out_specs=vmem,
         out_shape=jax.ShapeDtypeStruct((len(pieces), rows - skipped, width), pieces[0].dtype),
         compiler_params=pltpu.CompilerParams(vmem_limit_bytes=COPY_VMEM),
         name="join",
-    )(*pieces, *earlier)
+    )(*pieces)
 
 
 def flat(array):
@@ -560,10 +560,8 @@
         lax.ppermute(piece, "seq", xor_pairs(2 * m)) if m else piece
         for m, piece in zip(sending_order(len(packed)), packed)
     ]
-    half, other = len(own) // 2, []
-    for low in (0, half):
-        joined = join(own[low : low + half], other[-1:], queries.shape[0])
-        other.append(lax.ppermute(joined, "seq", xor_pairs(1)))
+    joined = join(own, queries.shape[0])
+    other = [lax.ppermute(joined, "seq", xor_pairs(1))]
     mixed = attend(own, other, queries.shape[0])
     returned = lax.all_to_all(mixed, "seq", 0, 0, axis_index_groups=groups, tiled=True)
     frames = decode_tile(

time: 41 us -> 36.6 us (0.89)
  waiting for transfers between devices: 11.3 us -> 7.46 us
  starting transfers between devices: 17.1 us -> 16.5 us
    ppermute x7, waiting for transfers between devices: 9.84 us -> 5.8 us  [on_device(): lax.ppermute(piece, 'seq', xor_pairs(2 * m))]
    ppermute x7, starting transfers between devices: 12.3 us -> 11.6 us  [on_device(): lax.ppermute(piece, 'seq', xor_pairs(2 * m))]
    ppermute x2 -> x1, waiting for transfers between devices: 1.41 us -> 1.66 us  [on_device(): other = [lax.ppermute(joined, 'seq', xor_pairs(1))]]
  transfers between devices with their start and end apart: 10 -> 9, of which waited for: 4 -> 5; matrix products, arithmetic and copies ran while one was open for 0% -> 0% of each run, Pallas kernels for 19% -> 22%
where the time goes in v16:
time: 36.6 us; the launch traced here: 36.3 us
  starting transfers between devices  16.5 us (45%)
  Pallas kernels  11.7 us (32%)
  waiting for transfers between devices  7.46 us (20%)
  between operations  0.68 us (2%)
    ppermute x7, starting transfers between devices, on_device(): lax.ppermute(piece, 'seq', xor_pairs(2 * m))  11.6 us
    pallas_call x1, Pallas kernels, decode_tile(): pl.pallas_call(functools.partial(decode_body, grid_rows, width, share_row...  7.95 us
    ppermute x7, waiting for transfers between devices, on_device(): lax.ppermute(piece, 'seq', xor_pairs(2 * m))  5.8 us
    all_to_all x1, starting transfers between devices, on_device(): lax.all_to_all(mixed, 'seq', 0, 0, axis_index_groups=groups, tiled=True)  4.82 us
    pallas_call x1, Pallas kernels, attend(): pl.pallas_call(attend_body, in_specs=[vmem] * (members + len(other)), out...  1.86 us
    ppermute x1, waiting for transfers between devices, on_device(): other = [lax.ppermute(joined, 'seq', xor_pairs(1))]  1.66 us
    pallas_call x1, Pallas kernels, pack_heads(): pl.pallas_call(pack_body, in_specs=[hbm] * 4, out_specs=[vmem] * heads, o...  1.12 us
  transfers between devices with their start and end apart: 9, of which 5 were waited for; matrix products, arithmetic and copies ran while one was open for 0% of the time, Pallas kernels for 22%

profile of v16, /device:TPU:0, one launch (start us, length us, event | category | flops | bytes accessed | tf_op | source)
XLA Modules:
  0.0 36.3 jit_solution(11205541407870829082)
XLA Ops:
  0.6 1.1 %pack_heads.1 = (bf16[240,128]{1,0:T(8,128)(2,1)S(1)}, bf16[240,128]{1,0:T(8,128)(2,1)S(1)}, bf16[240,128]{1,0:T(8,128)(2,1)S(1)}, bf16[240,128]{1,0:T(8,128)(2,...) custom-call(bf16[64,2048]{1,0:T(8,128)(2,1)} %query_ref.1, ...), custom_call_target="tpu_custom_call" | custom-call | tf_op jit(solution)/shard_map/pack_heads/pallas_call | solution.py:77
  1.8 4.1 %collective-permute-start = (bf16[240,128]{1,0:T(8,128)(2,1)S(1)}, bf16[240,128]{1,0:T(8,128)(2,1)S(1)}, u32[]{:S(2)}, u32[]{:S(2)}) collective-permute-start(bf16[240,128]{1,0:T(8,128)(2,1)S(1)} %get-tuple-element.11), channel_id=1, source_target_pairs={{0,8},{1,9},{2,10},{3,11},{4,12},{5,13},{6,14},{7,15},{8,0},{9,1},... | collective-permute-start | bytes 184328 | tf_op jit(solution)/shard_map/ppermute | solution.py:560
  5.9 1.3 %collective-permute-start.1 = (bf16[240,128]{1,0:T(8,128)(2,1)S(1)}, bf16[240,128]{1,0:T(8,128)(2,1)S(1)}, u32[]{:S(2)}, u32[]{:S(2)}) collective-permute-start(bf16[240,128]{1,0:T(8,128)(2,1)S(1)} %get-tuple-element.12), channel_id=1, source_target_pairs={{0,10},{1,11},{2,8},{3,9},{4,14},{5,15},{6,12},{7,13},{8,2},{9,3},... | collective-permute-start | bytes 184328 | tf_op jit(solution)/shard_map/ppermute | solution.py:560
  7.1 1.6 %collective-permute-start.2 = (bf16[240,128]{1,0:T(8,128)(2,1)S(1)}, bf16[240,128]{1,0:T(8,128)(2,1)S(1)}, u32[]{:S(2)}, u32[]{:S(2)}) collective-permute-start(bf16[240,128]{1,0:T(8,128)(2,1)S(1)} %get-tuple-element.13), channel_id=1, source_target_pairs={{0,4},{1,5},{2,6},{3,7},{4,0},{5,1},{6,2},{7,3},{8,12},{9,13},{10,... | collective-permute-start | bytes 184328 | tf_op jit(solution)/shard_map/ppermute | solution.py:560
  8.7 2.5 %collective-permute-start.3 = (bf16[240,128]{1,0:T(8,128)(2,1)S(1)}, bf16[240,128]{1,0:T(8,128)(2,1)S(1)}, u32[]{:S(2)}, u32[]{:S(2)}) collective-permute-start(bf16[240,128]{1,0:T(8,128)(2,1)S(1)} %get-tuple-element.14), channel_id=1, source_target_pairs={{0,12},{1,13},{2,14},{3,15},{4,8},{5,9},{6,10},{7,11},{8,4},{9,5},... | collective-permute-start | bytes 184328 | tf_op jit(solution)/shard_map/ppermute | solution.py:560
  11.2 1.3 %collective-permute-start.4 = (bf16[240,128]{1,0:T(8,128)(2,1)S(1)}, bf16[240,128]{1,0:T(8,128)(2,1)S(1)}, u32[]{:S(2)}, u32[]{:S(2)}) collective-permute-start(bf16[240,128]{1,0:T(8,128)(2,1)S(1)} %get-tuple-element.15), channel_id=1, source_target_pairs={{0,14},{1,15},{2,12},{3,13},{4,10},{5,11},{6,8},{7,9},{8,6},{9,7},... | collective-permute-start | bytes 184328 | tf_op jit(solution)/shard_map/ppermute | solution.py:560
  12.5 0.0 collective-permute-done.refs_1_
  12.5 0.3 collective-permute-start.5
  12.8 2.2 %collective-permute-done.1.refs_2_ = bf16[240,128]{1,0:T(8,128)(2,1)S(1)} collective-permute-done((bf16[240,128]{1,0:T(8,128)(2,1)S(1)}, bf16[240,128]{1,0:T(8,128)(2,1)S(1)}, u32[]{:S(2)}, u32[]{:S(2)}) %collective-permute-start.1) | collective-permute-done | bytes 61472 | tf_op jit(solution)/shard_map/ppermute | solution.py:560
  15.0 0.6 %collective-permute-start.6 = (bf16[240,128]{1,0:T(8,128)(2,1)S(1)}, bf16[240,128]{1,0:T(8,128)(2,1)S(1)}, u32[]{:S(2)}, u32[]{:S(2)}) collective-permute-start(bf16[240,128]{1,0:T(8,128)(2,1)S(1)} %get-tuple-element.17), channel_id=1, source_target_pairs={{0,2},{1,3},{2,0},{3,1},{4,6},{5,7},{6,4},{7,5},{8,10},{9,11},{10,... | collective-permute-start | bytes 184328 | tf_op jit(solution)/shard_map/ppermute | solution.py:560
  15.6 0.0 collective-permute-done.2.refs_3_
  15.6 0.0 collective-permute-done.3.refs_4_
  15.6 2.6 %collective-permute-done.4.refs_5_ = bf16[240,128]{1,0:T(8,128)(2,1)S(1)} collective-permute-done((bf16[240,128]{1,0:T(8,128)(2,1)S(1)}, bf16[240,128]{1,0:T(8,128)(2,1)S(1)}, u32[]{:S(2)}, u32[]{:S(2)}) %collective-permute-start.4) | collective-permute-done | bytes 61472 | tf_op jit(solution)/shard_map/ppermute | solution.py:560
  18.2 0.1 collective-permute-done.5.refs_6_
  18.3 0.9 %collective-permute-done.6.refs_7_ = bf16[240,128]{1,0:T(8,128)(2,1)S(1)} collective-permute-done((bf16[240,128]{1,0:T(8,128)(2,1)S(1)}, bf16[240,128]{1,0:T(8,128)(2,1)S(1)}, u32[]{:S(2)}, u32[]{:S(2)}) %collective-permute-start.6) | collective-permute-done | bytes 61472 | tf_op jit(solution)/shard_map/ppermute | solution.py:560
  19.2 0.1 collective-permute-start.7
  19.3 1.7 %collective-permute-done.7.refs_8_ = bf16[8,176,128]{2,1,0:T(8,128)(2,1)S(1)} collective-permute-done((bf16[8,176,128]{2,1,0:T(8,128)(2,1)S(1)}, bf16[8,176,128]{2,1,0:T(8,128)(2,1)S(1)}, u32[]{:S(2)}, u32[]{:S(2)}) %collective-permute-start.7) | collective-permute-done | bytes 360480 | tf_op jit(solution)/shard_map/ppermute | solution.py:564
  21.0 1.9 %attend.1 = bf16[8,64,128]{2,1,0:T(8,128)(2,1)} custom-call(bf16[240,128]{1,0:T(8,128)(2,1)S(1)} %get-tuple-element.10.refs_0_, bf16[240,128]{1,0:T(8,128)(2,1)S(1)} %collective-permute-done.refs_1_, bf16[240,128]{1,0:T(8,128)(2,1)S(1)} %collective-permute-done.1.refs_2_, bf16[240,128]{1,0:T(8,128)(2,1)S(1)} %collective-permute-done.2.refs_3_, ...), custom_call_target="tpu_custom_call" | custom-call | flops 268435456 | bytes 917504 | tf_op jit(solution)/shard_map/attend/pallas_call | solution.py:169
  22.8 4.8 %all-to-all-start = ((bf16[8,64,128]{2,1,0:T(8,128)(2,1)}), bf16[8,64,128]{2,1,0:T(8,128)(2,1)S(1)}, u32[]{:S(2)}, u32[]{:S(2)}) async-start(bf16[8,64,128]{2,1,0:T(8,128)(2,1)} %attend.1), calls=%async_computation | async-start | bytes 262144 | tf_op jit(solution)/shard_map/all_to_all | solution.py:566
  27.6 7.9 %decode_tile.1 = bf16[2,8,40,384]{3,2,1,0:T(8,128)(2,1)} custom-call(bf16[240,128]{1,0:T(8,128)(2,1)S(1)} %get-tuple-element.10.refs_0_, bf16[240,128]{1,0:T(8,128)(2,1)S(1)} %collective-permute-done.refs_1_, bf16[240,128]{1,0:T(8,128)(2,1)S(1)} %collective-permute-done.1.refs_2_, bf16[240,128]{1,0:T(8,128)(2,1)S(1)} %collective-permute-done.2.refs_3_, ...), custom_call_target="tpu_custom_call" | custom-call | flops 2548039680 | bytes 5308416 | tf_op jit(solution)/shard_map/decode_tile/pallas_call | solution.py:501
  35.6 0.0 all-to-all-done.in_ref
  35.6 0.7 %unpack_heads.1 = bf16[64,1024]{1,0:T(8,128)(2,1)} custom-call(bf16[8,64,128]{2,1,0:T(8,128)(2,1)S(1)} %all-to-all-done.in_ref), custom_call_target="tpu_custom_call" | custom-call | tf_op jit(solution)/shard_map/unpack_heads/pallas_call | solution.py:203
  (1 shorter events, 0.0 us)
Async XLA Ops:
  1.8 10.7 %collective-permute-start = (bf16[240,128]{1,0:T(8,128)(2,1)S(1)}, bf16[240,128]{1,0:T(8,128)(2,1)S(1)}, u32[]{:S(2)}, u32[]{:S(2)}) collective-permute-start(bf16[240,128]{1,0:T(8,128)(2,1)S(1)} %get-tuple-element.11), channel_id=1, source_target_pairs={{0,8},{1,9},{2,10},{3,11},{4,12},{5,13},{6,14},{7,15},{8,0},{9,1},... | collective-permute-start | bytes 184328 | tf_op jit(solution)/shard_map/ppermute | solution.py:560
  5.9 9.1 %collective-permute-start.1 = (bf16[240,128]{1,0:T(8,128)(2,1)S(1)}, bf16[240,128]{1,0:T(8,128)(2,1)S(1)}, u32[]{:S(2)}, u32[]{:S(2)}) collective-permute-start(bf16[240,128]{1,0:T(8,128)(2,1)S(1)} %get-tuple-element.12), channel_id=1, source_target_pairs={{0,10},{1,11},{2,8},{3,9},{4,14},{5,15},{6,12},{7,13},{8,2},{9,3},... | collective-permute-start | bytes 184328 | tf_op jit(solution)/shard_map/ppermute | solution.py:560
  7.1 8.5 %collective-permute-start.2 = (bf16[240,128]{1,0:T(8,128)(2,1)S(1)}, bf16[240,128]{1,0:T(8,128)(2,1)S(1)}, u32[]{:S(2)}, u32[]{:S(2)}) collective-permute-start(bf16[240,128]{1,0:T(8,128)(2,1)S(1)} %get-tuple-element.13), channel_id=1, source_target_pairs={{0,4},{1,5},{2,6},{3,7},{4,0},{5,1},{6,2},{7,3},{8,12},{9,13},{10,... | collective-permute-start | bytes 184328 | tf_op jit(solution)/shard_map/ppermute | solution.py:560
  8.7 6.9 %collective-permute-start.3 = (bf16[240,128]{1,0:T(8,128)(2,1)S(1)}, bf16[240,128]{1,0:T(8,128)(2,1)S(1)}, u32[]{:S(2)}, u32[]{:S(2)}) collective-permute-start(bf16[240,128]{1,0:T(8,128)(2,1)S(1)} %get-tuple-element.14), channel_id=1, source_target_pairs={{0,12},{1,13},{2,14},{3,15},{4,8},{5,9},{6,10},{7,11},{8,4},{9,5},... | collective-permute-start | bytes 184328 | tf_op jit(solution)/shard_map/ppermute | solution.py:560
  11.2 7.0 %collective-permute-start.4 = (bf16[240,128]{1,0:T(8,128)(2,1)S(1)}, bf16[240,128]{1,0:T(8,128)(2,1)S(1)}, u32[]{:S(2)}, u32[]{:S(2)}) collective-permute-start(bf16[240,128]{1,0:T(8,128)(2,1)S(1)} %get-tuple-element.15), channel_id=1, source_target_pairs={{0,14},{1,15},{2,12},{3,13},{4,10},{5,11},{6,8},{7,9},{8,6},{9,7},... | collective-permute-start | bytes 184328 | tf_op jit(solution)/shard_map/ppermute | solution.py:560
  12.5 5.8 %collective-permute-start.5 = (bf16[240,128]{1,0:T(8,128)(2,1)S(1)}, bf16[240,128]{1,0:T(8,128)(2,1)S(1)}, u32[]{:S(2)}, u32[]{:S(2)}) collective-permute-start(bf16[240,128]{1,0:T(8,128)(2,1)S(1)} %get-tuple-element.16), channel_id=1, source_target_pairs={{0,6},{1,7},{2,4},{3,5},{4,2},{5,3},{6,0},{7,1},{8,14},{9,15},{10,... | collective-permute-start | bytes 184328 | tf_op jit(solution)/shard_map/ppermute | solution.py:560
  15.0 4.2 %collective-permute-start.6 = (bf16[240,128]{1,0:T(8,128)(2,1)S(1)}, bf16[240,128]{1,0:T(8,128)(2,1)S(1)}, u32[]{:S(2)}, u32[]{:S(2)}) collective-permute-start(bf16[240,128]{1,0:T(8,128)(2,1)S(1)} %get-tuple-element.17), channel_id=1, source_target_pairs={{0,2},{1,3},{2,0},{3,1},{4,6},{5,7},{6,4},{7,5},{8,10},{9,11},{10,... | collective-permute-start | bytes 184328 | tf_op jit(solution)/shard_map/ppermute | solution.py:560
  19.2 1.7 %collective-permute-start.7 = (bf16[8,176,128]{2,1,0:T(8,128)(2,1)S(1)}, bf16[8,176,128]{2,1,0:T(8,128)(2,1)S(1)}, u32[]{:S(2)}, u32[]{:S(2)}) collective-permute-start(bf16[8,176,128]{2,1,0:T(8,128)(2,1)S(1)} %join.1), channel_id=1, source_target_pairs={{0,1},{1,0},{2,3},{3,2},{4,5},{5,4},{6,7},{7,6},{8,9},{9,8},{10,11... | collective-permute-start | bytes 1081352 | tf_op jit(solution)/shard_map/ppermute | solution.py:564
  22.8 12.8 %all-to-all-start = ((bf16[8,64,128]{2,1,0:T(8,128)(2,1)}), bf16[8,64,128]{2,1,0:T(8,128)(2,1)S(1)}, u32[]{:S(2)}, u32[]{:S(2)}) async-start(bf16[8,64,128]{2,1,0:T(8,128)(2,1)} %attend.1), calls=%async_computation | async-start | bytes 262144 | tf_op jit(solution)/shard_map/all_to_all | solution.py:566

commit v17 on v16

--- a/solution.py
+++ b/solution.py
@@ -121,40 +121,60 @@
     return array.reshape(-1, array.shape[-1])
 
 
+def softmax_part(query, keys, values):
+    scores = lax.dot_general(
+        query, keys, (((1,), (1,)), ((), ())), preferred_element_type=jnp.float32
+    ) * (1.0 / math.sqrt(DH))
+    largest = jnp.max(scores, axis=1, keepdims=True)
+    exponents = jnp.exp(scores - largest)
+    totals = jnp.sum(exponents, axis=1, keepdims=True)
+    mixed = jnp.dot(exponents.astype(jnp.bfloat16), values, preferred_element_type=jnp.float32)
+    return largest, totals, mixed
+
+
+def piece_rows(place, token_rows, pieces):
+    at = slice(place * token_rows, (place + 1) * token_rows)
+    return jnp.concatenate([ref[at] for ref in pieces], axis=0)
+
+
+def attend_own_body(token_rows, *refs):
+    pieces, (mixed_ref, stats_ref) = refs[:-2], refs[-2:]
+    block = min(4, len(pieces))
+    keys = piece_rows(1, token_rows, pieces)
+    values = piece_rows(2, token_rows, pieces)
+    for step in range(0, len(pieces), block):
+        query = piece_rows(0, token_rows, pieces[step : step + block])
+        largest, totals, mixed = softmax_part(query, keys, values)
+        at = slice(step * token_rows, (step + block) * token_rows)
+        mixed_ref[at] = mixed
+        stats_ref[0, at] = jnp.broadcast_to(largest, mixed.shape)
+        stats_ref[1, at] = jnp.broadcast_to(totals, mixed.shape)
+
+
 def attend_body(*refs):
-    out_hbm, out_ref, sems = refs[-3:]
+    other_ref, mixed_ref, stats_ref, out_hbm, out_ref, sems = refs[-6:]
+    pieces = refs[:-6]
     members, token_rows, _ = out_ref.shape
     block = min(4, members)
     chip = lax.axis_index("seq") // 2
     order = sending_order(members)
-    own, other = refs[:members], refs[members:-3]
-
-    def rows(place, chosen):
-        at = slice(place * token_rows, (place + 1) * token_rows)
-        return jnp.concatenate([ref[at] for ref in chosen], axis=0)
-
-    def both(place):
-        at = slice((place - 1) * token_rows, place * token_rows)
-        return jnp.concatenate([rows(place, own)] + [flat(ref[:, at]) for ref in other], axis=0)
 
     def leave(m):
         target = out_hbm.at[chip ^ order[m]]
         return pltpu.make_async_copy(out_ref.at[m], target, sems.at[m])
 
-    keys, values = both(1), both(2)
+    keys = flat(other_ref[:, :token_rows])
+    values = flat(other_ref[:, token_rows : 2 * token_rows])
     for step in range(0, members, block):
-        scores = lax.dot_general(
-            rows(0, own[step : step + block]),
-            keys,
-            (((1,), (1,)), ((), ())),
-            preferred_element_type=jnp.float32,
-        ) * (1.0 / math.sqrt(DH))
-        exponents = jnp.exp(scores - jnp.max(scores, axis=1, keepdims=True))
-        totals = jnp.sum(exponents, axis=1, keepdims=True)
-        mixed = jnp.dot(
-            exponents.astype(jnp.bfloat16), values, preferred_element_type=jnp.float32
-        )
-        mixed = (mixed / totals).astype(out_ref.dtype)
+        query = piece_rows(0, token_rows, pieces[step : step + block])
+        largest, totals, mixed = softmax_part(query, keys, values)
+        at = slice(step * token_rows, (step + block) * token_rows)
+        earlier = stats_ref[0, at]
+        top = jnp.maximum(earlier, largest)
+        before, now = jnp.exp(earlier - top), jnp.exp(largest - top)
+        totals = stats_ref[1, at] * before + totals * now
+        mixed = (mixed_ref[at] * before + mixed * now) / totals
+        mixed = mixed.astype(out_ref.dtype)
         for m in range(block):
             out_ref[step + m] = mixed[m * token_rows : (m + 1) * token_rows]
             leave(step + m).start()
@@ -166,23 +186,37 @@
     members = len(own)
     total = members * token_rows
     vmem = pl.BlockSpec(memory_space=pltpu.VMEM)
+    params = pltpu.CompilerParams(vmem_limit_bytes=ATTEND_VMEM)
+    cost = pl.CostEstimate(
+        flops=4 * total * total * DH,
+        bytes_accessed=7 * total * DH * 2,
+        transcendentals=total * total,
+    )
+    mixed, stats = pl.pallas_call(
+        functools.partial(attend_own_body, token_rows),
+        in_specs=[vmem] * members,
+        out_specs=[vmem] * 2,
+        out_shape=[
+            jax.ShapeDtypeStruct((total, DH), jnp.float32),
+            jax.ShapeDtypeStruct((2, total, DH), jnp.float32),
+        ],
+        compiler_params=params,
+        cost_estimate=cost,
+        name="attend_own",
+    )(*own)
     return pl.pallas_call(
         attend_body,
-        in_specs=[vmem] * (members + len(other)),
+        in_specs=[vmem] * (members + 3),
         out_specs=pl.BlockSpec(memory_space=pltpu.HBM),
         out_shape=jax.ShapeDtypeStruct((members, token_rows, DH), own[0].dtype),
         scratch_shapes=[
             pltpu.VMEM((members, token_rows, DH), own[0].dtype),
             pltpu.SemaphoreType.DMA((members,)),
         ],
-        compiler_params=pltpu.CompilerParams(vmem_limit_bytes=ATTEND_VMEM),
-        cost_estimate=pl.CostEstimate(
-            flops=8 * total * total * DH,
-            bytes_accessed=7 * total * DH * 2,
-            transcendentals=2 * total * total,
-        ),
+        compiler_params=params,
+        cost_estimate=cost,
         name="attend",
-    )(*own, *other)
+    )(*own, other, mixed, stats)
 
 
 def unpack_body(in_ref, out_ref, sems):
@@ -562,7 +596,7 @@
     ]
     joined = join(own, queries.shape[0])
     other = [lax.ppermute(joined, "seq", xor_pairs(1))]
-    mixed = attend(own, other, queries.shape[0])
+    mixed = attend(own, other[0], queries.shape[0])
     returned = lax.all_to_all(mixed, "seq", 0, 0, axis_index_groups=groups, tiled=True)
     frames = decode_tile(
         own,

time: 36.6 us -> 36.2 us (0.989)
  waiting for transfers between devices: 7.46 us -> 6.66 us
  Pallas kernels: 11.7 us -> 12.1 us
    ppermute x1, waiting for transfers between devices: 1.66 us -> 0.86 us  [on_device(): other = [lax.ppermute(joined, 'seq', xor_pairs(1))]]
    pallas_call x1 -> x2, Pallas kernels: 1.86 us -> 2.28 us  [the longest x1 1.49 us: attend(): pl.pallas_call(attend_body, in_specs=[vmem] * (members + 3), out_specs=pl...]
  transfers between devices with their start and end apart: 9 -> 9, of which waited for: 5 -> 5; matrix products, arithmetic and copies ran while one was open for 0% -> 0% of each run, Pallas kernels for 22% -> 24%
where the time goes in v17:
time: 36.2 us; the launch traced here: 36 us
  starting transfers between devices  16.5 us (46%)
  Pallas kernels  12.1 us (33%)
  waiting for transfers between devices  6.66 us (18%)
  between operations  0.69 us (2%)
    ppermute x7, starting transfers between devices, on_device(): lax.ppermute(piece, 'seq', xor_pairs(2 * m))  11.6 us
    pallas_call x1, Pallas kernels, decode_tile(): pl.pallas_call(functools.partial(decode_body, grid_rows, width, share_row...  7.95 us
    ppermute x7, waiting for transfers between devices, on_device(): lax.ppermute(piece, 'seq', xor_pairs(2 * m))  5.8 us
    all_to_all x1, starting transfers between devices, on_device(): lax.all_to_all(mixed, 'seq', 0, 0, axis_index_groups=groups, tiled=True)  4.82 us
    pallas_call x1, Pallas kernels, attend(): pl.pallas_call(attend_body, in_specs=[vmem] * (members + 3), out_specs=pl...  1.49 us
    pallas_call x1, Pallas kernels, pack_heads(): pl.pallas_call(pack_body, in_specs=[hbm] * 4, out_specs=[vmem] * heads, o...  1.12 us
    ppermute x1, waiting for transfers between devices, on_device(): other = [lax.ppermute(joined, 'seq', xor_pairs(1))]  0.86 us
    pallas_call x1, Pallas kernels, attend(): pl.pallas_call(functools.partial(attend_own_body, token_rows), in_specs=[...  0.79 us
  transfers between devices with their start and end apart: 9, of which 5 were waited for; matrix products, arithmetic and copies ran while one was open for 0% of the time, Pallas kernels for 24%

profile of v17, /device:TPU:0, one launch (start us, length us, event | category | flops | bytes accessed | tf_op | source)
XLA Modules:
  0.0 36.0 jit_solution(5881894939778678998)
XLA Ops:
  0.6 1.1 %pack_heads.1 = (bf16[240,128]{1,0:T(8,128)(2,1)S(1)}, bf16[240,128]{1,0:T(8,128)(2,1)S(1)}, bf16[240,128]{1,0:T(8,128)(2,1)S(1)}, bf16[240,128]{1,0:T(8,128)(2,...) custom-call(bf16[64,2048]{1,0:T(8,128)(2,1)} %query_ref.1, ...), custom_call_target="tpu_custom_call" | custom-call | tf_op jit(solution)/shard_map/pack_heads/pallas_call | solution.py:77
  1.8 4.1 %collective-permute-start = (bf16[240,128]{1,0:T(8,128)(2,1)S(1)}, bf16[240,128]{1,0:T(8,128)(2,1)S(1)}, u32[]{:S(2)}, u32[]{:S(2)}) collective-permute-start(bf16[240,128]{1,0:T(8,128)(2,1)S(1)} %get-tuple-element.13), channel_id=1, source_target_pairs={{0,8},{1,9},{2,10},{3,11},{4,12},{5,13},{6,14},{7,15},{8,0},{9,1},... | collective-permute-start | bytes 184328 | tf_op jit(solution)/shard_map/ppermute | solution.py:594
  5.9 1.3 %collective-permute-start.1 = (bf16[240,128]{1,0:T(8,128)(2,1)S(1)}, bf16[240,128]{1,0:T(8,128)(2,1)S(1)}, u32[]{:S(2)}, u32[]{:S(2)}) collective-permute-start(bf16[240,128]{1,0:T(8,128)(2,1)S(1)} %get-tuple-element.14), channel_id=1, source_target_pairs={{0,10},{1,11},{2,8},{3,9},{4,14},{5,15},{6,12},{7,13},{8,2},{9,3},... | collective-permute-start | bytes 184328 | tf_op jit(solution)/shard_map/ppermute | solution.py:594
  7.1 1.6 %collective-permute-start.2 = (bf16[240,128]{1,0:T(8,128)(2,1)S(1)}, bf16[240,128]{1,0:T(8,128)(2,1)S(1)}, u32[]{:S(2)}, u32[]{:S(2)}) collective-permute-start(bf16[240,128]{1,0:T(8,128)(2,1)S(1)} %get-tuple-element.15), channel_id=1, source_target_pairs={{0,4},{1,5},{2,6},{3,7},{4,0},{5,1},{6,2},{7,3},{8,12},{9,13},{10,... | collective-permute-start | bytes 184328 | tf_op jit(solution)/shard_map/ppermute | solution.py:594
  8.7 2.5 %collective-permute-start.3 = (bf16[240,128]{1,0:T(8,128)(2,1)S(1)}, bf16[240,128]{1,0:T(8,128)(2,1)S(1)}, u32[]{:S(2)}, u32[]{:S(2)}) collective-permute-start(bf16[240,128]{1,0:T(8,128)(2,1)S(1)} %get-tuple-element.16), channel_id=1, source_target_pairs={{0,12},{1,13},{2,14},{3,15},{4,8},{5,9},{6,10},{7,11},{8,4},{9,5},... | collective-permute-start | bytes 184328 | tf_op jit(solution)/shard_map/ppermute | solution.py:594
  11.2 1.3 %collective-permute-start.4 = (bf16[240,128]{1,0:T(8,128)(2,1)S(1)}, bf16[240,128]{1,0:T(8,128)(2,1)S(1)}, u32[]{:S(2)}, u32[]{:S(2)}) collective-permute-start(bf16[240,128]{1,0:T(8,128)(2,1)S(1)} %get-tuple-element.17), channel_id=1, source_target_pairs={{0,14},{1,15},{2,12},{3,13},{4,10},{5,11},{6,8},{7,9},{8,6},{9,7},... | collective-permute-start | bytes 184328 | tf_op jit(solution)/shard_map/ppermute | solution.py:594
  12.5 0.0 collective-permute-done.refs_1_
  12.5 0.3 collective-permute-start.5
  12.8 2.2 %collective-permute-done.1.refs_2_ = bf16[240,128]{1,0:T(8,128)(2,1)S(1)} collective-permute-done((bf16[240,128]{1,0:T(8,128)(2,1)S(1)}, bf16[240,128]{1,0:T(8,128)(2,1)S(1)}, u32[]{:S(2)}, u32[]{:S(2)}) %collective-permute-start.1) | collective-permute-done | bytes 61472 | tf_op jit(solution)/shard_map/ppermute | solution.py:594
  15.0 0.6 %collective-permute-start.6 = (bf16[240,128]{1,0:T(8,128)(2,1)S(1)}, bf16[240,128]{1,0:T(8,128)(2,1)S(1)}, u32[]{:S(2)}, u32[]{:S(2)}) collective-permute-start(bf16[240,128]{1,0:T(8,128)(2,1)S(1)} %get-tuple-element.19), channel_id=1, source_target_pairs={{0,2},{1,3},{2,0},{3,1},{4,6},{5,7},{6,4},{7,5},{8,10},{9,11},{10,... | collective-permute-start | bytes 184328 | tf_op jit(solution)/shard_map/ppermute | solution.py:594
  15.6 0.0 collective-permute-done.2.refs_3_
  15.6 0.0 collective-permute-done.3.refs_4_
  15.6 2.6 %collective-permute-done.4.refs_5_ = bf16[240,128]{1,0:T(8,128)(2,1)S(1)} collective-permute-done((bf16[240,128]{1,0:T(8,128)(2,1)S(1)}, bf16[240,128]{1,0:T(8,128)(2,1)S(1)}, u32[]{:S(2)}, u32[]{:S(2)}) %collective-permute-start.4) | collective-permute-done | bytes 61472 | tf_op jit(solution)/shard_map/ppermute | solution.py:594
  18.2 0.1 collective-permute-done.5.refs_6_
  18.3 0.9 %collective-permute-done.6.refs_7_ = bf16[240,128]{1,0:T(8,128)(2,1)S(1)} collective-permute-done((bf16[240,128]{1,0:T(8,128)(2,1)S(1)}, bf16[240,128]{1,0:T(8,128)(2,1)S(1)}, u32[]{:S(2)}, u32[]{:S(2)}) %collective-permute-start.6) | collective-permute-done | bytes 61472 | tf_op jit(solution)/shard_map/ppermute | solution.py:594
  19.2 0.1 collective-permute-start.7
  19.3 0.8 %attend_own.1 = (f32[512,128]{1,0:T(8,128)S(1)}, f32[2,512,128]{2,1,0:T(8,128)S(1)}) custom-call(bf16[240,128]{1,0:T(8,128)(2,1)S(1)} %get-tuple-element.12.refs_0_, bf16[240,128]{1,0:T(8,128)(2,1)S(1)} %collective-permute-done.refs_1_, bf16[240,128]{1,0:T(8,128)(2,1)S(1)} %collective-permute-done.1.refs_2_, ...), custom_call_target="tpu_custom_call" | custom-call | flops 134217728 | bytes 917504 | tf_op jit(solution)/shard_map/attend_own/pallas_call | solution.py:195
  20.1 0.9 %collective-permute-done.7.refs_8_ = bf16[8,176,128]{2,1,0:T(8,128)(2,1)S(1)} collective-permute-done((bf16[8,176,128]{2,1,0:T(8,128)(2,1)S(1)}, bf16[8,176,128]{2,1,0:T(8,128)(2,1)S(1)}, u32[]{:S(2)}, u32[]{:S(2)}) %collective-permute-start.7) | collective-permute-done | bytes 360480 | tf_op jit(solution)/shard_map/ppermute | solution.py:598
  21.0 1.5 %attend.1 = bf16[8,64,128]{2,1,0:T(8,128)(2,1)} custom-call(bf16[240,128]{1,0:T(8,128)(2,1)S(1)} %get-tuple-element.12.refs_0_, bf16[240,128]{1,0:T(8,128)(2,1)S(1)} %collective-permute-done.refs_1_, bf16[240,128]{1,0:T(8,128)(2,1)S(1)} %collective-permute-done.1.refs_2_, bf16[240,128]{1,0:T(8,128)(2,1)S(1)} %collective-permute-done.2.refs_3_, ...), custom_call_target="tpu_custom_call" | custom-call | flops 134217728 | bytes 917504 | tf_op jit(solution)/shard_map/attend/pallas_call | solution.py:207
  22.5 4.8 %all-to-all-start = ((bf16[8,64,128]{2,1,0:T(8,128)(2,1)}), bf16[8,64,128]{2,1,0:T(8,128)(2,1)S(1)}, u32[]{:S(2)}, u32[]{:S(2)}) async-start(bf16[8,64,128]{2,1,0:T(8,128)(2,1)} %attend.1), calls=%async_computation | async-start | bytes 262144 | tf_op jit(solution)/shard_map/all_to_all | solution.py:600
  27.3 7.9 %decode_tile.1 = bf16[2,8,40,384]{3,2,1,0:T(8,128)(2,1)} custom-call(bf16[240,128]{1,0:T(8,128)(2,1)S(1)} %get-tuple-element.12.refs_0_, bf16[240,128]{1,0:T(8,128)(2,1)S(1)} %collective-permute-done.refs_1_, bf16[240,128]{1,0:T(8,128)(2,1)S(1)} %collective-permute-done.1.refs_2_, bf16[240,128]{1,0:T(8,128)(2,1)S(1)} %collective-permute-done.2.refs_3_, ...), custom_call_target="tpu_custom_call" | custom-call | flops 2548039680 | bytes 5308416 | tf_op jit(solution)/shard_map/decode_tile/pallas_call | solution.py:535
  35.2 0.0 all-to-all-done.in_ref
  35.2 0.7 %unpack_heads.1 = bf16[64,1024]{1,0:T(8,128)(2,1)} custom-call(bf16[8,64,128]{2,1,0:T(8,128)(2,1)S(1)} %all-to-all-done.in_ref), custom_call_target="tpu_custom_call" | custom-call | tf_op jit(solution)/shard_map/unpack_heads/pallas_call | solution.py:237
  (1 shorter events, 0.0 us)
Async XLA Ops:
  1.8 10.7 %collective-permute-start = (bf16[240,128]{1,0:T(8,128)(2,1)S(1)}, bf16[240,128]{1,0:T(8,128)(2,1)S(1)}, u32[]{:S(2)}, u32[]{:S(2)}) collective-permute-start(bf16[240,128]{1,0:T(8,128)(2,1)S(1)} %get-tuple-element.13), channel_id=1, source_target_pairs={{0,8},{1,9},{2,10},{3,11},{4,12},{5,13},{6,14},{7,15},{8,0},{9,1},... | collective-permute-start | bytes 184328 | tf_op jit(solution)/shard_map/ppermute | solution.py:594
  5.9 9.1 %collective-permute-start.1 = (bf16[240,128]{1,0:T(8,128)(2,1)S(1)}, bf16[240,128]{1,0:T(8,128)(2,1)S(1)}, u32[]{:S(2)}, u32[]{:S(2)}) collective-permute-start(bf16[240,128]{1,0:T(8,128)(2,1)S(1)} %get-tuple-element.14), channel_id=1, source_target_pairs={{0,10},{1,11},{2,8},{3,9},{4,14},{5,15},{6,12},{7,13},{8,2},{9,3},... | collective-permute-start | bytes 184328 | tf_op jit(solution)/shard_map/ppermute | solution.py:594
  7.1 8.5 %collective-permute-start.2 = (bf16[240,128]{1,0:T(8,128)(2,1)S(1)}, bf16[240,128]{1,0:T(8,128)(2,1)S(1)}, u32[]{:S(2)}, u32[]{:S(2)}) collective-permute-start(bf16[240,128]{1,0:T(8,128)(2,1)S(1)} %get-tuple-element.15), channel_id=1, source_target_pairs={{0,4},{1,5},{2,6},{3,7},{4,0},{5,1},{6,2},{7,3},{8,12},{9,13},{10,... | collective-permute-start | bytes 184328 | tf_op jit(solution)/shard_map/ppermute | solution.py:594
  8.7 6.9 %collective-permute-start.3 = (bf16[240,128]{1,0:T(8,128)(2,1)S(1)}, bf16[240,128]{1,0:T(8,128)(2,1)S(1)}, u32[]{:S(2)}, u32[]{:S(2)}) collective-permute-start(bf16[240,128]{1,0:T(8,128)(2,1)S(1)} %get-tuple-element.16), channel_id=1, source_target_pairs={{0,12},{1,13},{2,14},{3,15},{4,8},{5,9},{6,10},{7,11},{8,4},{9,5},... | collective-permute-start | bytes 184328 | tf_op jit(solution)/shard_map/ppermute | solution.py:594
  11.2 7.0 %collective-permute-start.4 = (bf16[240,128]{1,0:T(8,128)(2,1)S(1)}, bf16[240,128]{1,0:T(8,128)(2,1)S(1)}, u32[]{:S(2)}, u32[]{:S(2)}) collective-permute-start(bf16[240,128]{1,0:T(8,128)(2,1)S(1)} %get-tuple-element.17), channel_id=1, source_target_pairs={{0,14},{1,15},{2,12},{3,13},{4,10},{5,11},{6,8},{7,9},{8,6},{9,7},... | collective-permute-start | bytes 184328 | tf_op jit(solution)/shard_map/ppermute | solution.py:594
  12.5 5.8 %collective-permute-start.5 = (bf16[240,128]{1,0:T(8,128)(2,1)S(1)}, bf16[240,128]{1,0:T(8,128)(2,1)S(1)}, u32[]{:S(2)}, u32[]{:S(2)}) collective-permute-start(bf16[240,128]{1,0:T(8,128)(2,1)S(1)} %get-tuple-element.18), channel_id=1, source_target_pairs={{0,6},{1,7},{2,4},{3,5},{4,2},{5,3},{6,0},{7,1},{8,14},{9,15},{10,... | collective-permute-start | bytes 184328 | tf_op jit(solution)/shard_map/ppermute | solution.py:594
  15.0 4.2 %collective-permute-start.6 = (bf16[240,128]{1,0:T(8,128)(2,1)S(1)}, bf16[240,128]{1,0:T(8,128)(2,1)S(1)}, u32[]{:S(2)}, u32[]{:S(2)}) collective-permute-start(bf16[240,128]{1,0:T(8,128)(2,1)S(1)} %get-tuple-element.19), channel_id=1, source_target_pairs={{0,2},{1,3},{2,0},{3,1},{4,6},{5,7},{6,4},{7,5},{8,10},{9,11},{10,... | collective-permute-start | bytes 184328 | tf_op jit(solution)/shard_map/ppermute | solution.py:594
  19.2 1.7 %collective-permute-start.7 = (bf16[8,176,128]{2,1,0:T(8,128)(2,1)S(1)}, bf16[8,176,128]{2,1,0:T(8,128)(2,1)S(1)}, u32[]{:S(2)}, u32[]{:S(2)}) collective-permute-start(bf16[8,176,128]{2,1,0:T(8,128)(2,1)S(1)} %join.1), channel_id=1, source_target_pairs={{0,1},{1,0},{2,3},{3,2},{4,5},{5,4},{6,7},{7,6},{8,9},{9,8},{10,11... | collective-permute-start | bytes 1081352 | tf_op jit(solution)/shard_map/ppermute | solution.py:598
  22.5 12.8 %all-to-all-start = ((bf16[8,64,128]{2,1,0:T(8,128)(2,1)}), bf16[8,64,128]{2,1,0:T(8,128)(2,1)S(1)}, u32[]{:S(2)}, u32[]{:S(2)}) async-start(bf16[8,64,128]{2,1,0:T(8,128)(2,1)} %attend.1), calls=%async_computation | async-start | bytes 262144 | tf_op jit(solution)/shard_map/all_to_all | solution.py:600

commit v18 on v17

--- a/solution.py
+++ b/solution.py
@@ -91,7 +91,7 @@
 
 def sending_order(chips):
     far, near = list(range(chips // 2, chips)), list(range(1, chips // 2))
-    return [0, *far[:2], *near[1:2], *far[2:], *near[2:], *near[:1]]
+    return [0, *far[:1], *near[1:2], *far[1:], *near[2:], *near[:1]]
 
 
 def xor_pairs(distance):

time: 36.2 us -> 34.8 us (0.961)
  waiting for transfers between devices: 6.66 us -> 5.21 us
    ppermute x7, waiting for transfers between devices: 5.8 us -> 4.34 us  [on_device(): lax.ppermute(piece, 'seq', xor_pairs(2 * m))]
    ppermute x7, starting transfers between devices: 11.6 us -> 12.3 us  [on_device(): lax.ppermute(piece, 'seq', xor_pairs(2 * m))]
    all_to_all x1, starting transfers between devices: 4.82 us -> 4.2 us  [on_device(): lax.all_to_all(mixed, 'seq', 0, 0, axis_index_groups=groups, tiled=True)]
  transfers between devices with their start and end apart: 9 -> 9, of which waited for: 5 -> 4; matrix products, arithmetic and copies ran while one was open for 0% -> 0% of each run, Pallas kernels for 24% -> 25%
where the time goes in v18:
time: 34.8 us; the launch traced here: 34.6 us
  starting transfers between devices  16.6 us (48%)
  Pallas kernels  12.1 us (35%)
  waiting for transfers between devices  5.21 us (15%)
  between operations  0.69 us (2%)
    ppermute x7, starting transfers between devices, on_device(): lax.ppermute(piece, 'seq', xor_pairs(2 * m))  12.3 us
    pallas_call x1, Pallas kernels, decode_tile(): pl.pallas_call(functools.partial(decode_body, grid_rows, width, share_row...  7.95 us
    ppermute x7, waiting for transfers between devices, on_device(): lax.ppermute(piece, 'seq', xor_pairs(2 * m))  4.34 us
    all_to_all x1, starting transfers between devices, on_device(): lax.all_to_all(mixed, 'seq', 0, 0, axis_index_groups=groups, tiled=True)  4.2 us
    pallas_call x1, Pallas kernels, attend(): pl.pallas_call(attend_body, in_specs=[vmem] * (members + 3), out_specs=pl...  1.48 us
    pallas_call x1, Pallas kernels, pack_heads(): pl.pallas_call(pack_body, in_specs=[hbm] * 4, out_specs=[vmem] * heads, o...  1.12 us
    ppermute x1, waiting for transfers between devices, on_device(): other = [lax.ppermute(joined, 'seq', xor_pairs(1))]  0.86 us
    pallas_call x1, Pallas kernels, attend(): pl.pallas_call(functools.partial(attend_own_body, token_rows), in_specs=[...  0.8 us
  transfers between devices with their start and end apart: 9, of which 4 were waited for; matrix products, arithmetic and copies ran while one was open for 0% of the time, Pallas kernels for 25%

profile of v18, /device:TPU:0, one launch (start us, length us, event | category | flops | bytes accessed | tf_op | source)
XLA Modules:
  0.0 34.6 jit_solution(15147951029397267518)
XLA Ops:
  0.6 1.1 %pack_heads.1 = (bf16[240,128]{1,0:T(8,128)(2,1)S(1)}, bf16[240,128]{1,0:T(8,128)(2,1)S(1)}, bf16[240,128]{1,0:T(8,128)(2,1)S(1)}, bf16[240,128]{1,0:T(8,128)(2,...) custom-call(bf16[64,2048]{1,0:T(8,128)(2,1)} %query_ref.1, ...), custom_call_target="tpu_custom_call" | custom-call | tf_op jit(solution)/shard_map/pack_heads/pallas_call | solution.py:77
  1.8 4.1 %collective-permute-start = (bf16[240,128]{1,0:T(8,128)(2,1)S(1)}, bf16[240,128]{1,0:T(8,128)(2,1)S(1)}, u32[]{:S(2)}, u32[]{:S(2)}) collective-permute-start(bf16[240,128]{1,0:T(8,128)(2,1)S(1)} %get-tuple-element.13), channel_id=1, source_target_pairs={{0,8},{1,9},{2,10},{3,11},{4,12},{5,13},{6,14},{7,15},{8,0},{9,1},... | collective-permute-start | bytes 184328 | tf_op jit(solution)/shard_map/ppermute | solution.py:594
  5.9 1.6 %collective-permute-start.1 = (bf16[240,128]{1,0:T(8,128)(2,1)S(1)}, bf16[240,128]{1,0:T(8,128)(2,1)S(1)}, u32[]{:S(2)}, u32[]{:S(2)}) collective-permute-start(bf16[240,128]{1,0:T(8,128)(2,1)S(1)} %get-tuple-element.14), channel_id=1, source_target_pairs={{0,4},{1,5},{2,6},{3,7},{4,0},{5,1},{6,2},{7,3},{8,12},{9,13},{10,... | collective-permute-start | bytes 184328 | tf_op jit(solution)/shard_map/ppermute | solution.py:594
  7.4 1.3 %collective-permute-start.2 = (bf16[240,128]{1,0:T(8,128)(2,1)S(1)}, bf16[240,128]{1,0:T(8,128)(2,1)S(1)}, u32[]{:S(2)}, u32[]{:S(2)}) collective-permute-start(bf16[240,128]{1,0:T(8,128)(2,1)S(1)} %get-tuple-element.15), channel_id=1, source_target_pairs={{0,10},{1,11},{2,8},{3,9},{4,14},{5,15},{6,12},{7,13},{8,2},{9,3},... | collective-permute-start | bytes 184328 | tf_op jit(solution)/shard_map/ppermute | solution.py:594
  8.7 2.5 %collective-permute-start.3 = (bf16[240,128]{1,0:T(8,128)(2,1)S(1)}, bf16[240,128]{1,0:T(8,128)(2,1)S(1)}, u32[]{:S(2)}, u32[]{:S(2)}) collective-permute-start(bf16[240,128]{1,0:T(8,128)(2,1)S(1)} %get-tuple-element.16), channel_id=1, source_target_pairs={{0,12},{1,13},{2,14},{3,15},{4,8},{5,9},{6,10},{7,11},{8,4},{9,5},... | collective-permute-start | bytes 184328 | tf_op jit(solution)/shard_map/ppermute | solution.py:594
  11.2 1.3 %collective-permute-start.4 = (bf16[240,128]{1,0:T(8,128)(2,1)S(1)}, bf16[240,128]{1,0:T(8,128)(2,1)S(1)}, u32[]{:S(2)}, u32[]{:S(2)}) collective-permute-start(bf16[240,128]{1,0:T(8,128)(2,1)S(1)} %get-tuple-element.17), channel_id=1, source_target_pairs={{0,14},{1,15},{2,12},{3,13},{4,10},{5,11},{6,8},{7,9},{8,6},{9,7},... | collective-permute-start | bytes 184328 | tf_op jit(solution)/shard_map/ppermute | solution.py:594
  12.5 0.0 collective-permute-done.refs_1_
  12.5 0.3 collective-permute-start.5
  12.8 0.0 collective-permute-done.1.refs_2_
  12.8 1.3 %collective-permute-start.6 = (bf16[240,128]{1,0:T(8,128)(2,1)S(1)}, bf16[240,128]{1,0:T(8,128)(2,1)S(1)}, u32[]{:S(2)}, u32[]{:S(2)}) collective-permute-start(bf16[240,128]{1,0:T(8,128)(2,1)S(1)} %get-tuple-element.19), channel_id=1, source_target_pairs={{0,2},{1,3},{2,0},{3,1},{4,6},{5,7},{6,4},{7,5},{8,10},{9,11},{10,... | collective-permute-start | bytes 184328 | tf_op jit(solution)/shard_map/ppermute | solution.py:594
  14.1 2.0 %collective-permute-done.2.refs_3_ = bf16[240,128]{1,0:T(8,128)(2,1)S(1)} collective-permute-done((bf16[240,128]{1,0:T(8,128)(2,1)S(1)}, bf16[240,128]{1,0:T(8,128)(2,1)S(1)}, u32[]{:S(2)}, u32[]{:S(2)}) %collective-permute-start.2) | collective-permute-done | bytes 61472 | tf_op jit(solution)/shard_map/ppermute | solution.py:594
  16.1 0.0 collective-permute-done.3.refs_4_
  16.1 2.2 %collective-permute-done.4.refs_5_ = bf16[240,128]{1,0:T(8,128)(2,1)S(1)} collective-permute-done((bf16[240,128]{1,0:T(8,128)(2,1)S(1)}, bf16[240,128]{1,0:T(8,128)(2,1)S(1)}, u32[]{:S(2)}, u32[]{:S(2)}) %collective-permute-start.4) | collective-permute-done | bytes 61472 | tf_op jit(solution)/shard_map/ppermute | solution.py:594
  18.3 0.1 collective-permute-done.5.refs_6_
  18.4 0.0 collective-permute-done.6.refs_7_
  18.4 0.1 collective-permute-start.7
  18.5 0.8 %attend_own.1 = (f32[512,128]{1,0:T(8,128)S(1)}, f32[2,512,128]{2,1,0:T(8,128)S(1)}) custom-call(bf16[240,128]{1,0:T(8,128)(2,1)S(1)} %get-tuple-element.12.refs_0_, bf16[240,128]{1,0:T(8,128)(2,1)S(1)} %collective-permute-done.refs_1_, bf16[240,128]{1,0:T(8,128)(2,1)S(1)} %collective-permute-done.1.refs_2_, ...), custom_call_target="tpu_custom_call" | custom-call | flops 134217728 | bytes 917504 | tf_op jit(solution)/shard_map/attend_own/pallas_call | solution.py:195
  19.3 0.9 %collective-permute-done.7.refs_8_ = bf16[8,176,128]{2,1,0:T(8,128)(2,1)S(1)} collective-permute-done((bf16[8,176,128]{2,1,0:T(8,128)(2,1)S(1)}, bf16[8,176,128]{2,1,0:T(8,128)(2,1)S(1)}, u32[]{:S(2)}, u32[]{:S(2)}) %collective-permute-start.7) | collective-permute-done | bytes 360480 | tf_op jit(solution)/shard_map/ppermute | solution.py:598
  20.2 1.5 %attend.1 = bf16[8,64,128]{2,1,0:T(8,128)(2,1)} custom-call(bf16[240,128]{1,0:T(8,128)(2,1)S(1)} %get-tuple-element.12.refs_0_, bf16[240,128]{1,0:T(8,128)(2,1)S(1)} %collective-permute-done.refs_1_, bf16[240,128]{1,0:T(8,128)(2,1)S(1)} %collective-permute-done.1.refs_2_, bf16[240,128]{1,0:T(8,128)(2,1)S(1)} %collective-permute-done.2.refs_3_, ...), custom_call_target="tpu_custom_call" | custom-call | flops 134217728 | bytes 917504 | tf_op jit(solution)/shard_map/attend/pallas_call | solution.py:207
  21.7 4.2 %all-to-all-start = ((bf16[8,64,128]{2,1,0:T(8,128)(2,1)}), bf16[8,64,128]{2,1,0:T(8,128)(2,1)S(1)}, u32[]{:S(2)}, u32[]{:S(2)}) async-start(bf16[8,64,128]{2,1,0:T(8,128)(2,1)} %attend.1), calls=%async_computation | async-start | bytes 262144 | tf_op jit(solution)/shard_map/all_to_all | solution.py:600
  25.9 7.9 %decode_tile.1 = bf16[2,8,40,384]{3,2,1,0:T(8,128)(2,1)} custom-call(bf16[240,128]{1,0:T(8,128)(2,1)S(1)} %get-tuple-element.12.refs_0_, bf16[240,128]{1,0:T(8,128)(2,1)S(1)} %collective-permute-done.refs_1_, bf16[240,128]{1,0:T(8,128)(2,1)S(1)} %collective-permute-done.1.refs_2_, bf16[240,128]{1,0:T(8,128)(2,1)S(1)} %collective-permute-done.2.refs_3_, ...), custom_call_target="tpu_custom_call" | custom-call | flops 2548039680 | bytes 5308416 | tf_op jit(solution)/shard_map/decode_tile/pallas_call | solution.py:535
  33.8 0.0 all-to-all-done.in_ref
  33.8 0.7 %unpack_heads.1 = bf16[64,1024]{1,0:T(8,128)(2,1)} custom-call(bf16[8,64,128]{2,1,0:T(8,128)(2,1)S(1)} %all-to-all-done.in_ref), custom_call_target="tpu_custom_call" | custom-call | tf_op jit(solution)/shard_map/unpack_heads/pallas_call | solution.py:237
  (1 shorter events, 0.0 us)
Async XLA Ops:
  1.8 10.7 %collective-permute-start = (bf16[240,128]{1,0:T(8,128)(2,1)S(1)}, bf16[240,128]{1,0:T(8,128)(2,1)S(1)}, u32[]{:S(2)}, u32[]{:S(2)}) collective-permute-start(bf16[240,128]{1,0:T(8,128)(2,1)S(1)} %get-tuple-element.13), channel_id=1, source_target_pairs={{0,8},{1,9},{2,10},{3,11},{4,12},{5,13},{6,14},{7,15},{8,0},{9,1},... | collective-permute-start | bytes 184328 | tf_op jit(solution)/shard_map/ppermute | solution.py:594
  5.9 6.9 %collective-permute-start.1 = (bf16[240,128]{1,0:T(8,128)(2,1)S(1)}, bf16[240,128]{1,0:T(8,128)(2,1)S(1)}, u32[]{:S(2)}, u32[]{:S(2)}) collective-permute-start(bf16[240,128]{1,0:T(8,128)(2,1)S(1)} %get-tuple-element.14), channel_id=1, source_target_pairs={{0,4},{1,5},{2,6},{3,7},{4,0},{5,1},{6,2},{7,3},{8,12},{9,13},{10,... | collective-permute-start | bytes 184328 | tf_op jit(solution)/shard_map/ppermute | solution.py:594
  7.4 8.7 %collective-permute-start.2 = (bf16[240,128]{1,0:T(8,128)(2,1)S(1)}, bf16[240,128]{1,0:T(8,128)(2,1)S(1)}, u32[]{:S(2)}, u32[]{:S(2)}) collective-permute-start(bf16[240,128]{1,0:T(8,128)(2,1)S(1)} %get-tuple-element.15), channel_id=1, source_target_pairs={{0,10},{1,11},{2,8},{3,9},{4,14},{5,15},{6,12},{7,13},{8,2},{9,3},... | collective-permute-start | bytes 184328 | tf_op jit(solution)/shard_map/ppermute | solution.py:594
  8.7 7.4 %collective-permute-start.3 = (bf16[240,128]{1,0:T(8,128)(2,1)S(1)}, bf16[240,128]{1,0:T(8,128)(2,1)S(1)}, u32[]{:S(2)}, u32[]{:S(2)}) collective-permute-start(bf16[240,128]{1,0:T(8,128)(2,1)S(1)} %get-tuple-element.16), channel_id=1, source_target_pairs={{0,12},{1,13},{2,14},{3,15},{4,8},{5,9},{6,10},{7,11},{8,4},{9,5},... | collective-permute-start | bytes 184328 | tf_op jit(solution)/shard_map/ppermute | solution.py:594
  11.2 7.1 %collective-permute-start.4 = (bf16[240,128]{1,0:T(8,128)(2,1)S(1)}, bf16[240,128]{1,0:T(8,128)(2,1)S(1)}, u32[]{:S(2)}, u32[]{:S(2)}) collective-permute-start(bf16[240,128]{1,0:T(8,128)(2,1)S(1)} %get-tuple-element.17), channel_id=1, source_target_pairs={{0,14},{1,15},{2,12},{3,13},{4,10},{5,11},{6,8},{7,9},{8,6},{9,7},... | collective-permute-start | bytes 184328 | tf_op jit(solution)/shard_map/ppermute | solution.py:594
  12.5 5.9 %collective-permute-start.5 = (bf16[240,128]{1,0:T(8,128)(2,1)S(1)}, bf16[240,128]{1,0:T(8,128)(2,1)S(1)}, u32[]{:S(2)}, u32[]{:S(2)}) collective-permute-start(bf16[240,128]{1,0:T(8,128)(2,1)S(1)} %get-tuple-element.18), channel_id=1, source_target_pairs={{0,6},{1,7},{2,4},{3,5},{4,2},{5,3},{6,0},{7,1},{8,14},{9,15},{10,... | collective-permute-start | bytes 184328 | tf_op jit(solution)/shard_map/ppermute | solution.py:594
  12.8 5.6 %collective-permute-start.6 = (bf16[240,128]{1,0:T(8,128)(2,1)S(1)}, bf16[240,128]{1,0:T(8,128)(2,1)S(1)}, u32[]{:S(2)}, u32[]{:S(2)}) collective-permute-start(bf16[240,128]{1,0:T(8,128)(2,1)S(1)} %get-tuple-element.19), channel_id=1, source_target_pairs={{0,2},{1,3},{2,0},{3,1},{4,6},{5,7},{6,4},{7,5},{8,10},{9,11},{10,... | collective-permute-start | bytes 184328 | tf_op jit(solution)/shard_map/ppermute | solution.py:594
  18.4 1.7 %collective-permute-start.7 = (bf16[8,176,128]{2,1,0:T(8,128)(2,1)S(1)}, bf16[8,176,128]{2,1,0:T(8,128)(2,1)S(1)}, u32[]{:S(2)}, u32[]{:S(2)}) collective-permute-start(bf16[8,176,128]{2,1,0:T(8,128)(2,1)S(1)} %join.1), channel_id=1, source_target_pairs={{0,1},{1,0},{2,3},{3,2},{4,5},{5,4},{6,7},{7,6},{8,9},{9,8},{10,11... | collective-permute-start | bytes 1081352 | tf_op jit(solution)/shard_map/ppermute | solution.py:598
  21.7 12.2 %all-to-all-start = ((bf16[8,64,128]{2,1,0:T(8,128)(2,1)}), bf16[8,64,128]{2,1,0:T(8,128)(2,1)S(1)}, u32[]{:S(2)}, u32[]{:S(2)}) async-start(bf16[8,64,128]{2,1,0:T(8,128)(2,1)} %attend.1), calls=%async_computation | async-start | bytes 262144 | tf_op jit(solution)/shard_map/all_to_all | solution.py:600

commit v19 on v18

--- a/solution.py
+++ b/solution.py
@@ -138,10 +138,14 @@
 
 
 def attend_own_body(token_rows, *refs):
-    pieces, (mixed_ref, stats_ref) = refs[:-2], refs[-2:]
+    pieces, (other_ref, mixed_ref, stats_ref) = refs[:-3], refs[-3:]
     block = min(4, len(pieces))
-    keys = piece_rows(1, token_rows, pieces)
-    values = piece_rows(2, token_rows, pieces)
+    keys = jnp.concatenate(
+        [piece_rows(1, token_rows, pieces), flat(other_ref[:, :token_rows])], axis=0
+    )
+    values = jnp.concatenate(
+        [piece_rows(2, token_rows, pieces), flat(other_ref[:, token_rows : 2 * token_rows])], axis=0
+    )
     for step in range(0, len(pieces), block):
         query = piece_rows(0, token_rows, pieces[step : step + block])
         largest, totals, mixed = softmax_part(query, keys, values)
@@ -194,7 +198,7 @@
     )
     mixed, stats = pl.pallas_call(
         functools.partial(attend_own_body, token_rows),
-        in_specs=[vmem] * members,
+        in_specs=[vmem] * (members + 1),
         out_specs=[vmem] * 2,
         out_shape=[
             jax.ShapeDtypeStruct((total, DH), jnp.float32),
@@ -203,7 +207,7 @@
         compiler_params=params,
         cost_estimate=cost,
         name="attend_own",
-    )(*own)
+    )(*own, other[0])
     return pl.pallas_call(
         attend_body,
         in_specs=[vmem] * (members + 3),
@@ -216,7 +220,7 @@
         compiler_params=params,
         cost_estimate=cost,
         name="attend",
-    )(*own, other, mixed, stats)
+    )(*own, other[1], mixed, stats)
 
 
 def unpack_body(in_ref, out_ref, sems):
@@ -594,9 +598,12 @@
         lax.ppermute(piece, "seq", xor_pairs(2 * m)) if m else piece
         for m, piece in zip(sending_order(len(packed)), packed)
     ]
-    joined = join(own, queries.shape[0])
-    other = [lax.ppermute(joined, "seq", xor_pairs(1))]
-    mixed = attend(own, other[0], queries.shape[0])
+    token_rows, half = queries.shape[0], len(own) // 2
+    other = [
+        lax.ppermute(join(part, token_rows), "seq", xor_pairs(1))
+        for part in (own[:half], own[half:])
+    ]
+    mixed = attend(own, other, token_rows)
     returned = lax.all_to_all(mixed, "seq", 0, 0, axis_index_groups=groups, tiled=True)
     frames = decode_tile(
         own,

time: 34.8 us -> 34.4 us (0.989)
  waiting for transfers between devices: 5.21 us -> 4.6 us
    ppermute x1 -> x2, waiting for transfers between devices: 0.86 us -> 0.35 us  [on_device(): lax.ppermute(join(part, token_rows), 'seq', xor_pairs(1))]
  transfers between devices with their start and end apart: 9 -> 10, of which waited for: 4 -> 4; matrix products, arithmetic and copies ran while one was open for 0% -> 0% of each run, Pallas kernels for 25% -> 26%
where the time goes in v19:
time: 34.4 us; the launch traced here: 34.2 us
  starting transfers between devices  16.6 us (48%)
  Pallas kernels  12.2 us (35%)
  waiting for transfers between devices  4.6 us (13%)
  between operations  0.72 us (2%)
    ppermute x7, starting transfers between devices, on_device(): lax.ppermute(piece, 'seq', xor_pairs(2 * m))  12.3 us
    pallas_call x1, Pallas kernels, decode_tile(): pl.pallas_call(functools.partial(decode_body, grid_rows, width, share_row...  7.95 us
    ppermute x7, waiting for transfers between devices, on_device(): lax.ppermute(piece, 'seq', xor_pairs(2 * m))  4.24 us
    all_to_all x1, starting transfers between devices, on_device(): lax.all_to_all(mixed, 'seq', 0, 0, axis_index_groups=groups, tiled=True)  4.2 us
    pallas_call x1, Pallas kernels, attend(): pl.pallas_call(attend_body, in_specs=[vmem] * (members + 3), out_specs=pl...  1.38 us
    pallas_call x1, Pallas kernels, pack_heads(): pl.pallas_call(pack_body, in_specs=[hbm] * 4, out_specs=[vmem] * heads, o...  1.12 us
    pallas_call x1, Pallas kernels, attend(): pl.pallas_call(functools.partial(attend_own_body, token_rows), in_specs=[...  1.04 us
    pallas_call x1, Pallas kernels, unpack_heads(): pl.pallas_call(unpack_body, in_specs=[pl.BlockSpec(memory_space=pltpu.VME...  0.72 us
  transfers between devices with their start and end apart: 10, of which 4 were waited for; matrix products, arithmetic and copies ran while one was open for 0% of the time, Pallas kernels for 26%

profile of v19, /device:TPU:0, one launch (start us, length us, event | category | flops | bytes accessed | tf_op | source)
XLA Modules:
  0.0 34.2 jit_solution(13749503825033706467)
XLA Ops:
  0.6 1.1 %pack_heads.1 = (bf16[240,128]{1,0:T(8,128)(2,1)S(1)}, bf16[240,128]{1,0:T(8,128)(2,1)S(1)}, bf16[240,128]{1,0:T(8,128)(2,1)S(1)}, bf16[240,128]{1,0:T(8,128)(2,...) custom-call(bf16[64,2048]{1,0:T(8,128)(2,1)} %query_ref.1, ...), custom_call_target="tpu_custom_call" | custom-call | tf_op jit(solution)/shard_map/pack_heads/pallas_call | solution.py:77
  1.8 4.1 %collective-permute-start = (bf16[240,128]{1,0:T(8,128)(2,1)S(1)}, bf16[240,128]{1,0:T(8,128)(2,1)S(1)}, u32[]{:S(2)}, u32[]{:S(2)}) collective-permute-start(bf16[240,128]{1,0:T(8,128)(2,1)S(1)} %get-tuple-element.13), channel_id=1, source_target_pairs={{0,8},{1,9},{2,10},{3,11},{4,12},{5,13},{6,14},{7,15},{8,0},{9,1},... | collective-permute-start | bytes 184328 | tf_op jit(solution)/shard_map/ppermute | solution.py:598
  5.9 1.6 %collective-permute-start.1 = (bf16[240,128]{1,0:T(8,128)(2,1)S(1)}, bf16[240,128]{1,0:T(8,128)(2,1)S(1)}, u32[]{:S(2)}, u32[]{:S(2)}) collective-permute-start(bf16[240,128]{1,0:T(8,128)(2,1)S(1)} %get-tuple-element.14), channel_id=1, source_target_pairs={{0,4},{1,5},{2,6},{3,7},{4,0},{5,1},{6,2},{7,3},{8,12},{9,13},{10,... | collective-permute-start | bytes 184328 | tf_op jit(solution)/shard_map/ppermute | solution.py:598
  7.4 1.3 %collective-permute-start.2 = (bf16[240,128]{1,0:T(8,128)(2,1)S(1)}, bf16[240,128]{1,0:T(8,128)(2,1)S(1)}, u32[]{:S(2)}, u32[]{:S(2)}) collective-permute-start(bf16[240,128]{1,0:T(8,128)(2,1)S(1)} %get-tuple-element.15), channel_id=1, source_target_pairs={{0,10},{1,11},{2,8},{3,9},{4,14},{5,15},{6,12},{7,13},{8,2},{9,3},... | collective-permute-start | bytes 184328 | tf_op jit(solution)/shard_map/ppermute | solution.py:598
  8.7 2.5 %collective-permute-start.3 = (bf16[240,128]{1,0:T(8,128)(2,1)S(1)}, bf16[240,128]{1,0:T(8,128)(2,1)S(1)}, u32[]{:S(2)}, u32[]{:S(2)}) collective-permute-start(bf16[240,128]{1,0:T(8,128)(2,1)S(1)} %get-tuple-element.16), channel_id=1, source_target_pairs={{0,12},{1,13},{2,14},{3,15},{4,8},{5,9},{6,10},{7,11},{8,4},{9,5},... | collective-permute-start | bytes 184328 | tf_op jit(solution)/shard_map/ppermute | solution.py:598
  11.2 1.3 %collective-permute-start.4 = (bf16[240,128]{1,0:T(8,128)(2,1)S(1)}, bf16[240,128]{1,0:T(8,128)(2,1)S(1)}, u32[]{:S(2)}, u32[]{:S(2)}) collective-permute-start(bf16[240,128]{1,0:T(8,128)(2,1)S(1)} %get-tuple-element.17), channel_id=1, source_target_pairs={{0,14},{1,15},{2,12},{3,13},{4,10},{5,11},{6,8},{7,9},{8,6},{9,7},... | collective-permute-start | bytes 184328 | tf_op jit(solution)/shard_map/ppermute | solution.py:598
  12.5 0.0 collective-permute-done.refs_1_
  12.5 0.3 collective-permute-start.5
  12.8 0.0 collective-permute-done.1.refs_2_
  12.8 1.3 %collective-permute-start.6 = (bf16[240,128]{1,0:T(8,128)(2,1)S(1)}, bf16[240,128]{1,0:T(8,128)(2,1)S(1)}, u32[]{:S(2)}, u32[]{:S(2)}) collective-permute-start(bf16[240,128]{1,0:T(8,128)(2,1)S(1)} %get-tuple-element.19), channel_id=1, source_target_pairs={{0,2},{1,3},{2,0},{3,1},{4,6},{5,7},{6,4},{7,5},{8,10},{9,11},{10,... | collective-permute-start | bytes 184328 | tf_op jit(solution)/shard_map/ppermute | solution.py:598
  14.1 2.0 %collective-permute-done.2.refs_3_ = bf16[240,128]{1,0:T(8,128)(2,1)S(1)} collective-permute-done((bf16[240,128]{1,0:T(8,128)(2,1)S(1)}, bf16[240,128]{1,0:T(8,128)(2,1)S(1)}, u32[]{:S(2)}, u32[]{:S(2)}) %collective-permute-start.2) | collective-permute-done | bytes 61472 | tf_op jit(solution)/shard_map/ppermute | solution.py:598
  16.1 0.1 collective-permute-start.8
  16.2 0.0 collective-permute-done.3.refs_0_.refs_4_
  16.2 2.1 %collective-permute-done.4.refs_1_.refs_5_ = bf16[240,128]{1,0:T(8,128)(2,1)S(1)} collective-permute-done((bf16[240,128]{1,0:T(8,128)(2,1)S(1)}, bf16[240,128]{1,0:T(8,128)(2,1)S(1)}, u32[]{:S(2)}, u32[]{:S(2)}) %collective-permute-start.4) | collective-permute-done | bytes 61472 | tf_op jit(solution)/shard_map/ppermute | solution.py:598
  18.3 0.1 collective-permute-done.5.refs_2_.refs_6_
  18.4 0.0 collective-permute-done.6.refs_3_.refs_7_
  18.4 0.1 collective-permute-start.7
  18.5 0.0 collective-permute-done.8.refs_8_
  18.5 1.0 %attend_own.1 = (f32[512,128]{1,0:T(8,128)S(1)}, f32[2,512,128]{2,1,0:T(8,128)S(1)}) custom-call(bf16[240,128]{1,0:T(8,128)(2,1)S(1)} %get-tuple-element.12.refs_0_, bf16[240,128]{1,0:T(8,128)(2,1)S(1)} %collective-permute-done.refs_1_, bf16[240,128]{1,0:T(8,128)(2,1)S(1)} %collective-permute-done.1.refs_2_, ...), custom_call_target="tpu_custom_call" | custom-call | flops 134217728 | bytes 917504 | tf_op jit(solution)/shard_map/attend_own/pallas_call | solution.py:199
  19.6 0.4 %collective-permute-done.7.refs_8_.refs_9_ = bf16[4,176,128]{2,1,0:T(8,128)(2,1)S(1)} collective-permute-done((bf16[4,176,128]{2,1,0:T(8,128)(2,1)S(1)}, bf16[4,176,128]{2,1,0:T(8,128)(2,1)S(1)}, u32[]{:S(2)}, u32[]{:S(2)}) %collective-permute-start.7) | collective-permute-done | bytes 180256 | tf_op jit(solution)/shard_map/ppermute | solution.py:603
  19.9 1.4 %attend.1 = bf16[8,64,128]{2,1,0:T(8,128)(2,1)} custom-call(bf16[240,128]{1,0:T(8,128)(2,1)S(1)} %get-tuple-element.12.refs_0_, bf16[240,128]{1,0:T(8,128)(2,1)S(1)} %collective-permute-done.refs_1_, bf16[240,128]{1,0:T(8,128)(2,1)S(1)} %collective-permute-done.1.refs_2_, bf16[240,128]{1,0:T(8,128)(2,1)S(1)} %collective-permute-done.2.refs_3_, ...), custom_call_target="tpu_custom_call" | custom-call | flops 134217728 | bytes 917504 | tf_op jit(solution)/shard_map/attend/pallas_call | solution.py:211
  21.3 4.2 %all-to-all-start = ((bf16[8,64,128]{2,1,0:T(8,128)(2,1)}), bf16[8,64,128]{2,1,0:T(8,128)(2,1)S(1)}, u32[]{:S(2)}, u32[]{:S(2)}) async-start(bf16[8,64,128]{2,1,0:T(8,128)(2,1)} %attend.1), calls=%async_computation | async-start | bytes 262144 | tf_op jit(solution)/shard_map/all_to_all | solution.py:607
  25.5 7.9 %decode_tile.1 = bf16[2,8,40,384]{3,2,1,0:T(8,128)(2,1)} custom-call(bf16[240,128]{1,0:T(8,128)(2,1)S(1)} %get-tuple-element.12.refs_0_, bf16[240,128]{1,0:T(8,128)(2,1)S(1)} %collective-permute-done.refs_1_, bf16[240,128]{1,0:T(8,128)(2,1)S(1)} %collective-permute-done.1.refs_2_, bf16[240,128]{1,0:T(8,128)(2,1)S(1)} %collective-permute-done.2.refs_3_, ...), custom_call_target="tpu_custom_call" | custom-call | flops 2548039680 | bytes 5308416 | tf_op jit(solution)/shard_map/decode_tile/pallas_call | solution.py:539
  33.4 0.0 all-to-all-done.in_ref
  33.5 0.7 %unpack_heads.1 = bf16[64,1024]{1,0:T(8,128)(2,1)} custom-call(bf16[8,64,128]{2,1,0:T(8,128)(2,1)S(1)} %all-to-all-done.in_ref), custom_call_target="tpu_custom_call" | custom-call | tf_op jit(solution)/shard_map/unpack_heads/pallas_call | solution.py:241
  (2 shorter events, 0.0 us)
Async XLA Ops:
  1.8 10.7 %collective-permute-start = (bf16[240,128]{1,0:T(8,128)(2,1)S(1)}, bf16[240,128]{1,0:T(8,128)(2,1)S(1)}, u32[]{:S(2)}, u32[]{:S(2)}) collective-permute-start(bf16[240,128]{1,0:T(8,128)(2,1)S(1)} %get-tuple-element.13), channel_id=1, source_target_pairs={{0,8},{1,9},{2,10},{3,11},{4,12},{5,13},{6,14},{7,15},{8,0},{9,1},... | collective-permute-start | bytes 184328 | tf_op jit(solution)/shard_map/ppermute | solution.py:598
  5.9 6.9 %collective-permute-start.1 = (bf16[240,128]{1,0:T(8,128)(2,1)S(1)}, bf16[240,128]{1,0:T(8,128)(2,1)S(1)}, u32[]{:S(2)}, u32[]{:S(2)}) collective-permute-start(bf16[240,128]{1,0:T(8,128)(2,1)S(1)} %get-tuple-element.14), channel_id=1, source_target_pairs={{0,4},{1,5},{2,6},{3,7},{4,0},{5,1},{6,2},{7,3},{8,12},{9,13},{10,... | collective-permute-start | bytes 184328 | tf_op jit(solution)/shard_map/ppermute | solution.py:598
  7.4 8.7 %collective-permute-start.2 = (bf16[240,128]{1,0:T(8,128)(2,1)S(1)}, bf16[240,128]{1,0:T(8,128)(2,1)S(1)}, u32[]{:S(2)}, u32[]{:S(2)}) collective-permute-start(bf16[240,128]{1,0:T(8,128)(2,1)S(1)} %get-tuple-element.15), channel_id=1, source_target_pairs={{0,10},{1,11},{2,8},{3,9},{4,14},{5,15},{6,12},{7,13},{8,2},{9,3},... | collective-permute-start | bytes 184328 | tf_op jit(solution)/shard_map/ppermute | solution.py:598
  8.7 7.5 %collective-permute-start.3 = (bf16[240,128]{1,0:T(8,128)(2,1)S(1)}, bf16[240,128]{1,0:T(8,128)(2,1)S(1)}, u32[]{:S(2)}, u32[]{:S(2)}) collective-permute-start(bf16[240,128]{1,0:T(8,128)(2,1)S(1)} %get-tuple-element.16), channel_id=1, source_target_pairs={{0,12},{1,13},{2,14},{3,15},{4,8},{5,9},{6,10},{7,11},{8,4},{9,5},... | collective-permute-start | bytes 184328 | tf_op jit(solution)/shard_map/ppermute | solution.py:598
  11.2 7.1 %collective-permute-start.4 = (bf16[240,128]{1,0:T(8,128)(2,1)S(1)}, bf16[240,128]{1,0:T(8,128)(2,1)S(1)}, u32[]{:S(2)}, u32[]{:S(2)}) collective-permute-start(bf16[240,128]{1,0:T(8,128)(2,1)S(1)} %get-tuple-element.17), channel_id=1, source_target_pairs={{0,14},{1,15},{2,12},{3,13},{4,10},{5,11},{6,8},{7,9},{8,6},{9,7},... | collective-permute-start | bytes 184328 | tf_op jit(solution)/shard_map/ppermute | solution.py:598
  12.5 5.9 %collective-permute-start.5 = (bf16[240,128]{1,0:T(8,128)(2,1)S(1)}, bf16[240,128]{1,0:T(8,128)(2,1)S(1)}, u32[]{:S(2)}, u32[]{:S(2)}) collective-permute-start(bf16[240,128]{1,0:T(8,128)(2,1)S(1)} %get-tuple-element.18), channel_id=1, source_target_pairs={{0,6},{1,7},{2,4},{3,5},{4,2},{5,3},{6,0},{7,1},{8,14},{9,15},{10,... | collective-permute-start | bytes 184328 | tf_op jit(solution)/shard_map/ppermute | solution.py:598
  12.8 5.6 %collective-permute-start.6 = (bf16[240,128]{1,0:T(8,128)(2,1)S(1)}, bf16[240,128]{1,0:T(8,128)(2,1)S(1)}, u32[]{:S(2)}, u32[]{:S(2)}) collective-permute-start(bf16[240,128]{1,0:T(8,128)(2,1)S(1)} %get-tuple-element.19), channel_id=1, source_target_pairs={{0,2},{1,3},{2,0},{3,1},{4,6},{5,7},{6,4},{7,5},{8,10},{9,11},{10,... | collective-permute-start | bytes 184328 | tf_op jit(solution)/shard_map/ppermute | solution.py:598
  16.1 2.4 %collective-permute-start.8 = (bf16[4,176,128]{2,1,0:T(8,128)(2,1)S(1)}, bf16[4,176,128]{2,1,0:T(8,128)(2,1)S(1)}, u32[]{:S(2)}, u32[]{:S(2)}) collective-permute-start(bf16[4,176,128]{2,1,0:T(8,128)(2,1)S(1)} %join.3), channel_id=1, source_target_pairs={{0,1},{1,0},{2,3},{3,2},{4,5},{5,4},{6,7},{7,6},{8,9},{9,8},{10,11... | collective-permute-start | bytes 540680 | tf_op jit(solution)/shard_map/ppermute | solution.py:603
  18.4 1.5 %collective-permute-start.7 = (bf16[4,176,128]{2,1,0:T(8,128)(2,1)S(1)}, bf16[4,176,128]{2,1,0:T(8,128)(2,1)S(1)}, u32[]{:S(2)}, u32[]{:S(2)}) collective-permute-start(bf16[4,176,128]{2,1,0:T(8,128)(2,1)S(1)} %join.2), channel_id=1, source_target_pairs={{0,1},{1,0},{2,3},{3,2},{4,5},{5,4},{6,7},{7,6},{8,9},{9,8},{10,11... | collective-permute-start | bytes 540680 | tf_op jit(solution)/shard_map/ppermute | solution.py:603
  21.3 12.2 %all-to-all-start = ((bf16[8,64,128]{2,1,0:T(8,128)(2,1)}), bf16[8,64,128]{2,1,0:T(8,128)(2,1)S(1)}, u32[]{:S(2)}, u32[]{:S(2)}) async-start(bf16[8,64,128]{2,1,0:T(8,128)(2,1)} %attend.1), calls=%async_computation | async-start | bytes 262144 | tf_op jit(solution)/shard_map/all_to_all | solution.py:607

commit v20 on v19

--- a/solution.py
+++ b/solution.py
@@ -139,7 +139,7 @@
 
 def attend_own_body(token_rows, *refs):
     pieces, (other_ref, mixed_ref, stats_ref) = refs[:-3], refs[-3:]
-    block = min(4, len(pieces))
+    block = len(pieces) if len(pieces) <= 8 else 4
     keys = jnp.concatenate(
         [piece_rows(1, token_rows, pieces), flat(other_ref[:, :token_rows])], axis=0
     )
@@ -159,7 +159,7 @@
     other_ref, mixed_ref, stats_ref, out_hbm, out_ref, sems = refs[-6:]
     pieces = refs[:-6]
     members, token_rows, _ = out_ref.shape
-    block = min(4, members)
+    block = members if members <= 8 else 4
     chip = lax.axis_index("seq") // 2
     order = sending_order(members)
 

time: 34.4 us -> 34.2 us (level)
  transfers between devices with their start and end apart: 10 -> 10, of which waited for: 4 -> 4; matrix products, arithmetic and copies ran while one was open for 0% -> 0% of each run, Pallas kernels for 26% -> 27%
where the time goes in v20:
time: 34.2 us; the launch traced here: 34 us
  starting transfers between devices  16.6 us (49%)
  Pallas kernels  12.2 us (36%)
  waiting for transfers between devices  4.44 us (13%)
  between operations  0.72 us (2%)
    ppermute x7, starting transfers between devices, on_device(): lax.ppermute(piece, 'seq', xor_pairs(2 * m))  12.3 us
    pallas_call x1, Pallas kernels, decode_tile(): pl.pallas_call(functools.partial(decode_body, grid_rows, width, share_row...  7.95 us
    ppermute x7, waiting for transfers between devices, on_device(): lax.ppermute(piece, 'seq', xor_pairs(2 * m))  4.24 us
    all_to_all x1, starting transfers between devices, on_device(): lax.all_to_all(mixed, 'seq', 0, 0, axis_index_groups=groups, tiled=True)  4.2 us
    pallas_call x1, Pallas kernels, attend(): pl.pallas_call(functools.partial(attend_own_body, token_rows), in_specs=[...  1.19 us
    pallas_call x1, Pallas kernels, attend(): pl.pallas_call(attend_body, in_specs=[vmem] * (members + 3), out_specs=pl...  1.18 us
    pallas_call x1, Pallas kernels, pack_heads(): pl.pallas_call(pack_body, in_specs=[hbm] * 4, out_specs=[vmem] * heads, o...  1.12 us
    pallas_call x1, Pallas kernels, unpack_heads(): pl.pallas_call(unpack_body, in_specs=[pl.BlockSpec(memory_space=pltpu.VME...  0.72 us
  transfers between devices with their start and end apart: 10, of which 4 were waited for; matrix products, arithmetic and copies ran while one was open for 0% of the time, Pallas kernels for 27%

profile of v20, /device:TPU:0, one launch (start us, length us, event | category | flops | bytes accessed | tf_op | source)
XLA Modules:
  0.0 34.0 jit_solution(8407225831536367740)
XLA Ops:
  0.6 1.1 %pack_heads.1 = (bf16[240,128]{1,0:T(8,128)(2,1)S(1)}, bf16[240,128]{1,0:T(8,128)(2,1)S(1)}, bf16[240,128]{1,0:T(8,128)(2,1)S(1)}, bf16[240,128]{1,0:T(8,128)(2,...) custom-call(bf16[64,2048]{1,0:T(8,128)(2,1)} %query_ref.1, ...), custom_call_target="tpu_custom_call" | custom-call | tf_op jit(solution)/shard_map/pack_heads/pallas_call | solution.py:77
  1.8 4.1 %collective-permute-start = (bf16[240,128]{1,0:T(8,128)(2,1)S(1)}, bf16[240,128]{1,0:T(8,128)(2,1)S(1)}, u32[]{:S(2)}, u32[]{:S(2)}) collective-permute-start(bf16[240,128]{1,0:T(8,128)(2,1)S(1)} %get-tuple-element.13), channel_id=1, source_target_pairs={{0,8},{1,9},{2,10},{3,11},{4,12},{5,13},{6,14},{7,15},{8,0},{9,1},... | collective-permute-start | bytes 184328 | tf_op jit(solution)/shard_map/ppermute | solution.py:598
  5.9 1.6 %collective-permute-start.1 = (bf16[240,128]{1,0:T(8,128)(2,1)S(1)}, bf16[240,128]{1,0:T(8,128)(2,1)S(1)}, u32[]{:S(2)}, u32[]{:S(2)}) collective-permute-start(bf16[240,128]{1,0:T(8,128)(2,1)S(1)} %get-tuple-element.14), channel_id=1, source_target_pairs={{0,4},{1,5},{2,6},{3,7},{4,0},{5,1},{6,2},{7,3},{8,12},{9,13},{10,... | collective-permute-start | bytes 184328 | tf_op jit(solution)/shard_map/ppermute | solution.py:598
  7.4 1.3 %collective-permute-start.2 = (bf16[240,128]{1,0:T(8,128)(2,1)S(1)}, bf16[240,128]{1,0:T(8,128)(2,1)S(1)}, u32[]{:S(2)}, u32[]{:S(2)}) collective-permute-start(bf16[240,128]{1,0:T(8,128)(2,1)S(1)} %get-tuple-element.15), channel_id=1, source_target_pairs={{0,10},{1,11},{2,8},{3,9},{4,14},{5,15},{6,12},{7,13},{8,2},{9,3},... | collective-permute-start | bytes 184328 | tf_op jit(solution)/shard_map/ppermute | solution.py:598
  8.7 2.5 %collective-permute-start.3 = (bf16[240,128]{1,0:T(8,128)(2,1)S(1)}, bf16[240,128]{1,0:T(8,128)(2,1)S(1)}, u32[]{:S(2)}, u32[]{:S(2)}) collective-permute-start(bf16[240,128]{1,0:T(8,128)(2,1)S(1)} %get-tuple-element.16), channel_id=1, source_target_pairs={{0,12},{1,13},{2,14},{3,15},{4,8},{5,9},{6,10},{7,11},{8,4},{9,5},... | collective-permute-start | bytes 184328 | tf_op jit(solution)/shard_map/ppermute | solution.py:598
  11.2 1.3 %collective-permute-start.4 = (bf16[240,128]{1,0:T(8,128)(2,1)S(1)}, bf16[240,128]{1,0:T(8,128)(2,1)S(1)}, u32[]{:S(2)}, u32[]{:S(2)}) collective-permute-start(bf16[240,128]{1,0:T(8,128)(2,1)S(1)} %get-tuple-element.17), channel_id=1, source_target_pairs={{0,14},{1,15},{2,12},{3,13},{4,10},{5,11},{6,8},{7,9},{8,6},{9,7},... | collective-permute-start | bytes 184328 | tf_op jit(solution)/shard_map/ppermute | solution.py:598
  12.5 0.0 collective-permute-done.refs_1_
  12.5 0.3 collective-permute-start.5
  12.8 0.0 collective-permute-done.1.refs_2_
  12.8 1.3 %collective-permute-start.6 = (bf16[240,128]{1,0:T(8,128)(2,1)S(1)}, bf16[240,128]{1,0:T(8,128)(2,1)S(1)}, u32[]{:S(2)}, u32[]{:S(2)}) collective-permute-start(bf16[240,128]{1,0:T(8,128)(2,1)S(1)} %get-tuple-element.19), channel_id=1, source_target_pairs={{0,2},{1,3},{2,0},{3,1},{4,6},{5,7},{6,4},{7,5},{8,10},{9,11},{10,... | collective-permute-start | bytes 184328 | tf_op jit(solution)/shard_map/ppermute | solution.py:598
  14.1 2.0 %collective-permute-done.2.refs_3_ = bf16[240,128]{1,0:T(8,128)(2,1)S(1)} collective-permute-done((bf16[240,128]{1,0:T(8,128)(2,1)S(1)}, bf16[240,128]{1,0:T(8,128)(2,1)S(1)}, u32[]{:S(2)}, u32[]{:S(2)}) %collective-permute-start.2) | collective-permute-done | bytes 61472 | tf_op jit(solution)/shard_map/ppermute | solution.py:598
  16.1 0.1 collective-permute-start.8
  16.2 0.0 collective-permute-done.3.refs_0_.refs_4_
  16.2 2.1 %collective-permute-done.4.refs_1_.refs_5_ = bf16[240,128]{1,0:T(8,128)(2,1)S(1)} collective-permute-done((bf16[240,128]{1,0:T(8,128)(2,1)S(1)}, bf16[240,128]{1,0:T(8,128)(2,1)S(1)}, u32[]{:S(2)}, u32[]{:S(2)}) %collective-permute-start.4) | collective-permute-done | bytes 61472 | tf_op jit(solution)/shard_map/ppermute | solution.py:598
  18.3 0.1 collective-permute-done.5.refs_2_.refs_6_
  18.4 0.0 collective-permute-done.6.refs_3_.refs_7_
  18.4 0.1 collective-permute-start.7
  18.5 0.0 collective-permute-done.8.refs_8_
  18.5 1.2 %attend_own.1 = (f32[512,128]{1,0:T(8,128)S(1)}, f32[2,512,128]{2,1,0:T(8,128)S(1)}) custom-call(bf16[240,128]{1,0:T(8,128)(2,1)S(1)} %get-tuple-element.12.refs_0_, bf16[240,128]{1,0:T(8,128)(2,1)S(1)} %collective-permute-done.refs_1_, bf16[240,128]{1,0:T(8,128)(2,1)S(1)} %collective-permute-done.1.refs_2_, ...), custom_call_target="tpu_custom_call" | custom-call | flops 134217728 | bytes 917504 | tf_op jit(solution)/shard_map/attend_own/pallas_call | solution.py:199
  19.7 0.2 collective-permute-done.7.refs_8_.refs_9_
  19.9 1.2 %attend.1 = bf16[8,64,128]{2,1,0:T(8,128)(2,1)} custom-call(bf16[240,128]{1,0:T(8,128)(2,1)S(1)} %get-tuple-element.12.refs_0_, bf16[240,128]{1,0:T(8,128)(2,1)S(1)} %collective-permute-done.refs_1_, bf16[240,128]{1,0:T(8,128)(2,1)S(1)} %collective-permute-done.1.refs_2_, bf16[240,128]{1,0:T(8,128)(2,1)S(1)} %collective-permute-done.2.refs_3_, ...), custom_call_target="tpu_custom_call" | custom-call | flops 134217728 | bytes 917504 | tf_op jit(solution)/shard_map/attend/pallas_call | solution.py:211
  21.1 4.2 %all-to-all-start = ((bf16[8,64,128]{2,1,0:T(8,128)(2,1)}), bf16[8,64,128]{2,1,0:T(8,128)(2,1)S(1)}, u32[]{:S(2)}, u32[]{:S(2)}) async-start(bf16[8,64,128]{2,1,0:T(8,128)(2,1)} %attend.1), calls=%async_computation | async-start | bytes 262144 | tf_op jit(solution)/shard_map/all_to_all | solution.py:607
  25.3 8.0 %decode_tile.1 = bf16[2,8,40,384]{3,2,1,0:T(8,128)(2,1)} custom-call(bf16[240,128]{1,0:T(8,128)(2,1)S(1)} %get-tuple-element.12.refs_0_, bf16[240,128]{1,0:T(8,128)(2,1)S(1)} %collective-permute-done.refs_1_, bf16[240,128]{1,0:T(8,128)(2,1)S(1)} %collective-permute-done.1.refs_2_, bf16[240,128]{1,0:T(8,128)(2,1)S(1)} %collective-permute-done.2.refs_3_, ...), custom_call_target="tpu_custom_call" | custom-call | flops 2548039680 | bytes 5308416 | tf_op jit(solution)/shard_map/decode_tile/pallas_call | solution.py:539
  33.2 0.0 all-to-all-done.in_ref
  33.3 0.7 %unpack_heads.1 = bf16[64,1024]{1,0:T(8,128)(2,1)} custom-call(bf16[8,64,128]{2,1,0:T(8,128)(2,1)S(1)} %all-to-all-done.in_ref), custom_call_target="tpu_custom_call" | custom-call | tf_op jit(solution)/shard_map/unpack_heads/pallas_call | solution.py:241
  (2 shorter events, 0.0 us)
Async XLA Ops:
  1.8 10.7 %collective-permute-start = (bf16[240,128]{1,0:T(8,128)(2,1)S(1)}, bf16[240,128]{1,0:T(8,128)(2,1)S(1)}, u32[]{:S(2)}, u32[]{:S(2)}) collective-permute-start(bf16[240,128]{1,0:T(8,128)(2,1)S(1)} %get-tuple-element.13), channel_id=1, source_target_pairs={{0,8},{1,9},{2,10},{3,11},{4,12},{5,13},{6,14},{7,15},{8,0},{9,1},... | collective-permute-start | bytes 184328 | tf_op jit(solution)/shard_map/ppermute | solution.py:598
  5.9 6.9 %collective-permute-start.1 = (bf16[240,128]{1,0:T(8,128)(2,1)S(1)}, bf16[240,128]{1,0:T(8,128)(2,1)S(1)}, u32[]{:S(2)}, u32[]{:S(2)}) collective-permute-start(bf16[240,128]{1,0:T(8,128)(2,1)S(1)} %get-tuple-element.14), channel_id=1, source_target_pairs={{0,4},{1,5},{2,6},{3,7},{4,0},{5,1},{6,2},{7,3},{8,12},{9,13},{10,... | collective-permute-start | bytes 184328 | tf_op jit(solution)/shard_map/ppermute | solution.py:598
  7.4 8.7 %collective-permute-start.2 = (bf16[240,128]{1,0:T(8,128)(2,1)S(1)}, bf16[240,128]{1,0:T(8,128)(2,1)S(1)}, u32[]{:S(2)}, u32[]{:S(2)}) collective-permute-start(bf16[240,128]{1,0:T(8,128)(2,1)S(1)} %get-tuple-element.15), channel_id=1, source_target_pairs={{0,10},{1,11},{2,8},{3,9},{4,14},{5,15},{6,12},{7,13},{8,2},{9,3},... | collective-permute-start | bytes 184328 | tf_op jit(solution)/shard_map/ppermute | solution.py:598
  8.7 7.5 %collective-permute-start.3 = (bf16[240,128]{1,0:T(8,128)(2,1)S(1)}, bf16[240,128]{1,0:T(8,128)(2,1)S(1)}, u32[]{:S(2)}, u32[]{:S(2)}) collective-permute-start(bf16[240,128]{1,0:T(8,128)(2,1)S(1)} %get-tuple-element.16), channel_id=1, source_target_pairs={{0,12},{1,13},{2,14},{3,15},{4,8},{5,9},{6,10},{7,11},{8,4},{9,5},... | collective-permute-start | bytes 184328 | tf_op jit(solution)/shard_map/ppermute | solution.py:598
  11.2 7.1 %collective-permute-start.4 = (bf16[240,128]{1,0:T(8,128)(2,1)S(1)}, bf16[240,128]{1,0:T(8,128)(2,1)S(1)}, u32[]{:S(2)}, u32[]{:S(2)}) collective-permute-start(bf16[240,128]{1,0:T(8,128)(2,1)S(1)} %get-tuple-element.17), channel_id=1, source_target_pairs={{0,14},{1,15},{2,12},{3,13},{4,10},{5,11},{6,8},{7,9},{8,6},{9,7},... | collective-permute-start | bytes 184328 | tf_op jit(solution)/shard_map/ppermute | solution.py:598
  12.5 5.9 %collective-permute-start.5 = (bf16[240,128]{1,0:T(8,128)(2,1)S(1)}, bf16[240,128]{1,0:T(8,128)(2,1)S(1)}, u32[]{:S(2)}, u32[]{:S(2)}) collective-permute-start(bf16[240,128]{1,0:T(8,128)(2,1)S(1)} %get-tuple-element.18), channel_id=1, source_target_pairs={{0,6},{1,7},{2,4},{3,5},{4,2},{5,3},{6,0},{7,1},{8,14},{9,15},{10,... | collective-permute-start | bytes 184328 | tf_op jit(solution)/shard_map/ppermute | solution.py:598
  12.8 5.6 %collective-permute-start.6 = (bf16[240,128]{1,0:T(8,128)(2,1)S(1)}, bf16[240,128]{1,0:T(8,128)(2,1)S(1)}, u32[]{:S(2)}, u32[]{:S(2)}) collective-permute-start(bf16[240,128]{1,0:T(8,128)(2,1)S(1)} %get-tuple-element.19), channel_id=1, source_target_pairs={{0,2},{1,3},{2,0},{3,1},{4,6},{5,7},{6,4},{7,5},{8,10},{9,11},{10,... | collective-permute-start | bytes 184328 | tf_op jit(solution)/shard_map/ppermute | solution.py:598
  16.1 2.4 %collective-permute-start.8 = (bf16[4,176,128]{2,1,0:T(8,128)(2,1)S(1)}, bf16[4,176,128]{2,1,0:T(8,128)(2,1)S(1)}, u32[]{:S(2)}, u32[]{:S(2)}) collective-permute-start(bf16[4,176,128]{2,1,0:T(8,128)(2,1)S(1)} %join.3), channel_id=1, source_target_pairs={{0,1},{1,0},{2,3},{3,2},{4,5},{5,4},{6,7},{7,6},{8,9},{9,8},{10,11... | collective-permute-start | bytes 540680 | tf_op jit(solution)/shard_map/ppermute | solution.py:603
  18.4 1.5 %collective-permute-start.7 = (bf16[4,176,128]{2,1,0:T(8,128)(2,1)S(1)}, bf16[4,176,128]{2,1,0:T(8,128)(2,1)S(1)}, u32[]{:S(2)}, u32[]{:S(2)}) collective-permute-start(bf16[4,176,128]{2,1,0:T(8,128)(2,1)S(1)} %join.2), channel_id=1, source_target_pairs={{0,1},{1,0},{2,3},{3,2},{4,5},{5,4},{6,7},{7,6},{8,9},{9,8},{10,11... | collective-permute-start | bytes 540680 | tf_op jit(solution)/shard_map/ppermute | solution.py:603
  21.1 12.2 %all-to-all-start = ((bf16[8,64,128]{2,1,0:T(8,128)(2,1)}), bf16[8,64,128]{2,1,0:T(8,128)(2,1)S(1)}, u32[]{:S(2)}, u32[]{:S(2)}) async-start(bf16[8,64,128]{2,1,0:T(8,128)(2,1)} %attend.1), calls=%async_computation | async-start | bytes 262144 | tf_op jit(solution)/shard_map/all_to_all | solution.py:607

commit v21 on v20

--- a/solution.py
+++ b/solution.py
@@ -139,7 +139,7 @@
 
 def attend_own_body(token_rows, *refs):
     pieces, (other_ref, mixed_ref, stats_ref) = refs[:-3], refs[-3:]
-    block = len(pieces) if len(pieces) <= 8 else 4
+    block = min(4, len(pieces))
     keys = jnp.concatenate(
         [piece_rows(1, token_rows, pieces), flat(other_ref[:, :token_rows])], axis=0
     )

time: 34.2 us -> 34.2 us (level)
  no operation moved by 1% of the time
where the time goes in v21:
time: 34.2 us; the launch traced here: 34 us
  starting transfers between devices  16.6 us (49%)
  Pallas kernels  12 us (35%)
  waiting for transfers between devices  4.6 us (13%)
  between operations  0.72 us (2%)
    ppermute x7, starting transfers between devices, on_device(): lax.ppermute(piece, 'seq', xor_pairs(2 * m))  12.3 us
    pallas_call x1, Pallas kernels, decode_tile(): pl.pallas_call(functools.partial(decode_body, grid_rows, width, share_row...  7.95 us
    ppermute x7, waiting for transfers between devices, on_device(): lax.ppermute(piece, 'seq', xor_pairs(2 * m))  4.24 us
    all_to_all x1, starting transfers between devices, on_device(): lax.all_to_all(mixed, 'seq', 0, 0, axis_index_groups=groups, tiled=True)  4.2 us
    pallas_call x1, Pallas kernels, attend(): pl.pallas_call(attend_body, in_specs=[vmem] * (members + 3), out_specs=pl...  1.18 us
    pallas_call x1, Pallas kernels, pack_heads(): pl.pallas_call(pack_body, in_specs=[hbm] * 4, out_specs=[vmem] * heads, o...  1.12 us
    pallas_call x1, Pallas kernels, attend(): pl.pallas_call(functools.partial(attend_own_body, token_rows), in_specs=[...  1.04 us
    pallas_call x1, Pallas kernels, unpack_heads(): pl.pallas_call(unpack_body, in_specs=[pl.BlockSpec(memory_space=pltpu.VME...  0.72 us
  transfers between devices with their start and end apart: 10, of which 4 were waited for; matrix products, arithmetic and copies ran while one was open for 0% of the time, Pallas kernels for 27%

profile of v21, /device:TPU:0, one launch (start us, length us, event | category | flops | bytes accessed | tf_op | source)
XLA Modules:
  0.0 34.0 jit_solution(7068992279102878775)
XLA Ops:
  0.6 1.1 %pack_heads.1 = (bf16[240,128]{1,0:T(8,128)(2,1)S(1)}, bf16[240,128]{1,0:T(8,128)(2,1)S(1)}, bf16[240,128]{1,0:T(8,128)(2,1)S(1)}, bf16[240,128]{1,0:T(8,128)(2,...) custom-call(bf16[64,2048]{1,0:T(8,128)(2,1)} %query_ref.1, ...), custom_call_target="tpu_custom_call" | custom-call | tf_op jit(solution)/shard_map/pack_heads/pallas_call | solution.py:77
  1.8 4.1 %collective-permute-start = (bf16[240,128]{1,0:T(8,128)(2,1)S(1)}, bf16[240,128]{1,0:T(8,128)(2,1)S(1)}, u32[]{:S(2)}, u32[]{:S(2)}) collective-permute-start(bf16[240,128]{1,0:T(8,128)(2,1)S(1)} %get-tuple-element.13), channel_id=1, source_target_pairs={{0,8},{1,9},{2,10},{3,11},{4,12},{5,13},{6,14},{7,15},{8,0},{9,1},... | collective-permute-start | bytes 184328 | tf_op jit(solution)/shard_map/ppermute | solution.py:598
  5.9 1.6 %collective-permute-start.1 = (bf16[240,128]{1,0:T(8,128)(2,1)S(1)}, bf16[240,128]{1,0:T(8,128)(2,1)S(1)}, u32[]{:S(2)}, u32[]{:S(2)}) collective-permute-start(bf16[240,128]{1,0:T(8,128)(2,1)S(1)} %get-tuple-element.14), channel_id=1, source_target_pairs={{0,4},{1,5},{2,6},{3,7},{4,0},{5,1},{6,2},{7,3},{8,12},{9,13},{10,... | collective-permute-start | bytes 184328 | tf_op jit(solution)/shard_map/ppermute | solution.py:598
  7.4 1.3 %collective-permute-start.2 = (bf16[240,128]{1,0:T(8,128)(2,1)S(1)}, bf16[240,128]{1,0:T(8,128)(2,1)S(1)}, u32[]{:S(2)}, u32[]{:S(2)}) collective-permute-start(bf16[240,128]{1,0:T(8,128)(2,1)S(1)} %get-tuple-element.15), channel_id=1, source_target_pairs={{0,10},{1,11},{2,8},{3,9},{4,14},{5,15},{6,12},{7,13},{8,2},{9,3},... | collective-permute-start | bytes 184328 | tf_op jit(solution)/shard_map/ppermute | solution.py:598
  8.7 2.5 %collective-permute-start.3 = (bf16[240,128]{1,0:T(8,128)(2,1)S(1)}, bf16[240,128]{1,0:T(8,128)(2,1)S(1)}, u32[]{:S(2)}, u32[]{:S(2)}) collective-permute-start(bf16[240,128]{1,0:T(8,128)(2,1)S(1)} %get-tuple-element.16), channel_id=1, source_target_pairs={{0,12},{1,13},{2,14},{3,15},{4,8},{5,9},{6,10},{7,11},{8,4},{9,5},... | collective-permute-start | bytes 184328 | tf_op jit(solution)/shard_map/ppermute | solution.py:598
  11.2 1.3 %collective-permute-start.4 = (bf16[240,128]{1,0:T(8,128)(2,1)S(1)}, bf16[240,128]{1,0:T(8,128)(2,1)S(1)}, u32[]{:S(2)}, u32[]{:S(2)}) collective-permute-start(bf16[240,128]{1,0:T(8,128)(2,1)S(1)} %get-tuple-element.17), channel_id=1, source_target_pairs={{0,14},{1,15},{2,12},{3,13},{4,10},{5,11},{6,8},{7,9},{8,6},{9,7},... | collective-permute-start | bytes 184328 | tf_op jit(solution)/shard_map/ppermute | solution.py:598
  12.5 0.0 collective-permute-done.refs_1_
  12.5 0.3 collective-permute-start.5
  12.8 0.0 collective-permute-done.1.refs_2_
  12.8 1.3 %collective-permute-start.6 = (bf16[240,128]{1,0:T(8,128)(2,1)S(1)}, bf16[240,128]{1,0:T(8,128)(2,1)S(1)}, u32[]{:S(2)}, u32[]{:S(2)}) collective-permute-start(bf16[240,128]{1,0:T(8,128)(2,1)S(1)} %get-tuple-element.19), channel_id=1, source_target_pairs={{0,2},{1,3},{2,0},{3,1},{4,6},{5,7},{6,4},{7,5},{8,10},{9,11},{10,... | collective-permute-start | bytes 184328 | tf_op jit(solution)/shard_map/ppermute | solution.py:598
  14.1 2.0 %collective-permute-done.2.refs_3_ = bf16[240,128]{1,0:T(8,128)(2,1)S(1)} collective-permute-done((bf16[240,128]{1,0:T(8,128)(2,1)S(1)}, bf16[240,128]{1,0:T(8,128)(2,1)S(1)}, u32[]{:S(2)}, u32[]{:S(2)}) %collective-permute-start.2) | collective-permute-done | bytes 61472 | tf_op jit(solution)/shard_map/ppermute | solution.py:598
  16.1 0.1 collective-permute-start.8
  16.2 0.0 collective-permute-done.3.refs_0_.refs_4_
  16.2 2.1 %collective-permute-done.4.refs_1_.refs_5_ = bf16[240,128]{1,0:T(8,128)(2,1)S(1)} collective-permute-done((bf16[240,128]{1,0:T(8,128)(2,1)S(1)}, bf16[240,128]{1,0:T(8,128)(2,1)S(1)}, u32[]{:S(2)}, u32[]{:S(2)}) %collective-permute-start.4) | collective-permute-done | bytes 61472 | tf_op jit(solution)/shard_map/ppermute | solution.py:598
  18.3 0.1 collective-permute-done.5.refs_2_.refs_6_
  18.4 0.0 collective-permute-done.6.refs_3_.refs_7_
  18.4 0.1 collective-permute-start.7
  18.5 0.0 collective-permute-done.8.refs_8_
  18.5 1.0 %attend_own.1 = (f32[512,128]{1,0:T(8,128)S(1)}, f32[2,512,128]{2,1,0:T(8,128)S(1)}) custom-call(bf16[240,128]{1,0:T(8,128)(2,1)S(1)} %get-tuple-element.12.refs_0_, bf16[240,128]{1,0:T(8,128)(2,1)S(1)} %collective-permute-done.refs_1_, bf16[240,128]{1,0:T(8,128)(2,1)S(1)} %collective-permute-done.1.refs_2_, ...), custom_call_target="tpu_custom_call" | custom-call | flops 134217728 | bytes 917504 | tf_op jit(solution)/shard_map/attend_own/pallas_call | solution.py:199
  19.6 0.4 %collective-permute-done.7.refs_8_.refs_9_ = bf16[4,176,128]{2,1,0:T(8,128)(2,1)S(1)} collective-permute-done((bf16[4,176,128]{2,1,0:T(8,128)(2,1)S(1)}, bf16[4,176,128]{2,1,0:T(8,128)(2,1)S(1)}, u32[]{:S(2)}, u32[]{:S(2)}) %collective-permute-start.7) | collective-permute-done | bytes 180256 | tf_op jit(solution)/shard_map/ppermute | solution.py:603
  19.9 1.2 %attend.1 = bf16[8,64,128]{2,1,0:T(8,128)(2,1)} custom-call(bf16[240,128]{1,0:T(8,128)(2,1)S(1)} %get-tuple-element.12.refs_0_, bf16[240,128]{1,0:T(8,128)(2,1)S(1)} %collective-permute-done.refs_1_, bf16[240,128]{1,0:T(8,128)(2,1)S(1)} %collective-permute-done.1.refs_2_, bf16[240,128]{1,0:T(8,128)(2,1)S(1)} %collective-permute-done.2.refs_3_, ...), custom_call_target="tpu_custom_call" | custom-call | flops 134217728 | bytes 917504 | tf_op jit(solution)/shard_map/attend/pallas_call | solution.py:211
  21.1 4.2 %all-to-all-start = ((bf16[8,64,128]{2,1,0:T(8,128)(2,1)}), bf16[8,64,128]{2,1,0:T(8,128)(2,1)S(1)}, u32[]{:S(2)}, u32[]{:S(2)}) async-start(bf16[8,64,128]{2,1,0:T(8,128)(2,1)} %attend.1), calls=%async_computation | async-start | bytes 262144 | tf_op jit(solution)/shard_map/all_to_all | solution.py:607
  25.3 8.0 %decode_tile.1 = bf16[2,8,40,384]{3,2,1,0:T(8,128)(2,1)} custom-call(bf16[240,128]{1,0:T(8,128)(2,1)S(1)} %get-tuple-element.12.refs_0_, bf16[240,128]{1,0:T(8,128)(2,1)S(1)} %collective-permute-done.refs_1_, bf16[240,128]{1,0:T(8,128)(2,1)S(1)} %collective-permute-done.1.refs_2_, bf16[240,128]{1,0:T(8,128)(2,1)S(1)} %collective-permute-done.2.refs_3_, ...), custom_call_target="tpu_custom_call" | custom-call | flops 2548039680 | bytes 5308416 | tf_op jit(solution)/shard_map/decode_tile/pallas_call | solution.py:539
  33.2 0.0 all-to-all-done.in_ref
  33.3 0.7 %unpack_heads.1 = bf16[64,1024]{1,0:T(8,128)(2,1)} custom-call(bf16[8,64,128]{2,1,0:T(8,128)(2,1)S(1)} %all-to-all-done.in_ref), custom_call_target="tpu_custom_call" | custom-call | tf_op jit(solution)/shard_map/unpack_heads/pallas_call | solution.py:241
  (2 shorter events, 0.0 us)
Async XLA Ops:
  1.8 10.7 %collective-permute-start = (bf16[240,128]{1,0:T(8,128)(2,1)S(1)}, bf16[240,128]{1,0:T(8,128)(2,1)S(1)}, u32[]{:S(2)}, u32[]{:S(2)}) collective-permute-start(bf16[240,128]{1,0:T(8,128)(2,1)S(1)} %get-tuple-element.13), channel_id=1, source_target_pairs={{0,8},{1,9},{2,10},{3,11},{4,12},{5,13},{6,14},{7,15},{8,0},{9,1},... | collective-permute-start | bytes 184328 | tf_op jit(solution)/shard_map/ppermute | solution.py:598
  5.9 6.9 %collective-permute-start.1 = (bf16[240,128]{1,0:T(8,128)(2,1)S(1)}, bf16[240,128]{1,0:T(8,128)(2,1)S(1)}, u32[]{:S(2)}, u32[]{:S(2)}) collective-permute-start(bf16[240,128]{1,0:T(8,128)(2,1)S(1)} %get-tuple-element.14), channel_id=1, source_target_pairs={{0,4},{1,5},{2,6},{3,7},{4,0},{5,1},{6,2},{7,3},{8,12},{9,13},{10,... | collective-permute-start | bytes 184328 | tf_op jit(solution)/shard_map/ppermute | solution.py:598
  7.4 8.7 %collective-permute-start.2 = (bf16[240,128]{1,0:T(8,128)(2,1)S(1)}, bf16[240,128]{1,0:T(8,128)(2,1)S(1)}, u32[]{:S(2)}, u32[]{:S(2)}) collective-permute-start(bf16[240,128]{1,0:T(8,128)(2,1)S(1)} %get-tuple-element.15), channel_id=1, source_target_pairs={{0,10},{1,11},{2,8},{3,9},{4,14},{5,15},{6,12},{7,13},{8,2},{9,3},... | collective-permute-start | bytes 184328 | tf_op jit(solution)/shard_map/ppermute | solution.py:598
  8.7 7.5 %collective-permute-start.3 = (bf16[240,128]{1,0:T(8,128)(2,1)S(1)}, bf16[240,128]{1,0:T(8,128)(2,1)S(1)}, u32[]{:S(2)}, u32[]{:S(2)}) collective-permute-start(bf16[240,128]{1,0:T(8,128)(2,1)S(1)} %get-tuple-element.16), channel_id=1, source_target_pairs={{0,12},{1,13},{2,14},{3,15},{4,8},{5,9},{6,10},{7,11},{8,4},{9,5},... | collective-permute-start | bytes 184328 | tf_op jit(solution)/shard_map/ppermute | solution.py:598
  11.2 7.1 %collective-permute-start.4 = (bf16[240,128]{1,0:T(8,128)(2,1)S(1)}, bf16[240,128]{1,0:T(8,128)(2,1)S(1)}, u32[]{:S(2)}, u32[]{:S(2)}) collective-permute-start(bf16[240,128]{1,0:T(8,128)(2,1)S(1)} %get-tuple-element.17), channel_id=1, source_target_pairs={{0,14},{1,15},{2,12},{3,13},{4,10},{5,11},{6,8},{7,9},{8,6},{9,7},... | collective-permute-start | bytes 184328 | tf_op jit(solution)/shard_map/ppermute | solution.py:598
  12.5 5.9 %collective-permute-start.5 = (bf16[240,128]{1,0:T(8,128)(2,1)S(1)}, bf16[240,128]{1,0:T(8,128)(2,1)S(1)}, u32[]{:S(2)}, u32[]{:S(2)}) collective-permute-start(bf16[240,128]{1,0:T(8,128)(2,1)S(1)} %get-tuple-element.18), channel_id=1, source_target_pairs={{0,6},{1,7},{2,4},{3,5},{4,2},{5,3},{6,0},{7,1},{8,14},{9,15},{10,... | collective-permute-start | bytes 184328 | tf_op jit(solution)/shard_map/ppermute | solution.py:598
  12.8 5.6 %collective-permute-start.6 = (bf16[240,128]{1,0:T(8,128)(2,1)S(1)}, bf16[240,128]{1,0:T(8,128)(2,1)S(1)}, u32[]{:S(2)}, u32[]{:S(2)}) collective-permute-start(bf16[240,128]{1,0:T(8,128)(2,1)S(1)} %get-tuple-element.19), channel_id=1, source_target_pairs={{0,2},{1,3},{2,0},{3,1},{4,6},{5,7},{6,4},{7,5},{8,10},{9,11},{10,... | collective-permute-start | bytes 184328 | tf_op jit(solution)/shard_map/ppermute | solution.py:598
  16.1 2.4 %collective-permute-start.8 = (bf16[4,176,128]{2,1,0:T(8,128)(2,1)S(1)}, bf16[4,176,128]{2,1,0:T(8,128)(2,1)S(1)}, u32[]{:S(2)}, u32[]{:S(2)}) collective-permute-start(bf16[4,176,128]{2,1,0:T(8,128)(2,1)S(1)} %join.3), channel_id=1, source_target_pairs={{0,1},{1,0},{2,3},{3,2},{4,5},{5,4},{6,7},{7,6},{8,9},{9,8},{10,11... | collective-permute-start | bytes 540680 | tf_op jit(solution)/shard_map/ppermute | solution.py:603
  18.4 1.5 %collective-permute-start.7 = (bf16[4,176,128]{2,1,0:T(8,128)(2,1)S(1)}, bf16[4,176,128]{2,1,0:T(8,128)(2,1)S(1)}, u32[]{:S(2)}, u32[]{:S(2)}) collective-permute-start(bf16[4,176,128]{2,1,0:T(8,128)(2,1)S(1)} %join.2), channel_id=1, source_target_pairs={{0,1},{1,0},{2,3},{3,2},{4,5},{5,4},{6,7},{7,6},{8,9},{9,8},{10,11... | collective-permute-start | bytes 540680 | tf_op jit(solution)/shard_map/ppermute | solution.py:603
  21.1 12.2 %all-to-all-start = ((bf16[8,64,128]{2,1,0:T(8,128)(2,1)}), bf16[8,64,128]{2,1,0:T(8,128)(2,1)S(1)}, u32[]{:S(2)}, u32[]{:S(2)}) async-start(bf16[8,64,128]{2,1,0:T(8,128)(2,1)} %attend.1), calls=%async_computation | async-start | bytes 262144 | tf_op jit(solution)/shard_map/all_to_all | solution.py:607

commit v22 on v20

--- a/solution.py
+++ b/solution.py
@@ -91,7 +91,7 @@
 
 def sending_order(chips):
     far, near = list(range(chips // 2, chips)), list(range(1, chips // 2))
-    return [0, *far[:1], *near[1:2], *far[1:], *near[2:], *near[:1]]
+    return [0, *far[:1], *near[1:2], *far[2:3], *far[1:2], *far[3:], *near[2:], *near[:1]]
 
 
 def xor_pairs(distance):

time: 34.2 us -> 35.2 us (1.029)
  starting transfers between devices: 16.6 us -> 17.4 us
    all_to_all x1, starting transfers between devices: 4.2 us -> 4.76 us  [on_device(): lax.all_to_all(mixed, 'seq', 0, 0, axis_index_groups=groups, tiled=True)]
  transfers between devices with their start and end apart: 10 -> 10, of which waited for: 4 -> 4; matrix products, arithmetic and copies ran while one was open for 0% -> 0% of each run, Pallas kernels for 27% -> 26%
where the time goes in v22:
time: 35.2 us; the launch traced here: 34.9 us
  starting transfers between devices  17.4 us (49%)
  Pallas kernels  12.2 us (35%)
  waiting for transfers between devices  4.66 us (13%)
  between operations  0.71 us (2%)
    ppermute x7, starting transfers between devices, on_device(): lax.ppermute(piece, 'seq', xor_pairs(2 * m))  12.5 us
    pallas_call x1, Pallas kernels, decode_tile(): pl.pallas_call(functools.partial(decode_body, grid_rows, width, share_row...  7.95 us
    all_to_all x1, starting transfers between devices, on_device(): lax.all_to_all(mixed, 'seq', 0, 0, axis_index_groups=groups, tiled=True)  4.76 us
    ppermute x7, waiting for transfers between devices, on_device(): lax.ppermute(piece, 'seq', xor_pairs(2 * m))  4.45 us
    pallas_call x1, Pallas kernels, attend(): pl.pallas_call(functools.partial(attend_own_body, token_rows), in_specs=[...  1.19 us
    pallas_call x1, Pallas kernels, attend(): pl.pallas_call(attend_body, in_specs=[vmem] * (members + 3), out_specs=pl...  1.18 us
    pallas_call x1, Pallas kernels, pack_heads(): pl.pallas_call(pack_body, in_specs=[hbm] * 4, out_specs=[vmem] * heads, o...  1.12 us
    pallas_call x1, Pallas kernels, unpack_heads(): pl.pallas_call(unpack_body, in_specs=[pl.BlockSpec(memory_space=pltpu.VME...  0.72 us
  transfers between devices with their start and end apart: 10, of which 4 were waited for; matrix products, arithmetic and copies ran while one was open for 0% of the time, Pallas kernels for 26%

profile of v22, /device:TPU:0, one launch (start us, length us, event | category | flops | bytes accessed | tf_op | source)
XLA Modules:
  0.0 34.9 jit_solution(16483471571123352715)
XLA Ops:
  0.6 1.1 %pack_heads.1 = (bf16[240,128]{1,0:T(8,128)(2,1)S(1)}, bf16[240,128]{1,0:T(8,128)(2,1)S(1)}, bf16[240,128]{1,0:T(8,128)(2,1)S(1)}, bf16[240,128]{1,0:T(8,128)(2,...) custom-call(bf16[64,2048]{1,0:T(8,128)(2,1)} %query_ref.1, ...), custom_call_target="tpu_custom_call" | custom-call | tf_op jit(solution)/shard_map/pack_heads/pallas_call | solution.py:77
  1.8 4.1 %collective-permute-start = (bf16[240,128]{1,0:T(8,128)(2,1)S(1)}, bf16[240,128]{1,0:T(8,128)(2,1)S(1)}, u32[]{:S(2)}, u32[]{:S(2)}) collective-permute-start(bf16[240,128]{1,0:T(8,128)(2,1)S(1)} %get-tuple-element.13), channel_id=1, source_target_pairs={{0,8},{1,9},{2,10},{3,11},{4,12},{5,13},{6,14},{7,15},{8,0},{9,1},... | collective-permute-start | bytes 184328 | tf_op jit(solution)/shard_map/ppermute | solution.py:598
  5.9 1.6 %collective-permute-start.1 = (bf16[240,128]{1,0:T(8,128)(2,1)S(1)}, bf16[240,128]{1,0:T(8,128)(2,1)S(1)}, u32[]{:S(2)}, u32[]{:S(2)}) collective-permute-start(bf16[240,128]{1,0:T(8,128)(2,1)S(1)} %get-tuple-element.14), channel_id=1, source_target_pairs={{0,4},{1,5},{2,6},{3,7},{4,0},{5,1},{6,2},{7,3},{8,12},{9,13},{10,... | collective-permute-start | bytes 184328 | tf_op jit(solution)/shard_map/ppermute | solution.py:598
  7.4 0.0 collective-permute-start.2
  7.4 2.8 %collective-permute-start.3 = (bf16[240,128]{1,0:T(8,128)(2,1)S(1)}, bf16[240,128]{1,0:T(8,128)(2,1)S(1)}, u32[]{:S(2)}, u32[]{:S(2)}) collective-permute-start(bf16[240,128]{1,0:T(8,128)(2,1)S(1)} %get-tuple-element.16), channel_id=1, source_target_pairs={{0,10},{1,11},{2,8},{3,9},{4,14},{5,15},{6,12},{7,13},{8,2},{9,3},... | collective-permute-start | bytes 184328 | tf_op jit(solution)/shard_map/ppermute | solution.py:598
  10.3 1.9 %collective-permute-start.4 = (bf16[240,128]{1,0:T(8,128)(2,1)S(1)}, bf16[240,128]{1,0:T(8,128)(2,1)S(1)}, u32[]{:S(2)}, u32[]{:S(2)}) collective-permute-start(bf16[240,128]{1,0:T(8,128)(2,1)S(1)} %get-tuple-element.17), channel_id=1, source_target_pairs={{0,14},{1,15},{2,12},{3,13},{4,10},{5,11},{6,8},{7,9},{8,6},{9,7},... | collective-permute-start | bytes 184328 | tf_op jit(solution)/shard_map/ppermute | solution.py:598
  12.2 0.0 collective-permute-done.refs_1_
  12.2 0.8 %collective-permute-start.5 = (bf16[240,128]{1,0:T(8,128)(2,1)S(1)}, bf16[240,128]{1,0:T(8,128)(2,1)S(1)}, u32[]{:S(2)}, u32[]{:S(2)}) collective-permute-start(bf16[240,128]{1,0:T(8,128)(2,1)S(1)} %get-tuple-element.18), channel_id=1, source_target_pairs={{0,6},{1,7},{2,4},{3,5},{4,2},{5,3},{6,0},{7,1},{8,14},{9,15},{10,... | collective-permute-start | bytes 184328 | tf_op jit(solution)/shard_map/ppermute | solution.py:598
  13.0 0.0 collective-permute-done.1.refs_2_
  13.0 1.2 %collective-permute-start.6 = (bf16[240,128]{1,0:T(8,128)(2,1)S(1)}, bf16[240,128]{1,0:T(8,128)(2,1)S(1)}, u32[]{:S(2)}, u32[]{:S(2)}) collective-permute-start(bf16[240,128]{1,0:T(8,128)(2,1)S(1)} %get-tuple-element.19), channel_id=1, source_target_pairs={{0,2},{1,3},{2,0},{3,1},{4,6},{5,7},{6,4},{7,5},{8,10},{9,11},{10,... | collective-permute-start | bytes 184328 | tf_op jit(solution)/shard_map/ppermute | solution.py:598
  14.2 0.0 collective-permute-done.2.refs_3_
  14.2 0.1 collective-permute-start.8
  14.3 3.4 %collective-permute-done.3.refs_0_.refs_4_ = bf16[240,128]{1,0:T(8,128)(2,1)S(1)} collective-permute-done((bf16[240,128]{1,0:T(8,128)(2,1)S(1)}, bf16[240,128]{1,0:T(8,128)(2,1)S(1)}, u32[]{:S(2)}, u32[]{:S(2)}) %collective-permute-start.3) | collective-permute-done | bytes 61472 | tf_op jit(solution)/shard_map/ppermute | solution.py:598
  17.8 0.0 collective-permute-done.4.refs_1_.refs_5_
  17.8 0.5 %collective-permute-done.5.refs_2_.refs_6_ = bf16[240,128]{1,0:T(8,128)(2,1)S(1)} collective-permute-done((bf16[240,128]{1,0:T(8,128)(2,1)S(1)}, bf16[240,128]{1,0:T(8,128)(2,1)S(1)}, u32[]{:S(2)}, u32[]{:S(2)}) %collective-permute-start.5) | collective-permute-done | bytes 61472 | tf_op jit(solution)/shard_map/ppermute | solution.py:598
  18.2 0.5 %collective-permute-done.6.refs_3_.refs_7_ = bf16[240,128]{1,0:T(8,128)(2,1)S(1)} collective-permute-done((bf16[240,128]{1,0:T(8,128)(2,1)S(1)}, bf16[240,128]{1,0:T(8,128)(2,1)S(1)}, u32[]{:S(2)}, u32[]{:S(2)}) %collective-permute-start.6) | collective-permute-done | bytes 61472 | tf_op jit(solution)/shard_map/ppermute | solution.py:598
  18.8 0.1 collective-permute-start.7
  18.9 0.0 collective-permute-done.8.refs_8_
  18.9 1.2 %attend_own.1 = (f32[512,128]{1,0:T(8,128)S(1)}, f32[2,512,128]{2,1,0:T(8,128)S(1)}) custom-call(bf16[240,128]{1,0:T(8,128)(2,1)S(1)} %get-tuple-element.12.refs_0_, bf16[240,128]{1,0:T(8,128)(2,1)S(1)} %collective-permute-done.refs_1_, bf16[240,128]{1,0:T(8,128)(2,1)S(1)} %collective-permute-done.1.refs_2_, ...), custom_call_target="tpu_custom_call" | custom-call | flops 134217728 | bytes 917504 | tf_op jit(solution)/shard_map/attend_own/pallas_call | solution.py:199
  20.1 0.2 collective-permute-done.7.refs_8_.refs_9_
  20.3 1.2 %attend.1 = bf16[8,64,128]{2,1,0:T(8,128)(2,1)} custom-call(bf16[240,128]{1,0:T(8,128)(2,1)S(1)} %get-tuple-element.12.refs_0_, bf16[240,128]{1,0:T(8,128)(2,1)S(1)} %collective-permute-done.refs_1_, bf16[240,128]{1,0:T(8,128)(2,1)S(1)} %collective-permute-done.1.refs_2_, bf16[240,128]{1,0:T(8,128)(2,1)S(1)} %collective-permute-done.2.refs_3_, ...), custom_call_target="tpu_custom_call" | custom-call | flops 134217728 | bytes 917504 | tf_op jit(solution)/shard_map/attend/pallas_call | solution.py:211
  21.5 4.8 %all-to-all-start = ((bf16[8,64,128]{2,1,0:T(8,128)(2,1)}), bf16[8,64,128]{2,1,0:T(8,128)(2,1)S(1)}, u32[]{:S(2)}, u32[]{:S(2)}) async-start(bf16[8,64,128]{2,1,0:T(8,128)(2,1)} %attend.1), calls=%async_computation | async-start | bytes 262144 | tf_op jit(solution)/shard_map/all_to_all | solution.py:607
  26.2 7.9 %decode_tile.1 = bf16[2,8,40,384]{3,2,1,0:T(8,128)(2,1)} custom-call(bf16[240,128]{1,0:T(8,128)(2,1)S(1)} %get-tuple-element.12.refs_0_, bf16[240,128]{1,0:T(8,128)(2,1)S(1)} %collective-permute-done.refs_1_, bf16[240,128]{1,0:T(8,128)(2,1)S(1)} %collective-permute-done.1.refs_2_, bf16[240,128]{1,0:T(8,128)(2,1)S(1)} %collective-permute-done.2.refs_3_, ...), custom_call_target="tpu_custom_call" | custom-call | flops 2548039680 | bytes 5308416 | tf_op jit(solution)/shard_map/decode_tile/pallas_call | solution.py:539
  34.2 0.0 all-to-all-done.in_ref
  34.2 0.7 %unpack_heads.1 = bf16[64,1024]{1,0:T(8,128)(2,1)} custom-call(bf16[8,64,128]{2,1,0:T(8,128)(2,1)S(1)} %all-to-all-done.in_ref), custom_call_target="tpu_custom_call" | custom-call | tf_op jit(solution)/shard_map/unpack_heads/pallas_call | solution.py:241
  (2 shorter events, 0.0 us)
Async XLA Ops:
  1.8 10.4 %collective-permute-start = (bf16[240,128]{1,0:T(8,128)(2,1)S(1)}, bf16[240,128]{1,0:T(8,128)(2,1)S(1)}, u32[]{:S(2)}, u32[]{:S(2)}) collective-permute-start(bf16[240,128]{1,0:T(8,128)(2,1)S(1)} %get-tuple-element.13), channel_id=1, source_target_pairs={{0,8},{1,9},{2,10},{3,11},{4,12},{5,13},{6,14},{7,15},{8,0},{9,1},... | collective-permute-start | bytes 184328 | tf_op jit(solution)/shard_map/ppermute | solution.py:598
  5.9 7.1 %collective-permute-start.1 = (bf16[240,128]{1,0:T(8,128)(2,1)S(1)}, bf16[240,128]{1,0:T(8,128)(2,1)S(1)}, u32[]{:S(2)}, u32[]{:S(2)}) collective-permute-start(bf16[240,128]{1,0:T(8,128)(2,1)S(1)} %get-tuple-element.14), channel_id=1, source_target_pairs={{0,4},{1,5},{2,6},{3,7},{4,0},{5,1},{6,2},{7,3},{8,12},{9,13},{10,... | collective-permute-start | bytes 184328 | tf_op jit(solution)/shard_map/ppermute | solution.py:598
  7.4 6.8 %collective-permute-start.2 = (bf16[240,128]{1,0:T(8,128)(2,1)S(1)}, bf16[240,128]{1,0:T(8,128)(2,1)S(1)}, u32[]{:S(2)}, u32[]{:S(2)}) collective-permute-start(bf16[240,128]{1,0:T(8,128)(2,1)S(1)} %get-tuple-element.15), channel_id=1, source_target_pairs={{0,12},{1,13},{2,14},{3,15},{4,8},{5,9},{6,10},{7,11},{8,4},{9,5},... | collective-permute-start | bytes 184328 | tf_op jit(solution)/shard_map/ppermute | solution.py:598
  7.4 10.3 %collective-permute-start.3 = (bf16[240,128]{1,0:T(8,128)(2,1)S(1)}, bf16[240,128]{1,0:T(8,128)(2,1)S(1)}, u32[]{:S(2)}, u32[]{:S(2)}) collective-permute-start(bf16[240,128]{1,0:T(8,128)(2,1)S(1)} %get-tuple-element.16), channel_id=1, source_target_pairs={{0,10},{1,11},{2,8},{3,9},{4,14},{5,15},{6,12},{7,13},{8,2},{9,3},... | collective-permute-start | bytes 184328 | tf_op jit(solution)/shard_map/ppermute | solution.py:598
  10.3 7.5 %collective-permute-start.4 = (bf16[240,128]{1,0:T(8,128)(2,1)S(1)}, bf16[240,128]{1,0:T(8,128)(2,1)S(1)}, u32[]{:S(2)}, u32[]{:S(2)}) collective-permute-start(bf16[240,128]{1,0:T(8,128)(2,1)S(1)} %get-tuple-element.17), channel_id=1, source_target_pairs={{0,14},{1,15},{2,12},{3,13},{4,10},{5,11},{6,8},{7,9},{8,6},{9,7},... | collective-permute-start | bytes 184328 | tf_op jit(solution)/shard_map/ppermute | solution.py:598
  12.2 6.0 %collective-permute-start.5 = (bf16[240,128]{1,0:T(8,128)(2,1)S(1)}, bf16[240,128]{1,0:T(8,128)(2,1)S(1)}, u32[]{:S(2)}, u32[]{:S(2)}) collective-permute-start(bf16[240,128]{1,0:T(8,128)(2,1)S(1)} %get-tuple-element.18), channel_id=1, source_target_pairs={{0,6},{1,7},{2,4},{3,5},{4,2},{5,3},{6,0},{7,1},{8,14},{9,15},{10,... | collective-permute-start | bytes 184328 | tf_op jit(solution)/shard_map/ppermute | solution.py:598
  13.0 5.8 %collective-permute-start.6 = (bf16[240,128]{1,0:T(8,128)(2,1)S(1)}, bf16[240,128]{1,0:T(8,128)(2,1)S(1)}, u32[]{:S(2)}, u32[]{:S(2)}) collective-permute-start(bf16[240,128]{1,0:T(8,128)(2,1)S(1)} %get-tuple-element.19), channel_id=1, source_target_pairs={{0,2},{1,3},{2,0},{3,1},{4,6},{5,7},{6,4},{7,5},{8,10},{9,11},{10,... | collective-permute-start | bytes 184328 | tf_op jit(solution)/shard_map/ppermute | solution.py:598
  14.2 4.6 %collective-permute-start.8 = (bf16[4,176,128]{2,1,0:T(8,128)(2,1)S(1)}, bf16[4,176,128]{2,1,0:T(8,128)(2,1)S(1)}, u32[]{:S(2)}, u32[]{:S(2)}) collective-permute-start(bf16[4,176,128]{2,1,0:T(8,128)(2,1)S(1)} %join.3), channel_id=1, source_target_pairs={{0,1},{1,0},{2,3},{3,2},{4,5},{5,4},{6,7},{7,6},{8,9},{9,8},{10,11... | collective-permute-start | bytes 540680 | tf_op jit(solution)/shard_map/ppermute | solution.py:603
  18.8 1.5 %collective-permute-start.7 = (bf16[4,176,128]{2,1,0:T(8,128)(2,1)S(1)}, bf16[4,176,128]{2,1,0:T(8,128)(2,1)S(1)}, u32[]{:S(2)}, u32[]{:S(2)}) collective-permute-start(bf16[4,176,128]{2,1,0:T(8,128)(2,1)S(1)} %join.2), channel_id=1, source_target_pairs={{0,1},{1,0},{2,3},{3,2},{4,5},{5,4},{6,7},{7,6},{8,9},{9,8},{10,11... | collective-permute-start | bytes 540680 | tf_op jit(solution)/shard_map/ppermute | solution.py:603
  21.5 12.7 %all-to-all-start = ((bf16[8,64,128]{2,1,0:T(8,128)(2,1)}), bf16[8,64,128]{2,1,0:T(8,128)(2,1)S(1)}, u32[]{:S(2)}, u32[]{:S(2)}) async-start(bf16[8,64,128]{2,1,0:T(8,128)(2,1)} %attend.1), calls=%async_computation | async-start | bytes 262144 | tf_op jit(solution)/shard_map/all_to_all | solution.py:607
